TPU v7x, 32 devices: a whole 2x2x4 slice. The times are simulated.
32 devices in a mesh: tx: 4 (over z), ty: 8 (over y, x, core).
Axes of the slice: x: 2, y: 2, z: 4, core: 2. Of those that a mesh axis runs over, the one named last changes fastest.
Arguments:
- points: bfloat16 [32, 1024, 256], P(('tx', 'ty')), may hold values from -6 to 6
- counts: int32 [32], P(('tx', 'ty')), may hold values from 512 to 1024, as said below
- owner: int32 [32, 1024], P(('tx', 'ty')), may hold values from 0 to 31, as said below
- zorder: int32 [32, 2048], P(('tx', 'ty')), may hold values from 0 to 2047, as said below
- border: int32 [32, 4, 64], P(('tx', 'ty')), may hold values from 0 to 1023, as said below
- near: int32 [32, 16, 1024], P(('tx', 'ty')), may hold values from 0 to 1279, as said below
- w_near: bfloat16 [256, 256], replicated, may hold values from -0.375 to 0.375
- gain_one: float32 [256], replicated, may hold values from 0.1 to 1.9
- conv_w: bfloat16 [3, 8, 32, 32], replicated, may hold values from -0.625 to 0.625
- gain_two: float32 [256], replicated, may hold values from 0.1 to 1.9
- w_up: bfloat16 [256, 1024], replicated, may hold values from -0.375 to 0.375
- w_down: bfloat16 [1024, 256], replicated, may hold values from -0.1875 to 0.1875
- grad_out: bfloat16 [32, 1024, 256], P(('tx', 'ty')), may hold values from -6 to 6
Outputs:
- out_rows: bfloat16 [32, 1024, 256], P(('tx', 'ty'))
- grad_points: bfloat16 [32, 1024, 256], P(('tx', 'ty'))
- grad_w_near: float32 [256, 256], replicated
- grad_gain_one: float32 [256], replicated
- grad_conv: float32 [3, 8, 32, 32], replicated
- grad_gain_two: float32 [256], replicated
- grad_w_up: float32 [256, 1024], replicated
- grad_w_down: float32 [1024, 256], replicated
Inputs may be any that keep to these rules, and one draw needn't show every extreme that they name: `counts`: every tile has at least half of its slots live, and some tile has all of them live. Only live rows count. Among the live rows of one tile at most 64 name the same owner. One particular owner receives exactly 64 live rows from every tile; every other owner receives at most 64 live rows from each tile, so its receive buffer may be partly empty. `zorder`: each owner's entry is a permutation of its 2048 receive slots whose first entries name exactly the filled slots. `border`: each list names distinct live rows of its tile; lists toward a side outside the grid are never read. `near`: indices below 1024 name live rows of the tile; the others name halo rows of blocks whose neighbour tile exists.
All inputs are finite; a program needn't handle non-finite values.
Results may differ from a plain program's by a relative error of at most 0.015.
Values may be sent and summed in bfloat16 or wider, within the bound.
No kernel may reach another device: no remote copies, remote signals or barrier semaphores. Data moves between devices by JAX's collectives and lax.ppermute only.
A program may use at most 64 MiB of HBM per device.

v0:
```python
import functools
import math

import jax
import jax.numpy as jnp
from jax import lax
from jax.experimental import pallas as pl
from jax.experimental.pallas import tpu as pltpu
from jax.sharding import PartitionSpec as P

PATCH = 1024
CHUNK = 256
LANES = 128
PAD = 8

eps_norm = 1e-06
gelu_coef = 0.7978845608028654
cubic_coef = 0.044715

bf16 = jnp.bfloat16
f32 = jnp.float32
NN = (((1,), (0,)), ((), ()))
NT = (((1,), (1,)), ((), ()))
TN = (((0,), (0,)), ((), ()))


def dot(left, right, dims=NN):
    return lax.dot_general(left, right, dims, preferred_element_type=f32)


def iota(shape, axis):
    return lax.broadcasted_iota(jnp.int32, shape, axis)


def marks(mask):
    return jnp.where(mask, 1.0, 0.0).astype(bf16)


def gelu_parts(value):
    square = value * value
    tangent = jnp.tanh(value * (gelu_coef + (gelu_coef * cubic_coef) * square))
    return square, tangent


def gelu_tanh(value):
    _, tangent = gelu_parts(value)
    half = 0.5 * value
    return half + half * tangent


def slope_of(value, square, tangent):
    inner_slope = gelu_coef + (3.0 * gelu_coef * cubic_coef) * square
    return 0.5 * (1.0 + tangent) + (0.5 * value) * (1.0 - tangent * tangent) * inner_slope


def inverse_rms(value):
    return lax.rsqrt(jnp.mean(value * value, axis=-1, keepdims=True) + eps_norm)


def column_of(row, count):
    return jnp.transpose(jnp.broadcast_to(row, (LANES, count)))


def pick_rows(column, depth):
    count = column.shape[0]
    lane = iota((count, LANES), 1)
    return jnp.concatenate(
        [marks(column == lane + base) for base in range(0, depth, LANES)], axis=1
    )


def mark_slots(row, start, count):
    return marks(iota((count, row.shape[1]), 0) + start == row)


def chunks(total):
    return lax.div(total, CHUNK)


def route_kernel(counts_ref, owner_ref, lists_ref, points_ref, slots_ref, sent_ref, *, tiles, capacity):
    rows = owner_ref.shape[1]
    live = iota((1, rows), 1) < counts_ref[0]
    owned = jnp.where(live, owner_ref[...], tiles)
    members = owned == iota((tiles, rows), 0)
    earlier = marks(iota((rows, rows), 0) < iota((rows, rows), 1))
    before = dot(marks(members), earlier)
    rank = jnp.sum(jnp.where(members, before, 0.0), axis=0, keepdims=True)
    slots_ref[...] = jnp.where(live, owned * capacity + rank.astype(jnp.int32), -1)
    lists = lists_ref[...]
    chosen = marks(iota((rows, lists.shape[1]), 0) == lists)
    sent_ref[...] = dot(chosen, points_ref[...], TN).astype(bf16)


def pack_kernel(slots_ref, rows_ref, packed_ref):
    slots = slots_ref[...]

    def one(at, _):
        start = pl.multiple_of(at * CHUNK, CHUNK)
        packed_ref[pl.ds(start, CHUNK), :] = dot(
            mark_slots(slots, start, CHUNK), rows_ref[...]
        ).astype(bf16)
        return 0

    lax.fori_loop(0, packed_ref.shape[0] // CHUNK, one, 0)


def unpack_kernel(slots_ref, packed_ref, rows_ref):
    for start in range(0, rows_ref.shape[0], CHUNK):
        column = column_of(slots_ref[:, start : start + CHUNK], CHUNK)
        rows_ref[pl.ds(start, CHUNK), :] = dot(
            pick_rows(column, packed_ref.shape[0]), packed_ref[...]
        ).astype(bf16)


def count_kernel(near_ref, table_ref):
    neighbours, rows = near_ref.shape
    step = 16
    zero = jnp.zeros((step, LANES), bf16)
    one = jnp.ones((step, LANES), bf16)

    def block(at, _):
        lane_block = lax.rem(at, rows // LANES)
        row_block = lax.div(at, rows // LANES)
        lane_at = pl.multiple_of(lane_block * LANES, LANES)
        row_at = pl.multiple_of(row_block * CHUNK, CHUNK)
        local = (near_ref[:, pl.ds(lane_at, LANES)] - row_at).astype(f32)
        spread = [
            jnp.broadcast_to(local[k : k + 1, :], (step, LANES)).astype(bf16)
            for k in range(neighbours)
        ]
        base = iota((step, LANES), 0).astype(f32)
        for inner in range(0, CHUNK, step):
            here = (base + float(inner)).astype(bf16)
            total = zero
            for k in range(neighbours):
                total = total + jnp.where(spread[k] == here, one, zero)
            table_ref[pl.ds(row_at + inner, step), pl.ds(lane_at, LANES)] = total
        return 0

    lax.fori_loop(0, (rows // LANES) * (table_ref.shape[0] // CHUNK), block, 0)


def lift_kernel(
    slots_ref, points_ref, halo0, halo1, halo2, halo3, table_ref, w_ref, average_ref, pre_ref, packed_ref,
    lifted_ref, *, neighbours
):
    ext = jnp.concatenate([points_ref[...], halo0[...], halo1[...], halo2[...], halo3[...]], axis=0)
    average = (dot(ext, table_ref[...], TN) * (1.0 / neighbours)).astype(bf16)
    average_ref[...] = average
    pre_act = dot(average, w_ref[...], TN)
    pre_ref[...] = pre_act
    lifted_ref[...] = (points_ref[...].astype(f32) + gelu_tanh(pre_act)).astype(bf16)
    pack_kernel(slots_ref, lifted_ref, packed_ref)


def tile_back_kernel(
    slots_ref, back_ref, table_ref, average_ref, pre_ref, w_ref, near_ref, row_ref, halo_ref,
    act_ref, spread_ref, *, neighbours
):
    rows = row_ref.shape[0]
    for start in range(0, rows, CHUNK):
        here = pl.ds(start, CHUNK)
        column = column_of(slots_ref[:, start : start + CHUNK], CHUNK)
        lifted_grad = dot(pick_rows(column, back_ref.shape[0]), back_ref[...])
        row_ref[here, :] = lifted_grad
        value = pre_ref[here, :]
        square, tangent = gelu_parts(value)
        act_grad = (lifted_grad * slope_of(value, square, tangent)).astype(bf16)
        act_ref[here, :] = act_grad
        spread_ref[here, :] = (dot(act_grad, w_ref[...], NT) * (1.0 / neighbours)).astype(bf16)
    near_ref[...] = dot(average_ref[...], act_ref[...]).astype(near_ref.dtype)
    for start in range(0, rows, CHUNK):
        here = pl.ds(start, CHUNK)
        row_ref[here, :] = row_ref[here, :] + dot(table_ref[here, :], spread_ref[...])
    halo_ref[...] = dot(table_ref[rows:, :], spread_ref[...]).astype(bf16)


def finish_kernel(lists_ref, row_ref, back0, back1, back2, back3, out_ref):
    lists = lists_ref[...]
    came = jnp.concatenate([back0[...], back1[...], back2[...], back3[...]], axis=0)
    chosen = marks(iota((row_ref.shape[0], lists.shape[1]), 0) == lists)
    out_ref[...] = (row_ref[...] + dot(chosen, came)).astype(bf16)


def full_taps(conv_ref, groups, inner):
    width = groups * inner
    rows = conv_ref.shape[0]
    repeat = marks(lax.rem(iota((inner, width), 1), inner) == iota((inner, width), 0))
    wide = dot(conv_ref[...], repeat)
    row_group = lax.div(lax.rem(iota((rows, width), 0), width), inner)
    same = row_group == lax.div(iota((rows, width), 1), inner)
    return jnp.where(same, wide, 0.0).astype(bf16)


def padded_zeros(ref):
    edge = jnp.zeros((PAD, ref.shape[1]), f32)
    ref[0:PAD, :] = edge
    ref[PAD + PATCH :, :] = edge


def write_back(zorder_ref, rows_ref, out_ref):
    zorder = zorder_ref[...]

    def one(at, _):
        start = pl.multiple_of(at * CHUNK, CHUNK)
        out_ref[pl.ds(start, CHUNK), :] = dot(
            mark_slots(zorder, start, CHUNK), rows_ref[...]
        ).astype(bf16)
        return 0

    lax.fori_loop(0, out_ref.shape[0] // CHUNK, one, 0)


def forward_kernel(
    zorder_ref, lifted_ref, grad_ref, conv_ref, gain_one_ref, gain_two_ref, up_ref, down_ref,
    serial_ref, out_grad_ref, state_ref, back_ref,
    taps_ref, normed_ref, before_ref, here_ref, after_ref, result_ref, *, groups, inner
):
    slots, width = lifted_ref.shape
    taps_ref[...] = full_taps(conv_ref, groups, inner)
    padded_zeros(before_ref)
    padded_zeros(after_ref)

    def patch(at, _):
        origin = pl.multiple_of(at * PATCH, PATCH)
        for start in range(0, PATCH, CHUNK):
            column = column_of(zorder_ref[:, pl.ds(origin + start, CHUNK)], CHUNK)
            chosen = pick_rows(column, slots)
            serial = dot(chosen, lifted_ref[...])
            serial_ref[pl.ds(origin + start, CHUNK), :] = serial.astype(bf16)
            out_grad_ref[pl.ds(origin + start, CHUNK), :] = dot(chosen, grad_ref[...]).astype(bf16)
            normed = (serial * inverse_rms(serial) * gain_one_ref[...]).astype(bf16)
            before_ref[pl.ds(PAD + start, CHUNK), :] = dot(normed, taps_ref[0:width, :])
            here_ref[pl.ds(start, CHUNK), :] = dot(normed, taps_ref[width : 2 * width, :])
            after_ref[pl.ds(PAD + start, CHUNK), :] = dot(normed, taps_ref[2 * width :, :])
        for start in range(0, PATCH, CHUNK):
            place = pl.ds(origin + start, CHUNK)
            mixed = (
                before_ref[pl.ds(PAD + start - 1, CHUNK), :]
                + here_ref[pl.ds(start, CHUNK), :]
                + after_ref[pl.ds(PAD + start + 1, CHUNK), :]
            )
            state = serial_ref[place, :].astype(f32) + mixed
            state_ref[place, :] = state
            second = (state * inverse_rms(state) * gain_two_ref[...]).astype(bf16)
            hidden = gelu_tanh(dot(second, up_ref[...])).astype(bf16)
            result_ref[place, :] = (state + dot(hidden, down_ref[...])).astype(bf16)
        return 0

    lax.fori_loop(0, slots // PATCH, patch, 0)
    write_back(zorder_ref, result_ref, back_ref)


def backward_kernel(
    zorder_ref, serial_ref, out_grad_ref, state_ref, conv_ref, gain_one_ref, gain_two_ref, up_ref, down_ref,
    back_ref, weights_ref,
    taps_ref, second_ref, hidden_ref, pre_grad_ref, state_grad_ref, mixed_ref, before_ref, here_ref,
    after_ref, normed_ref, serial_grad_ref, conv_sum_ref, gains_ref, *, groups, inner
):
    slots, width = serial_ref.shape
    hidden_width = up_ref.shape[1]
    taps_ref[...] = full_taps(conv_ref, groups, inner)
    padded_zeros(before_ref)
    padded_zeros(after_ref)
    padded_zeros(mixed_ref)
    conv_sum_ref[...] = jnp.zeros_like(conv_sum_ref)
    gains_ref[...] = jnp.zeros_like(gains_ref)

    def patch(at, _):
        origin = pl.multiple_of(at * PATCH, PATCH)
        for start in range(0, PATCH, CHUNK):
            place = pl.ds(origin + start, CHUNK)
            state = state_ref[place, :]
            scale_two = inverse_rms(state)
            unit_two = state * scale_two
            second = (unit_two * gain_two_ref[...]).astype(bf16)
            second_ref[place, :] = second
            value = dot(second, up_ref[...])
            square, tangent = gelu_parts(value)
            half = 0.5 * value
            hidden_ref[place, :] = (half + half * tangent).astype(bf16)
            out_grad = out_grad_ref[place, :]
            hidden_grad = dot(out_grad, down_ref[...], NT).astype(bf16).astype(f32)
            pre_grad = (hidden_grad * slope_of(value, square, tangent)).astype(bf16)
            pre_grad_ref[place, :] = pre_grad
            second_grad = dot(pre_grad, up_ref[...], NT).astype(bf16).astype(f32)
            weighted = second_grad * gain_two_ref[...]
            gains_ref[1:2, :] += jnp.sum(second_grad * unit_two, axis=0, keepdims=True)
            middle = jnp.mean(weighted * unit_two, axis=-1, keepdims=True)
            state_grad = out_grad.astype(f32) + scale_two * (weighted - unit_two * middle)
            state_grad_ref[pl.ds(start, CHUNK), :] = state_grad
            mixed_grad = state_grad.astype(bf16)
            mixed_ref[pl.ds(PAD + start, CHUNK), :] = mixed_grad.astype(f32)
            before_ref[pl.ds(PAD + start, CHUNK), :] = dot(mixed_grad, taps_ref[0:width, :], NT)
            here_ref[pl.ds(start, CHUNK), :] = dot(mixed_grad, taps_ref[width : 2 * width, :], NT)
            after_ref[pl.ds(PAD + start, CHUNK), :] = dot(mixed_grad, taps_ref[2 * width :, :], NT)
        for start in range(0, PATCH, CHUNK):
            place = pl.ds(origin + start, CHUNK)
            serial = serial_ref[place, :].astype(f32)
            scale_one = inverse_rms(serial)
            unit_one = serial * scale_one
            normed_ref[pl.ds(start, CHUNK), :] = (unit_one * gain_one_ref[...]).astype(bf16)
            normed_grad = (
                before_ref[pl.ds(PAD + start + 1, CHUNK), :]
                + here_ref[pl.ds(start, CHUNK), :]
                + after_ref[pl.ds(PAD + start - 1, CHUNK), :]
            ).astype(bf16).astype(f32)
            gains_ref[0:1, :] += jnp.sum(normed_grad * unit_one, axis=0, keepdims=True)
            weighted = normed_grad * gain_one_ref[...]
            middle = jnp.mean(weighted * unit_one, axis=-1, keepdims=True)
            serial_grad_ref[place, :] = (
                state_grad_ref[pl.ds(start, CHUNK), :] + scale_one * (weighted - unit_one * middle)
            ).astype(bf16)
        for tap in range(3):
            moved = mixed_ref[pl.ds(PAD + 1 - tap, PATCH), :].astype(bf16)
            conv_sum_ref[tap] += dot(normed_ref[...], moved, TN)
        return 0

    lax.fori_loop(0, slots // PATCH, patch, 0)
    write_back(zorder_ref, serial_grad_ref, back_ref)
    for start in range(0, hidden_width, width):
        weights_ref[start : start + width, :] = dot(
            hidden_ref[:, start : start + width], out_grad_ref[...], TN
        ).astype(weights_ref.dtype)
        weights_ref[hidden_width + start : hidden_width + start + width, :] = dot(
            second_ref[...], pre_grad_ref[:, start : start + width], TN
        ).astype(weights_ref.dtype)
    same = lax.div(iota((width, width), 0), inner) == lax.div(iota((width, width), 1), inner)
    for tap in range(3):
        kept = jnp.where(same, conv_sum_ref[tap], 0.0).reshape(groups, inner, width)
        at = 2 * hidden_width + tap * inner
        weights_ref[at : at + inner, :] = jnp.sum(kept, axis=0).astype(weights_ref.dtype)
    at = 2 * hidden_width + 3 * inner
    weights_ref[at:, :] = gains_ref[...].astype(weights_ref.dtype)


def call(kernel, outs, args, scratch=(), smem=0, flops=0, limit=32, **static):
    moved = sum(math.prod(a.shape) * a.dtype.itemsize for a in (*args, *outs))
    specs = [pl.BlockSpec(memory_space=pltpu.SMEM)] * smem
    specs += [pl.BlockSpec(memory_space=pltpu.VMEM)] * (len(args) - smem)
    return pl.pallas_call(
        functools.partial(kernel, **static) if static else kernel,
        out_shape=tuple(outs),
        in_specs=specs,
        out_specs=tuple(pl.BlockSpec(memory_space=pltpu.VMEM) for _ in outs),
        scratch_shapes=list(scratch),
        compiler_params=pltpu.CompilerParams(vmem_limit_bytes=limit * 1024 * 1024),
        cost_estimate=pl.CostEstimate(flops=int(flops), bytes_accessed=moved, transcendentals=0),
    )(*args)


def shaped(*shape, dtype=bf16):
    return jax.ShapeDtypeStruct(shape, dtype)


def shifted(value, axis, steps):
    count = lax.axis_size(axis)
    initial, last = (max(0, -steps), min(count, count - steps))
    return lax.ppermute(value, axis, [(source, source + steps) for source in range(initial, last)])


def exchange(rows, tiles):
    return lax.all_to_all(rows, ("tx", "ty"), split_axis=0, concat_axis=0, tiled=True)


def body(
    points,
    counts,
    owner,
    zorder,
    border,
    near,
    w_near,
    gain_one,
    conv_w,
    gain_two,
    w_up,
    w_down,
    grad_out,
):
    points_tile = points[0]
    tile_rows, width = points_tile.shape
    border_rows = border.shape[2]
    edge = 4 * border_rows
    ext = tile_rows + edge
    lists = border.reshape(1, edge)
    near_tile = near[0]
    neighbours = near_tile.shape[0]
    tiles = lax.axis_size("tx") * lax.axis_size("ty")
    slots_count = zorder.shape[1]
    capacity = slots_count // tiles
    taps, groups, inner = conv_w.shape[:3]
    conv_rows = conv_w.reshape(taps * groups * inner, inner)
    gain_one_row = gain_one.reshape(1, width)
    gain_two_row = gain_two.reshape(1, width)
    hidden = w_up.shape[1]

    slots, sent = call(
        route_kernel,
        [shaped(1, tile_rows, dtype=jnp.int32), shaped(edge, width)],
        [counts, owner, lists, points_tile],
        smem=1,
        flops=4e9,
        tiles=tiles,
        capacity=capacity,
    )
    halos = [
        shifted(sent[0:border_rows], "tx", -1),
        shifted(sent[border_rows : 2 * border_rows], "tx", 1),
        shifted(sent[2 * border_rows : 3 * border_rows], "ty", -1),
        shifted(sent[3 * border_rows :], "ty", 1),
    ]
    (packed_grad,) = call(
        pack_kernel, [shaped(slots_count, width)], [slots, grad_out[0]], flops=4e9
    )
    came_grad = exchange(packed_grad, tiles)
    (table,) = call(count_kernel, [shaped(ext, tile_rows)], [near_tile], flops=8e9)
    average, pre_act, packed_lifted = call(
        lift_kernel,
        [
            shaped(width, tile_rows),
            shaped(tile_rows, width, dtype=f32),
            shaped(slots_count, width),
        ],
        [slots, points_tile, *halos, table, w_near],
        scratch=[pltpu.VMEM((tile_rows, width), bf16)],
        flops=4e9,
        neighbours=neighbours,
    )
    came_lifted = exchange(packed_lifted, tiles)
    patch_scratch = [
        pltpu.VMEM((PATCH + 2 * PAD, width), f32),
        pltpu.VMEM((PATCH, width), f32),
        pltpu.VMEM((PATCH + 2 * PAD, width), f32),
    ]
    serial, serial_out_grad, state, back_result = call(
        forward_kernel,
        [
            shaped(slots_count, width),
            shaped(slots_count, width),
            shaped(slots_count, width, dtype=f32),
            shaped(slots_count, width),
        ],
        [zorder, came_lifted, came_grad, conv_rows, gain_one_row, gain_two_row, w_up, w_down],
        scratch=[
            pltpu.VMEM((taps * width, width), bf16),
            pltpu.VMEM((PATCH, width), bf16),
            *patch_scratch,
            pltpu.VMEM((slots_count, width), bf16),
        ],
        flops=10e9,
        limit=48,
        groups=groups,
        inner=inner,
    )
    came_result = exchange(back_result, tiles)
    sums_rows = 2 * hidden + taps * inner + 16
    back_grad, sums = call(
        backward_kernel,
        [shaped(slots_count, width), shaped(sums_rows, width)],
        [
            zorder,
            serial,
            serial_out_grad,
            state,
            conv_rows,
            gain_one_row,
            gain_two_row,
            w_up,
            w_down,
        ],
        scratch=[
            pltpu.VMEM((taps * width, width), bf16),
            pltpu.VMEM((slots_count, width), bf16),
            pltpu.VMEM((slots_count, hidden), bf16),
            pltpu.VMEM((slots_count, hidden), bf16),
            pltpu.VMEM((PATCH, width), f32),
            pltpu.VMEM((PATCH + 2 * PAD, width), f32),
            *patch_scratch,
            pltpu.VMEM((PATCH, width), bf16),
            pltpu.VMEM((slots_count, width), bf16),
            pltpu.VMEM((taps, width, width), f32),
            pltpu.VMEM((16, width), f32),
        ],
        flops=15e9,
        limit=48,
        groups=groups,
        inner=inner,
    )
    came_back = exchange(back_grad, tiles)
    totals = lax.psum(sums, ("tx", "ty"))
    (out_rows,) = call(
        unpack_kernel, [shaped(tile_rows, width)], [slots, came_result], flops=4e9
    )
    near_grad, row_grad, halo_grad = call(
        tile_back_kernel,
        [
            shaped(width, width),
            shaped(tile_rows, width, dtype=f32),
            shaped(edge, width),
        ],
        [slots, came_back, table, average, pre_act, w_near],
        scratch=[pltpu.VMEM((tile_rows, width), bf16), pltpu.VMEM((tile_rows, width), bf16)],
        flops=6e9,
        neighbours=neighbours,
    )
    returned = [
        shifted(halo_grad[0:border_rows], "tx", 1),
        shifted(halo_grad[border_rows : 2 * border_rows], "tx", -1),
        shifted(halo_grad[2 * border_rows : 3 * border_rows], "ty", 1),
        shifted(halo_grad[3 * border_rows :], "ty", -1),
    ]
    near_sum = lax.psum(near_grad, ("tx", "ty"))
    (grad_points,) = call(
        finish_kernel, [shaped(tile_rows, width)], [lists, row_grad, *returned], flops=1e9
    )
    scale = 1.0 / math.sqrt(tiles * tile_rows)
    scaled = totals.astype(f32) * scale
    down_sum = scaled[0:hidden]
    up_sum = jnp.concatenate(
        [scaled[hidden + at : hidden + at + width] for at in range(0, hidden, width)], axis=1
    )
    conv_sum = scaled[2 * hidden : 2 * hidden + taps * inner].reshape(taps, inner, groups, inner)
    gains = scaled[2 * hidden + taps * inner :]
    return (
        out_rows[None],
        grad_points[None],
        near_sum.astype(f32) * scale,
        gains[0],
        conv_sum.transpose(0, 2, 1, 3),
        gains[1],
        up_sum,
        down_sum,
    )


def solution(mesh):
    placed = (
        P(("tx", "ty"), None, None),
        P(("tx", "ty")),
        P(("tx", "ty"), None),
        P(("tx", "ty"), None),
        P(("tx", "ty"), None, None),
        P(("tx", "ty"), None, None),
        P(),
        P(),
        P(),
        P(),
        P(),
        P(),
        P(("tx", "ty"), None, None),
    )
    return jax.shard_map(
        body,
        mesh=mesh,
        in_specs=placed,
        out_specs=(
            P(("tx", "ty"), None, None),
            P(("tx", "ty"), None, None),
            P(),
            P(),
            P(),
            P(),
            P(),
            P(),
        ),
        check_vma=False,
    )
```

profile of v0, /device:TPU:0, one launch (start us, length us, event | category | flops | bytes accessed | tf_op | source)
XLA Modules:
  0.0 312.0 jit_solution(9445539952970187846)
XLA Ops:
  11.3 3.4 %shard_map.191 = bf16[2048,256]{1,0:T(8,128)(2,1)} custom-call(s32[1,1024]{1,0:T(1,128)S(1)} %get-tuple-element.22.slots_ref, bf16[1024,256]{1,0:T(8,128)(2,1)S(1)} %bitcast.26), custom_call_target="tpu_custom_call" | custom-call | flops 4000000000 | bytes 1576960 | tf_op jit(solution)/shard_map/pallas_call | solution.py:341
  14.8 7.4 %all-to-all-start.1 = ((bf16[32,64,256]{2,1,0:T(8,128)(2,1)}), bf16[32,64,256]{2,1,0:T(8,128)(2,1)}, u32[]{:S(2)}, u32[]{:S(2)}) async-start(bf16[32,64,256]{2,1,0:T(8,128)(2,1)} %bitcast.5), calls=%async_computation.1 | async-start | bytes 2097152 | tf_op jit(solution)/shard_map/all_to_all | solution.py:363
  22.2 2.1 collective-permute-start.3
  24.3 1.3 collective-permute-start.2
  25.6 3.6 %collective-permute-start.1 = (bf16[64,256]{1,0:T(8,128)(2,1)S(1)}, bf16[64,256]{1,0:T(8,128)(2,1)S(1)}, u32[]{:S(2)}, u32[]{:S(2)}) collective-permute-start(bf16[64,256]{1,0:T(8,128)(2,1)S(1)} %get-tuple-element.50), channel_id=1, source_target_pairs={{0,8},{8,16},{16,24},{1,9},{9,17},{17,25},{2,10},{10,18},{18,26},{... | collective-permute-start | bytes 98312 | tf_op jit(solution)/shard_map/ppermute | solution.py:359
  29.2 1.3 collective-permute-start
  30.5 5.1 %shard_map.189.table_ref = bf16[1280,1024]{1,0:T(8,128)(2,1)S(1)} custom-call(s32[16,1024]{1,0:T(8,128)S(1)} %bitcast.31), custom_call_target="tpu_custom_call" | custom-call | flops 8000000000 | bytes 2686976 | tf_op jit(solution)/shard_map/pallas_call | solution.py:341
  35.7 4.7 %collective-permute-done.1.halo1 = bf16[64,256]{1,0:T(8,128)(2,1)S(1)} collective-permute-done((bf16[64,256]{1,0:T(8,128)(2,1)S(1)}, bf16[64,256]{1,0:T(8,128)(2,1)S(1)}, u32[]{:S(2)}, u32[]{:S(2)}) %collective-permute-start.1) | collective-permute-done | bytes 32800 | tf_op jit(solution)/shard_map/ppermute | solution.py:359
  40.4 3.8 %shard_map.190 = (bf16[256,1024]{1,0:T(8,128)(2,1)S(1)}, f32[1024,256]{1,0:T(8,128)S(1)}, bf16[2048,256]{1,0:T(8,128)(2,1)S(1)}) custom-call(s32[1,1024]{1,0:T(1,128)S(1)} %get-tuple-element.22.slots_ref, bf16[1024,256]{1,0:T(8,128)(2,1)S(1)} %bitcast.28, bf16[64,256]{1,0:T(8,128)(2,1)S(1)} %collective-permute-done.halo0, ...), custom_call_target="tpu_custom_call" | custom-call | flops 4000000000 | bytes 6033408 | tf_op jit(solution)/shard_map/pallas_call | solution.py:341
  44.2 1.5 copy-done.14
  47.5 1.3 all-to-all-done.1
  48.8 36.1 %all_to_all.44 = bf16[32,64,256]{2,1,0:T(8,128)(2,1)S(1)} all-to-all(bf16[32,64,256]{2,1,0:T(8,128)(2,1)S(1)} %bitcast.23), channel_id=1, replica_groups=mesh['tx'=4,'ty'=8] {'tx','ty'}, dimensions={0} | all-to-all | bytes 2097152 | tf_op jit(solution)/shard_map/all_to_all | solution.py:363
  84.9 16.8 %shard_map.192 = (bf16[2048,256]{1,0:T(8,128)(2,1)S(1)}, bf16[2048,256]{1,0:T(8,128)(2,1)S(1)}, f32[2048,256]{1,0:T(8,128)}, bf16[2048,256]{1,0:T(8,128)(2,1)}) custom-call(s32[1,2048]{1,0:T(1,128)S(1)} %copy-done.8, bf16[2048,256]{1,0:T(8,128)(2,1)S(1)} %bitcast.24, bf16[2048,256]{1,0:T(8,128)(2,1)} %bitcast.6.grad_ref, bf16[768,32]{1,0:T(8,128)(2,1)S(1)} %bitcast.29, ...), custom_call_target="tpu_custom_call" | custom-call | flops 10000000000 | bytes 8448000 | tf_op jit(solution)/shard_map/pallas_call | solution.py:341
  101.7 22.3 %shard_map.194 = (bf16[2048,256]{1,0:T(8,128)(2,1)S(1)}, bf16[2160,256]{1,0:T(8,128)(2,1)}) custom-call(s32[1,2048]{1,0:T(1,128)S(1)} %copy-done.8, bf16[2048,256]{1,0:T(8,128)(2,1)S(1)} %get-tuple-element.26.serial_ref, bf16[2048,256]{1,0:T(8,128)(2,1)S(1)} %get-tuple-element.27.out_grad_ref, f32[2048,256]{1,0:T(8,128)} %get-tuple-element.28.state_ref, ...), custom_call_target="tpu_custom_call" | custom-call | flops 15000000512 | bytes 7456768 | tf_op jit(solution)/shard_map/pallas_call | solution.py:341
  124.0 29.7 %all_to_all.45 = bf16[32,64,256]{2,1,0:T(8,128)(2,1)S(1)} all-to-all(bf16[32,64,256]{2,1,0:T(8,128)(2,1)S(1)} %bitcast.25), channel_id=1, replica_groups=mesh['tx'=4,'ty'=8] {'tx','ty'}, dimensions={0} | all-to-all | bytes 2097152 | tf_op jit(solution)/shard_map/all_to_all | solution.py:363
  153.7 3.6 %all-to-all-start.2 = ((bf16[32,64,256]{2,1,0:T(8,128)(2,1)}), bf16[32,64,256]{2,1,0:T(8,128)(2,1)S(1)}, u32[]{:S(2)}, u32[]{:S(2)}) async-start(bf16[32,64,256]{2,1,0:T(8,128)(2,1)} %bitcast.10), calls=%async_computation.2 | async-start | bytes 2097152 | tf_op jit(solution)/shard_map/all_to_all | solution.py:363
  157.6 1.7 copy-done.15
  160.6 3.9 %shard_map.195 = (bf16[256,256]{1,0:T(8,128)(2,1)}, f32[1024,256]{1,0:T(8,128)S(1)}, bf16[256,256]{1,0:T(8,128)(2,1)S(1)}) custom-call(s32[1,1024]{1,0:T(1,128)S(1)} %get-tuple-element.22.slots_ref, bf16[2048,256]{1,0:T(8,128)(2,1)S(1)} %bitcast.22, bf16[1280,1024]{1,0:T(8,128)(2,1)S(1)} %copy-done.15, bf16[256,1024]{1,0:T(8,128)(2,1)S(1)} %copy-done.19, ...), custom_call_target="tpu_custom_call" | custom-call | flops 6000000000 | bytes 6688768 | tf_op jit(solution)/shard_map/pallas_call | solution.py:341
  166.7 3.0 collective-permute-start.6
  171.1 4.5 %collective-permute-start.4 = (bf16[64,256]{1,0:T(8,128)(2,1)S(1)}, bf16[64,256]{1,0:T(8,128)(2,1)S(1)}, u32[]{:S(2)}, u32[]{:S(2)}) collective-permute-start(bf16[64,256]{1,0:T(8,128)(2,1)S(1)} %get-tuple-element.47), channel_id=1, source_target_pairs={{0,8},{8,16},{16,24},{1,9},{9,17},{17,25},{2,10},{10,18},{18,26},{... | collective-permute-start | bytes 98312 | tf_op jit(solution)/shard_map/ppermute | solution.py:359
  175.6 11.4 %all-to-all-done.2 = bf16[32,64,256]{2,1,0:T(8,128)(2,1)S(1)} async-done(((bf16[32,64,256]{2,1,0:T(8,128)(2,1)}), bf16[32,64,256]{2,1,0:T(8,128)(2,1)S(1)}, u32[]{:S(2)}, u32[]{:S(2)}) %all-to-all-start.2) | async-done | bytes 1048608 | tf_op jit(solution)/shard_map/all_to_all | solution.py:363
  187.0 2.1 shard_map.193
  190.2 108.9 %all-reduce.3.cloned.1.call-done = (bf16[256,256]{1,0:T(8,128)(2,1)}, bf16[2160,256]{1,0:T(8,128)(2,1)}) async-done(((bf16[256,256]{1,0:T(8,128)(2,1)}, bf16[2160,256]{1,0:T(8,128)(2,1)}), (bf16[256,256]{1,0:T(8,128)(2,1)}, bf16[2160,256]{1,0:T(8,128)(2,1)})) %all-reduce.3.cloned.1.call-update) | async-done | bytes 1237008 | tf_op jit(solution)/shard_map/psum | solution.py:513
  299.2 1.4 convert_multiply_fusion
  (64 shorter events, 16.0 us)
Async XLA Ops:
  14.8 15.7 %copy-start.7 = (s32[1,16,1024]{2,1,0:T(8,128)S(1)}, s32[1,16,1024]{2,1,0:T(8,128)}, u32[]{:S(2)}) copy-start(s32[1,16,1024]{2,1,0:T(8,128)} %param.18) | copy-start | bytes 196612
  14.8 34.0 %all-to-all-start.1 = ((bf16[32,64,256]{2,1,0:T(8,128)(2,1)}), bf16[32,64,256]{2,1,0:T(8,128)(2,1)}, u32[]{:S(2)}, u32[]{:S(2)}) async-start(bf16[32,64,256]{2,1,0:T(8,128)(2,1)} %bitcast.5), calls=%async_computation.1 | async-start | bytes 2097152 | tf_op jit(solution)/shard_map/all_to_all | solution.py:363
  22.2 13.5 %collective-permute-start.3 = (bf16[64,256]{1,0:T(8,128)(2,1)S(1)}, bf16[64,256]{1,0:T(8,128)(2,1)S(1)}, u32[]{:S(2)}, u32[]{:S(2)}) collective-permute-start(bf16[64,256]{1,0:T(8,128)(2,1)S(1)} %get-tuple-element.48), channel_id=1, source_target_pairs={{0,1},{1,2},{2,3},{3,4},{4,5},{5,6},{6,7},{8,9},{9,10},{10,11},{11... | collective-permute-start | bytes 98312 | tf_op jit(solution)/shard_map/ppermute | solution.py:359
  24.3 11.4 %collective-permute-start.2 = (bf16[64,256]{1,0:T(8,128)(2,1)S(1)}, bf16[64,256]{1,0:T(8,128)(2,1)S(1)}, u32[]{:S(2)}, u32[]{:S(2)}) collective-permute-start(bf16[64,256]{1,0:T(8,128)(2,1)S(1)} %get-tuple-element.49), channel_id=1, source_target_pairs={{1,0},{2,1},{3,2},{4,3},{5,4},{6,5},{7,6},{9,8},{10,9},{11,10},{12... | collective-permute-start | bytes 98312 | tf_op jit(solution)/shard_map/ppermute | solution.py:359
  25.6 14.8 %collective-permute-start.1 = (bf16[64,256]{1,0:T(8,128)(2,1)S(1)}, bf16[64,256]{1,0:T(8,128)(2,1)S(1)}, u32[]{:S(2)}, u32[]{:S(2)}) collective-permute-start(bf16[64,256]{1,0:T(8,128)(2,1)S(1)} %get-tuple-element.50), channel_id=1, source_target_pairs={{0,8},{8,16},{16,24},{1,9},{9,17},{17,25},{2,10},{10,18},{18,26},{... | collective-permute-start | bytes 98312 | tf_op jit(solution)/shard_map/ppermute | solution.py:359
  29.2 11.2 %collective-permute-start = (bf16[64,256]{1,0:T(8,128)(2,1)S(1)}, bf16[64,256]{1,0:T(8,128)(2,1)S(1)}, u32[]{:S(2)}, u32[]{:S(2)}) collective-permute-start(bf16[64,256]{1,0:T(8,128)(2,1)S(1)} %get-tuple-element.51), channel_id=1, source_target_pairs={{8,0},{16,8},{24,16},{9,1},{17,9},{25,17},{10,2},{18,10},{26,18},{... | collective-permute-start | bytes 98312 | tf_op jit(solution)/shard_map/ppermute | solution.py:359
  30.5 9.9 %copy-start.2 = (bf16[1,1024,256]{2,1,0:T(8,128)(2,1)S(1)}, bf16[1,1024,256]{2,1,0:T(8,128)(2,1)}, u32[]{:S(2)}) copy-start(bf16[1,1024,256]{2,1,0:T(8,128)(2,1)} %param.13) | copy-start | bytes 1572868
  30.5 9.9 %copy-start.6 = (bf16[256,256]{1,0:T(8,128)(2,1)S(1)}, bf16[256,256]{1,0:T(8,128)(2,1)}, u32[]{:S(2)}) copy-start(bf16[256,256]{1,0:T(8,128)(2,1)} %w_ref.3) | copy-start | bytes 393220
  35.6 49.2 %copy-start.3 = (bf16[256,1024]{1,0:T(8,128)(2,1)S(1)}, bf16[256,1024]{1,0:T(8,128)(2,1)}, u32[]{:S(2)}) copy-start(bf16[256,1024]{1,0:T(8,128)(2,1)} %up_ref.3) | copy-start | bytes 1572868
  35.6 49.2 %copy-start.4 = (bf16[1024,256]{1,0:T(8,128)(2,1)S(1)}, bf16[1024,256]{1,0:T(8,128)(2,1)}, u32[]{:S(2)}) copy-start(bf16[1024,256]{1,0:T(8,128)(2,1)} %down_ref.3) | copy-start | bytes 1572868
  35.7 49.2 %copy-start.5 = (bf16[3,8,32,32]{3,2,1,0:T(8,128)(2,1)S(1)}, bf16[3,8,32,32]{3,2,1,0:T(8,128)(2,1)}, u32[]{:S(2)}) copy-start(bf16[3,8,32,32]{3,2,1,0:T(8,128)(2,1)} %param.21) | copy-start | bytes 147460
  35.7 49.2 %copy-start.8 = (s32[1,2048]{1,0:T(1,128)S(1)}, s32[1,2048]{1,0:T(1,128)}, u32[]{:S(2)}) copy-start(s32[1,2048]{1,0:T(1,128)} %zorder_ref.3) | copy-start | bytes 24580
  35.7 49.2 %copy-start.10 = (f32[256]{0:T(256)S(1)}, f32[256]{0:T(256)}, u32[]{:S(2)}) copy-start(f32[256]{0:T(256)} %param.20) | copy-start | bytes 3076
  35.7 49.2 %copy-start.11 = (f32[256]{0:T(256)S(1)}, f32[256]{0:T(256)}, u32[]{:S(2)}) copy-start(f32[256]{0:T(256)} %param.22) | copy-start | bytes 3076
  124.0 33.6 %copy-start.19 = (bf16[256,1024]{1,0:T(8,128)(2,1)S(1)}, bf16[256,1024]{1,0:T(8,128)(2,1)}, u32[]{:S(2)}) copy-start(bf16[256,1024]{1,0:T(8,128)(2,1)} %copy-done.18) | copy-start | bytes 1572868
  153.7 33.3 %all-to-all-start.2 = ((bf16[32,64,256]{2,1,0:T(8,128)(2,1)}), bf16[32,64,256]{2,1,0:T(8,128)(2,1)S(1)}, u32[]{:S(2)}, u32[]{:S(2)}) async-start(bf16[32,64,256]{2,1,0:T(8,128)(2,1)} %bitcast.10), calls=%async_computation.2 | async-start | bytes 2097152 | tf_op jit(solution)/shard_map/all_to_all | solution.py:363
  157.3 141.8 %all-reduce.3.cloned.1.call-start = ((), (), s32[]{:S(2)}) async-start(), calls=%async_computation.4 | async-start | bytes 2473984 | tf_op jit(solution)/shard_map/psum | solution.py:513
  157.6 1.7 copy-start.15
  165.4 23.7 %collective-permute-start.7 = (bf16[64,256]{1,0:T(8,128)(2,1)S(1)}, bf16[64,256]{1,0:T(8,128)(2,1)S(1)}, u32[]{:S(2)}, u32[]{:S(2)}) collective-permute-start(bf16[64,256]{1,0:T(8,128)(2,1)S(1)} %get-tuple-element.44), channel_id=1, source_target_pairs={{1,0},{2,1},{3,2},{4,3},{5,4},{6,5},{7,6},{9,8},{10,9},{11,10},{12... | collective-permute-start | bytes 98312 | tf_op jit(solution)/shard_map/ppermute | solution.py:359
  166.7 22.4 %collective-permute-start.6 = (bf16[64,256]{1,0:T(8,128)(2,1)S(1)}, bf16[64,256]{1,0:T(8,128)(2,1)S(1)}, u32[]{:S(2)}, u32[]{:S(2)}) collective-permute-start(bf16[64,256]{1,0:T(8,128)(2,1)S(1)} %get-tuple-element.45), channel_id=1, source_target_pairs={{0,1},{1,2},{2,3},{3,4},{4,5},{5,6},{6,7},{8,9},{9,10},{10,11},{11... | collective-permute-start | bytes 98312 | tf_op jit(solution)/shard_map/ppermute | solution.py:359
  169.8 19.3 %collective-permute-start.5 = (bf16[64,256]{1,0:T(8,128)(2,1)S(1)}, bf16[64,256]{1,0:T(8,128)(2,1)S(1)}, u32[]{:S(2)}, u32[]{:S(2)}) collective-permute-start(bf16[64,256]{1,0:T(8,128)(2,1)S(1)} %get-tuple-element.46), channel_id=1, source_target_pairs={{8,0},{16,8},{24,16},{9,1},{17,9},{25,17},{10,2},{18,10},{26,18},{... | collective-permute-start | bytes 98312 | tf_op jit(solution)/shard_map/ppermute | solution.py:359
  171.1 18.1 %collective-permute-start.4 = (bf16[64,256]{1,0:T(8,128)(2,1)S(1)}, bf16[64,256]{1,0:T(8,128)(2,1)S(1)}, u32[]{:S(2)}, u32[]{:S(2)}) collective-permute-start(bf16[64,256]{1,0:T(8,128)(2,1)S(1)} %get-tuple-element.47), channel_id=1, source_target_pairs={{0,8},{8,16},{16,24},{1,9},{9,17},{17,25},{2,10},{10,18},{18,26},{... | collective-permute-start | bytes 98312 | tf_op jit(solution)/shard_map/ppermute | solution.py:359
  187.0 2.1 copy-start.13
  300.6 1.7 copy-start.20
  (8 other events, 8.2 us)
Sparse Core Ops, SparseCore 0:
  165.5 133.5 all-reduce.2
where the time goes:
time: 313 us; the launch traced here: 312 us
  waiting for transfers between devices  126 us (40%)
  blocking collectives  65.7 us (21%)
  Pallas kernels  59 us (19%)
  starting transfers between devices  29.7 us (9%)
  between operations  15 us (5%)
  local copies, waits for them, and re-layouts  12.9 us (4%)
  other arithmetic  3.27 us (1%)
    psum x1, waiting for transfers between devices, body(): near_sum = lax.psum(near_grad, ('tx', 'ty'))  109 us
    all_to_all x2, blocking collectives, exchange(): lax.all_to_all(rows, ('tx', 'ty'), split_axis=0, concat_axis=0, tiled=True)  65.7 us
    pallas_call x9, Pallas kernels, call(): pl.pallas_call(functools.partial(kernel, **static) if static else kernel,...  59 us
    ppermute x8, starting transfers between devices, shifted(): lax.ppermute(value, axis, [(source, source + steps) for source in range(i...  18.4 us
    all_to_all x2, waiting for transfers between devices, exchange(): lax.all_to_all(rows, ('tx', 'ty'), split_axis=0, concat_axis=0, tiled=True)  12.7 us
    all_to_all x2, starting transfers between devices, exchange(): lax.all_to_all(rows, ('tx', 'ty'), split_axis=0, concat_axis=0, tiled=True)  11 us
    unnamed x42, local copies, waits for them, and re-layouts  9.47 us
  transfers between devices with their start and end apart: 11, of which 4 were waited for; matrix products, arithmetic and copies ran while one was open for 0% of the time, Pallas kernels for 5%

commit v1 on v0

--- a/solution.py
+++ b/solution.py
@@ -10,6 +10,8 @@
 
 PATCH = 1024
 CHUNK = 256
+WIDE = 512
+BLOCK = 64
 LANES = 128
 PAD = 8
 
@@ -71,10 +73,6 @@
 
 def mark_slots(row, start, count):
     return marks(iota((count, row.shape[1]), 0) + start == row)
-
-
-def chunks(total):
-    return lax.div(total, CHUNK)
 
 
 def route_kernel(counts_ref, owner_ref, lists_ref, points_ref, slots_ref, sent_ref, *, tiles, capacity):
@@ -93,15 +91,10 @@
 
 def pack_kernel(slots_ref, rows_ref, packed_ref):
     slots = slots_ref[...]
-
-    def one(at, _):
-        start = pl.multiple_of(at * CHUNK, CHUNK)
-        packed_ref[pl.ds(start, CHUNK), :] = dot(
-            mark_slots(slots, start, CHUNK), rows_ref[...]
+    for start in range(0, packed_ref.shape[0], WIDE):
+        packed_ref[pl.ds(start, WIDE), :] = dot(
+            mark_slots(slots, start, WIDE), rows_ref[...]
         ).astype(bf16)
-        return 0
-
-    lax.fori_loop(0, packed_ref.shape[0] // CHUNK, one, 0)
 
 
 def unpack_kernel(slots_ref, packed_ref, rows_ref):
@@ -153,26 +146,27 @@
     pack_kernel(slots_ref, lifted_ref, packed_ref)
 
 
-def tile_back_kernel(
-    slots_ref, back_ref, table_ref, average_ref, pre_ref, w_ref, near_ref, row_ref, halo_ref,
-    act_ref, spread_ref, *, neighbours
-):
-    rows = row_ref.shape[0]
-    for start in range(0, rows, CHUNK):
+def act_kernel(slots_ref, back_ref, average_ref, pre_ref, lifted_ref, act_ref, near_ref):
+    for start in range(0, lifted_ref.shape[0], CHUNK):
         here = pl.ds(start, CHUNK)
         column = column_of(slots_ref[:, start : start + CHUNK], CHUNK)
         lifted_grad = dot(pick_rows(column, back_ref.shape[0]), back_ref[...])
-        row_ref[here, :] = lifted_grad
+        lifted_ref[here, :] = lifted_grad.astype(bf16)
         value = pre_ref[here, :]
         square, tangent = gelu_parts(value)
-        act_grad = (lifted_grad * slope_of(value, square, tangent)).astype(bf16)
-        act_ref[here, :] = act_grad
-        spread_ref[here, :] = (dot(act_grad, w_ref[...], NT) * (1.0 / neighbours)).astype(bf16)
+        act_ref[here, :] = (lifted_grad * slope_of(value, square, tangent)).astype(bf16)
     near_ref[...] = dot(average_ref[...], act_ref[...]).astype(near_ref.dtype)
-    for start in range(0, rows, CHUNK):
-        here = pl.ds(start, CHUNK)
-        row_ref[here, :] = row_ref[here, :] + dot(table_ref[here, :], spread_ref[...])
+
+
+def spread_rows_kernel(
+    lifted_ref, act_ref, table_ref, w_ref, row_ref, halo_ref, spread_ref, *, neighbours
+):
+    rows = row_ref.shape[0]
+    spread_ref[...] = (dot(act_ref[...], w_ref[...], NT) * (1.0 / neighbours)).astype(bf16)
     halo_ref[...] = dot(table_ref[rows:, :], spread_ref[...]).astype(bf16)
+    for start in range(0, rows, WIDE):
+        here = pl.ds(start, WIDE)
+        row_ref[here, :] = lifted_ref[here, :].astype(f32) + dot(table_ref[here, :], spread_ref[...])
 
 
 def finish_kernel(lists_ref, row_ref, back0, back1, back2, back3, out_ref):
@@ -199,63 +193,79 @@
 
 
 def write_back(zorder_ref, rows_ref, out_ref):
-    zorder = zorder_ref[...]
-
-    def one(at, _):
-        start = pl.multiple_of(at * CHUNK, CHUNK)
-        out_ref[pl.ds(start, CHUNK), :] = dot(
-            mark_slots(zorder, start, CHUNK), rows_ref[...]
+    pack_kernel(zorder_ref, rows_ref, out_ref)
+
+
+def order_kernel(zorder_ref, slots_ref, rows_ref):
+    for start in range(0, rows_ref.shape[0], WIDE):
+        column = column_of(zorder_ref[:, start : start + WIDE], WIDE)
+        rows_ref[pl.ds(start, WIDE), :] = dot(
+            pick_rows(column, slots_ref.shape[0]), slots_ref[...]
         ).astype(bf16)
-        return 0
-
-    lax.fori_loop(0, out_ref.shape[0] // CHUNK, one, 0)
 
 
 def forward_kernel(
-    zorder_ref, lifted_ref, grad_ref, conv_ref, gain_one_ref, gain_two_ref, up_ref, down_ref,
-    serial_ref, out_grad_ref, state_ref, back_ref,
-    taps_ref, normed_ref, before_ref, here_ref, after_ref, result_ref, *, groups, inner
+    zorder_ref, lifted_ref, conv_ref, gain_one_ref, gain_two_ref, up_ref, down_ref,
+    serial_ref, state_ref, back_ref,
+    taps_ref, normed_ref, before_ref, here_ref, after_ref, second_ref, hidden_ref, result_ref,
+    *, groups, inner
 ):
     slots, width = lifted_ref.shape
+    hidden_width = up_ref.shape[1]
     taps_ref[...] = full_taps(conv_ref, groups, inner)
     padded_zeros(before_ref)
     padded_zeros(after_ref)
 
     def patch(at, _):
         origin = pl.multiple_of(at * PATCH, PATCH)
+        for start in range(0, PATCH, WIDE):
+            column = column_of(zorder_ref[:, pl.ds(origin + start, WIDE)], WIDE)
+            wide = dot(pick_rows(column, slots), lifted_ref[...])
+            for row in range(0, WIDE, BLOCK):
+                serial = wide[row : row + BLOCK]
+                serial_ref[pl.ds(origin + start + row, BLOCK), :] = serial.astype(bf16)
+                normed = serial * inverse_rms(serial) * gain_one_ref[...]
+                normed_ref[pl.ds(start + row, BLOCK), :] = normed.astype(bf16)
+        before_ref[pl.ds(PAD, PATCH), :] = dot(normed_ref[...], taps_ref[0:width, :])
+        here_ref[...] = dot(normed_ref[...], taps_ref[width : 2 * width, :])
+        after_ref[pl.ds(PAD, PATCH), :] = dot(normed_ref[...], taps_ref[2 * width :, :])
+        for row in range(0, PATCH, BLOCK):
+            place = pl.ds(origin + row, BLOCK)
+            state = serial_ref[place, :].astype(f32) + (
+                before_ref[pl.ds(PAD + row - 1, BLOCK), :]
+                + here_ref[pl.ds(row, BLOCK), :]
+                + after_ref[pl.ds(PAD + row + 1, BLOCK), :]
+            )
+            state_ref[place, :] = state
+            second = state * inverse_rms(state) * gain_two_ref[...]
+            second_ref[pl.ds(row, BLOCK), :] = second.astype(bf16)
         for start in range(0, PATCH, CHUNK):
-            column = column_of(zorder_ref[:, pl.ds(origin + start, CHUNK)], CHUNK)
-            chosen = pick_rows(column, slots)
-            serial = dot(chosen, lifted_ref[...])
-            serial_ref[pl.ds(origin + start, CHUNK), :] = serial.astype(bf16)
-            out_grad_ref[pl.ds(origin + start, CHUNK), :] = dot(chosen, grad_ref[...]).astype(bf16)
-            normed = (serial * inverse_rms(serial) * gain_one_ref[...]).astype(bf16)
-            before_ref[pl.ds(PAD + start, CHUNK), :] = dot(normed, taps_ref[0:width, :])
-            here_ref[pl.ds(start, CHUNK), :] = dot(normed, taps_ref[width : 2 * width, :])
-            after_ref[pl.ds(PAD + start, CHUNK), :] = dot(normed, taps_ref[2 * width :, :])
-        for start in range(0, PATCH, CHUNK):
-            place = pl.ds(origin + start, CHUNK)
-            mixed = (
-                before_ref[pl.ds(PAD + start - 1, CHUNK), :]
-                + here_ref[pl.ds(start, CHUNK), :]
-                + after_ref[pl.ds(PAD + start + 1, CHUNK), :]
-            )
-            state = serial_ref[place, :].astype(f32) + mixed
-            state_ref[place, :] = state
-            second = (state * inverse_rms(state) * gain_two_ref[...]).astype(bf16)
-            hidden = gelu_tanh(dot(second, up_ref[...])).astype(bf16)
-            result_ref[place, :] = (state + dot(hidden, down_ref[...])).astype(bf16)
+            value = dot(second_ref[pl.ds(start, CHUNK), :], up_ref[...])
+            for row in range(0, CHUNK, 16):
+                for col in range(0, hidden_width, 2 * LANES):
+                    hidden_ref[pl.ds(start + row, 16), pl.ds(col, 2 * LANES)] = gelu_tanh(
+                        value[row : row + 16, col : col + 2 * LANES]
+                    ).astype(bf16)
+        for start in range(0, PATCH, WIDE):
+            place = pl.ds(origin + start, WIDE)
+            result_ref[place, :] = (
+                state_ref[place, :] + dot(hidden_ref[pl.ds(start, WIDE), :], down_ref[...])
+            ).astype(bf16)
         return 0
 
     lax.fori_loop(0, slots // PATCH, patch, 0)
     write_back(zorder_ref, result_ref, back_ref)
 
 
+def hold_kernel(zorder_ref, rows_ref, _, back_ref):
+    write_back(zorder_ref, rows_ref, back_ref)
+
+
 def backward_kernel(
-    zorder_ref, serial_ref, out_grad_ref, state_ref, conv_ref, gain_one_ref, gain_two_ref, up_ref, down_ref,
-    back_ref, weights_ref,
+    serial_ref, out_grad_ref, state_ref, conv_ref, gain_one_ref, gain_two_ref, up_ref, down_ref,
+    serial_grad_ref, weights_ref,
     taps_ref, second_ref, hidden_ref, pre_grad_ref, state_grad_ref, mixed_ref, before_ref, here_ref,
-    after_ref, normed_ref, serial_grad_ref, conv_sum_ref, gains_ref, *, groups, inner
+    after_ref, normed_ref, conv_sum_ref, gains_ref, *, groups, inner
 ):
     slots, width = serial_ref.shape
     hidden_width = up_ref.shape[1]
@@ -317,7 +327,6 @@
         return 0
 
     lax.fori_loop(0, slots // PATCH, patch, 0)
-    write_back(zorder_ref, serial_grad_ref, back_ref)
     for start in range(0, hidden_width, width):
         weights_ref[start : start + width, :] = dot(
             hidden_ref[:, start : start + width], out_grad_ref[...], TN
@@ -331,13 +340,35 @@
         at = 2 * hidden_width + tap * inner
         weights_ref[at : at + inner, :] = jnp.sum(kept, axis=0).astype(weights_ref.dtype)
     at = 2 * hidden_width + 3 * inner
-    weights_ref[at:, :] = gains_ref[...].astype(weights_ref.dtype)
-
-
-def call(kernel, outs, args, scratch=(), smem=0, flops=0, limit=32, **static):
+    weights_ref[at : at + 16, :] = gains_ref[...].astype(weights_ref.dtype)
+    at = at + 16
+    weights_ref[at:, :] = jnp.zeros((weights_ref.shape[0] - at, width), weights_ref.dtype)
+
+
+def spread_kernel(sums_ref, up_ref, down_ref, conv_ref, gain_one_ref, gain_two_ref, *, scale):
+    width, hidden_width = up_ref.shape
+    taps, groups, inner = conv_ref.shape[:3]
+    down_ref[...] = sums_ref[0:hidden_width, :].astype(f32) * scale
+    for start in range(0, hidden_width, width):
+        up_ref[:, start : start + width] = (
+            sums_ref[hidden_width + start : hidden_width + start + width, :].astype(f32) * scale
+        )
+    for tap in range(taps):
+        at = 2 * hidden_width + tap * inner
+        rows = sums_ref[at : at + inner, :].astype(f32) * scale
+        for group in range(groups):
+            conv_ref[tap, group] = rows[:, group * inner : (group + 1) * inner]
+    at = 2 * hidden_width + taps * inner
+    gains = sums_ref[at : at + 16, :].astype(f32) * scale
+    gain_one_ref[...] = gains[0:1, :]
+    gain_two_ref[...] = gains[1:2, :]
+
+
+def call(kernel, outs, args, scratch=(), smem=0, flops=0, limit=16, held=0, **static):
     moved = sum(math.prod(a.shape) * a.dtype.itemsize for a in (*args, *outs))
     specs = [pl.BlockSpec(memory_space=pltpu.SMEM)] * smem
-    specs += [pl.BlockSpec(memory_space=pltpu.VMEM)] * (len(args) - smem)
+    specs += [pl.BlockSpec(memory_space=pltpu.VMEM)] * (len(args) - smem - held)
+    specs += [pl.BlockSpec(memory_space=pl.ANY)] * held
     return pl.pallas_call(
         functools.partial(kernel, **static) if static else kernel,
         out_shape=tuple(outs),
@@ -433,33 +464,38 @@
         pltpu.VMEM((PATCH, width), f32),
         pltpu.VMEM((PATCH + 2 * PAD, width), f32),
     ]
-    serial, serial_out_grad, state, back_result = call(
+    (serial_out_grad,) = call(
+        order_kernel, [shaped(slots_count, width)], [zorder, came_grad], flops=8e9
+    )
+    serial, state, back_result = call(
         forward_kernel,
         [
-            shaped(slots_count, width),
             shaped(slots_count, width),
             shaped(slots_count, width, dtype=f32),
             shaped(slots_count, width),
         ],
-        [zorder, came_lifted, came_grad, conv_rows, gain_one_row, gain_two_row, w_up, w_down],
+        [zorder, came_lifted, conv_rows, gain_one_row, gain_two_row, w_up, w_down],
         scratch=[
             pltpu.VMEM((taps * width, width), bf16),
             pltpu.VMEM((PATCH, width), bf16),
             *patch_scratch,
+            pltpu.VMEM((PATCH, width), bf16),
+            pltpu.VMEM((PATCH, hidden), bf16),
             pltpu.VMEM((slots_count, width), bf16),
         ],
         flops=10e9,
-        limit=48,
+        limit=32,
         groups=groups,
         inner=inner,
     )
     came_result = exchange(back_result, tiles)
+    lines = lax.axis_size("ty")
     sums_rows = 2 * hidden + taps * inner + 16
-    back_grad, sums = call(
+    sums_rows = -(-sums_rows // (16 * lines)) * (16 * lines)
+    serial_grad, sums = call(
         backward_kernel,
         [shaped(slots_count, width), shaped(sums_rows, width)],
         [
-            zorder,
             serial,
             serial_out_grad,
             state,
@@ -478,30 +514,43 @@
             pltpu.VMEM((PATCH + 2 * PAD, width), f32),
             *patch_scratch,
             pltpu.VMEM((PATCH, width), bf16),
-            pltpu.VMEM((slots_count, width), bf16),
             pltpu.VMEM((taps, width, width), f32),
             pltpu.VMEM((16, width), f32),
         ],
-        flops=15e9,
-        limit=48,
+        flops=40e9,
+        limit=40,
         groups=groups,
         inner=inner,
     )
+    (back_grad,) = call(
+        hold_kernel,
+        [shaped(slots_count, width)],
+        [zorder, serial_grad, came_result],
+        held=1,
+        flops=4e9,
+    )
     came_back = exchange(back_grad, tiles)
-    totals = lax.psum(sums, ("tx", "ty"))
+    share = lax.psum_scatter(sums, "ty", scatter_dimension=0, tiled=True)
+    totals = lax.all_gather(lax.psum(share, "tx"), "ty", axis=0, tiled=True)
     (out_rows,) = call(
         unpack_kernel, [shaped(tile_rows, width)], [slots, came_result], flops=4e9
     )
-    near_grad, row_grad, halo_grad = call(
-        tile_back_kernel,
-        [
-            shaped(width, width),
-            shaped(tile_rows, width, dtype=f32),
-            shaped(edge, width),
-        ],
-        [slots, came_back, table, average, pre_act, w_near],
-        scratch=[pltpu.VMEM((tile_rows, width), bf16), pltpu.VMEM((tile_rows, width), bf16)],
-        flops=6e9,
+    lifted_grad, act_grad, near_grad = call(
+        act_kernel,
+        [shaped(tile_rows, width), shaped(tile_rows, width), shaped(width, width)],
+        [slots, came_back, average, pre_act],
+        flops=3e9,
+    )
+    near_parts = exchange(near_grad, tiles).reshape(tiles, width // tiles, width)
+    near_share = jnp.sum(near_parts.astype(f32), axis=0)
+    near_all = jnp.broadcast_to(near_share.astype(bf16), (tiles, *near_share.shape))
+    near_sum = exchange(near_all.reshape(width, width), tiles)
+    row_grad, halo_grad = call(
+        spread_rows_kernel,
+        [shaped(tile_rows, width, dtype=f32), shaped(edge, width)],
+        [lifted_grad, act_grad, table, w_near],
+        scratch=[pltpu.VMEM((tile_rows, width), bf16)],
+        flops=3e9,
         neighbours=neighbours,
     )
     returned = [
@@ -510,25 +559,30 @@
         shifted(halo_grad[2 * border_rows : 3 * border_rows], "ty", 1),
         shifted(halo_grad[3 * border_rows :], "ty", -1),
     ]
-    near_sum = lax.psum(near_grad, ("tx", "ty"))
     (grad_points,) = call(
         finish_kernel, [shaped(tile_rows, width)], [lists, row_grad, *returned], flops=1e9
     )
     scale = 1.0 / math.sqrt(tiles * tile_rows)
-    scaled = totals.astype(f32) * scale
-    down_sum = scaled[0:hidden]
-    up_sum = jnp.concatenate(
-        [scaled[hidden + at : hidden + at + width] for at in range(0, hidden, width)], axis=1
-    )
-    conv_sum = scaled[2 * hidden : 2 * hidden + taps * inner].reshape(taps, inner, groups, inner)
-    gains = scaled[2 * hidden + taps * inner :]
+    up_sum, down_sum, conv_sum, gain_one_sum, gain_two_sum = call(
+        spread_kernel,
+        [
+            shaped(width, hidden, dtype=f32),
+            shaped(hidden, width, dtype=f32),
+            shaped(*conv_w.shape, dtype=f32),
+            shaped(1, width, dtype=f32),
+            shaped(1, width, dtype=f32),
+        ],
+        [totals],
+        flops=1e6,
+        scale=scale,
+    )
     return (
         out_rows[None],
         grad_points[None],
         near_sum.astype(f32) * scale,
-        gains[0],
-        conv_sum.transpose(0, 2, 1, 3),
-        gains[1],
+        gain_one_sum[0],
+        conv_sum,
+        gain_two_sum[0],
         up_sum,
         down_sum,
     )

time: 313 us -> 248 us (0.79)
  blocking collectives: 65.7 us -> 0 us
  waiting for transfers between devices: 126 us -> 98.8 us
  starting transfers between devices: 29.7 us -> 56.7 us
  local copies, waits for them, and re-layouts: 12.9 us -> 22 us
  Pallas kernels: 59 us -> 53.6 us
    psum x1, waiting for transfers between devices: 109 us -> 36.2 us  [body(): totals = lax.all_gather(lax.psum(share, 'tx'), 'ty', axis=0, tiled=True)]
    all_to_all x2 -> x0, blocking collectives: 65.7 us -> none  [exchange(): lax.all_to_all(rows, ('tx', 'ty'), split_axis=0, concat_axis=0, tiled=True)]
    reduce_scatter x0 -> x1, waiting for transfers between devices: none -> 27.7 us  [body(): share = lax.psum_scatter(sums, 'ty', scatter_dimension=0, tiled=True)]
    all_to_all x2 -> x6, starting transfers between devices: 11 us -> 38.1 us  [exchange(): lax.all_to_all(rows, ('tx', 'ty'), split_axis=0, concat_axis=0, tiled=True)]
    all_to_all x2 -> x6, waiting for transfers between devices: 12.7 us -> 31.8 us  [exchange(): lax.all_to_all(rows, ('tx', 'ty'), split_axis=0, concat_axis=0, tiled=True)]
    unnamed x42 -> x58, local copies, waits for them, and re-layouts: 9.47 us -> 20.6 us
    pallas_call x9 -> x13, Pallas kernels: 59 us -> 53.6 us  [call(): pl.pallas_call(functools.partial(kernel, **static) if static else kernel,...]
  transfers between devices with their start and end apart: 11 -> 17, of which waited for: 4 -> 7; matrix products, arithmetic and copies ran while one was open for 0% -> 0% of each run, Pallas kernels for 5% -> 16%
where the time goes in v1:
time: 248 us; the launch traced here: 247 us
  waiting for transfers between devices  98.8 us (40%)
  starting transfers between devices  56.7 us (23%)
  Pallas kernels  53.6 us (22%)
  local copies, waits for them, and re-layouts  22 us (9%)
  between operations  14.8 us (6%)
    pallas_call x13, Pallas kernels, call(): pl.pallas_call(functools.partial(kernel, **static) if static else kernel,...  53.6 us
    all_to_all x6, starting transfers between devices, exchange(): lax.all_to_all(rows, ('tx', 'ty'), split_axis=0, concat_axis=0, tiled=True)  38.1 us
    psum x1, waiting for transfers between devices, body(): totals = lax.all_gather(lax.psum(share, 'tx'), 'ty', axis=0, tiled=True)  36.2 us
    all_to_all x6, waiting for transfers between devices, exchange(): lax.all_to_all(rows, ('tx', 'ty'), split_axis=0, concat_axis=0, tiled=True)  31.8 us
    reduce_scatter x1, waiting for transfers between devices, body(): share = lax.psum_scatter(sums, 'ty', scatter_dimension=0, tiled=True)  27.7 us
    unnamed x58, local copies, waits for them, and re-layouts  20.6 us
    ppermute x8, starting transfers between devices, shifted(): lax.ppermute(value, axis, [(source, source + steps) for source in range(i...  18.2 us
  transfers between devices with their start and end apart: 17, of which 7 were waited for; matrix products, arithmetic and copies ran while one was open for 0% of the time, Pallas kernels for 16%

profile of v1, /device:TPU:0, one launch (start us, length us, event | category | flops | bytes accessed | tf_op | source)
XLA Modules:
  0.0 246.6 jit_solution(10902905059221780424)
XLA Ops:
  11.4 2.2 shard_map.193
  13.6 7.3 %all-to-all-start.2 = ((bf16[32,64,256]{2,1,0:T(8,128)(2,1)}), bf16[32,64,256]{2,1,0:T(8,128)(2,1)S(1)}, u32[]{:S(2)}, u32[]{:S(2)}) async-start(bf16[32,64,256]{2,1,0:T(8,128)(2,1)} %bitcast.11), calls=%async_computation.2 | async-start | bytes 2097152 | tf_op jit(solution)/shard_map/all_to_all | solution.py:394
  22.2 4.5 %collective-permute-start.1 = (bf16[64,256]{1,0:T(8,128)(2,1)S(1)}, bf16[64,256]{1,0:T(8,128)(2,1)S(1)}, u32[]{:S(2)}, u32[]{:S(2)}) collective-permute-start(bf16[64,256]{1,0:T(8,128)(2,1)S(1)} %get-tuple-element.54), channel_id=1, source_target_pairs={{0,8},{8,16},{16,24},{1,9},{9,17},{17,25},{2,10},{10,18},{18,26},{... | collective-permute-start | bytes 98312 | tf_op jit(solution)/shard_map/ppermute | solution.py:390
  28.1 3.0 %collective-permute-start.3 = (bf16[64,256]{1,0:T(8,128)(2,1)S(1)}, bf16[64,256]{1,0:T(8,128)(2,1)S(1)}, u32[]{:S(2)}, u32[]{:S(2)}) collective-permute-start(bf16[64,256]{1,0:T(8,128)(2,1)S(1)} %get-tuple-element.52), channel_id=1, source_target_pairs={{0,1},{1,2},{2,3},{3,4},{4,5},{5,6},{6,7},{8,9},{9,10},{10,11},{11... | collective-permute-start | bytes 98312 | tf_op jit(solution)/shard_map/ppermute | solution.py:390
  31.1 5.1 %shard_map.189.table_ref = bf16[1280,1024]{1,0:T(8,128)(2,1)S(1)} custom-call(s32[16,1024]{1,0:T(8,128)S(1)} %bitcast.31), custom_call_target="tpu_custom_call" | custom-call | flops 8000000000 | bytes 2686976 | tf_op jit(solution)/shard_map/pallas_call | solution.py:372
  36.2 3.0 %collective-permute-done.1.halo1 = bf16[64,256]{1,0:T(8,128)(2,1)S(1)} collective-permute-done((bf16[64,256]{1,0:T(8,128)(2,1)S(1)}, bf16[64,256]{1,0:T(8,128)(2,1)S(1)}, u32[]{:S(2)}, u32[]{:S(2)}) %collective-permute-start.1) | collective-permute-done | bytes 32800 | tf_op jit(solution)/shard_map/ppermute | solution.py:390
  39.2 3.4 %shard_map.190 = (bf16[256,1024]{1,0:T(8,128)(2,1)S(1)}, f32[1024,256]{1,0:T(8,128)S(1)}, bf16[2048,256]{1,0:T(8,128)(2,1)}) custom-call(s32[1,1024]{1,0:T(1,128)S(1)} %get-tuple-element.28.slots_ref, bf16[1024,256]{1,0:T(8,128)(2,1)S(1)} %bitcast.28, bf16[64,256]{1,0:T(8,128)(2,1)S(1)} %collective-permute-done.halo0, ...), custom_call_target="tpu_custom_call" | custom-call | flops 4000000000 | bytes 6033408 | tf_op jit(solution)/shard_map/pallas_call | solution.py:372
  47.5 9.8 %all-to-all-start = ((bf16[32,64,256]{2,1,0:T(8,128)(2,1)}), bf16[32,64,256]{2,1,0:T(8,128)(2,1)S(1)}, u32[]{:S(2)}, u32[]{:S(2)}) async-start(bf16[32,64,256]{2,1,0:T(8,128)(2,1)} %bitcast.2), calls=%async_computation | async-start | bytes 2097152 | tf_op jit(solution)/shard_map/all_to_all | solution.py:394
  57.3 2.4 shard_map.194.out_grad_ref
  60.7 22.8 %all-to-all-done = bf16[32,64,256]{2,1,0:T(8,128)(2,1)S(1)} async-done(((bf16[32,64,256]{2,1,0:T(8,128)(2,1)}), bf16[32,64,256]{2,1,0:T(8,128)(2,1)S(1)}, u32[]{:S(2)}, u32[]{:S(2)}) %all-to-all-start) | async-done | bytes 1048608 | tf_op jit(solution)/shard_map/all_to_all | solution.py:394
  83.5 11.3 %shard_map.191 = (bf16[2048,256]{1,0:T(8,128)(2,1)S(1)}, f32[2048,256]{1,0:T(8,128)S(1)}, bf16[2048,256]{1,0:T(8,128)(2,1)}) custom-call(s32[1,2048]{1,0:T(1,128)S(1)} %copy-done.9, bf16[2048,256]{1,0:T(8,128)(2,1)S(1)} %bitcast.25, bf16[768,32]{1,0:T(8,128)(2,1)S(1)} %bitcast.29, f32[1,256]{1,0:T(1,128)S(1)} %bitcast.32, f32[1,256]{1,0:T(1,128)S(1)} %bitcast.34, ...), custom_call_target="tpu_custom_call" | custom-call | flops 10000000000 | bytes 6350848 | tf_op jit(solution)/shard_map/pallas_call | solution.py:372
  97.2 3.6 %all-to-all-start.1 = ((bf16[32,64,256]{2,1,0:T(8,128)(2,1)}), bf16[32,64,256]{2,1,0:T(8,128)(2,1)S(1)}, u32[]{:S(2)}, u32[]{:S(2)}) async-start(bf16[32,64,256]{2,1,0:T(8,128)(2,1)} %bitcast.7), calls=%async_computation.1 | async-start | bytes 2097152 | tf_op jit(solution)/shard_map/all_to_all | solution.py:394
  104.9 16.9 %shard_map.195 = (bf16[2048,256]{1,0:T(8,128)(2,1)S(1)}, bf16[2176,256]{1,0:T(8,128)(2,1)}) custom-call(bf16[2048,256]{1,0:T(8,128)(2,1)S(1)} %copy-done.28, bf16[2048,256]{1,0:T(8,128)(2,1)S(1)} %copy-done.26, f32[2048,256]{1,0:T(8,128)S(1)} %copy-done.24, bf16[768,32]{1,0:T(8,128)(2,1)S(1)} %bitcast.30, f32[1,256]{1,0:T(1,128)S(1)} %bitcast.33, ...), custom_call_target="tpu_custom_call" | custom-call | flops 40000000000 | bytes 7456768 | tf_op jit(solution)/shard_map/pallas_call | solution.py:372
  121.8 5.2 %all-to-all-done.1 = bf16[32,64,256]{2,1,0:T(8,128)(2,1)S(1)} async-done(((bf16[32,64,256]{2,1,0:T(8,128)(2,1)}), bf16[32,64,256]{2,1,0:T(8,128)(2,1)S(1)}, u32[]{:S(2)}, u32[]{:S(2)}) %all-to-all-start.1) | async-done | bytes 1048608 | tf_op jit(solution)/shard_map/all_to_all | solution.py:394
  127.1 3.3 %shard_map.196 = bf16[2048,256]{1,0:T(8,128)(2,1)} custom-call(s32[1,2048]{1,0:T(1,128)S(1)} %copy-done.9, bf16[2048,256]{1,0:T(8,128)(2,1)S(1)} %get-tuple-element.34.rows_ref, bf16[2048,256]{1,0:T(8,128)(2,1)S(1)} %bitcast.21), custom_call_target="tpu_custom_call" | custom-call | flops 4000000000 | bytes 3153920 | tf_op jit(solution)/shard_map/pallas_call | solution.py:372
  130.4 3.6 %all-to-all-start.3 = ((bf16[32,64,256]{2,1,0:T(8,128)(2,1)}), bf16[32,64,256]{2,1,0:T(8,128)(2,1)S(1)}, u32[]{:S(2)}, u32[]{:S(2)}) async-start(bf16[32,64,256]{2,1,0:T(8,128)(2,1)} %bitcast.13), calls=%async_computation.3 | async-start | bytes 2097152 | tf_op jit(solution)/shard_map/all_to_all | solution.py:394
  134.1 27.7 %reduce-scatter.2.cloned.1.call-done = bf16[272,256]{1,0:T(8,128)(2,1)} async-done(((bf16[2176,256]{1,0:T(8,128)(2,1)}), bf16[272,256]{1,0:T(8,128)(2,1)}) %reduce-scatter.2.cloned.1.call-update) | async-done | bytes 139280 | tf_op jit(solution)/shard_map/reduce_scatter | solution.py:533
  162.1 36.2 %all-reduce.2.cloned.1.call-done = bf16[272,256]{1,0:T(8,128)(2,1)} async-done(((bf16[272,256]{1,0:T(8,128)(2,1)}), bf16[272,256]{1,0:T(8,128)(2,1)}) %all-reduce.2.cloned.1.call-update) | async-done | bytes 139280 | tf_op jit(solution)/shard_map/psum | solution.py:534
  199.4 2.5 %shard_map.197 = (bf16[1024,256]{1,0:T(8,128)(2,1)S(1)}, bf16[1024,256]{1,0:T(8,128)(2,1)S(1)}, bf16[256,256]{1,0:T(8,128)(2,1)}) custom-call(s32[1,1024]{1,0:T(1,128)S(1)} %get-tuple-element.28.slots_ref, bf16[2048,256]{1,0:T(8,128)(2,1)S(1)} %bitcast.24, bf16[256,1024]{1,0:T(8,128)(2,1)S(1)} %copy-done.22, f32[1024,256]{1,0:T(8,128)S(1)} %copy-done.16), custom_call_target="tpu_custom_call" | custom-call | flops 3000000000 | bytes 3805184 | tf_op jit(solution)/shard_map/pallas_call | solution.py:372
  203.5 4.6 %all-to-all-start.4 = ((bf16[32,8,256]{2,1,0:T(8,128)(2,1)}), bf16[32,8,256]{2,1,0:T(8,128)(2,1)S(1)}, u32[]{:S(2)}, u32[]{:S(2)}) async-start(bf16[32,8,256]{2,1,0:T(8,128)(2,1)} %bitcast.16), calls=%async_computation.4 | async-start | bytes 262144 | tf_op jit(solution)/shard_map/all_to_all | solution.py:394
  213.1 3.7 %collective-permute-start.4 = (bf16[64,256]{1,0:T(8,128)(2,1)S(1)}, bf16[64,256]{1,0:T(8,128)(2,1)S(1)}, u32[]{:S(2)}, u32[]{:S(2)}) collective-permute-start(bf16[64,256]{1,0:T(8,128)(2,1)S(1)} %get-tuple-element.51), channel_id=1, source_target_pairs={{0,8},{8,16},{16,24},{1,9},{9,17},{17,25},{2,10},{10,18},{18,26},{... | collective-permute-start | bytes 98312 | tf_op jit(solution)/shard_map/ppermute | solution.py:390
  221.9 9.2 %all-to-all-start.5 = ((bf16[32,8,256]{2,1,0:T(8,128)(2,1)}), bf16[32,8,256]{2,1,0:T(8,128)(2,1)S(1)}, u32[]{:S(2)}, u32[]{:S(2)}) async-start(bf16[32,8,256]{2,1,0:T(8,128)(2,1)} %broadcast_in_dim.11), calls=%async_computation.5 | async-start | bytes 262144 | tf_op jit(solution)/shard_map/all_to_all | solution.py:394
  231.1 2.1 shard_map.192
  237.2 2.1 all-to-all-done.5
  (90 shorter events, 36.2 us)
Async XLA Ops:
  13.6 17.5 %copy-start.8 = (s32[1,16,1024]{2,1,0:T(8,128)S(1)}, s32[1,16,1024]{2,1,0:T(8,128)}, u32[]{:S(2)}) copy-start(s32[1,16,1024]{2,1,0:T(8,128)} %param.18) | copy-start | bytes 196612
  13.6 33.9 %all-to-all-start.2 = ((bf16[32,64,256]{2,1,0:T(8,128)(2,1)}), bf16[32,64,256]{2,1,0:T(8,128)(2,1)S(1)}, u32[]{:S(2)}, u32[]{:S(2)}) async-start(bf16[32,64,256]{2,1,0:T(8,128)(2,1)} %bitcast.11), calls=%async_computation.2 | async-start | bytes 2097152 | tf_op jit(solution)/shard_map/all_to_all | solution.py:394
  20.9 15.3 %collective-permute-start = (bf16[64,256]{1,0:T(8,128)(2,1)S(1)}, bf16[64,256]{1,0:T(8,128)(2,1)S(1)}, u32[]{:S(2)}, u32[]{:S(2)}) collective-permute-start(bf16[64,256]{1,0:T(8,128)(2,1)S(1)} %get-tuple-element.55), channel_id=1, source_target_pairs={{8,0},{16,8},{24,16},{9,1},{17,9},{25,17},{10,2},{18,10},{26,18},{... | collective-permute-start | bytes 98312 | tf_op jit(solution)/shard_map/ppermute | solution.py:390
  22.2 17.0 %collective-permute-start.1 = (bf16[64,256]{1,0:T(8,128)(2,1)S(1)}, bf16[64,256]{1,0:T(8,128)(2,1)S(1)}, u32[]{:S(2)}, u32[]{:S(2)}) collective-permute-start(bf16[64,256]{1,0:T(8,128)(2,1)S(1)} %get-tuple-element.54), channel_id=1, source_target_pairs={{0,8},{8,16},{16,24},{1,9},{9,17},{17,25},{2,10},{10,18},{18,26},{... | collective-permute-start | bytes 98312 | tf_op jit(solution)/shard_map/ppermute | solution.py:390
  26.8 12.5 %collective-permute-start.2 = (bf16[64,256]{1,0:T(8,128)(2,1)S(1)}, bf16[64,256]{1,0:T(8,128)(2,1)S(1)}, u32[]{:S(2)}, u32[]{:S(2)}) collective-permute-start(bf16[64,256]{1,0:T(8,128)(2,1)S(1)} %get-tuple-element.53), channel_id=1, source_target_pairs={{1,0},{2,1},{3,2},{4,3},{5,4},{6,5},{7,6},{9,8},{10,9},{11,10},{12... | collective-permute-start | bytes 98312 | tf_op jit(solution)/shard_map/ppermute | solution.py:390
  28.1 11.2 %collective-permute-start.3 = (bf16[64,256]{1,0:T(8,128)(2,1)S(1)}, bf16[64,256]{1,0:T(8,128)(2,1)S(1)}, u32[]{:S(2)}, u32[]{:S(2)}) collective-permute-start(bf16[64,256]{1,0:T(8,128)(2,1)S(1)} %get-tuple-element.52), channel_id=1, source_target_pairs={{0,1},{1,2},{2,3},{3,4},{4,5},{5,6},{6,7},{8,9},{9,10},{10,11},{11... | collective-permute-start | bytes 98312 | tf_op jit(solution)/shard_map/ppermute | solution.py:390
  47.5 36.0 %all-to-all-start = ((bf16[32,64,256]{2,1,0:T(8,128)(2,1)}), bf16[32,64,256]{2,1,0:T(8,128)(2,1)S(1)}, u32[]{:S(2)}, u32[]{:S(2)}) async-start(bf16[32,64,256]{2,1,0:T(8,128)(2,1)} %bitcast.2), calls=%async_computation | async-start | bytes 2097152 | tf_op jit(solution)/shard_map/all_to_all | solution.py:394
  57.3 26.2 %copy-start.4 = (bf16[256,1024]{1,0:T(8,128)(2,1)S(1)}, bf16[256,1024]{1,0:T(8,128)(2,1)}, u32[]{:S(2)}) copy-start(bf16[256,1024]{1,0:T(8,128)(2,1)} %up_ref.3) | copy-start | bytes 1572868
  57.3 26.2 %copy-start.5 = (bf16[1024,256]{1,0:T(8,128)(2,1)S(1)}, bf16[1024,256]{1,0:T(8,128)(2,1)}, u32[]{:S(2)}) copy-start(bf16[1024,256]{1,0:T(8,128)(2,1)} %down_ref.3) | copy-start | bytes 1572868
  57.3 26.2 %copy-start.6 = (bf16[3,8,32,32]{3,2,1,0:T(8,128)(2,1)S(1)}, bf16[3,8,32,32]{3,2,1,0:T(8,128)(2,1)}, u32[]{:S(2)}) copy-start(bf16[3,8,32,32]{3,2,1,0:T(8,128)(2,1)} %param.21) | copy-start | bytes 147460
  57.3 26.2 %copy-start.11 = (f32[256]{0:T(256)S(1)}, f32[256]{0:T(256)}, u32[]{:S(2)}) copy-start(f32[256]{0:T(256)} %param.20) | copy-start | bytes 3076
  57.3 26.2 %copy-start.12 = (f32[256]{0:T(256)S(1)}, f32[256]{0:T(256)}, u32[]{:S(2)}) copy-start(f32[256]{0:T(256)} %param.22) | copy-start | bytes 3076
  97.2 29.9 %all-to-all-start.1 = ((bf16[32,64,256]{2,1,0:T(8,128)(2,1)}), bf16[32,64,256]{2,1,0:T(8,128)(2,1)S(1)}, u32[]{:S(2)}, u32[]{:S(2)}) async-start(bf16[32,64,256]{2,1,0:T(8,128)(2,1)} %bitcast.7), calls=%async_computation.1 | async-start | bytes 2097152 | tf_op jit(solution)/shard_map/all_to_all | solution.py:394
  100.9 60.9 %reduce-scatter.2.cloned.1.call-start = ((), (), s32[]{:S(2)}) async-start(), calls=%async_computation.7 | async-start | bytes 1253376 | tf_op jit(solution)/shard_map/reduce_scatter | solution.py:533
  130.4 67.9 %copy-start.16 = (f32[1024,256]{1,0:T(8,128)S(1)}, f32[1024,256]{1,0:T(8,128)}, u32[]{:S(2)}) copy-start(f32[1024,256]{1,0:T(8,128)} %copy-done.15) | copy-start | bytes 3145732
  130.4 67.9 %all-to-all-start.3 = ((bf16[32,64,256]{2,1,0:T(8,128)(2,1)}), bf16[32,64,256]{2,1,0:T(8,128)(2,1)S(1)}, u32[]{:S(2)}, u32[]{:S(2)}) async-start(bf16[32,64,256]{2,1,0:T(8,128)(2,1)} %bitcast.13), calls=%async_computation.3 | async-start | bytes 2097152 | tf_op jit(solution)/shard_map/all_to_all | solution.py:394
  134.0 64.3 %all-reduce.2.cloned.1.call-start = ((), (), s32[]{:S(2)}) async-start(), calls=%async_computation.8 | async-start | bytes 278528 | tf_op jit(solution)/shard_map/psum | solution.py:534
  161.8 71.4 %all-gather.2.cloned.1.call-start = ((), (), s32[]{:S(2)}) async-start(), calls=%async_computation.9 | async-start | bytes 1253376 | tf_op jit(solution)/shard_map/all_gather | solution.py:534
  203.5 17.7 %all-to-all-start.4 = ((bf16[32,8,256]{2,1,0:T(8,128)(2,1)}), bf16[32,8,256]{2,1,0:T(8,128)(2,1)S(1)}, u32[]{:S(2)}, u32[]{:S(2)}) async-start(bf16[32,8,256]{2,1,0:T(8,128)(2,1)} %bitcast.16), calls=%async_computation.4 | async-start | bytes 262144 | tf_op jit(solution)/shard_map/all_to_all | solution.py:394
  213.1 23.0 %collective-permute-start.4 = (bf16[64,256]{1,0:T(8,128)(2,1)S(1)}, bf16[64,256]{1,0:T(8,128)(2,1)S(1)}, u32[]{:S(2)}, u32[]{:S(2)}) collective-permute-start(bf16[64,256]{1,0:T(8,128)(2,1)S(1)} %get-tuple-element.51), channel_id=1, source_target_pairs={{0,8},{8,16},{16,24},{1,9},{9,17},{17,25},{2,10},{10,18},{18,26},{... | collective-permute-start | bytes 98312 | tf_op jit(solution)/shard_map/ppermute | solution.py:390
  216.8 19.3 %collective-permute-start.5 = (bf16[64,256]{1,0:T(8,128)(2,1)S(1)}, bf16[64,256]{1,0:T(8,128)(2,1)S(1)}, u32[]{:S(2)}, u32[]{:S(2)}) collective-permute-start(bf16[64,256]{1,0:T(8,128)(2,1)S(1)} %get-tuple-element.50), channel_id=1, source_target_pairs={{8,0},{16,8},{24,16},{9,1},{17,9},{25,17},{10,2},{18,10},{26,18},{... | collective-permute-start | bytes 98312 | tf_op jit(solution)/shard_map/ppermute | solution.py:390
  218.1 18.0 %collective-permute-start.6 = (bf16[64,256]{1,0:T(8,128)(2,1)S(1)}, bf16[64,256]{1,0:T(8,128)(2,1)S(1)}, u32[]{:S(2)}, u32[]{:S(2)}) collective-permute-start(bf16[64,256]{1,0:T(8,128)(2,1)S(1)} %get-tuple-element.49), channel_id=1, source_target_pairs={{0,1},{1,2},{2,3},{3,4},{4,5},{5,6},{6,7},{8,9},{9,10},{10,11},{11... | collective-permute-start | bytes 98312 | tf_op jit(solution)/shard_map/ppermute | solution.py:390
  219.9 16.2 %collective-permute-start.7 = (bf16[64,256]{1,0:T(8,128)(2,1)S(1)}, bf16[64,256]{1,0:T(8,128)(2,1)S(1)}, u32[]{:S(2)}, u32[]{:S(2)}) collective-permute-start(bf16[64,256]{1,0:T(8,128)(2,1)S(1)} %get-tuple-element.48), channel_id=1, source_target_pairs={{1,0},{2,1},{3,2},{4,3},{5,4},{6,5},{7,6},{9,8},{10,9},{11,10},{12... | collective-permute-start | bytes 98312 | tf_op jit(solution)/shard_map/ppermute | solution.py:390
  221.9 17.4 %all-to-all-start.5 = ((bf16[32,8,256]{2,1,0:T(8,128)(2,1)}), bf16[32,8,256]{2,1,0:T(8,128)(2,1)S(1)}, u32[]{:S(2)}, u32[]{:S(2)}) async-start(bf16[32,8,256]{2,1,0:T(8,128)(2,1)} %broadcast_in_dim.11), calls=%async_computation.5 | async-start | bytes 262144 | tf_op jit(solution)/shard_map/all_to_all | solution.py:394
  (22 other events, 48.7 us)
Sparse Core Ops, SparseCore 0:
  122.0 39.7 reduce-scatter.1
  164.1 34.1 all-reduce.1
  200.3 25.1 all-gather.1

commit v2 on v1

--- a/solution.py
+++ b/solution.py
@@ -1,4 +1,3 @@
-import functools
 import math
 
 import jax
@@ -89,12 +88,16 @@
     sent_ref[...] = dot(chosen, points_ref[...], TN).astype(bf16)
 
 
-def pack_kernel(slots_ref, rows_ref, packed_ref):
+def pack_rows(slots_ref, rows_ref, packed_out, stage_ref, sems):
     slots = slots_ref[...]
-    for start in range(0, packed_ref.shape[0], WIDE):
-        packed_ref[pl.ds(start, WIDE), :] = dot(
-            mark_slots(slots, start, WIDE), rows_ref[...]
-        ).astype(bf16)
+    copies = []
+    for at, start in enumerate(range(0, packed_out.shape[0], WIDE)):
+        place = pl.ds(start, WIDE)
+        stage_ref[place, :] = dot(mark_slots(slots, start, WIDE), rows_ref[...]).astype(bf16)
+        copies.append(pltpu.make_async_copy(stage_ref.at[place], packed_out.at[place], sems.at[at]))
+        copies[-1].start()
+    for copy in copies:
+        copy.wait()
 
 
 def unpack_kernel(slots_ref, packed_ref, rows_ref):
@@ -105,68 +108,109 @@
         ).astype(bf16)
 
 
-def count_kernel(near_ref, table_ref):
+def count_kernel(near_ref, kept_ref, table_ref, sems):
     neighbours, rows = near_ref.shape
     step = 16
     zero = jnp.zeros((step, LANES), bf16)
     one = jnp.ones((step, LANES), bf16)
-
-    def block(at, _):
-        lane_block = lax.rem(at, rows // LANES)
-        row_block = lax.div(at, rows // LANES)
-        lane_at = pl.multiple_of(lane_block * LANES, LANES)
+    row_blocks = table_ref.shape[0] // CHUNK
+
+    def copy_out(row_block):
+        place = pl.ds(pl.multiple_of(row_block * CHUNK, CHUNK), CHUNK)
+        return pltpu.make_async_copy(table_ref.at[place], kept_ref.at[place], sems.at[row_block])
+
+    def rows_of(row_block, _):
         row_at = pl.multiple_of(row_block * CHUNK, CHUNK)
-        local = (near_ref[:, pl.ds(lane_at, LANES)] - row_at).astype(f32)
-        spread = [
-            jnp.broadcast_to(local[k : k + 1, :], (step, LANES)).astype(bf16)
-            for k in range(neighbours)
-        ]
-        base = iota((step, LANES), 0).astype(f32)
-        for inner in range(0, CHUNK, step):
-            here = (base + float(inner)).astype(bf16)
-            total = zero
-            for k in range(neighbours):
-                total = total + jnp.where(spread[k] == here, one, zero)
-            table_ref[pl.ds(row_at + inner, step), pl.ds(lane_at, LANES)] = total
+
+        def block(lane_block, _):
+            lane_at = pl.multiple_of(lane_block * LANES, LANES)
+            local = (near_ref[:, pl.ds(lane_at, LANES)] - row_at).astype(f32)
+            spread = [
+                jnp.broadcast_to(local[k : k + 1, :], (step, LANES)).astype(bf16)
+                for k in range(neighbours)
+            ]
+            base = iota((step, LANES), 0).astype(f32)
+            for inner in range(0, CHUNK, step):
+                here = (base + float(inner)).astype(bf16)
+                total = zero
+                for k in range(neighbours):
+                    total = total + jnp.where(spread[k] == here, one, zero)
+                table_ref[pl.ds(row_at + inner, step), pl.ds(lane_at, LANES)] = total
+            return 0
+
+        lax.fori_loop(0, rows // LANES, block, 0)
+        copy_out(row_block).start()
         return 0
 
-    lax.fori_loop(0, (rows // LANES) * (table_ref.shape[0] // CHUNK), block, 0)
+    lax.fori_loop(0, row_blocks, rows_of, 0)
+    for row_block in range(row_blocks):
+        copy_out(row_block).wait()
 
 
 def lift_kernel(
-    slots_ref, points_ref, halo0, halo1, halo2, halo3, table_ref, w_ref, average_ref, pre_ref, packed_ref,
-    lifted_ref, *, neighbours
+    slots_ref, points_ref, grad_ref, halo0, halo1, halo2, halo3, table_ref, w_ref,
+    average_out, pre_out, packed_out,
+    average_ref, pre_ref, both_ref, stage_ref, sems, pack_sems, *, neighbours
 ):
+    width = points_ref.shape[1]
     ext = jnp.concatenate([points_ref[...], halo0[...], halo1[...], halo2[...], halo3[...]], axis=0)
     average = (dot(ext, table_ref[...], TN) * (1.0 / neighbours)).astype(bf16)
     average_ref[...] = average
-    pre_act = dot(average, w_ref[...], TN)
-    pre_ref[...] = pre_act
-    lifted_ref[...] = (points_ref[...].astype(f32) + gelu_tanh(pre_act)).astype(bf16)
-    pack_kernel(slots_ref, lifted_ref, packed_ref)
-
-
-def act_kernel(slots_ref, back_ref, average_ref, pre_ref, lifted_ref, act_ref, near_ref):
-    for start in range(0, lifted_ref.shape[0], CHUNK):
-        here = pl.ds(start, CHUNK)
-        column = column_of(slots_ref[:, start : start + CHUNK], CHUNK)
-        lifted_grad = dot(pick_rows(column, back_ref.shape[0]), back_ref[...])
-        lifted_ref[here, :] = lifted_grad.astype(bf16)
-        value = pre_ref[here, :]
-        square, tangent = gelu_parts(value)
-        act_ref[here, :] = (lifted_grad * slope_of(value, square, tangent)).astype(bf16)
-    near_ref[...] = dot(average_ref[...], act_ref[...]).astype(near_ref.dtype)
-
-
-def spread_rows_kernel(
-    lifted_ref, act_ref, table_ref, w_ref, row_ref, halo_ref, spread_ref, *, neighbours
+    keep_average = pltpu.make_async_copy(average_ref, average_out, sems.at[0])
+    keep_average.start()
+    pre_ref[...] = dot(average, w_ref[...], TN)
+    keep_pre = pltpu.make_async_copy(pre_ref, pre_out, sems.at[1])
+    keep_pre.start()
+    for row in range(0, points_ref.shape[0], BLOCK):
+        here = pl.ds(row, BLOCK)
+        both_ref[here, 0:width] = (
+            points_ref[here, :].astype(f32) + gelu_tanh(pre_ref[here, :])
+        ).astype(bf16)
+    both_ref[:, width:] = grad_ref[...]
+    pack_rows(slots_ref, both_ref, packed_out, stage_ref, pack_sems)
+    keep_average.wait()
+    keep_pre.wait()
+
+
+def tile_back_kernel(
+    slots_ref, back_ref, w_ref, table_in, average_in, pre_in,
+    row_out, near_ref, halo_ref,
+    row_ref, table_ref, average_ref, pre_ref, act_ref, spread_ref, sems, *, neighbours
 ):
     rows = row_ref.shape[0]
+    fetch_pre = pltpu.make_async_copy(pre_in, pre_ref, sems.at[0])
+    fetch_average = pltpu.make_async_copy(average_in, average_ref, sems.at[1])
+    fetch_table = pltpu.make_async_copy(table_in, table_ref, sems.at[2])
+
+    def keep_row(start):
+        place = pl.ds(start, WIDE)
+        return pltpu.make_async_copy(row_ref.at[place], row_out.at[place], sems.at[3 + start // WIDE])
+
+    fetch_pre.start()
+    fetch_average.start()
+    fetch_table.start()
+    fetch_pre.wait()
+    for start in range(0, rows, CHUNK):
+        column = column_of(slots_ref[:, start : start + CHUNK], CHUNK)
+        wide = dot(pick_rows(column, back_ref.shape[0]), back_ref[...])
+        for row in range(0, CHUNK, BLOCK):
+            here = pl.ds(start + row, BLOCK)
+            lifted_grad = wide[row : row + BLOCK]
+            row_ref[here, :] = lifted_grad
+            value = pre_ref[here, :]
+            square, tangent = gelu_parts(value)
+            act_ref[here, :] = (lifted_grad * slope_of(value, square, tangent)).astype(bf16)
+    fetch_average.wait()
+    near_ref[...] = dot(average_ref[...], act_ref[...]).astype(near_ref.dtype)
     spread_ref[...] = (dot(act_ref[...], w_ref[...], NT) * (1.0 / neighbours)).astype(bf16)
+    fetch_table.wait()
     halo_ref[...] = dot(table_ref[rows:, :], spread_ref[...]).astype(bf16)
     for start in range(0, rows, WIDE):
         here = pl.ds(start, WIDE)
-        row_ref[here, :] = lifted_ref[here, :].astype(f32) + dot(table_ref[here, :], spread_ref[...])
+        row_ref[here, :] = row_ref[here, :] + dot(table_ref[here, :], spread_ref[...])
+        keep_row(start).start()
+    for start in range(0, rows, WIDE):
+        keep_row(start).wait()
 
 
 def finish_kernel(lists_ref, row_ref, back0, back1, back2, back3, out_ref):
@@ -192,29 +236,26 @@
     ref[PAD + PATCH :, :] = edge
 
 
-def write_back(zorder_ref, rows_ref, out_ref):
-    pack_kernel(zorder_ref, rows_ref, out_ref)
-
-
-def order_kernel(zorder_ref, slots_ref, rows_ref):
-    for start in range(0, rows_ref.shape[0], WIDE):
-        column = column_of(zorder_ref[:, start : start + WIDE], WIDE)
-        rows_ref[pl.ds(start, WIDE), :] = dot(
-            pick_rows(column, slots_ref.shape[0]), slots_ref[...]
-        ).astype(bf16)
-
-
 def forward_kernel(
-    zorder_ref, lifted_ref, conv_ref, gain_one_ref, gain_two_ref, up_ref, down_ref,
-    serial_ref, state_ref, back_ref,
-    taps_ref, normed_ref, before_ref, here_ref, after_ref, second_ref, hidden_ref, result_ref,
-    *, groups, inner
+    zorder_ref, conv_ref, gain_one_ref, gain_two_ref, up_ref, down_ref, came_in,
+    serial_out, state_out, back_out,
+    lifted_ref, serial_ref, state_ref, taps_ref, normed_ref, before_ref, here_ref, after_ref, second_ref, hidden_ref,
+    result_ref, stage_ref, sems, pack_sems, *, groups, inner
 ):
     slots, width = lifted_ref.shape
+    fetch = pltpu.make_async_copy(came_in.at[:, pl.ds(0, width)], lifted_ref, sems.at[2, 0])
+    fetch.start()
     hidden_width = up_ref.shape[1]
     taps_ref[...] = full_taps(conv_ref, groups, inner)
     padded_zeros(before_ref)
     padded_zeros(after_ref)
+
+    def keep(at):
+        place = pl.ds(pl.multiple_of(at * PATCH, PATCH), PATCH)
+        return (
+            pltpu.make_async_copy(serial_ref.at[place], serial_out.at[place], sems.at[0, at]),
+            pltpu.make_async_copy(state_ref.at[place], state_out.at[place], sems.at[1, at]),
+        )
 
     def patch(at, _):
         origin = pl.multiple_of(at * PATCH, PATCH)
@@ -239,6 +280,8 @@
             state_ref[place, :] = state
             second = state * inverse_rms(state) * gain_two_ref[...]
             second_ref[pl.ds(row, BLOCK), :] = second.astype(bf16)
+        for copy in keep(at):
+            copy.start()
         for start in range(0, PATCH, CHUNK):
             value = dot(second_ref[pl.ds(start, CHUNK), :], up_ref[...])
             for row in range(0, CHUNK, 16):
@@ -253,21 +296,27 @@
             ).astype(bf16)
         return 0
 
+    fetch.wait()
     lax.fori_loop(0, slots // PATCH, patch, 0)
-    write_back(zorder_ref, result_ref, back_ref)
-
-
-def hold_kernel(zorder_ref, rows_ref, _, back_ref):
-    write_back(zorder_ref, rows_ref, back_ref)
+    pack_rows(zorder_ref, result_ref, back_out, stage_ref, pack_sems)
+    for at in range(slots // PATCH):
+        for copy in keep(at):
+            copy.wait()
 
 
 def backward_kernel(
-    serial_ref, out_grad_ref, state_ref, conv_ref, gain_one_ref, gain_two_ref, up_ref, down_ref,
-    serial_grad_ref, weights_ref,
-    taps_ref, second_ref, hidden_ref, pre_grad_ref, state_grad_ref, mixed_ref, before_ref, here_ref,
-    after_ref, normed_ref, conv_sum_ref, gains_ref, *, groups, inner
+    bit_ref, zorder_ref, conv_ref, gain_one_ref, gain_two_ref, up_ref, down_ref, came_in, serial_in, state_in,
+    serial_grad_out, keep_ref, send_ref,
+    grad_ref, serial_ref, state_ref, out_grad_ref, serial_grad_ref, weights_ref, taps_ref, second_ref, hidden_ref, pre_grad_ref, state_grad_ref, mixed_ref, before_ref, here_ref,
+    after_ref, normed_ref, conv_sum_ref, gains_ref, sems, *, groups, inner
 ):
     slots, width = serial_ref.shape
+    fetch_grad = pltpu.make_async_copy(came_in.at[:, pl.ds(width, width)], grad_ref, sems.at[1, 0])
+    fetch_state = pltpu.make_async_copy(state_in, state_ref, sems.at[2, 0])
+    fetch_serial = pltpu.make_async_copy(serial_in, serial_ref, sems.at[3, 0])
+    fetch_grad.start()
+    fetch_state.start()
+    fetch_serial.start()
     hidden_width = up_ref.shape[1]
     taps_ref[...] = full_taps(conv_ref, groups, inner)
     padded_zeros(before_ref)
@@ -276,8 +325,17 @@
     conv_sum_ref[...] = jnp.zeros_like(conv_sum_ref)
     gains_ref[...] = jnp.zeros_like(gains_ref)
 
+    def keep_grad(at):
+        place = pl.ds(pl.multiple_of(at * PATCH, PATCH), PATCH)
+        return pltpu.make_async_copy(serial_grad_ref.at[place], serial_grad_out.at[place], sems.at[0, at])
+
     def patch(at, _):
         origin = pl.multiple_of(at * PATCH, PATCH)
+        for start in range(0, PATCH, WIDE):
+            column = column_of(zorder_ref[:, pl.ds(origin + start, WIDE)], WIDE)
+            out_grad_ref[pl.ds(origin + start, WIDE), :] = dot(
+                pick_rows(column, slots), grad_ref[...]
+            ).astype(bf16)
         for start in range(0, PATCH, CHUNK):
             place = pl.ds(origin + start, CHUNK)
             state = state_ref[place, :]
@@ -321,11 +379,15 @@
             serial_grad_ref[place, :] = (
                 state_grad_ref[pl.ds(start, CHUNK), :] + scale_one * (weighted - unit_one * middle)
             ).astype(bf16)
+        keep_grad(at).start()
         for tap in range(3):
             moved = mixed_ref[pl.ds(PAD + 1 - tap, PATCH), :].astype(bf16)
             conv_sum_ref[tap] += dot(normed_ref[...], moved, TN)
         return 0
 
+    fetch_grad.wait()
+    fetch_state.wait()
+    fetch_serial.wait()
     lax.fori_loop(0, slots // PATCH, patch, 0)
     for start in range(0, hidden_width, width):
         weights_ref[start : start + width, :] = dot(
@@ -343,9 +405,37 @@
     weights_ref[at : at + 16, :] = gains_ref[...].astype(weights_ref.dtype)
     at = at + 16
     weights_ref[at:, :] = jnp.zeros((weights_ref.shape[0] - at, width), weights_ref.dtype)
-
-
-def spread_kernel(sums_ref, up_ref, down_ref, conv_ref, gain_one_ref, gain_two_ref, *, scale):
+    split_rows(bit_ref[0], weights_ref, keep_ref, send_ref)
+    for at in range(slots // PATCH):
+        keep_grad(at).wait()
+
+
+def split_rows(bit, rows_ref, keep_ref, send_ref):
+    half = keep_ref.shape[0]
+    keep_ref[...] = rows_ref[pl.ds(pl.multiple_of(bit * half, 16), half), :]
+    send_ref[...] = rows_ref[pl.ds(pl.multiple_of((1 - bit) * half, 16), half), :]
+
+
+def add_split_kernel(bit_ref, mine_ref, came_ref, keep_ref, send_ref, total_ref):
+    total_ref[...] = (mine_ref[...].astype(f32) + came_ref[...].astype(f32)).astype(bf16)
+    split_rows(bit_ref[0], total_ref, keep_ref, send_ref)
+
+
+def add_kernel(mine_ref, came_ref, total_ref):
+    total_ref[...] = (mine_ref[...].astype(f32) + came_ref[...].astype(f32)).astype(bf16)
+
+
+def join_kernel(bit_ref, mine_ref, came_ref, both_ref):
+    half = mine_ref.shape[0]
+    bit = bit_ref[0]
+    both_ref[pl.ds(pl.multiple_of(bit * half, 16), half), :] = mine_ref[...]
+    both_ref[pl.ds(pl.multiple_of((1 - bit) * half, 16), half), :] = came_ref[...]
+
+
+def spread_kernel(
+    bit_ref, mine_ref, came_ref, up_ref, down_ref, conv_ref, gain_one_ref, gain_two_ref, sums_ref, *, scale
+):
+    join_kernel(bit_ref, mine_ref, came_ref, sums_ref)
     width, hidden_width = up_ref.shape
     taps, groups, inner = conv_ref.shape[:3]
     down_ref[...] = sums_ref[0:hidden_width, :].astype(f32) * scale
@@ -364,20 +454,31 @@
     gain_two_ref[...] = gains[1:2, :]
 
 
-def call(kernel, outs, args, scratch=(), smem=0, flops=0, limit=16, held=0, **static):
+def call(kernel, outs, args, scratch=(), smem=0, flops=0, limit=16, held=0, stored=0, after=(), **static):
     moved = sum(math.prod(a.shape) * a.dtype.itemsize for a in (*args, *outs))
     specs = [pl.BlockSpec(memory_space=pltpu.SMEM)] * smem
     specs += [pl.BlockSpec(memory_space=pltpu.VMEM)] * (len(args) - smem - held)
-    specs += [pl.BlockSpec(memory_space=pl.ANY)] * held
+    specs += [pl.BlockSpec(memory_space=pltpu.HBM)] * held
+    specs += [pl.BlockSpec(memory_space=pl.ANY)] * len(after)
+    out_specs = [pl.BlockSpec(memory_space=pltpu.HBM)] * stored
+    shapes = [pltpu.HBM(a.shape, a.dtype) for a in outs[:stored]] + list(outs[stored:])
+    first_held = len(args) - held
+    args = [*args[:first_held], *(pltpu.with_memory_space_constraint(a, pltpu.HBM) for a in args[first_held:])]
+    out_specs += [pl.BlockSpec(memory_space=pltpu.VMEM)] * (len(outs) - stored)
+    count = len(args)
+
+    def run(*refs):
+        kernel(*refs[:count], *refs[count + len(after) :], **static)
+
     return pl.pallas_call(
-        functools.partial(kernel, **static) if static else kernel,
-        out_shape=tuple(outs),
+        run,
+        out_shape=tuple(shapes),
         in_specs=specs,
-        out_specs=tuple(pl.BlockSpec(memory_space=pltpu.VMEM) for _ in outs),
+        out_specs=tuple(out_specs),
         scratch_shapes=list(scratch),
         compiler_params=pltpu.CompilerParams(vmem_limit_bytes=limit * 1024 * 1024),
         cost_estimate=pl.CostEstimate(flops=int(flops), bytes_accessed=moved, transcendentals=0),
-    )(*args)
+    )(*args, *after)
 
 
 def shaped(*shape, dtype=bf16):
@@ -388,6 +489,51 @@
     count = lax.axis_size(axis)
     initial, last = (max(0, -steps), min(count, count - steps))
     return lax.ppermute(value, axis, [(source, source + steps) for source in range(initial, last)])
+
+
+def partner(value, axis, step):
+    return lax.ppermute(value, axis, [(at, at ^ step) for at in range(lax.axis_size(axis))])
+
+
+def bit_of(axis, step):
+    return lax.rem(lax.div(lax.axis_index(axis), step), 2).astype(jnp.int32).reshape(1)
+
+
+def steps_of(axis):
+    return [1 << at for at in range(int(math.log2(lax.axis_size(axis))))]
+
+
+def sum_over_mesh(keep, send):
+    width = keep.shape[1]
+    steps = steps_of("ty")
+    for step, later in zip(steps, steps[1:] + [0]):
+        came = partner(send, "ty", step)
+        rows = keep.shape[0]
+        if later:
+            half = shaped(rows // 2, width)
+            keep, send = call(
+                add_split_kernel,
+                [half, half],
+                [bit_of("ty", later), keep, came],
+                scratch=[pltpu.VMEM((rows, width), bf16)],
+                smem=1,
+                flops=1e6,
+            )
+        else:
+            (share,) = call(add_kernel, [shaped(rows, width)], [keep, came], flops=1e6)
+    for step in steps_of("tx"):
+        (share,) = call(
+            add_kernel, [shaped(*share.shape)], [share, partner(share, "tx", step)], flops=1e6
+        )
+    for step in steps[:0:-1]:
+        (share,) = call(
+            join_kernel,
+            [shaped(2 * share.shape[0], width)],
+            [bit_of("ty", step), share, partner(share, "ty", step)],
+            smem=1,
+            flops=1e6,
+        )
+    return share, partner(share, "ty", steps[0])
 
 
 def exchange(rows, tiles):
@@ -441,32 +587,40 @@
         shifted(sent[2 * border_rows : 3 * border_rows], "ty", -1),
         shifted(sent[3 * border_rows :], "ty", 1),
     ]
-    (packed_grad,) = call(
-        pack_kernel, [shaped(slots_count, width)], [slots, grad_out[0]], flops=4e9
-    )
-    came_grad = exchange(packed_grad, tiles)
-    (table,) = call(count_kernel, [shaped(ext, tile_rows)], [near_tile], flops=8e9)
-    average, pre_act, packed_lifted = call(
+    kept_table, table = call(
+        count_kernel,
+        [shaped(ext, tile_rows), shaped(ext, tile_rows)],
+        [near_tile],
+        scratch=[pltpu.SemaphoreType.DMA((ext // CHUNK,))],
+        flops=8e9,
+        stored=1,
+    )
+    average, pre_act, packed = call(
         lift_kernel,
         [
             shaped(width, tile_rows),
             shaped(tile_rows, width, dtype=f32),
-            shaped(slots_count, width),
-        ],
-        [slots, points_tile, *halos, table, w_near],
-        scratch=[pltpu.VMEM((tile_rows, width), bf16)],
+            shaped(slots_count, 2 * width),
+        ],
+        [slots, points_tile, grad_out[0], *halos, table, w_near],
+        scratch=[
+            pltpu.VMEM((width, tile_rows), bf16),
+            pltpu.VMEM((tile_rows, width), f32),
+            pltpu.VMEM((tile_rows, 2 * width), bf16),
+            pltpu.VMEM((slots_count, 2 * width), bf16),
+            pltpu.SemaphoreType.DMA((2,)),
+            pltpu.SemaphoreType.DMA((slots_count // WIDE,)),
+        ],
         flops=4e9,
+        stored=3,
         neighbours=neighbours,
     )
-    came_lifted = exchange(packed_lifted, tiles)
+    came = exchange(packed, tiles)
     patch_scratch = [
         pltpu.VMEM((PATCH + 2 * PAD, width), f32),
         pltpu.VMEM((PATCH, width), f32),
         pltpu.VMEM((PATCH + 2 * PAD, width), f32),
     ]
-    (serial_out_grad,) = call(
-        order_kernel, [shaped(slots_count, width)], [zorder, came_grad], flops=8e9
-    )
     serial, state, back_result = call(
         forward_kernel,
         [
@@ -474,17 +628,25 @@
             shaped(slots_count, width, dtype=f32),
             shaped(slots_count, width),
         ],
-        [zorder, came_lifted, conv_rows, gain_one_row, gain_two_row, w_up, w_down],
+        [zorder, conv_rows, gain_one_row, gain_two_row, w_up, w_down, came],
+        held=1,
         scratch=[
+            pltpu.VMEM((slots_count, width), bf16),
+            pltpu.VMEM((slots_count, width), bf16),
+            pltpu.VMEM((slots_count, width), f32),
             pltpu.VMEM((taps * width, width), bf16),
             pltpu.VMEM((PATCH, width), bf16),
             *patch_scratch,
             pltpu.VMEM((PATCH, width), bf16),
             pltpu.VMEM((PATCH, hidden), bf16),
             pltpu.VMEM((slots_count, width), bf16),
+            pltpu.VMEM((slots_count, width), bf16),
+            pltpu.SemaphoreType.DMA((3, slots_count // PATCH)),
+            pltpu.SemaphoreType.DMA((slots_count // WIDE,)),
         ],
         flops=10e9,
         limit=32,
+        stored=3,
         groups=groups,
         inner=inner,
     )
@@ -492,20 +654,33 @@
     lines = lax.axis_size("ty")
     sums_rows = 2 * hidden + taps * inner + 16
     sums_rows = -(-sums_rows // (16 * lines)) * (16 * lines)
-    serial_grad, sums = call(
+    serial_grad, keep, send = call(
         backward_kernel,
-        [shaped(slots_count, width), shaped(sums_rows, width)],
         [
-            serial,
-            serial_out_grad,
-            state,
+            shaped(slots_count, width),
+            shaped(sums_rows // 2, width),
+            shaped(sums_rows // 2, width),
+        ],
+        [
+            bit_of("ty", 1),
+            zorder,
             conv_rows,
             gain_one_row,
             gain_two_row,
             w_up,
             w_down,
-        ],
+            came,
+            serial,
+            state,
+        ],
+        held=3,
         scratch=[
+            pltpu.VMEM((slots_count, width), bf16),
+            pltpu.VMEM((slots_count, width), bf16),
+            pltpu.VMEM((slots_count, width), f32),
+            pltpu.VMEM((slots_count, width), bf16),
+            pltpu.VMEM((slots_count, width), bf16),
+            pltpu.VMEM((sums_rows, width), bf16),
             pltpu.VMEM((taps * width, width), bf16),
             pltpu.VMEM((slots_count, width), bf16),
             pltpu.VMEM((slots_count, hidden), bf16),
@@ -516,43 +691,56 @@
             pltpu.VMEM((PATCH, width), bf16),
             pltpu.VMEM((taps, width, width), f32),
             pltpu.VMEM((16, width), f32),
-        ],
+            pltpu.SemaphoreType.DMA((4, slots_count // PATCH)),
+        ],
+        stored=1,
+        smem=1,
         flops=40e9,
         limit=40,
         groups=groups,
         inner=inner,
     )
     (back_grad,) = call(
-        hold_kernel,
+        pack_rows,
         [shaped(slots_count, width)],
-        [zorder, serial_grad, came_result],
-        held=1,
+        [zorder, serial_grad],
+        after=[came_result],
+        scratch=[
+            pltpu.VMEM((slots_count, width), bf16),
+            pltpu.SemaphoreType.DMA((slots_count // WIDE,)),
+        ],
+        stored=1,
         flops=4e9,
     )
     came_back = exchange(back_grad, tiles)
-    share = lax.psum_scatter(sums, "ty", scatter_dimension=0, tiled=True)
-    totals = lax.all_gather(lax.psum(share, "tx"), "ty", axis=0, tiled=True)
+    totals = sum_over_mesh(keep, send)
     (out_rows,) = call(
         unpack_kernel, [shaped(tile_rows, width)], [slots, came_result], flops=4e9
     )
-    lifted_grad, act_grad, near_grad = call(
-        act_kernel,
-        [shaped(tile_rows, width), shaped(tile_rows, width), shaped(width, width)],
-        [slots, came_back, average, pre_act],
-        flops=3e9,
+    row_grad, near_grad, halo_grad = call(
+        tile_back_kernel,
+        [shaped(tile_rows, width, dtype=f32), shaped(width, width), shaped(edge, width)],
+        [slots, came_back, w_near, kept_table, average, pre_act],
+        after=[out_rows],
+        scratch=[
+            pltpu.VMEM((tile_rows, width), f32),
+            pltpu.VMEM((ext, tile_rows), bf16),
+            pltpu.VMEM((width, tile_rows), bf16),
+            pltpu.VMEM((tile_rows, width), f32),
+            pltpu.VMEM((tile_rows, width), bf16),
+            pltpu.VMEM((tile_rows, width), bf16),
+            pltpu.SemaphoreType.DMA((3 + tile_rows // WIDE,)),
+        ],
+        flops=6e9,
+        limit=24,
+        held=3,
+        stored=1,
+        neighbours=neighbours,
     )
     near_parts = exchange(near_grad, tiles).reshape(tiles, width // tiles, width)
     near_share = jnp.sum(near_parts.astype(f32), axis=0)
     near_all = jnp.broadcast_to(near_share.astype(bf16), (tiles, *near_share.shape))
     near_sum = exchange(near_all.reshape(width, width), tiles)
-    row_grad, halo_grad = call(
-        spread_rows_kernel,
-        [shaped(tile_rows, width, dtype=f32), shaped(edge, width)],
-        [lifted_grad, act_grad, table, w_near],
-        scratch=[pltpu.VMEM((tile_rows, width), bf16)],
-        flops=3e9,
-        neighbours=neighbours,
-    )
     returned = [
         shifted(halo_grad[0:border_rows], "tx", 1),
         shifted(halo_grad[border_rows : 2 * border_rows], "tx", -1),
@@ -572,7 +760,9 @@
             shaped(1, width, dtype=f32),
             shaped(1, width, dtype=f32),
         ],
-        [totals],
+        [bit_of("ty", 1), *totals],
+        scratch=[pltpu.VMEM((sums_rows, width), bf16)],
+        smem=1,
         flops=1e6,
         scale=scale,
     )

time: 248 us -> 223 us (0.90)
  local copies, waits for them, and re-layouts: 22 us -> 5.52 us
  between operations: 14.8 us -> 1.74 us
  blocking collectives: 0 us -> 12.7 us
  starting transfers between devices: 56.7 us -> 46.4 us
  Pallas kernels: 53.6 us -> 58.4 us
  waiting for transfers between devices: 98.8 us -> 95.8 us
    ppermute x0 -> x8, waiting for transfers between devices: none -> 41.9 us  [partner(): lax.ppermute(value, axis, [(at, at ^ step) for at in range(lax.axis_size(...]
    psum x1 -> x0, waiting for transfers between devices: 36.2 us -> none  [body(): totals = lax.all_gather(lax.psum(share, 'tx'), 'ty', axis=0, tiled=True)]
    reduce_scatter x1 -> x0, waiting for transfers between devices: 27.7 us -> none  [body(): share = lax.psum_scatter(sums, 'ty', scatter_dimension=0, tiled=True)]
    all_to_all x6 -> x4, waiting for transfers between devices: 31.8 us -> 53.9 us  [exchange(): lax.all_to_all(rows, ('tx', 'ty'), split_axis=0, concat_axis=0, tiled=True)]
    all_to_all x6 -> x4, starting transfers between devices: 38.1 us -> 20.2 us  [exchange(): lax.all_to_all(rows, ('tx', 'ty'), split_axis=0, concat_axis=0, tiled=True)]
    unnamed x58 -> x32, local copies, waits for them, and re-layouts: 20.6 us -> 4.07 us
    all_to_all x0 -> x1, blocking collectives: none -> 12.7 us  [exchange(): lax.all_to_all(rows, ('tx', 'ty'), split_axis=0, concat_axis=0, tiled=True)]
    ppermute x0 -> x8, starting transfers between devices: none -> 6.81 us  [partner(): lax.ppermute(value, axis, [(at, at ^ step) for at in range(lax.axis_size(...]
  transfers between devices with their start and end apart: 17 -> 20, of which waited for: 7 -> 8; matrix products, arithmetic and copies ran while one was open for 0% -> 0% of each run, Pallas kernels for 16% -> 19%
where the time goes in v2:
time: 223 us; the launch traced here: 221 us
  waiting for transfers between devices  95.8 us (43%)
  Pallas kernels  58.4 us (26%)
  starting transfers between devices  46.4 us (21%)
  blocking collectives  12.7 us (6%)
  local copies, waits for them, and re-layouts  5.52 us (2%)
    pallas_call x17, Pallas kernels, call(): pl.pallas_call(run, out_shape=tuple(shapes), in_specs=specs, out_specs=tu...  58.4 us
    all_to_all x4, waiting for transfers between devices, exchange(): lax.all_to_all(rows, ('tx', 'ty'), split_axis=0, concat_axis=0, tiled=True)  53.9 us
    ppermute x8, waiting for transfers between devices, partner(): lax.ppermute(value, axis, [(at, at ^ step) for at in range(lax.axis_size(...  41.9 us
    all_to_all x4, starting transfers between devices, exchange(): lax.all_to_all(rows, ('tx', 'ty'), split_axis=0, concat_axis=0, tiled=True)  20.2 us
    ppermute x8, starting transfers between devices, shifted(): lax.ppermute(value, axis, [(source, source + steps) for source in range(i...  19.4 us
    all_to_all x1, blocking collectives, exchange(): lax.all_to_all(rows, ('tx', 'ty'), split_axis=0, concat_axis=0, tiled=True)  12.7 us
    ppermute x8, starting transfers between devices, partner(): lax.ppermute(value, axis, [(at, at ^ step) for at in range(lax.axis_size(...  6.81 us
  transfers between devices with their start and end apart: 20, of which 8 were waited for; matrix products, arithmetic and copies ran while one was open for 0% of the time, Pallas kernels for 19%

profile of v2, /device:TPU:0, one launch (start us, length us, event | category | flops | bytes accessed | tf_op | source)
XLA Modules:
  0.0 221.4 jit_solution(13160494964124972026)
XLA Ops:
  4.3 2.4 %collective-permute-start.3 = (bf16[64,256]{1,0:T(8,128)(2,1)S(1)}, bf16[64,256]{1,0:T(8,128)(2,1)S(1)}, u32[]{:S(2)}, u32[]{:S(2)}) collective-permute-start(bf16[64,256]{1,0:T(8,128)(2,1)S(1)} %get-tuple-element.62), channel_id=1, source_target_pairs={{0,1},{1,2},{2,3},{3,4},{4,5},{5,6},{6,7},{8,9},{9,10},{10,11},{11... | collective-permute-start | bytes 98312 | tf_op jit(solution)/shard_map/ppermute | solution.py:491
  8.0 4.3 %collective-permute-start.1 = (bf16[64,256]{1,0:T(8,128)(2,1)S(1)}, bf16[64,256]{1,0:T(8,128)(2,1)S(1)}, u32[]{:S(2)}, u32[]{:S(2)}) collective-permute-start(bf16[64,256]{1,0:T(8,128)(2,1)S(1)} %get-tuple-element.64), channel_id=1, source_target_pairs={{0,8},{8,16},{16,24},{1,9},{9,17},{17,25},{2,10},{10,18},{18,26},{... | collective-permute-start | bytes 98312 | tf_op jit(solution)/shard_map/ppermute | solution.py:491
  13.6 5.8 %shard_map.189 = (bf16[1280,1024]{1,0:T(8,128)(2,1)}, bf16[1280,1024]{1,0:T(8,128)(2,1)S(1)}) custom-call(s32[16,1024]{1,0:T(8,128)S(1)} %bitcast.31), custom_call_target="tpu_custom_call" | custom-call | flops 8000000000 | bytes 5308416 | tf_op jit(solution)/shard_map/pallas_call | solution.py:473
  19.6 4.3 %shard_map.190 = (bf16[256,1024]{1,0:T(8,128)(2,1)}, f32[1024,256]{1,0:T(8,128)}, bf16[2048,512]{1,0:T(8,128)(2,1)}) custom-call(s32[1,1024]{1,0:T(1,128)S(1)} %get-tuple-element.33.refs_0_, bf16[1024,256]{1,0:T(8,128)(2,1)S(1)} %bitcast.27, bf16[1024,256]{1,0:T(8,128)(2,1)S(1)} %bitcast.28, bf16[64,256]{1,0:T(8,128)(2,1)S(1)} %collective-permute-done.refs_3_, ...), custom_call_target="tpu_custom_call" | custom-call | flops 4000000000 | bytes 7606272 | tf_op jit(solution)/shard_map/pallas_call | solution.py:473
  24.0 9.6 %all-to-all-start = ((bf16[32,64,512]{2,1,0:T(8,128)(2,1)}), bf16[32,64,512]{2,1,0:T(8,128)(2,1)}, u32[]{:S(2)}, u32[]{:S(2)}) async-start(bf16[32,64,512]{2,1,0:T(8,128)(2,1)} %bitcast.37), calls=%async_computation | async-start | bytes 4194304 | tf_op jit(solution)/shard_map/all_to_all | solution.py:540
  33.6 48.9 %all-to-all-done = bf16[32,64,512]{2,1,0:T(8,128)(2,1)} async-done(((bf16[32,64,512]{2,1,0:T(8,128)(2,1)}), bf16[32,64,512]{2,1,0:T(8,128)(2,1)}, u32[]{:S(2)}, u32[]{:S(2)}) %all-to-all-start) | async-done | bytes 2097184 | tf_op jit(solution)/shard_map/all_to_all | solution.py:540
  82.5 12.3 %shard_map.191 = (bf16[2048,256]{1,0:T(8,128)(2,1)}, f32[2048,256]{1,0:T(8,128)}, bf16[2048,256]{1,0:T(8,128)(2,1)}) custom-call(s32[1,2048]{1,0:T(1,128)S(1)} %copy-done.9, bf16[768,32]{1,0:T(8,128)(2,1)S(1)} %bitcast.29, f32[1,256]{1,0:T(1,128)S(1)} %bitcast.32, f32[1,256]{1,0:T(1,128)S(1)} %bitcast.34, bf16[256,1024]{1,0:T(8,128)(2,1)S(1)} %copy-done.3, ...), custom_call_target="tpu_custom_call" | custom-call | flops 10000000000 | bytes 7399424 | tf_op jit(solution)/shard_map/pallas_call | solution.py:473
  94.7 4.2 %all-to-all-start.1 = ((bf16[32,64,256]{2,1,0:T(8,128)(2,1)}), bf16[32,64,256]{2,1,0:T(8,128)(2,1)S(1)}, u32[]{:S(2)}, u32[]{:S(2)}) async-start(bf16[32,64,256]{2,1,0:T(8,128)(2,1)} %bitcast.39), calls=%async_computation.1 | async-start | bytes 2097152 | tf_op jit(solution)/shard_map/all_to_all | solution.py:540
  98.9 20.9 %shard_map.193 = (bf16[2048,256]{1,0:T(8,128)(2,1)}, bf16[1088,256]{1,0:T(8,128)(2,1)S(1)}, bf16[1088,256]{1,0:T(8,128)(2,1)}) custom-call(s32[1]{0:T(128)} %bitcast.11.refs_0_, s32[1,2048]{1,0:T(1,128)S(1)} %copy-done.9, bf16[768,32]{1,0:T(8,128)(2,1)S(1)} %bitcast.30, f32[1,256]{1,0:T(1,128)S(1)} %bitcast.33, f32[1,256]{1,0:T(1,128)S(1)} %bitcast.35, ...), custom_call_target="tpu_custom_call" | custom-call | flops 40000000000 | bytes 8513540 | tf_op jit(solution)/shard_map/pallas_call | solution.py:473
  120.0 5.0 %all-to-all-done.1 = bf16[32,64,256]{2,1,0:T(8,128)(2,1)S(1)} async-done(((bf16[32,64,256]{2,1,0:T(8,128)(2,1)}), bf16[32,64,256]{2,1,0:T(8,128)(2,1)S(1)}, u32[]{:S(2)}, u32[]{:S(2)}) %all-to-all-start.1) | async-done | bytes 1048608 | tf_op jit(solution)/shard_map/all_to_all | solution.py:540
  126.2 3.2 %shard_map.194 = bf16[2048,256]{1,0:T(8,128)(2,1)} custom-call(s32[1,2048]{1,0:T(1,128)S(1)} %copy-done.9, bf16[2048,256]{1,0:T(8,128)(2,1)S(1)} %copy-done.15, bf16[2048,256]{1,0:T(8,128)(2,1)S(1)} %bitcast.22), custom_call_target="tpu_custom_call" | custom-call | flops 4000000000 | bytes 2105344 | tf_op jit(solution)/shard_map/pallas_call | solution.py:473
  129.4 3.8 %all-to-all-start.2 = ((bf16[32,64,256]{2,1,0:T(8,128)(2,1)}), bf16[32,64,256]{2,1,0:T(8,128)(2,1)S(1)}, u32[]{:S(2)}, u32[]{:S(2)}) async-start(bf16[32,64,256]{2,1,0:T(8,128)(2,1)} %bitcast.38), calls=%async_computation.2 | async-start | bytes 2097152 | tf_op jit(solution)/shard_map/all_to_all | solution.py:540
  135.9 15.8 %collective-permute-done.9.refs_2_ = bf16[544,256]{1,0:T(8,128)(2,1)S(1)} collective-permute-done((bf16[544,256]{1,0:T(8,128)(2,1)}, bf16[544,256]{1,0:T(8,128)(2,1)S(1)}, u32[]{:S(2)}, u32[]{:S(2)}) %collective-permute-start.9) | collective-permute-done | bytes 278560 | tf_op jit(solution)/shard_map/ppermute | solution.py:495
  153.0 5.7 %collective-permute-done.10.refs_1_ = bf16[272,256]{1,0:T(8,128)(2,1)S(1)} collective-permute-done((bf16[272,256]{1,0:T(8,128)(2,1)S(1)}, bf16[272,256]{1,0:T(8,128)(2,1)S(1)}, u32[]{:S(2)}, u32[]{:S(2)}) %collective-permute-start.10) | collective-permute-done | bytes 139296 | tf_op jit(solution)/shard_map/ppermute | solution.py:495
  158.8 5.0 %collective-permute-done.11.refs_1_ = bf16[272,256]{1,0:T(8,128)(2,1)S(1)} collective-permute-done((bf16[272,256]{1,0:T(8,128)(2,1)S(1)}, bf16[272,256]{1,0:T(8,128)(2,1)S(1)}, u32[]{:S(2)}, u32[]{:S(2)}) %collective-permute-start.11) | collective-permute-done | bytes 139296 | tf_op jit(solution)/shard_map/ppermute | solution.py:495
  165.4 5.9 %collective-permute-done.12.refs_1_ = bf16[272,256]{1,0:T(8,128)(2,1)S(1)} collective-permute-done((bf16[272,256]{1,0:T(8,128)(2,1)S(1)}, bf16[272,256]{1,0:T(8,128)(2,1)S(1)}, u32[]{:S(2)}, u32[]{:S(2)}) %collective-permute-start.12) | collective-permute-done | bytes 139296 | tf_op jit(solution)/shard_map/ppermute | solution.py:495
  172.7 3.8 %collective-permute-done.13.refs_2_ = bf16[272,256]{1,0:T(8,128)(2,1)S(1)} collective-permute-done((bf16[272,256]{1,0:T(8,128)(2,1)S(1)}, bf16[272,256]{1,0:T(8,128)(2,1)S(1)}, u32[]{:S(2)}, u32[]{:S(2)}) %collective-permute-start.13) | collective-permute-done | bytes 139296 | tf_op jit(solution)/shard_map/ppermute | solution.py:495
  177.5 5.6 %collective-permute-done.14.refs_2_ = bf16[544,256]{1,0:T(8,128)(2,1)S(1)} collective-permute-done((bf16[544,256]{1,0:T(8,128)(2,1)S(1)}, bf16[544,256]{1,0:T(8,128)(2,1)S(1)}, u32[]{:S(2)}, u32[]{:S(2)}) %collective-permute-start.14) | collective-permute-done | bytes 278560 | tf_op jit(solution)/shard_map/ppermute | solution.py:495
  183.2 2.1 shard_map.192.refs_6_
  186.4 5.1 %shard_map.195 = (f32[1024,256]{1,0:T(8,128)}, bf16[256,256]{1,0:T(8,128)(2,1)S(1)}, bf16[256,256]{1,0:T(8,128)(2,1)S(1)}) custom-call(s32[1,1024]{1,0:T(1,128)S(1)} %get-tuple-element.33.refs_0_, bf16[2048,256]{1,0:T(8,128)(2,1)S(1)} %bitcast.24, bf16[256,256]{1,0:T(8,128)(2,1)S(1)} %copy-done.7, bf16[1280,1024]{1,0:T(8,128)(2,1)} %get-tuple-element.41.refs_3_, ...), custom_call_target="tpu_custom_call" | custom-call | flops 6000000000 | bytes 6688768 | tf_op jit(solution)/shard_map/pallas_call | solution.py:473
  191.5 12.7 %all_to_all.48 = bf16[32,8,256]{2,1,0:T(8,128)(2,1)S(1)} all-to-all(bf16[32,8,256]{2,1,0:T(8,128)(2,1)S(1)} %bitcast.25), channel_id=1, replica_groups=mesh['tx'=4,'ty'=8] {'tx','ty'}, dimensions={0} | all-to-all | bytes 262144 | tf_op jit(solution)/shard_map/all_to_all | solution.py:540
  204.9 2.6 %all-to-all-start.4 = ((bf16[32,8,256]{2,1,0:T(8,128)(2,1)}), bf16[32,8,256]{2,1,0:T(8,128)(2,1)S(1)}, u32[]{:S(2)}, u32[]{:S(2)}) async-start(bf16[32,8,256]{2,1,0:T(8,128)(2,1)} %broadcast_in_dim.11), calls=%async_computation.4 | async-start | bytes 262144 | tf_op jit(solution)/shard_map/all_to_all | solution.py:540
  208.8 3.0 %collective-permute-start.6 = (bf16[64,256]{1,0:T(8,128)(2,1)S(1)}, bf16[64,256]{1,0:T(8,128)(2,1)S(1)}, u32[]{:S(2)}, u32[]{:S(2)}) collective-permute-start(bf16[64,256]{1,0:T(8,128)(2,1)S(1)} %get-tuple-element.59), channel_id=1, source_target_pairs={{0,1},{1,2},{2,3},{3,4},{4,5},{5,6},{6,7},{8,9},{9,10},{10,11},{11... | collective-permute-start | bytes 98312 | tf_op jit(solution)/shard_map/ppermute | solution.py:491
  213.2 4.5 %collective-permute-start.4 = (bf16[64,256]{1,0:T(8,128)(2,1)S(1)}, bf16[64,256]{1,0:T(8,128)(2,1)S(1)}, u32[]{:S(2)}, u32[]{:S(2)}) collective-permute-start(bf16[64,256]{1,0:T(8,128)(2,1)S(1)} %get-tuple-element.61), channel_id=1, source_target_pairs={{0,8},{8,16},{16,24},{1,9},{9,17},{17,25},{2,10},{10,18},{18,26},{... | collective-permute-start | bytes 98312 | tf_op jit(solution)/shard_map/ppermute | solution.py:491
  (72 shorter events, 23.0 us)
Async XLA Ops:
  4.3 15.2 %collective-permute-start.3 = (bf16[64,256]{1,0:T(8,128)(2,1)S(1)}, bf16[64,256]{1,0:T(8,128)(2,1)S(1)}, u32[]{:S(2)}, u32[]{:S(2)}) collective-permute-start(bf16[64,256]{1,0:T(8,128)(2,1)S(1)} %get-tuple-element.62), channel_id=1, source_target_pairs={{0,1},{1,2},{2,3},{3,4},{4,5},{5,6},{6,7},{8,9},{9,10},{10,11},{11... | collective-permute-start | bytes 98312 | tf_op jit(solution)/shard_map/ppermute | solution.py:491
  6.7 12.8 %collective-permute-start.2 = (bf16[64,256]{1,0:T(8,128)(2,1)S(1)}, bf16[64,256]{1,0:T(8,128)(2,1)S(1)}, u32[]{:S(2)}, u32[]{:S(2)}) collective-permute-start(bf16[64,256]{1,0:T(8,128)(2,1)S(1)} %get-tuple-element.63), channel_id=1, source_target_pairs={{1,0},{2,1},{3,2},{4,3},{5,4},{6,5},{7,6},{9,8},{10,9},{11,10},{12... | collective-permute-start | bytes 98312 | tf_op jit(solution)/shard_map/ppermute | solution.py:491
  8.0 11.5 %collective-permute-start.1 = (bf16[64,256]{1,0:T(8,128)(2,1)S(1)}, bf16[64,256]{1,0:T(8,128)(2,1)S(1)}, u32[]{:S(2)}, u32[]{:S(2)}) collective-permute-start(bf16[64,256]{1,0:T(8,128)(2,1)S(1)} %get-tuple-element.64), channel_id=1, source_target_pairs={{0,8},{8,16},{16,24},{1,9},{9,17},{17,25},{2,10},{10,18},{18,26},{... | collective-permute-start | bytes 98312 | tf_op jit(solution)/shard_map/ppermute | solution.py:491
  12.3 7.2 %collective-permute-start = (bf16[64,256]{1,0:T(8,128)(2,1)S(1)}, bf16[64,256]{1,0:T(8,128)(2,1)S(1)}, u32[]{:S(2)}, u32[]{:S(2)}) collective-permute-start(bf16[64,256]{1,0:T(8,128)(2,1)S(1)} %get-tuple-element.65), channel_id=1, source_target_pairs={{8,0},{16,8},{24,16},{9,1},{17,9},{25,17},{10,2},{18,10},{26,18},{... | collective-permute-start | bytes 98312 | tf_op jit(solution)/shard_map/ppermute | solution.py:491
  23.9 58.5 %copy-start.3 = (bf16[256,1024]{1,0:T(8,128)(2,1)S(1)}, bf16[256,1024]{1,0:T(8,128)(2,1)}, u32[]{:S(2)}) copy-start(bf16[256,1024]{1,0:T(8,128)(2,1)} %refs_5_.3) | copy-start | bytes 1572868
  23.9 58.5 %copy-start.4 = (bf16[1024,256]{1,0:T(8,128)(2,1)S(1)}, bf16[1024,256]{1,0:T(8,128)(2,1)}, u32[]{:S(2)}) copy-start(bf16[1024,256]{1,0:T(8,128)(2,1)} %refs_6_.1) | copy-start | bytes 1572868
  23.9 58.5 %copy-start.5 = (bf16[3,8,32,32]{3,2,1,0:T(8,128)(2,1)S(1)}, bf16[3,8,32,32]{3,2,1,0:T(8,128)(2,1)}, u32[]{:S(2)}) copy-start(bf16[3,8,32,32]{3,2,1,0:T(8,128)(2,1)} %param.21) | copy-start | bytes 147460
  23.9 58.5 %copy-start.9 = (s32[1,2048]{1,0:T(1,128)S(1)}, s32[1,2048]{1,0:T(1,128)}, u32[]{:S(2)}) copy-start(s32[1,2048]{1,0:T(1,128)} %refs_0_.4) | copy-start | bytes 24580
  24.0 58.5 %all-to-all-start = ((bf16[32,64,512]{2,1,0:T(8,128)(2,1)}), bf16[32,64,512]{2,1,0:T(8,128)(2,1)}, u32[]{:S(2)}, u32[]{:S(2)}) async-start(bf16[32,64,512]{2,1,0:T(8,128)(2,1)} %bitcast.37), calls=%async_computation | async-start | bytes 4194304 | tf_op jit(solution)/shard_map/all_to_all | solution.py:540
  94.7 30.3 %all-to-all-start.1 = ((bf16[32,64,256]{2,1,0:T(8,128)(2,1)}), bf16[32,64,256]{2,1,0:T(8,128)(2,1)S(1)}, u32[]{:S(2)}, u32[]{:S(2)}) async-start(bf16[32,64,256]{2,1,0:T(8,128)(2,1)} %bitcast.39), calls=%async_computation.1 | async-start | bytes 2097152 | tf_op jit(solution)/shard_map/all_to_all | solution.py:540
  119.9 13.4 %collective-permute-start.8 = (bf16[1088,256]{1,0:T(8,128)(2,1)}, bf16[1088,256]{1,0:T(8,128)(2,1)S(1)}, u32[]{:S(2)}, u32[]{:S(2)}) collective-permute-start(bf16[1088,256]{1,0:T(8,128)(2,1)} %get-tuple-element.48), channel_id=1, source_target_pairs={{0,1},{1,0},{2,3},{3,2},{4,5},{5,4},{6,7},{7,6},{8,9},{9,8},{10,11... | collective-permute-start | bytes 1671176 | tf_op jit(solution)/shard_map/ppermute | solution.py:495
  129.4 55.9 %all-to-all-start.2 = ((bf16[32,64,256]{2,1,0:T(8,128)(2,1)}), bf16[32,64,256]{2,1,0:T(8,128)(2,1)S(1)}, u32[]{:S(2)}, u32[]{:S(2)}) async-start(bf16[32,64,256]{2,1,0:T(8,128)(2,1)} %bitcast.38), calls=%async_computation.2 | async-start | bytes 2097152 | tf_op jit(solution)/shard_map/all_to_all | solution.py:540
  134.3 17.4 %collective-permute-start.9 = (bf16[544,256]{1,0:T(8,128)(2,1)}, bf16[544,256]{1,0:T(8,128)(2,1)S(1)}, u32[]{:S(2)}, u32[]{:S(2)}) collective-permute-start(bf16[544,256]{1,0:T(8,128)(2,1)} %get-tuple-element.50), channel_id=1, source_target_pairs={{0,2},{1,3},{2,0},{3,1},{4,6},{5,7},{6,4},{7,5},{8,10},{9,11},{10,... | collective-permute-start | bytes 835592 | tf_op jit(solution)/shard_map/ppermute | solution.py:495
  151.9 6.8 %collective-permute-start.10 = (bf16[272,256]{1,0:T(8,128)(2,1)S(1)}, bf16[272,256]{1,0:T(8,128)(2,1)S(1)}, u32[]{:S(2)}, u32[]{:S(2)}) collective-permute-start(bf16[272,256]{1,0:T(8,128)(2,1)S(1)} %get-tuple-element.52), channel_id=1, source_target_pairs={{0,4},{1,5},{2,6},{3,7},{4,0},{5,1},{6,2},{7,3},{8,12},{9,13},{10,... | collective-permute-start | bytes 417800 | tf_op jit(solution)/shard_map/ppermute | solution.py:495
  158.7 5.1 %collective-permute-start.11 = (bf16[272,256]{1,0:T(8,128)(2,1)S(1)}, bf16[272,256]{1,0:T(8,128)(2,1)S(1)}, u32[]{:S(2)}, u32[]{:S(2)}) collective-permute-start(bf16[272,256]{1,0:T(8,128)(2,1)S(1)} %shard_map.199.refs_0_), channel_id=1, source_target_pairs={{0,8},{8,0},{16,24},{24,16},{1,9},{9,1},{17,25},{25,17},{2,10},{10... | collective-permute-start | bytes 417800 | tf_op jit(solution)/shard_map/ppermute | solution.py:495
  163.9 7.4 %collective-permute-start.12 = (bf16[272,256]{1,0:T(8,128)(2,1)S(1)}, bf16[272,256]{1,0:T(8,128)(2,1)S(1)}, u32[]{:S(2)}, u32[]{:S(2)}) collective-permute-start(bf16[272,256]{1,0:T(8,128)(2,1)S(1)} %shard_map.200.refs_0_), channel_id=1, source_target_pairs={{0,16},{8,24},{16,0},{24,8},{1,17},{9,25},{17,1},{25,9},{2,18},{10... | collective-permute-start | bytes 417800 | tf_op jit(solution)/shard_map/ppermute | solution.py:495
  171.3 5.1 %collective-permute-start.13 = (bf16[272,256]{1,0:T(8,128)(2,1)S(1)}, bf16[272,256]{1,0:T(8,128)(2,1)S(1)}, u32[]{:S(2)}, u32[]{:S(2)}) collective-permute-start(bf16[272,256]{1,0:T(8,128)(2,1)S(1)} %shard_map.201.refs_1_), channel_id=1, source_target_pairs={{0,4},{1,5},{2,6},{3,7},{4,0},{5,1},{6,2},{7,3},{8,12},{9,13},{10,... | collective-permute-start | bytes 417800 | tf_op jit(solution)/shard_map/ppermute | solution.py:495
  176.5 6.6 %collective-permute-start.14 = (bf16[544,256]{1,0:T(8,128)(2,1)S(1)}, bf16[544,256]{1,0:T(8,128)(2,1)S(1)}, u32[]{:S(2)}, u32[]{:S(2)}) collective-permute-start(bf16[544,256]{1,0:T(8,128)(2,1)S(1)} %shard_map.202.refs_1_), channel_id=1, source_target_pairs={{0,2},{1,3},{2,0},{3,1},{4,6},{5,7},{6,4},{7,5},{8,10},{9,11},{10,... | collective-permute-start | bytes 835592 | tf_op jit(solution)/shard_map/ppermute | solution.py:495
  183.2 34.6 %collective-permute-start.15 = (bf16[1088,256]{1,0:T(8,128)(2,1)S(1)}, bf16[1088,256]{1,0:T(8,128)(2,1)S(1)}, u32[]{:S(2)}, u32[]{:S(2)}) collective-permute-start(bf16[1088,256]{1,0:T(8,128)(2,1)S(1)} %shard_map.203.refs_1_), channel_id=1, source_target_pairs={{0,1},{1,0},{2,3},{3,2},{4,5},{5,4},{6,7},{7,6},{8,9},{9,8},{10,11... | collective-permute-start | bytes 1671176 | tf_op jit(solution)/shard_map/ppermute | solution.py:495
  204.9 15.7 %all-to-all-start.4 = ((bf16[32,8,256]{2,1,0:T(8,128)(2,1)}), bf16[32,8,256]{2,1,0:T(8,128)(2,1)S(1)}, u32[]{:S(2)}, u32[]{:S(2)}) async-start(bf16[32,8,256]{2,1,0:T(8,128)(2,1)} %broadcast_in_dim.11), calls=%async_computation.4 | async-start | bytes 262144 | tf_op jit(solution)/shard_map/all_to_all | solution.py:540
  207.5 12.0 %collective-permute-start.7 = (bf16[64,256]{1,0:T(8,128)(2,1)S(1)}, bf16[64,256]{1,0:T(8,128)(2,1)S(1)}, u32[]{:S(2)}, u32[]{:S(2)}) collective-permute-start(bf16[64,256]{1,0:T(8,128)(2,1)S(1)} %get-tuple-element.58), channel_id=1, source_target_pairs={{1,0},{2,1},{3,2},{4,3},{5,4},{6,5},{7,6},{9,8},{10,9},{11,10},{12... | collective-permute-start | bytes 98312 | tf_op jit(solution)/shard_map/ppermute | solution.py:491
  208.8 10.7 %collective-permute-start.6 = (bf16[64,256]{1,0:T(8,128)(2,1)S(1)}, bf16[64,256]{1,0:T(8,128)(2,1)S(1)}, u32[]{:S(2)}, u32[]{:S(2)}) collective-permute-start(bf16[64,256]{1,0:T(8,128)(2,1)S(1)} %get-tuple-element.59), channel_id=1, source_target_pairs={{0,1},{1,2},{2,3},{3,4},{4,5},{5,6},{6,7},{8,9},{9,10},{10,11},{11... | collective-permute-start | bytes 98312 | tf_op jit(solution)/shard_map/ppermute | solution.py:491
  211.9 7.7 %collective-permute-start.5 = (bf16[64,256]{1,0:T(8,128)(2,1)S(1)}, bf16[64,256]{1,0:T(8,128)(2,1)S(1)}, u32[]{:S(2)}, u32[]{:S(2)}) collective-permute-start(bf16[64,256]{1,0:T(8,128)(2,1)S(1)} %get-tuple-element.60), channel_id=1, source_target_pairs={{8,0},{16,8},{24,16},{9,1},{17,9},{25,17},{10,2},{18,10},{26,18},{... | collective-permute-start | bytes 98312 | tf_op jit(solution)/shard_map/ppermute | solution.py:491
  213.2 6.4 %collective-permute-start.4 = (bf16[64,256]{1,0:T(8,128)(2,1)S(1)}, bf16[64,256]{1,0:T(8,128)(2,1)S(1)}, u32[]{:S(2)}, u32[]{:S(2)}) collective-permute-start(bf16[64,256]{1,0:T(8,128)(2,1)S(1)} %get-tuple-element.61), channel_id=1, source_target_pairs={{0,8},{8,16},{16,24},{1,9},{9,17},{17,25},{2,10},{10,18},{18,26},{... | collective-permute-start | bytes 98312 | tf_op jit(solution)/shard_map/ppermute | solution.py:491
  (12 other events, 178.9 us)

commit v3 on v2

--- a/solution.py
+++ b/solution.py
@@ -306,28 +306,25 @@
 
 def backward_kernel(
     bit_ref, zorder_ref, conv_ref, gain_one_ref, gain_two_ref, up_ref, down_ref, came_in, serial_in, state_in,
-    serial_grad_out, keep_ref, send_ref,
-    grad_ref, serial_ref, state_ref, out_grad_ref, serial_grad_ref, weights_ref, taps_ref, second_ref, hidden_ref, pre_grad_ref, state_grad_ref, mixed_ref, before_ref, here_ref,
-    after_ref, normed_ref, conv_sum_ref, gains_ref, sems, *, groups, inner
+    back_out, keep_out, send_out,
+    grad_ref, serial_ref, state_ref, out_grad_ref, serial_grad_ref, stage_ref, weights_ref, taps_ref,
+    second_ref, hidden_ref, pre_grad_ref, state_grad_ref, mixed_ref, mixed_half_ref, before_ref, here_ref,
+    after_ref, normed_ref, conv_sum_ref, gains_ref, sems, pack_sems, *, groups, inner
 ):
     slots, width = serial_ref.shape
-    fetch_grad = pltpu.make_async_copy(came_in.at[:, pl.ds(width, width)], grad_ref, sems.at[1, 0])
-    fetch_state = pltpu.make_async_copy(state_in, state_ref, sems.at[2, 0])
-    fetch_serial = pltpu.make_async_copy(serial_in, serial_ref, sems.at[3, 0])
+    hidden_width = up_ref.shape[1]
+    fetch_grad = pltpu.make_async_copy(came_in.at[:, pl.ds(width, width)], grad_ref, sems.at[0])
+    fetch_state = pltpu.make_async_copy(state_in, state_ref, sems.at[1])
+    fetch_serial = pltpu.make_async_copy(serial_in, serial_ref, sems.at[2])
     fetch_grad.start()
     fetch_state.start()
     fetch_serial.start()
-    hidden_width = up_ref.shape[1]
     taps_ref[...] = full_taps(conv_ref, groups, inner)
     padded_zeros(before_ref)
     padded_zeros(after_ref)
     padded_zeros(mixed_ref)
     conv_sum_ref[...] = jnp.zeros_like(conv_sum_ref)
     gains_ref[...] = jnp.zeros_like(gains_ref)
-
-    def keep_grad(at):
-        place = pl.ds(pl.multiple_of(at * PATCH, PATCH), PATCH)
-        return pltpu.make_async_copy(serial_grad_ref.at[place], serial_grad_out.at[place], sems.at[0, at])
 
     def patch(at, _):
         origin = pl.multiple_of(at * PATCH, PATCH)
@@ -338,48 +335,60 @@
             ).astype(bf16)
         for start in range(0, PATCH, CHUNK):
             place = pl.ds(origin + start, CHUNK)
-            state = state_ref[place, :]
-            scale_two = inverse_rms(state)
-            unit_two = state * scale_two
-            second = (unit_two * gain_two_ref[...]).astype(bf16)
-            second_ref[place, :] = second
-            value = dot(second, up_ref[...])
-            square, tangent = gelu_parts(value)
-            half = 0.5 * value
-            hidden_ref[place, :] = (half + half * tangent).astype(bf16)
-            out_grad = out_grad_ref[place, :]
-            hidden_grad = dot(out_grad, down_ref[...], NT).astype(bf16).astype(f32)
-            pre_grad = (hidden_grad * slope_of(value, square, tangent)).astype(bf16)
-            pre_grad_ref[place, :] = pre_grad
-            second_grad = dot(pre_grad, up_ref[...], NT).astype(bf16).astype(f32)
-            weighted = second_grad * gain_two_ref[...]
-            gains_ref[1:2, :] += jnp.sum(second_grad * unit_two, axis=0, keepdims=True)
-            middle = jnp.mean(weighted * unit_two, axis=-1, keepdims=True)
-            state_grad = out_grad.astype(f32) + scale_two * (weighted - unit_two * middle)
-            state_grad_ref[pl.ds(start, CHUNK), :] = state_grad
-            mixed_grad = state_grad.astype(bf16)
-            mixed_ref[pl.ds(PAD + start, CHUNK), :] = mixed_grad.astype(f32)
-            before_ref[pl.ds(PAD + start, CHUNK), :] = dot(mixed_grad, taps_ref[0:width, :], NT)
-            here_ref[pl.ds(start, CHUNK), :] = dot(mixed_grad, taps_ref[width : 2 * width, :], NT)
-            after_ref[pl.ds(PAD + start, CHUNK), :] = dot(mixed_grad, taps_ref[2 * width :, :], NT)
-        for start in range(0, PATCH, CHUNK):
-            place = pl.ds(origin + start, CHUNK)
+            for row in range(start, start + CHUNK, BLOCK):
+                state = state_ref[pl.ds(origin + row, BLOCK), :]
+                second = state * inverse_rms(state) * gain_two_ref[...]
+                second_ref[pl.ds(origin + row, BLOCK), :] = second.astype(bf16)
+            value_all = dot(second_ref[place, :], up_ref[...])
+            hidden_grad_all = dot(out_grad_ref[place, :], down_ref[...], NT)
+            for row in range(0, CHUNK, 16):
+                for col in range(0, hidden_width, 2 * LANES):
+                    value = value_all[row : row + 16, col : col + 2 * LANES]
+                    hidden_grad = hidden_grad_all[row : row + 16, col : col + 2 * LANES]
+                    square, tangent = gelu_parts(value)
+                    half = 0.5 * value
+                    piece = pl.ds(origin + start + row, 16), pl.ds(col, 2 * LANES)
+                    hidden_ref[piece] = (half + half * tangent).astype(bf16)
+                    pre_grad_ref[piece] = (
+                        hidden_grad.astype(bf16).astype(f32) * slope_of(value, square, tangent)
+                    ).astype(bf16)
+            second_grad_all = dot(pre_grad_ref[place, :], up_ref[...], NT)
+            for row in range(0, CHUNK, BLOCK):
+                here = pl.ds(origin + start + row, BLOCK)
+                state = state_ref[here, :]
+                scale_two = inverse_rms(state)
+                unit_two = state * scale_two
+                second_grad = second_grad_all[row : row + BLOCK].astype(bf16).astype(f32)
+                weighted = second_grad * gain_two_ref[...]
+                product = second_grad * unit_two
+                gains_ref[1:2, :] += jnp.sum(product, axis=0, keepdims=True)
+                middle = jnp.mean(product * gain_two_ref[...], axis=-1, keepdims=True)
+                state_grad = out_grad_ref[here, :].astype(f32) + scale_two * (weighted - unit_two * middle)
+                state_grad_ref[pl.ds(start + row, BLOCK), :] = state_grad
+                mixed_grad = state_grad.astype(bf16)
+                mixed_half_ref[pl.ds(start + row, BLOCK), :] = mixed_grad
+                mixed_ref[pl.ds(PAD + start + row, BLOCK), :] = mixed_grad.astype(f32)
+        before_ref[pl.ds(PAD, PATCH), :] = dot(mixed_half_ref[...], taps_ref[0:width, :], NT)
+        here_ref[...] = dot(mixed_half_ref[...], taps_ref[width : 2 * width, :], NT)
+        after_ref[pl.ds(PAD, PATCH), :] = dot(mixed_half_ref[...], taps_ref[2 * width :, :], NT)
+        for row in range(0, PATCH, BLOCK):
+            place = pl.ds(origin + row, BLOCK)
             serial = serial_ref[place, :].astype(f32)
             scale_one = inverse_rms(serial)
             unit_one = serial * scale_one
-            normed_ref[pl.ds(start, CHUNK), :] = (unit_one * gain_one_ref[...]).astype(bf16)
+            normed_ref[pl.ds(row, BLOCK), :] = (unit_one * gain_one_ref[...]).astype(bf16)
             normed_grad = (
-                before_ref[pl.ds(PAD + start + 1, CHUNK), :]
-                + here_ref[pl.ds(start, CHUNK), :]
-                + after_ref[pl.ds(PAD + start - 1, CHUNK), :]
+                before_ref[pl.ds(PAD + row + 1, BLOCK), :]
+                + here_ref[pl.ds(row, BLOCK), :]
+                + after_ref[pl.ds(PAD + row - 1, BLOCK), :]
             ).astype(bf16).astype(f32)
-            gains_ref[0:1, :] += jnp.sum(normed_grad * unit_one, axis=0, keepdims=True)
+            product = normed_grad * unit_one
+            gains_ref[0:1, :] += jnp.sum(product, axis=0, keepdims=True)
+            middle = jnp.mean(product * gain_one_ref[...], axis=-1, keepdims=True)
             weighted = normed_grad * gain_one_ref[...]
-            middle = jnp.mean(weighted * unit_one, axis=-1, keepdims=True)
             serial_grad_ref[place, :] = (
-                state_grad_ref[pl.ds(start, CHUNK), :] + scale_one * (weighted - unit_one * middle)
+                state_grad_ref[pl.ds(row, BLOCK), :] + scale_one * (weighted - unit_one * middle)
             ).astype(bf16)
-        keep_grad(at).start()
         for tap in range(3):
             moved = mixed_ref[pl.ds(PAD + 1 - tap, PATCH), :].astype(bf16)
             conv_sum_ref[tap] += dot(normed_ref[...], moved, TN)
@@ -390,24 +399,39 @@
     fetch_serial.wait()
     lax.fori_loop(0, slots // PATCH, patch, 0)
     for start in range(0, hidden_width, width):
-        weights_ref[start : start + width, :] = dot(
-            hidden_ref[:, start : start + width], out_grad_ref[...], TN
-        ).astype(weights_ref.dtype)
+        block = slice(start, start + width)
+        weights_ref[start : start + width, :] = jnp.transpose(
+            dot(out_grad_ref[...], hidden_ref[:, block], TN)
+        ).astype(bf16)
         weights_ref[hidden_width + start : hidden_width + start + width, :] = dot(
-            second_ref[...], pre_grad_ref[:, start : start + width], TN
-        ).astype(weights_ref.dtype)
+            second_ref[...], pre_grad_ref[:, block], TN
+        ).astype(bf16)
     same = lax.div(iota((width, width), 0), inner) == lax.div(iota((width, width), 1), inner)
     for tap in range(3):
         kept = jnp.where(same, conv_sum_ref[tap], 0.0).reshape(groups, inner, width)
         at = 2 * hidden_width + tap * inner
-        weights_ref[at : at + inner, :] = jnp.sum(kept, axis=0).astype(weights_ref.dtype)
+        weights_ref[at : at + inner, :] = jnp.sum(kept, axis=0).astype(bf16)
     at = 2 * hidden_width + 3 * inner
-    weights_ref[at : at + 16, :] = gains_ref[...].astype(weights_ref.dtype)
+    weights_ref[at : at + 16, :] = gains_ref[...].astype(bf16)
     at = at + 16
-    weights_ref[at:, :] = jnp.zeros((weights_ref.shape[0] - at, width), weights_ref.dtype)
-    split_rows(bit_ref[0], weights_ref, keep_ref, send_ref)
-    for at in range(slots // PATCH):
-        keep_grad(at).wait()
+    weights_ref[at:, :] = jnp.zeros((weights_ref.shape[0] - at, width), bf16)
+    half = keep_out.shape[0]
+    bit = bit_ref[0]
+    hand_out = [
+        pltpu.make_async_copy(
+            weights_ref.at[pl.ds(pl.multiple_of(at * half, 16), half)], out, sems.at[3 + which]
+        )
+        for which, (at, out) in enumerate(((bit, keep_out), (1 - bit, send_out)))
+    ]
+    for copy in hand_out:
+        copy.start()
+    pack_rows(zorder_ref, serial_grad_ref, back_out, stage_ref, pack_sems)
+    for copy in hand_out:
+        copy.wait()
+
+
+def hold_kernel(rows_in, rows_out):
+    pass
 
 
 def split_rows(bit, rows_ref, keep_ref, send_ref):
@@ -425,17 +449,13 @@
     total_ref[...] = (mine_ref[...].astype(f32) + came_ref[...].astype(f32)).astype(bf16)
 
 
-def join_kernel(bit_ref, mine_ref, came_ref, both_ref):
-    half = mine_ref.shape[0]
-    bit = bit_ref[0]
-    both_ref[pl.ds(pl.multiple_of(bit * half, 16), half), :] = mine_ref[...]
-    both_ref[pl.ds(pl.multiple_of((1 - bit) * half, 16), half), :] = came_ref[...]
-
-
 def spread_kernel(
-    bit_ref, mine_ref, came_ref, up_ref, down_ref, conv_ref, gain_one_ref, gain_two_ref, sums_ref, *, scale
+    shares_ref, up_ref, down_ref, conv_ref, gain_one_ref, gain_two_ref, sums_ref, *, bits, scale
 ):
-    join_kernel(bit_ref, mine_ref, came_ref, sums_ref)
+    share = shares_ref.shape[0] >> bits
+    for at in range(1 << bits):
+        source = sum(((at >> bit) & 1) << (bits - 1 - bit) for bit in range(bits))
+        sums_ref[at * share : (at + 1) * share, :] = shares_ref[source * share : (source + 1) * share, :]
     width, hidden_width = up_ref.shape
     taps, groups, inner = conv_ref.shape[:3]
     down_ref[...] = sums_ref[0:hidden_width, :].astype(f32) * scale
@@ -454,7 +474,7 @@
     gain_two_ref[...] = gains[1:2, :]
 
 
-def call(kernel, outs, args, scratch=(), smem=0, flops=0, limit=16, held=0, stored=0, after=(), **static):
+def call(kernel, outs, args, scratch=(), smem=0, flops=0, limit=16, held=0, stored=0, after=(), same=None, **static):
     moved = sum(math.prod(a.shape) * a.dtype.itemsize for a in (*args, *outs))
     specs = [pl.BlockSpec(memory_space=pltpu.SMEM)] * smem
     specs += [pl.BlockSpec(memory_space=pltpu.VMEM)] * (len(args) - smem - held)
@@ -476,6 +496,7 @@
         in_specs=specs,
         out_specs=tuple(out_specs),
         scratch_shapes=list(scratch),
+        input_output_aliases=same or {},
         compiler_params=pltpu.CompilerParams(vmem_limit_bytes=limit * 1024 * 1024),
         cost_estimate=pl.CostEstimate(flops=int(flops), bytes_accessed=moved, transcendentals=0),
     )(*args, *after)
@@ -503,7 +524,7 @@
     return [1 << at for at in range(int(math.log2(lax.axis_size(axis))))]
 
 
-def sum_over_mesh(keep, send):
+def sum_over_mesh(keep, send, after):
     width = keep.shape[1]
     steps = steps_of("ty")
     for step, later in zip(steps, steps[1:] + [0]):
@@ -521,19 +542,16 @@
             )
         else:
             (share,) = call(add_kernel, [shaped(rows, width)], [keep, came], flops=1e6)
-    for step in steps_of("tx"):
+    steps = steps_of("tx")
+    for step in steps:
         (share,) = call(
-            add_kernel, [shaped(*share.shape)], [share, partner(share, "tx", step)], flops=1e6
-        )
-    for step in steps[:0:-1]:
-        (share,) = call(
-            join_kernel,
-            [shaped(2 * share.shape[0], width)],
-            [bit_of("ty", step), share, partner(share, "ty", step)],
-            smem=1,
+            add_kernel,
+            [shaped(*share.shape)],
+            [share, partner(share, "tx", step)],
+            after=after if step == steps[-1] else (),
             flops=1e6,
         )
-    return share, partner(share, "ty", steps[0])
+    return lax.all_gather(share, "ty", axis=0, tiled=True)
 
 
 def exchange(rows, tiles):
@@ -654,7 +672,7 @@
     lines = lax.axis_size("ty")
     sums_rows = 2 * hidden + taps * inner + 16
     sums_rows = -(-sums_rows // (16 * lines)) * (16 * lines)
-    serial_grad, keep, send = call(
+    back_grad, keep, send = call(
         backward_kernel,
         [
             shaped(slots_count, width),
@@ -680,6 +698,7 @@
             pltpu.VMEM((slots_count, width), f32),
             pltpu.VMEM((slots_count, width), bf16),
             pltpu.VMEM((slots_count, width), bf16),
+            pltpu.VMEM((slots_count, width), bf16),
             pltpu.VMEM((sums_rows, width), bf16),
             pltpu.VMEM((taps * width, width), bf16),
             pltpu.VMEM((slots_count, width), bf16),
@@ -687,33 +706,31 @@
             pltpu.VMEM((slots_count, hidden), bf16),
             pltpu.VMEM((PATCH, width), f32),
             pltpu.VMEM((PATCH + 2 * PAD, width), f32),
+            pltpu.VMEM((PATCH, width), bf16),
             *patch_scratch,
             pltpu.VMEM((PATCH, width), bf16),
             pltpu.VMEM((taps, width, width), f32),
             pltpu.VMEM((16, width), f32),
-            pltpu.SemaphoreType.DMA((4, slots_count // PATCH)),
+            pltpu.SemaphoreType.DMA((5,)),
+            pltpu.SemaphoreType.DMA((slots_count // WIDE,)),
         ],
-        stored=1,
+        stored=3,
         smem=1,
         flops=40e9,
-        limit=40,
+        limit=44,
         groups=groups,
         inner=inner,
     )
     (back_grad,) = call(
-        pack_rows,
+        hold_kernel,
         [shaped(slots_count, width)],
-        [zorder, serial_grad],
+        [back_grad],
         after=[came_result],
-        scratch=[
-            pltpu.VMEM((slots_count, width), bf16),
-            pltpu.SemaphoreType.DMA((slots_count // WIDE,)),
-        ],
+        held=1,
         stored=1,
-        flops=4e9,
+        same={0: 0},
     )
     came_back = exchange(back_grad, tiles)
-    totals = sum_over_mesh(keep, send)
     (out_rows,) = call(
         unpack_kernel, [shaped(tile_rows, width)], [slots, came_result], flops=4e9
     )
@@ -737,6 +754,7 @@
         stored=1,
         neighbours=neighbours,
     )
+    totals = sum_over_mesh(keep, send, [near_grad])
     near_parts = exchange(near_grad, tiles).reshape(tiles, width // tiles, width)
     near_share = jnp.sum(near_parts.astype(f32), axis=0)
     near_all = jnp.broadcast_to(near_share.astype(bf16), (tiles, *near_share.shape))
@@ -760,10 +778,10 @@
             shaped(1, width, dtype=f32),
             shaped(1, width, dtype=f32),
         ],
-        [bit_of("ty", 1), *totals],
+        [totals],
         scratch=[pltpu.VMEM((sums_rows, width), bf16)],
-        smem=1,
         flops=1e6,
+        bits=len(steps_of("ty")),
         scale=scale,
     )
     return (

time: 223 us -> 217 us (0.973)
  waiting for transfers between devices: 95.8 us -> 79.1 us
  between operations: 1.74 us -> 15.1 us
  starting transfers between devices: 46.4 us -> 44 us
    ppermute x8 -> x5, waiting for transfers between devices: 41.9 us -> 26.6 us  [partner(): lax.ppermute(value, axis, [(at, at ^ step) for at in range(lax.axis_size(...]
    all_to_all x4, waiting for transfers between devices: 53.9 us -> 50.8 us  [exchange(): lax.all_to_all(rows, ('tx', 'ty'), split_axis=0, concat_axis=0, tiled=True)]
    ppermute x8 -> x5, starting transfers between devices: 6.81 us -> 4.45 us  [partner(): lax.ppermute(value, axis, [(at, at ^ step) for at in range(lax.axis_size(...]
    unnamed x32 -> x34, local copies, waits for them, and re-layouts: 4.07 us -> 5.31 us
    pallas_call x17 -> x15, Pallas kernels: 58.4 us -> 59 us  [call(): pl.pallas_call(run, out_shape=tuple(shapes), in_specs=specs, out_specs=tu...]
  transfers between devices with their start and end apart: 20 -> 18, of which waited for: 8 -> 7; matrix products, arithmetic and copies ran while one was open for 0% -> 1% of each run, Pallas kernels for 19% -> 18%
where the time goes in v3:
time: 217 us; the launch traced here: 216 us
  waiting for transfers between devices  79.1 us (36%)
  Pallas kernels  59 us (27%)
  starting transfers between devices  44 us (20%)
  between operations  15.1 us (7%)
  blocking collectives  11.5 us (5%)
  local copies, waits for them, and re-layouts  6.76 us (3%)
    pallas_call x15, Pallas kernels, call(): pl.pallas_call(run, out_shape=tuple(shapes), in_specs=specs, out_specs=tu...  59 us
    all_to_all x4, waiting for transfers between devices, exchange(): lax.all_to_all(rows, ('tx', 'ty'), split_axis=0, concat_axis=0, tiled=True)  50.8 us
    ppermute x5, waiting for transfers between devices, partner(): lax.ppermute(value, axis, [(at, at ^ step) for at in range(lax.axis_size(...  26.6 us
    all_to_all x4, starting transfers between devices, exchange(): lax.all_to_all(rows, ('tx', 'ty'), split_axis=0, concat_axis=0, tiled=True)  20.1 us
    ppermute x8, starting transfers between devices, shifted(): lax.ppermute(value, axis, [(source, source + steps) for source in range(i...  19.4 us
    all_to_all x1, blocking collectives, exchange(): lax.all_to_all(rows, ('tx', 'ty'), split_axis=0, concat_axis=0, tiled=True)  11.5 us
    unnamed x34, local copies, waits for them, and re-layouts  5.31 us
    ppermute x5, starting transfers between devices, partner(): lax.ppermute(value, axis, [(at, at ^ step) for at in range(lax.axis_size(...  4.45 us
  transfers between devices with their start and end apart: 18, of which 7 were waited for; matrix products, arithmetic and copies ran while one was open for 1% of the time, Pallas kernels for 18%

profile of v3, /device:TPU:0, one launch (start us, length us, event | category | flops | bytes accessed | tf_op | source)
XLA Modules:
  0.0 216.2 jit_solution(8797537368485463847)
XLA Ops:
  10.8 2.4 %collective-permute-start.3 = (bf16[64,256]{1,0:T(8,128)(2,1)S(1)}, bf16[64,256]{1,0:T(8,128)(2,1)S(1)}, u32[]{:S(2)}, u32[]{:S(2)}) collective-permute-start(bf16[64,256]{1,0:T(8,128)(2,1)S(1)} %get-tuple-element.62), channel_id=1, source_target_pairs={{0,1},{1,2},{2,3},{3,4},{4,5},{5,6},{6,7},{8,9},{9,10},{10,11},{11... | collective-permute-start | bytes 98312 | tf_op jit(solution)/shard_map/ppermute | solution.py:512
  14.5 4.3 %collective-permute-start.1 = (bf16[64,256]{1,0:T(8,128)(2,1)S(1)}, bf16[64,256]{1,0:T(8,128)(2,1)S(1)}, u32[]{:S(2)}, u32[]{:S(2)}) collective-permute-start(bf16[64,256]{1,0:T(8,128)(2,1)S(1)} %get-tuple-element.64), channel_id=1, source_target_pairs={{0,8},{8,16},{16,24},{1,9},{9,17},{17,25},{2,10},{10,18},{18,26},{... | collective-permute-start | bytes 98312 | tf_op jit(solution)/shard_map/ppermute | solution.py:512
  20.2 5.8 %shard_map.189 = (bf16[1280,1024]{1,0:T(8,128)(2,1)}, bf16[1280,1024]{1,0:T(8,128)(2,1)S(1)}) custom-call(s32[16,1024]{1,0:T(8,128)S(1)} %bitcast.31), custom_call_target="tpu_custom_call" | custom-call | flops 8000000000 | bytes 5308416 | tf_op jit(solution)/shard_map/pallas_call | solution.py:493
  26.1 4.3 %shard_map.190 = (bf16[256,1024]{1,0:T(8,128)(2,1)}, f32[1024,256]{1,0:T(8,128)}, bf16[2048,512]{1,0:T(8,128)(2,1)}) custom-call(s32[1,1024]{1,0:T(1,128)S(1)} %get-tuple-element.33.refs_0_, bf16[1024,256]{1,0:T(8,128)(2,1)S(1)} %bitcast.27, bf16[1024,256]{1,0:T(8,128)(2,1)S(1)} %bitcast.28, bf16[64,256]{1,0:T(8,128)(2,1)S(1)} %collective-permute-done.refs_3_, ...), custom_call_target="tpu_custom_call" | custom-call | flops 4000000000 | bytes 7606272 | tf_op jit(solution)/shard_map/pallas_call | solution.py:493
  30.5 9.6 %all-to-all-start = ((bf16[32,64,512]{2,1,0:T(8,128)(2,1)}), bf16[32,64,512]{2,1,0:T(8,128)(2,1)}, u32[]{:S(2)}, u32[]{:S(2)}) async-start(bf16[32,64,512]{2,1,0:T(8,128)(2,1)} %bitcast.38), calls=%async_computation | async-start | bytes 4194304 | tf_op jit(solution)/shard_map/all_to_all | solution.py:558
  40.1 48.9 %all-to-all-done = bf16[32,64,512]{2,1,0:T(8,128)(2,1)} async-done(((bf16[32,64,512]{2,1,0:T(8,128)(2,1)}), bf16[32,64,512]{2,1,0:T(8,128)(2,1)}, u32[]{:S(2)}, u32[]{:S(2)}) %all-to-all-start) | async-done | bytes 2097184 | tf_op jit(solution)/shard_map/all_to_all | solution.py:558
  89.0 12.3 %shard_map.191 = (bf16[2048,256]{1,0:T(8,128)(2,1)}, f32[2048,256]{1,0:T(8,128)}, bf16[2048,256]{1,0:T(8,128)(2,1)}) custom-call(s32[1,2048]{1,0:T(1,128)S(1)} %copy-done.11, bf16[768,32]{1,0:T(8,128)(2,1)S(1)} %bitcast.29, f32[1,256]{1,0:T(1,128)S(1)} %bitcast.32, f32[1,256]{1,0:T(1,128)S(1)} %bitcast.34, bf16[256,1024]{1,0:T(8,128)(2,1)S(1)} %copy-done.5, ...), custom_call_target="tpu_custom_call" | custom-call | flops 10000000000 | bytes 7399424 | tf_op jit(solution)/shard_map/pallas_call | solution.py:493
  101.4 4.2 %all-to-all-start.1 = ((bf16[32,64,256]{2,1,0:T(8,128)(2,1)}), bf16[32,64,256]{2,1,0:T(8,128)(2,1)S(1)}, u32[]{:S(2)}, u32[]{:S(2)}) async-start(bf16[32,64,256]{2,1,0:T(8,128)(2,1)} %bitcast.39), calls=%async_computation.1 | async-start | bytes 2097152 | tf_op jit(solution)/shard_map/all_to_all | solution.py:558
  105.6 24.1 %shard_map.193 = (bf16[2048,256]{1,0:T(8,128)(2,1)}, bf16[1088,256]{1,0:T(8,128)(2,1)}, bf16[1088,256]{1,0:T(8,128)(2,1)}) custom-call(s32[1]{0:T(128)} %bitcast.11.refs_0_, s32[1,2048]{1,0:T(1,128)S(1)} %copy-done.11, bf16[768,32]{1,0:T(8,128)(2,1)S(1)} %bitcast.30, f32[1,256]{1,0:T(1,128)S(1)} %bitcast.33, f32[1,256]{1,0:T(1,128)S(1)} %bitcast.35, ...), custom_call_target="tpu_custom_call" | custom-call | flops 40000000000 | bytes 8513540 | tf_op jit(solution)/shard_map/pallas_call | solution.py:493
  129.7 1.9 all-to-all-done.1
  131.6 3.8 %all-to-all-start.2 = ((bf16[32,64,256]{2,1,0:T(8,128)(2,1)}), bf16[32,64,256]{2,1,0:T(8,128)(2,1)S(1)}, u32[]{:S(2)}, u32[]{:S(2)}) async-start(bf16[32,64,256]{2,1,0:T(8,128)(2,1)} %bitcast.37), calls=%async_computation.2 | async-start | bytes 2097152 | tf_op jit(solution)/shard_map/all_to_all | solution.py:558
  135.8 1.9 collective-permute-done.8.refs_2_
  138.7 1.8 collective-permute-start.9
  140.5 13.7 %collective-permute-done.9.refs_2_ = bf16[544,256]{1,0:T(8,128)(2,1)S(1)} collective-permute-done((bf16[544,256]{1,0:T(8,128)(2,1)}, bf16[544,256]{1,0:T(8,128)(2,1)S(1)}, u32[]{:S(2)}, u32[]{:S(2)}) %collective-permute-start.9) | collective-permute-done | bytes 278560 | tf_op jit(solution)/shard_map/ppermute | solution.py:516
  155.4 6.0 %collective-permute-done.10.refs_1_ = bf16[272,256]{1,0:T(8,128)(2,1)S(1)} collective-permute-done((bf16[272,256]{1,0:T(8,128)(2,1)S(1)}, bf16[272,256]{1,0:T(8,128)(2,1)S(1)}, u32[]{:S(2)}, u32[]{:S(2)}) %collective-permute-start.10) | collective-permute-done | bytes 139296 | tf_op jit(solution)/shard_map/ppermute | solution.py:516
  161.5 5.0 %collective-permute-done.11.refs_1_ = bf16[272,256]{1,0:T(8,128)(2,1)S(1)} collective-permute-done((bf16[272,256]{1,0:T(8,128)(2,1)S(1)}, bf16[272,256]{1,0:T(8,128)(2,1)S(1)}, u32[]{:S(2)}, u32[]{:S(2)}) %collective-permute-start.11) | collective-permute-done | bytes 139296 | tf_op jit(solution)/shard_map/ppermute | solution.py:516
  167.8 2.1 shard_map.192.refs_6_
  170.9 5.1 %shard_map.195 = (f32[1024,256]{1,0:T(8,128)}, bf16[256,256]{1,0:T(8,128)(2,1)S(1)}, bf16[256,256]{1,0:T(8,128)(2,1)S(1)}) custom-call(s32[1,1024]{1,0:T(1,128)S(1)} %get-tuple-element.33.refs_0_, bf16[2048,256]{1,0:T(8,128)(2,1)S(1)} %bitcast.24, bf16[256,256]{1,0:T(8,128)(2,1)S(1)} %copy-done.9, bf16[1280,1024]{1,0:T(8,128)(2,1)} %get-tuple-element.41.refs_3_, ...), custom_call_target="tpu_custom_call" | custom-call | flops 6000000000 | bytes 6688768 | tf_op jit(solution)/shard_map/pallas_call | solution.py:493
  176.7 11.5 %all_to_all.48 = bf16[32,8,256]{2,1,0:T(8,128)(2,1)S(1)} all-to-all(bf16[32,8,256]{2,1,0:T(8,128)(2,1)S(1)} %bitcast.25), channel_id=1, replica_groups=mesh['tx'=4,'ty'=8] {'tx','ty'}, dimensions={0} | all-to-all | bytes 262144 | tf_op jit(solution)/shard_map/all_to_all | solution.py:558
  188.9 2.6 %all-to-all-start.4 = ((bf16[32,8,256]{2,1,0:T(8,128)(2,1)}), bf16[32,8,256]{2,1,0:T(8,128)(2,1)S(1)}, u32[]{:S(2)}, u32[]{:S(2)}) async-start(bf16[32,8,256]{2,1,0:T(8,128)(2,1)} %broadcast_in_dim.11), calls=%async_computation.4 | async-start | bytes 262144 | tf_op jit(solution)/shard_map/all_to_all | solution.py:558
  192.8 3.0 %collective-permute-start.6 = (bf16[64,256]{1,0:T(8,128)(2,1)S(1)}, bf16[64,256]{1,0:T(8,128)(2,1)S(1)}, u32[]{:S(2)}, u32[]{:S(2)}) collective-permute-start(bf16[64,256]{1,0:T(8,128)(2,1)S(1)} %get-tuple-element.59), channel_id=1, source_target_pairs={{0,1},{1,2},{2,3},{3,4},{4,5},{5,6},{6,7},{8,9},{9,10},{10,11},{11... | collective-permute-start | bytes 98312 | tf_op jit(solution)/shard_map/ppermute | solution.py:512
  197.2 4.5 %collective-permute-start.4 = (bf16[64,256]{1,0:T(8,128)(2,1)S(1)}, bf16[64,256]{1,0:T(8,128)(2,1)S(1)}, u32[]{:S(2)}, u32[]{:S(2)}) collective-permute-start(bf16[64,256]{1,0:T(8,128)(2,1)S(1)} %get-tuple-element.61), channel_id=1, source_target_pairs={{0,8},{8,16},{16,24},{1,9},{9,17},{17,25},{2,10},{10,18},{18,26},{... | collective-permute-start | bytes 98312 | tf_op jit(solution)/shard_map/ppermute | solution.py:512
  201.8 1.6 collective-permute-done.4.refs_2_
  207.7 1.7 shard_map.202
  (69 shorter events, 19.0 us)
Async XLA Ops:
  10.8 15.2 %collective-permute-start.3 = (bf16[64,256]{1,0:T(8,128)(2,1)S(1)}, bf16[64,256]{1,0:T(8,128)(2,1)S(1)}, u32[]{:S(2)}, u32[]{:S(2)}) collective-permute-start(bf16[64,256]{1,0:T(8,128)(2,1)S(1)} %get-tuple-element.62), channel_id=1, source_target_pairs={{0,1},{1,2},{2,3},{3,4},{4,5},{5,6},{6,7},{8,9},{9,10},{10,11},{11... | collective-permute-start | bytes 98312 | tf_op jit(solution)/shard_map/ppermute | solution.py:512
  13.2 12.8 %collective-permute-start.2 = (bf16[64,256]{1,0:T(8,128)(2,1)S(1)}, bf16[64,256]{1,0:T(8,128)(2,1)S(1)}, u32[]{:S(2)}, u32[]{:S(2)}) collective-permute-start(bf16[64,256]{1,0:T(8,128)(2,1)S(1)} %get-tuple-element.63), channel_id=1, source_target_pairs={{1,0},{2,1},{3,2},{4,3},{5,4},{6,5},{7,6},{9,8},{10,9},{11,10},{12... | collective-permute-start | bytes 98312 | tf_op jit(solution)/shard_map/ppermute | solution.py:512
  14.5 11.5 %collective-permute-start.1 = (bf16[64,256]{1,0:T(8,128)(2,1)S(1)}, bf16[64,256]{1,0:T(8,128)(2,1)S(1)}, u32[]{:S(2)}, u32[]{:S(2)}) collective-permute-start(bf16[64,256]{1,0:T(8,128)(2,1)S(1)} %get-tuple-element.64), channel_id=1, source_target_pairs={{0,8},{8,16},{16,24},{1,9},{9,17},{17,25},{2,10},{10,18},{18,26},{... | collective-permute-start | bytes 98312 | tf_op jit(solution)/shard_map/ppermute | solution.py:512
  18.8 7.2 %collective-permute-start = (bf16[64,256]{1,0:T(8,128)(2,1)S(1)}, bf16[64,256]{1,0:T(8,128)(2,1)S(1)}, u32[]{:S(2)}, u32[]{:S(2)}) collective-permute-start(bf16[64,256]{1,0:T(8,128)(2,1)S(1)} %get-tuple-element.65), channel_id=1, source_target_pairs={{8,0},{16,8},{24,16},{9,1},{17,9},{25,17},{10,2},{18,10},{26,18},{... | collective-permute-start | bytes 98312 | tf_op jit(solution)/shard_map/ppermute | solution.py:512
  30.4 58.5 %copy-start.5 = (bf16[256,1024]{1,0:T(8,128)(2,1)S(1)}, bf16[256,1024]{1,0:T(8,128)(2,1)}, u32[]{:S(2)}) copy-start(bf16[256,1024]{1,0:T(8,128)(2,1)} %refs_5_.3) | copy-start | bytes 1572868
  30.5 58.5 %copy-start.6 = (bf16[1024,256]{1,0:T(8,128)(2,1)S(1)}, bf16[1024,256]{1,0:T(8,128)(2,1)}, u32[]{:S(2)}) copy-start(bf16[1024,256]{1,0:T(8,128)(2,1)} %refs_6_.1) | copy-start | bytes 1572868
  30.5 58.5 %copy-start.7 = (bf16[3,8,32,32]{3,2,1,0:T(8,128)(2,1)S(1)}, bf16[3,8,32,32]{3,2,1,0:T(8,128)(2,1)}, u32[]{:S(2)}) copy-start(bf16[3,8,32,32]{3,2,1,0:T(8,128)(2,1)} %param.21) | copy-start | bytes 147460
  30.5 58.5 %copy-start.11 = (s32[1,2048]{1,0:T(1,128)S(1)}, s32[1,2048]{1,0:T(1,128)}, u32[]{:S(2)}) copy-start(s32[1,2048]{1,0:T(1,128)} %refs_1_.3) | copy-start | bytes 24580
  30.5 58.5 %copy-start.13 = (f32[256]{0:T(256)S(1)}, f32[256]{0:T(256)}, u32[]{:S(2)}) copy-start(f32[256]{0:T(256)} %param.20) | copy-start | bytes 3076
  30.5 58.5 %copy-start.14 = (f32[256]{0:T(256)S(1)}, f32[256]{0:T(256)}, u32[]{:S(2)}) copy-start(f32[256]{0:T(256)} %param.22) | copy-start | bytes 3076
  30.5 58.5 %all-to-all-start = ((bf16[32,64,512]{2,1,0:T(8,128)(2,1)}), bf16[32,64,512]{2,1,0:T(8,128)(2,1)}, u32[]{:S(2)}, u32[]{:S(2)}) async-start(bf16[32,64,512]{2,1,0:T(8,128)(2,1)} %bitcast.38), calls=%async_computation | async-start | bytes 4194304 | tf_op jit(solution)/shard_map/all_to_all | solution.py:558
  101.4 30.3 %all-to-all-start.1 = ((bf16[32,64,256]{2,1,0:T(8,128)(2,1)}), bf16[32,64,256]{2,1,0:T(8,128)(2,1)S(1)}, u32[]{:S(2)}, u32[]{:S(2)}) async-start(bf16[32,64,256]{2,1,0:T(8,128)(2,1)} %bitcast.39), calls=%async_computation.1 | async-start | bytes 2097152 | tf_op jit(solution)/shard_map/all_to_all | solution.py:558
  131.6 38.2 %all-to-all-start.2 = ((bf16[32,64,256]{2,1,0:T(8,128)(2,1)}), bf16[32,64,256]{2,1,0:T(8,128)(2,1)S(1)}, u32[]{:S(2)}, u32[]{:S(2)}) async-start(bf16[32,64,256]{2,1,0:T(8,128)(2,1)} %bitcast.37), calls=%async_computation.2 | async-start | bytes 2097152 | tf_op jit(solution)/shard_map/all_to_all | solution.py:558
  135.4 71.0 %all-gather.2.cloned.1.call-start = ((), (), s32[]{:S(2)}) async-start(), calls=%async_computation.5 | async-start | bytes 1253376 | tf_op jit(solution)/shard_map/all_gather | solution.py:554
  135.5 2.2 %collective-permute-start.8 = (bf16[1088,256]{1,0:T(8,128)(2,1)}, bf16[1088,256]{1,0:T(8,128)(2,1)S(1)}, u32[]{:S(2)}, u32[]{:S(2)}) collective-permute-start(bf16[1088,256]{1,0:T(8,128)(2,1)} %get-tuple-element.48), channel_id=1, source_target_pairs={{0,1},{1,0},{2,3},{3,2},{4,5},{5,4},{6,7},{7,6},{8,9},{9,8},{10,11... | collective-permute-start | bytes 1671176 | tf_op jit(solution)/shard_map/ppermute | solution.py:516
  138.7 15.5 %collective-permute-start.9 = (bf16[544,256]{1,0:T(8,128)(2,1)}, bf16[544,256]{1,0:T(8,128)(2,1)S(1)}, u32[]{:S(2)}, u32[]{:S(2)}) collective-permute-start(bf16[544,256]{1,0:T(8,128)(2,1)} %get-tuple-element.50), channel_id=1, source_target_pairs={{0,2},{1,3},{2,0},{3,1},{4,6},{5,7},{6,4},{7,5},{8,10},{9,11},{10,... | collective-permute-start | bytes 835592 | tf_op jit(solution)/shard_map/ppermute | solution.py:516
  154.3 7.0 %collective-permute-start.10 = (bf16[272,256]{1,0:T(8,128)(2,1)S(1)}, bf16[272,256]{1,0:T(8,128)(2,1)S(1)}, u32[]{:S(2)}, u32[]{:S(2)}) collective-permute-start(bf16[272,256]{1,0:T(8,128)(2,1)S(1)} %get-tuple-element.52), channel_id=1, source_target_pairs={{0,4},{1,5},{2,6},{3,7},{4,0},{5,1},{6,2},{7,3},{8,12},{9,13},{10,... | collective-permute-start | bytes 417800 | tf_op jit(solution)/shard_map/ppermute | solution.py:516
  161.4 5.1 %collective-permute-start.11 = (bf16[272,256]{1,0:T(8,128)(2,1)S(1)}, bf16[272,256]{1,0:T(8,128)(2,1)S(1)}, u32[]{:S(2)}, u32[]{:S(2)}) collective-permute-start(bf16[272,256]{1,0:T(8,128)(2,1)S(1)} %shard_map.199.refs_0_), channel_id=1, source_target_pairs={{0,8},{8,0},{16,24},{24,16},{1,9},{9,1},{17,25},{25,17},{2,10},{10... | collective-permute-start | bytes 417800 | tf_op jit(solution)/shard_map/ppermute | solution.py:516
  166.6 9.4 %collective-permute-start.12 = (bf16[272,256]{1,0:T(8,128)(2,1)S(1)}, bf16[272,256]{1,0:T(8,128)(2,1)S(1)}, u32[]{:S(2)}, u32[]{:S(2)}) collective-permute-start(bf16[272,256]{1,0:T(8,128)(2,1)S(1)} %shard_map.200.refs_0_), channel_id=1, source_target_pairs={{0,16},{8,24},{16,0},{24,8},{1,17},{9,25},{17,1},{25,9},{2,18},{10... | collective-permute-start | bytes 417800 | tf_op jit(solution)/shard_map/ppermute | solution.py:516
  188.9 16.8 %all-to-all-start.4 = ((bf16[32,8,256]{2,1,0:T(8,128)(2,1)}), bf16[32,8,256]{2,1,0:T(8,128)(2,1)S(1)}, u32[]{:S(2)}, u32[]{:S(2)}) async-start(bf16[32,8,256]{2,1,0:T(8,128)(2,1)} %broadcast_in_dim.11), calls=%async_computation.4 | async-start | bytes 262144 | tf_op jit(solution)/shard_map/all_to_all | solution.py:558
  191.5 10.2 %collective-permute-start.7 = (bf16[64,256]{1,0:T(8,128)(2,1)S(1)}, bf16[64,256]{1,0:T(8,128)(2,1)S(1)}, u32[]{:S(2)}, u32[]{:S(2)}) collective-permute-start(bf16[64,256]{1,0:T(8,128)(2,1)S(1)} %get-tuple-element.58), channel_id=1, source_target_pairs={{1,0},{2,1},{3,2},{4,3},{5,4},{6,5},{7,6},{9,8},{10,9},{11,10},{12... | collective-permute-start | bytes 98312 | tf_op jit(solution)/shard_map/ppermute | solution.py:512
  192.8 8.9 %collective-permute-start.6 = (bf16[64,256]{1,0:T(8,128)(2,1)S(1)}, bf16[64,256]{1,0:T(8,128)(2,1)S(1)}, u32[]{:S(2)}, u32[]{:S(2)}) collective-permute-start(bf16[64,256]{1,0:T(8,128)(2,1)S(1)} %get-tuple-element.59), channel_id=1, source_target_pairs={{0,1},{1,2},{2,3},{3,4},{4,5},{5,6},{6,7},{8,9},{9,10},{10,11},{11... | collective-permute-start | bytes 98312 | tf_op jit(solution)/shard_map/ppermute | solution.py:512
  195.9 5.9 %collective-permute-start.5 = (bf16[64,256]{1,0:T(8,128)(2,1)S(1)}, bf16[64,256]{1,0:T(8,128)(2,1)S(1)}, u32[]{:S(2)}, u32[]{:S(2)}) collective-permute-start(bf16[64,256]{1,0:T(8,128)(2,1)S(1)} %get-tuple-element.60), channel_id=1, source_target_pairs={{8,0},{16,8},{24,16},{9,1},{17,9},{25,17},{10,2},{18,10},{26,18},{... | collective-permute-start | bytes 98312 | tf_op jit(solution)/shard_map/ppermute | solution.py:512
  197.2 6.2 %collective-permute-start.4 = (bf16[64,256]{1,0:T(8,128)(2,1)S(1)}, bf16[64,256]{1,0:T(8,128)(2,1)S(1)}, u32[]{:S(2)}, u32[]{:S(2)}) collective-permute-start(bf16[64,256]{1,0:T(8,128)(2,1)S(1)} %get-tuple-element.61), channel_id=1, source_target_pairs={{0,8},{8,16},{16,24},{1,9},{9,17},{17,25},{2,10},{10,18},{18,26},{... | collective-permute-start | bytes 98312 | tf_op jit(solution)/shard_map/ppermute | solution.py:512
  (11 other events, 42.2 us)
Sparse Core Ops, SparseCore 0:
  176.9 24.0 all-gather.1

commit v4 on v3

--- a/solution.py
+++ b/solution.py
@@ -74,7 +74,20 @@
     return marks(iota((count, row.shape[1]), 0) + start == row)
 
 
-def route_kernel(counts_ref, owner_ref, lists_ref, points_ref, slots_ref, sent_ref, *, tiles, capacity):
+def route_kernel(
+    counts_ref, owner_in, lists_in, points_in, slots_ref, sent0, sent1, sent2, sent3,
+    owner_ref, lists_ref, points_ref, sems, *, tiles, capacity
+):
+    fetches = [
+        pltpu.make_async_copy(source, target, sems.at[at])
+        for at, (source, target) in enumerate(
+            ((owner_in, owner_ref), (lists_in, lists_ref), (points_in, points_ref))
+        )
+    ]
+    for fetch in fetches:
+        fetch.start()
+    for fetch in fetches:
+        fetch.wait()
     rows = owner_ref.shape[1]
     live = iota((1, rows), 1) < counts_ref[0]
     owned = jnp.where(live, owner_ref[...], tiles)
@@ -83,9 +96,13 @@
     before = dot(marks(members), earlier)
     rank = jnp.sum(jnp.where(members, before, 0.0), axis=0, keepdims=True)
     slots_ref[...] = jnp.where(live, owned * capacity + rank.astype(jnp.int32), -1)
-    lists = lists_ref[...]
-    chosen = marks(iota((rows, lists.shape[1]), 0) == lists)
-    sent_ref[...] = dot(chosen, points_ref[...], TN).astype(bf16)
+    for direction, sent_ref in enumerate((sent0, sent1, sent2, sent3)):
+        sent_ref[...] = dot(chosen_rows(lists_ref, direction, rows), points_ref[...], TN).astype(bf16)
+
+
+def chosen_rows(lists_ref, direction, rows):
+    listed = lists_ref[direction : direction + 1, :]
+    return marks(iota((rows, listed.shape[1]), 0) == listed)
 
 
 def pack_rows(slots_ref, rows_ref, packed_out, stage_ref, sems):
@@ -174,7 +191,7 @@
 
 def tile_back_kernel(
     slots_ref, back_ref, w_ref, table_in, average_in, pre_in,
-    row_out, near_ref, halo_ref,
+    row_out, near_ref, halo0, halo1, halo2, halo3,
     row_ref, table_ref, average_ref, pre_ref, act_ref, spread_ref, sems, *, neighbours
 ):
     rows = row_ref.shape[0]
@@ -204,7 +221,10 @@
     near_ref[...] = dot(average_ref[...], act_ref[...]).astype(near_ref.dtype)
     spread_ref[...] = (dot(act_ref[...], w_ref[...], NT) * (1.0 / neighbours)).astype(bf16)
     fetch_table.wait()
-    halo_ref[...] = dot(table_ref[rows:, :], spread_ref[...]).astype(bf16)
+    halo = dot(table_ref[rows:, :], spread_ref[...]).astype(bf16)
+    size = halo0.shape[0]
+    for direction, halo_ref in enumerate((halo0, halo1, halo2, halo3)):
+        halo_ref[...] = halo[direction * size : (direction + 1) * size]
     for start in range(0, rows, WIDE):
         here = pl.ds(start, WIDE)
         row_ref[here, :] = row_ref[here, :] + dot(table_ref[here, :], spread_ref[...])
@@ -213,11 +233,22 @@
         keep_row(start).wait()
 
 
-def finish_kernel(lists_ref, row_ref, back0, back1, back2, back3, out_ref):
-    lists = lists_ref[...]
-    came = jnp.concatenate([back0[...], back1[...], back2[...], back3[...]], axis=0)
-    chosen = marks(iota((row_ref.shape[0], lists.shape[1]), 0) == lists)
-    out_ref[...] = (row_ref[...] + dot(chosen, came)).astype(bf16)
+def finish_kernel(lists_ref, back0, back1, back2, back3, row_in, out_ref, row_ref, sems):
+    fetch = pltpu.make_async_copy(row_in, row_ref, sems.at[0])
+    fetch.start()
+    rows = row_ref.shape[0]
+    total = sum(
+        dot(chosen_rows(lists_ref, direction, rows), came[...])
+        for direction, came in enumerate((back0, back1, back2, back3))
+    )
+    fetch.wait()
+    out_ref[...] = (row_ref[...] + total).astype(bf16)
+
+
+def near_sum_kernel(parts_ref, share_ref, *, share):
+    rows = parts_ref.shape[0]
+    same = lax.rem(iota((rows, rows), 0), share) == lax.rem(iota((rows, rows), 1), share)
+    share_ref[...] = dot(marks(same), parts_ref[...]).astype(bf16)
 
 
 def full_taps(conv_ref, groups, inner):
@@ -434,28 +465,66 @@
     pass
 
 
-def split_rows(bit, rows_ref, keep_ref, send_ref):
+def split_rows(bit, rows, scratch_ref, keep_ref, send_ref):
+    scratch_ref[...] = rows.astype(bf16)
     half = keep_ref.shape[0]
-    keep_ref[...] = rows_ref[pl.ds(pl.multiple_of(bit * half, 16), half), :]
-    send_ref[...] = rows_ref[pl.ds(pl.multiple_of((1 - bit) * half, 16), half), :]
-
-
-def add_split_kernel(bit_ref, mine_ref, came_ref, keep_ref, send_ref, total_ref):
-    total_ref[...] = (mine_ref[...].astype(f32) + came_ref[...].astype(f32)).astype(bf16)
-    split_rows(bit_ref[0], total_ref, keep_ref, send_ref)
+    keep_ref[...] = scratch_ref[pl.ds(pl.multiple_of(bit * half, 16), half), :]
+    send_ref[...] = scratch_ref[pl.ds(pl.multiple_of((1 - bit) * half, 16), half), :]
+
+
+def added(mine_ref, came_ref):
+    return mine_ref[...].astype(f32) + came_ref[...].astype(f32)
+
+
+def first_split_kernel(
+    bit0_ref, bit1_ref, mine_ref, came_ref, keep0, send0, keep1, send1, scratch0, scratch1
+):
+    half = scratch0.shape[0]
+    total = added(mine_ref, came_ref)
+    split_rows(bit0_ref[0], total[:half], scratch0, keep0, send0)
+    split_rows(bit1_ref[0], total[half:], scratch1, keep1, send1)
+
+
+def next_split_kernel(
+    bit0_ref, bit1_ref, mine0, came0, mine1, came1, keep0, send0, keep1, send1, scratch0, scratch1
+):
+    split_rows(bit0_ref[0], added(mine0, came0), scratch0, keep0, send0)
+    split_rows(bit1_ref[0], added(mine1, came1), scratch1, keep1, send1)
+
+
+def add_join_kernel(mine0, came0, mine1, came1, share_ref):
+    half = mine0.shape[0]
+    share_ref[0:half, :] = added(mine0, came0).astype(bf16)
+    share_ref[half:, :] = added(mine1, came1).astype(bf16)
 
 
 def add_kernel(mine_ref, came_ref, total_ref):
-    total_ref[...] = (mine_ref[...].astype(f32) + came_ref[...].astype(f32)).astype(bf16)
+    total_ref[...] = added(mine_ref, came_ref).astype(bf16)
+
+
+def join_kernel(bit_ref, mine_ref, came_ref, both_ref):
+    half = mine_ref.shape[0]
+    bit = bit_ref[0]
+    both_ref[pl.ds(pl.multiple_of(bit * half, 16), half), :] = mine_ref[...]
+    both_ref[pl.ds(pl.multiple_of((1 - bit) * half, 16), half), :] = came_ref[...]
 
 
 def spread_kernel(
-    shares_ref, up_ref, down_ref, conv_ref, gain_one_ref, gain_two_ref, sums_ref, *, bits, scale
+    bit_ref, mine_ref, came_ref, up_ref, down_ref, conv_ref, gain_one_ref, gain_two_ref,
+    joined_ref, sums_ref, *, bits, scale
 ):
-    share = shares_ref.shape[0] >> bits
+    join_kernel(bit_ref, mine_ref, came_ref, joined_ref)
+    rows = sums_ref.shape[0]
+    piece = (rows >> bits) // 2
     for at in range(1 << bits):
-        source = sum(((at >> bit) & 1) << (bits - 1 - bit) for bit in range(bits))
-        sums_ref[at * share : (at + 1) * share, :] = shares_ref[source * share : (source + 1) * share, :]
+        digits = [(at >> (bits - 1 - bit)) & 1 for bit in range(bits)]
+        for part, order in enumerate((digits[1:], digits[:0:-1])):
+            place = 0
+            for digit in order:
+                place = 2 * place + digit
+            start = digits[0] * (rows // 2) + part * (rows // 4) + place * piece
+            source = (2 * at + part) * piece
+            sums_ref[start : start + piece, :] = joined_ref[source : source + piece, :]
     width, hidden_width = up_ref.shape
     taps, groups, inner = conv_ref.shape[:3]
     down_ref[...] = sums_ref[0:hidden_width, :].astype(f32) * scale
@@ -524,34 +593,51 @@
     return [1 << at for at in range(int(math.log2(lax.axis_size(axis))))]
 
 
-def sum_over_mesh(keep, send, after):
+def sum_over_mesh(keep, send, early, late, returned):
     width = keep.shape[1]
     steps = steps_of("ty")
-    for step, later in zip(steps, steps[1:] + [0]):
-        came = partner(send, "ty", step)
-        rows = keep.shape[0]
-        if later:
-            half = shaped(rows // 2, width)
-            keep, send = call(
-                add_split_kernel,
-                [half, half],
-                [bit_of("ty", later), keep, came],
-                scratch=[pltpu.VMEM((rows, width), bf16)],
-                smem=1,
-                flops=1e6,
-            )
-        else:
-            (share,) = call(add_kernel, [shaped(rows, width)], [keep, came], flops=1e6)
-    steps = steps_of("tx")
-    for step in steps:
+    orders = steps[1:], steps[:0:-1]
+
+    def halves(kernel, rows, at, args, **options):
+        return call(
+            kernel,
+            [shaped(rows // 2, width)] * 4,
+            [bit_of("ty", order[at]) for order in orders] + list(args),
+            scratch=[pltpu.VMEM((rows, width), bf16)] * 2,
+            smem=2,
+            flops=1e6,
+            **options,
+        )
+
+    came = partner(send, "ty", steps[0])
+    rows = keep.shape[0] // 2
+    parts = halves(first_split_kernel, rows, 0, [keep, came], after=early)
+    for at in range(len(orders[0])):
+        rows = rows // 2
+        pairs = []
+        for which, order in enumerate(orders):
+            pairs += [parts[2 * which], partner(parts[2 * which + 1], "ty", order[at])]
+        if at + 1 < len(orders[0]):
+            parts = halves(next_split_kernel, rows, at + 1, pairs)
+    (share,) = call(add_join_kernel, [shaped(2 * rows, width)], pairs, flops=1e6)
+    for step in steps_of("tx"):
         (share,) = call(
             add_kernel,
             [shaped(*share.shape)],
             [share, partner(share, "tx", step)],
-            after=after if step == steps[-1] else (),
+            after=late if step == steps_of("tx")[-1] else (),
             flops=1e6,
         )
-    return lax.all_gather(share, "ty", axis=0, tiled=True)
+    for at, step in enumerate(steps[:0:-1]):
+        (share,) = call(
+            join_kernel,
+            [shaped(2 * share.shape[0], width)],
+            [bit_of("ty", step), share, partner(share, "ty", step)],
+            after=returned[2 * at : 2 * at + 2],
+            smem=1,
+            flops=1e6,
+        )
+    return share, partner(share, "ty", steps[0])
 
 
 def exchange(rows, tiles):
@@ -578,7 +664,7 @@
     border_rows = border.shape[2]
     edge = 4 * border_rows
     ext = tile_rows + edge
-    lists = border.reshape(1, edge)
+    lists = border[0]
     near_tile = near[0]
     neighbours = near_tile.shape[0]
     tiles = lax.axis_size("tx") * lax.axis_size("ty")
@@ -590,20 +676,27 @@
     gain_two_row = gain_two.reshape(1, width)
     hidden = w_up.shape[1]
 
-    slots, sent = call(
+    slots, *sent = call(
         route_kernel,
-        [shaped(1, tile_rows, dtype=jnp.int32), shaped(edge, width)],
+        [shaped(1, tile_rows, dtype=jnp.int32)] + [shaped(border_rows, width)] * 4,
         [counts, owner, lists, points_tile],
+        scratch=[
+            pltpu.VMEM((1, tile_rows), jnp.int32),
+            pltpu.VMEM((4, border_rows), jnp.int32),
+            pltpu.VMEM((tile_rows, width), bf16),
+            pltpu.SemaphoreType.DMA((3,)),
+        ],
         smem=1,
+        held=3,
         flops=4e9,
         tiles=tiles,
         capacity=capacity,
     )
     halos = [
-        shifted(sent[0:border_rows], "tx", -1),
-        shifted(sent[border_rows : 2 * border_rows], "tx", 1),
-        shifted(sent[2 * border_rows : 3 * border_rows], "ty", -1),
-        shifted(sent[3 * border_rows :], "ty", 1),
+        shifted(sent[0], "tx", -1),
+        shifted(sent[1], "tx", 1),
+        shifted(sent[2], "ty", -1),
+        shifted(sent[3], "ty", 1),
     ]
     kept_table, table = call(
         count_kernel,
@@ -671,7 +764,7 @@
     came_result = exchange(back_result, tiles)
     lines = lax.axis_size("ty")
     sums_rows = 2 * hidden + taps * inner + 16
-    sums_rows = -(-sums_rows // (16 * lines)) * (16 * lines)
+    sums_rows = -(-sums_rows // (32 * lines)) * (32 * lines)
     back_grad, keep, send = call(
         backward_kernel,
         [
@@ -734,9 +827,10 @@
     (out_rows,) = call(
         unpack_kernel, [shaped(tile_rows, width)], [slots, came_result], flops=4e9
     )
-    row_grad, near_grad, halo_grad = call(
+    row_grad, near_grad, *halo_grad = call(
         tile_back_kernel,
-        [shaped(tile_rows, width, dtype=f32), shaped(width, width), shaped(edge, width)],
+        [shaped(tile_rows, width, dtype=f32), shaped(width, width)]
+        + [shaped(border_rows, width)] * 4,
         [slots, came_back, w_near, kept_table, average, pre_act],
         after=[out_rows],
         scratch=[
@@ -754,19 +848,29 @@
         stored=1,
         neighbours=neighbours,
     )
-    totals = sum_over_mesh(keep, send, [near_grad])
-    near_parts = exchange(near_grad, tiles).reshape(tiles, width // tiles, width)
-    near_share = jnp.sum(near_parts.astype(f32), axis=0)
-    near_all = jnp.broadcast_to(near_share.astype(bf16), (tiles, *near_share.shape))
-    near_sum = exchange(near_all.reshape(width, width), tiles)
     returned = [
-        shifted(halo_grad[0:border_rows], "tx", 1),
-        shifted(halo_grad[border_rows : 2 * border_rows], "tx", -1),
-        shifted(halo_grad[2 * border_rows : 3 * border_rows], "ty", 1),
-        shifted(halo_grad[3 * border_rows :], "ty", -1),
+        shifted(halo_grad[0], "tx", 1),
+        shifted(halo_grad[1], "tx", -1),
+        shifted(halo_grad[2], "ty", 1),
+        shifted(halo_grad[3], "ty", -1),
     ]
+    totals = sum_over_mesh(keep, send, [out_rows], [near_grad], returned)
+    (near_share,) = call(
+        near_sum_kernel,
+        [shaped(width, width)],
+        [exchange(near_grad, tiles)],
+        after=returned,
+        flops=1e6,
+        share=width // tiles,
+    )
+    near_sum = exchange(near_share, tiles)
     (grad_points,) = call(
-        finish_kernel, [shaped(tile_rows, width)], [lists, row_grad, *returned], flops=1e9
+        finish_kernel,
+        [shaped(tile_rows, width)],
+        [lists, *returned, row_grad],
+        scratch=[pltpu.VMEM((tile_rows, width), f32), pltpu.SemaphoreType.DMA((1,))],
+        held=1,
+        flops=1e9,
     )
     scale = 1.0 / math.sqrt(tiles * tile_rows)
     up_sum, down_sum, conv_sum, gain_one_sum, gain_two_sum = call(
@@ -778,8 +882,9 @@
             shaped(1, width, dtype=f32),
             shaped(1, width, dtype=f32),
         ],
-        [totals],
-        scratch=[pltpu.VMEM((sums_rows, width), bf16)],
+        [bit_of("ty", 1), *totals],
+        scratch=[pltpu.VMEM((sums_rows, width), bf16)] * 2,
+        smem=1,
         flops=1e6,
         bits=len(steps_of("ty")),
         scale=scale,

time: 217 us -> 202 us (0.931)
  between operations: 15.1 us -> 1.69 us
  blocking collectives: 11.5 us -> 0 us
  starting transfers between devices: 44 us -> 53.2 us
  local copies, waits for them, and re-layouts: 6.76 us -> 1.12 us
  waiting for transfers between devices: 79.1 us -> 82.6 us
  Pallas kernels: 59 us -> 62.1 us
    all_to_all x1 -> x0, blocking collectives: 11.5 us -> none  [exchange(): lax.all_to_all(rows, ('tx', 'ty'), split_axis=0, concat_axis=0, tiled=True)]
    ppermute x5 -> x10, starting transfers between devices: 4.45 us -> 12.5 us  [partner(): lax.ppermute(value, axis, [(at, at ^ step) for at in range(lax.axis_size(...]
    ppermute x5 -> x10, waiting for transfers between devices: 26.6 us -> 18.7 us  [partner(): lax.ppermute(value, axis, [(at, at ^ step) for at in range(lax.axis_size(...]
    ppermute x8, waiting for transfers between devices: 1.65 us -> 7.45 us  [shifted(): lax.ppermute(value, axis, [(source, source + steps) for source in range(i...]
    all_to_all x4 -> x5, waiting for transfers between devices: 50.8 us -> 56.5 us  [exchange(): lax.all_to_all(rows, ('tx', 'ty'), split_axis=0, concat_axis=0, tiled=True)]
    unnamed x34 -> x30, local copies, waits for them, and re-layouts: 5.31 us -> 1.12 us
    pallas_call x15 -> x18, Pallas kernels: 59 us -> 62.1 us  [call(): pl.pallas_call(run, out_shape=tuple(shapes), in_specs=specs, out_specs=tu...]
    all_to_all x4 -> x5, starting transfers between devices: 20.1 us -> 22.3 us  [exchange(): lax.all_to_all(rows, ('tx', 'ty'), split_axis=0, concat_axis=0, tiled=True)]
  transfers between devices with their start and end apart: 18 -> 23, of which waited for: 7 -> 12; matrix products, arithmetic and copies ran while one was open for 1% -> 0% of each run, Pallas kernels for 18% -> 21%
where the time goes in v4:
time: 202 us; the launch traced here: 201 us
  waiting for transfers between devices  82.6 us (41%)
  Pallas kernels  62.1 us (31%)
  starting transfers between devices  53.2 us (26%)
    pallas_call x18, Pallas kernels, call(): pl.pallas_call(run, out_shape=tuple(shapes), in_specs=specs, out_specs=tu...  62.1 us
    all_to_all x5, waiting for transfers between devices, exchange(): lax.all_to_all(rows, ('tx', 'ty'), split_axis=0, concat_axis=0, tiled=True)  56.5 us
    all_to_all x5, starting transfers between devices, exchange(): lax.all_to_all(rows, ('tx', 'ty'), split_axis=0, concat_axis=0, tiled=True)  22.3 us
    ppermute x10, waiting for transfers between devices, partner(): lax.ppermute(value, axis, [(at, at ^ step) for at in range(lax.axis_size(...  18.7 us
    ppermute x8, starting transfers between devices, shifted(): lax.ppermute(value, axis, [(source, source + steps) for source in range(i...  18.4 us
    ppermute x10, starting transfers between devices, partner(): lax.ppermute(value, axis, [(at, at ^ step) for at in range(lax.axis_size(...  12.5 us
    ppermute x8, waiting for transfers between devices, shifted(): lax.ppermute(value, axis, [(source, source + steps) for source in range(i...  7.45 us
  transfers between devices with their start and end apart: 23, of which 12 were waited for; matrix products, arithmetic and copies ran while one was open for 0% of the time, Pallas kernels for 21%

profile of v4, /device:TPU:0, one launch (start us, length us, event | category | flops | bytes accessed | tf_op | source)
XLA Modules:
  0.0 201.4 jit_solution(1921227809304995834)
XLA Ops:
  4.5 5.6 %collective-permute-start.1 = (bf16[64,256]{1,0:T(8,128)(2,1)S(1)}, bf16[64,256]{1,0:T(8,128)(2,1)S(1)}, u32[]{:S(2)}, u32[]{:S(2)}) collective-permute-start(bf16[64,256]{1,0:T(8,128)(2,1)S(1)} %get-tuple-element.45), channel_id=1, source_target_pairs={{0,8},{8,16},{16,24},{1,9},{9,17},{17,25},{2,10},{10,18},{18,26},{... | collective-permute-start | bytes 98312 | tf_op jit(solution)/shard_map/ppermute | solution.py:581
  11.4 3.0 %collective-permute-start.3 = (bf16[64,256]{1,0:T(8,128)(2,1)S(1)}, bf16[64,256]{1,0:T(8,128)(2,1)S(1)}, u32[]{:S(2)}, u32[]{:S(2)}) collective-permute-start(bf16[64,256]{1,0:T(8,128)(2,1)S(1)} %get-tuple-element.47), channel_id=1, source_target_pairs={{0,1},{1,2},{2,3},{3,4},{4,5},{5,6},{6,7},{8,9},{9,10},{10,11},{11... | collective-permute-start | bytes 98312 | tf_op jit(solution)/shard_map/ppermute | solution.py:581
  14.4 5.8 %shard_map.189 = (bf16[1280,1024]{1,0:T(8,128)(2,1)}, bf16[1280,1024]{1,0:T(8,128)(2,1)S(1)}) custom-call(s32[16,1024]{1,0:T(8,128)S(1)} %bitcast.35), custom_call_target="tpu_custom_call" | custom-call | flops 8000000000 | bytes 5308416 | tf_op jit(solution)/shard_map/pallas_call | solution.py:562
  20.4 4.3 %shard_map.190 = (bf16[256,1024]{1,0:T(8,128)(2,1)}, f32[1024,256]{1,0:T(8,128)}, bf16[2048,512]{1,0:T(8,128)(2,1)}) custom-call(s32[1,1024]{1,0:T(1,128)S(1)} %get-tuple-element.43.refs_0_, bf16[1024,256]{1,0:T(8,128)(2,1)S(1)} %bitcast.31, bf16[1024,256]{1,0:T(8,128)(2,1)S(1)} %bitcast.32, bf16[64,256]{1,0:T(8,128)(2,1)S(1)} %collective-permute-done.refs_3_, ...), custom_call_target="tpu_custom_call" | custom-call | flops 4000000000 | bytes 7606272 | tf_op jit(solution)/shard_map/pallas_call | solution.py:562
  24.8 5.5 %all-to-all-start = ((bf16[32,64,512]{2,1,0:T(8,128)(2,1)}), bf16[32,64,512]{2,1,0:T(8,128)(2,1)}, u32[]{:S(2)}, u32[]{:S(2)}) async-start(bf16[32,64,512]{2,1,0:T(8,128)(2,1)} %bitcast.43), calls=%async_computation | async-start | bytes 4194304 | tf_op jit(solution)/shard_map/all_to_all | solution.py:644
  30.2 48.9 %all-to-all-done = bf16[32,64,512]{2,1,0:T(8,128)(2,1)} async-done(((bf16[32,64,512]{2,1,0:T(8,128)(2,1)}), bf16[32,64,512]{2,1,0:T(8,128)(2,1)}, u32[]{:S(2)}, u32[]{:S(2)}) %all-to-all-start) | async-done | bytes 2097184 | tf_op jit(solution)/shard_map/all_to_all | solution.py:644
  79.2 12.3 %shard_map.191 = (bf16[2048,256]{1,0:T(8,128)(2,1)}, f32[2048,256]{1,0:T(8,128)}, bf16[2048,256]{1,0:T(8,128)(2,1)}) custom-call(s32[1,2048]{1,0:T(1,128)S(1)} %copy-done.10, bf16[768,32]{1,0:T(8,128)(2,1)S(1)} %bitcast.33, f32[1,256]{1,0:T(1,128)S(1)} %bitcast.38, f32[1,256]{1,0:T(1,128)S(1)} %bitcast.40, bf16[256,1024]{1,0:T(8,128)(2,1)S(1)} %copy-done.5, ...), custom_call_target="tpu_custom_call" | custom-call | flops 10000000000 | bytes 7399424 | tf_op jit(solution)/shard_map/pallas_call | solution.py:562
  91.5 4.2 %all-to-all-start.1 = ((bf16[32,64,256]{2,1,0:T(8,128)(2,1)}), bf16[32,64,256]{2,1,0:T(8,128)(2,1)S(1)}, u32[]{:S(2)}, u32[]{:S(2)}) async-start(bf16[32,64,256]{2,1,0:T(8,128)(2,1)} %bitcast.44), calls=%async_computation.1 | async-start | bytes 2097152 | tf_op jit(solution)/shard_map/all_to_all | solution.py:644
  95.7 24.0 %shard_map.193 = (bf16[2048,256]{1,0:T(8,128)(2,1)}, bf16[1152,256]{1,0:T(8,128)(2,1)}, bf16[1152,256]{1,0:T(8,128)(2,1)}) custom-call(s32[1]{0:T(128)} %bitcast.12.refs_0_, s32[1,2048]{1,0:T(1,128)S(1)} %copy-done.10, bf16[768,32]{1,0:T(8,128)(2,1)S(1)} %bitcast.34, f32[1,256]{1,0:T(1,128)S(1)} %bitcast.39, f32[1,256]{1,0:T(1,128)S(1)} %bitcast.41, ...), custom_call_target="tpu_custom_call" | custom-call | flops 40000000000 | bytes 8579076 | tf_op jit(solution)/shard_map/pallas_call | solution.py:562
  121.7 3.7 %all-to-all-start.2 = ((bf16[32,64,256]{2,1,0:T(8,128)(2,1)}), bf16[32,64,256]{2,1,0:T(8,128)(2,1)S(1)}, u32[]{:S(2)}, u32[]{:S(2)}) async-start(bf16[32,64,256]{2,1,0:T(8,128)(2,1)} %bitcast.42), calls=%async_computation.2 | async-start | bytes 2097152 | tf_op jit(solution)/shard_map/all_to_all | solution.py:644
  125.7 2.1 %shard_map.192.refs_6_.refs_4_ = bf16[1024,256]{1,0:T(8,128)(2,1)} custom-call(s32[1,1024]{1,0:T(1,128)S(1)} %get-tuple-element.43.refs_0_, bf16[2048,256]{1,0:T(8,128)(2,1)S(1)} %bitcast.26), custom_call_target="tpu_custom_call" | custom-call | flops 4000000000 | bytes 1576960 | tf_op jit(solution)/shard_map/pallas_call | solution.py:562
  132.4 7.7 %collective-permute-done.9.refs_3_ = bf16[288,256]{1,0:T(8,128)(2,1)S(1)} collective-permute-done((bf16[288,256]{1,0:T(8,128)(2,1)S(1)}, bf16[288,256]{1,0:T(8,128)(2,1)S(1)}, u32[]{:S(2)}, u32[]{:S(2)}) %collective-permute-start.9) | collective-permute-done | bytes 147488 | tf_op jit(solution)/shard_map/ppermute | solution.py:585
  142.1 3.1 %collective-permute-done.11.refs_1_ = bf16[144,256]{1,0:T(8,128)(2,1)S(1)} collective-permute-done((bf16[144,256]{1,0:T(8,128)(2,1)S(1)}, bf16[144,256]{1,0:T(8,128)(2,1)S(1)}, u32[]{:S(2)}, u32[]{:S(2)}) %collective-permute-start.11) | collective-permute-done | bytes 73760 | tf_op jit(solution)/shard_map/ppermute | solution.py:585
  147.3 5.5 %collective-permute-done.13.refs_1_ = bf16[288,256]{1,0:T(8,128)(2,1)S(1)} collective-permute-done((bf16[288,256]{1,0:T(8,128)(2,1)S(1)}, bf16[288,256]{1,0:T(8,128)(2,1)S(1)}, u32[]{:S(2)}, u32[]{:S(2)}) %collective-permute-start.13) | collective-permute-done | bytes 147488 | tf_op jit(solution)/shard_map/ppermute | solution.py:585
  153.7 5.7 %shard_map.195 = (f32[1024,256]{1,0:T(8,128)}, bf16[256,256]{1,0:T(8,128)(2,1)}, bf16[64,256]{1,0:T(8,128)(2,1)S(1)}, bf16[64,256]{1,0:T(8,128)(2,1)S(1)}, bf16[...) custom-call(s32[1,1024]{1,0:T(1,128)S(1)} %get-tuple-element.43.refs_0_, bf16[2048,256]{1,0:T(8,128)(2,1)S(1)} %bitcast.27, ...), custom_call_target="tpu_custom_call" | custom-call | flops 6000000000 | bytes 6688768 | tf_op jit(solution)/shard_map/pallas_call | solution.py:562
  162.7 2.5 %collective-permute-start.4 = (bf16[64,256]{1,0:T(8,128)(2,1)S(1)}, bf16[64,256]{1,0:T(8,128)(2,1)S(1)}, u32[]{:S(2)}, u32[]{:S(2)}) collective-permute-start(bf16[64,256]{1,0:T(8,128)(2,1)S(1)} %get-tuple-element.57), channel_id=1, source_target_pairs={{0,8},{8,16},{16,24},{1,9},{9,17},{17,25},{2,10},{10,18},{18,26},{... | collective-permute-start | bytes 98312 | tf_op jit(solution)/shard_map/ppermute | solution.py:581
  166.7 4.2 %collective-permute-done.5.refs_2_.refs_4_ = bf16[64,256]{1,0:T(8,128)(2,1)S(1)} collective-permute-done((bf16[64,256]{1,0:T(8,128)(2,1)S(1)}, bf16[64,256]{1,0:T(8,128)(2,1)S(1)}, u32[]{:S(2)}, u32[]{:S(2)}) %collective-permute-start.5) | collective-permute-done | bytes 32800 | tf_op jit(solution)/shard_map/ppermute | solution.py:581
  171.7 3.5 %all-to-all-start.3 = ((bf16[32,8,256]{2,1,0:T(8,128)(2,1)}), bf16[32,8,256]{2,1,0:T(8,128)(2,1)S(1)}, u32[]{:S(2)}, u32[]{:S(2)}) async-start(bf16[32,8,256]{2,1,0:T(8,128)(2,1)} %bitcast.16), calls=%async_computation.3 | async-start | bytes 262144 | tf_op jit(solution)/shard_map/all_to_all | solution.py:644
  175.2 2.2 %collective-permute-start.6 = (bf16[64,256]{1,0:T(8,128)(2,1)S(1)}, bf16[64,256]{1,0:T(8,128)(2,1)S(1)}, u32[]{:S(2)}, u32[]{:S(2)}) collective-permute-start(bf16[64,256]{1,0:T(8,128)(2,1)S(1)} %get-tuple-element.59), channel_id=1, source_target_pairs={{0,1},{1,2},{2,3},{3,4},{4,5},{5,6},{6,7},{8,9},{9,10},{10,11},{11... | collective-permute-start | bytes 98312 | tf_op jit(solution)/shard_map/ppermute | solution.py:581
  178.7 2.9 %collective-permute-done.7.refs_4_ = bf16[64,256]{1,0:T(8,128)(2,1)S(1)} collective-permute-done((bf16[64,256]{1,0:T(8,128)(2,1)S(1)}, bf16[64,256]{1,0:T(8,128)(2,1)S(1)}, u32[]{:S(2)}, u32[]{:S(2)}) %collective-permute-start.7) | collective-permute-done | bytes 32800 | tf_op jit(solution)/shard_map/ppermute | solution.py:581
  181.6 2.7 %collective-permute-start.17 = (bf16[1152,256]{1,0:T(8,128)(2,1)S(1)}, bf16[1152,256]{1,0:T(8,128)(2,1)S(1)}, u32[]{:S(2)}, u32[]{:S(2)}) collective-permute-start(bf16[1152,256]{1,0:T(8,128)(2,1)S(1)} %shard_map.204.refs_1_), channel_id=1, source_target_pairs={{0,1},{1,0},{2,3},{3,2},{4,5},{5,4},{6,7},{7,6},{8,9},{9,8},{10,11... | collective-permute-start | bytes 1769480 | tf_op jit(solution)/shard_map/ppermute | solution.py:585
  185.2 5.5 %all-to-all-start.4 = ((bf16[32,8,256]{2,1,0:T(8,128)(2,1)}), bf16[32,8,256]{2,1,0:T(8,128)(2,1)S(1)}, u32[]{:S(2)}, u32[]{:S(2)}) async-start(bf16[32,8,256]{2,1,0:T(8,128)(2,1)} %bitcast.18), calls=%async_computation.4 | async-start | bytes 262144 | tf_op jit(solution)/shard_map/all_to_all | solution.py:644
  190.7 2.6 %shard_map.196 = bf16[1024,256]{1,0:T(8,128)(2,1)} custom-call(s32[4,64]{1,0:T(4,128)S(1)} %bitcast.37, bf16[64,256]{1,0:T(8,128)(2,1)S(1)} %collective-permute-done.4.refs_1_.refs_3_, bf16[64,256]{1,0:T(8,128)(2,1)S(1)} %collective-permute-done.5.refs_2_.refs_4_, bf16[64,256]{1,0:T(8,128)(2,1)S(1)} %collective-permute-done.6.refs_3_, ...), custom_call_target="tpu_custom_call" | custom-call | flops 1000000000 | bytes 1704960 | tf_op jit(solution)/shard_map/pallas_call | solution.py:562
  193.3 5.6 %all-to-all-done.4 = bf16[32,8,256]{2,1,0:T(8,128)(2,1)S(1)} async-done(((bf16[32,8,256]{2,1,0:T(8,128)(2,1)}), bf16[32,8,256]{2,1,0:T(8,128)(2,1)S(1)}, u32[]{:S(2)}, u32[]{:S(2)}) %all-to-all-start.4) | async-done | bytes 131104 | tf_op jit(solution)/shard_map/all_to_all | solution.py:644
  (71 shorter events, 26.6 us)
Async XLA Ops:
  3.2 17.1 %collective-permute-start = (bf16[64,256]{1,0:T(8,128)(2,1)S(1)}, bf16[64,256]{1,0:T(8,128)(2,1)S(1)}, u32[]{:S(2)}, u32[]{:S(2)}) collective-permute-start(bf16[64,256]{1,0:T(8,128)(2,1)S(1)} %get-tuple-element.44), channel_id=1, source_target_pairs={{8,0},{16,8},{24,16},{9,1},{17,9},{25,17},{10,2},{18,10},{26,18},{... | collective-permute-start | bytes 98312 | tf_op jit(solution)/shard_map/ppermute | solution.py:581
  4.5 15.8 %collective-permute-start.1 = (bf16[64,256]{1,0:T(8,128)(2,1)S(1)}, bf16[64,256]{1,0:T(8,128)(2,1)S(1)}, u32[]{:S(2)}, u32[]{:S(2)}) collective-permute-start(bf16[64,256]{1,0:T(8,128)(2,1)S(1)} %get-tuple-element.45), channel_id=1, source_target_pairs={{0,8},{8,16},{16,24},{1,9},{9,17},{17,25},{2,10},{10,18},{18,26},{... | collective-permute-start | bytes 98312 | tf_op jit(solution)/shard_map/ppermute | solution.py:581
  10.1 10.2 %collective-permute-start.2 = (bf16[64,256]{1,0:T(8,128)(2,1)S(1)}, bf16[64,256]{1,0:T(8,128)(2,1)S(1)}, u32[]{:S(2)}, u32[]{:S(2)}) collective-permute-start(bf16[64,256]{1,0:T(8,128)(2,1)S(1)} %get-tuple-element.46), channel_id=1, source_target_pairs={{1,0},{2,1},{3,2},{4,3},{5,4},{6,5},{7,6},{9,8},{10,9},{11,10},{12... | collective-permute-start | bytes 98312 | tf_op jit(solution)/shard_map/ppermute | solution.py:581
  11.4 9.0 %collective-permute-start.3 = (bf16[64,256]{1,0:T(8,128)(2,1)S(1)}, bf16[64,256]{1,0:T(8,128)(2,1)S(1)}, u32[]{:S(2)}, u32[]{:S(2)}) collective-permute-start(bf16[64,256]{1,0:T(8,128)(2,1)S(1)} %get-tuple-element.47), channel_id=1, source_target_pairs={{0,1},{1,2},{2,3},{3,4},{4,5},{5,6},{6,7},{8,9},{9,10},{10,11},{11... | collective-permute-start | bytes 98312 | tf_op jit(solution)/shard_map/ppermute | solution.py:581
  24.7 54.4 %copy-start.5 = (bf16[256,1024]{1,0:T(8,128)(2,1)S(1)}, bf16[256,1024]{1,0:T(8,128)(2,1)}, u32[]{:S(2)}) copy-start(bf16[256,1024]{1,0:T(8,128)(2,1)} %refs_5_.3) | copy-start | bytes 1572868
  24.8 54.3 %all-to-all-start = ((bf16[32,64,512]{2,1,0:T(8,128)(2,1)}), bf16[32,64,512]{2,1,0:T(8,128)(2,1)}, u32[]{:S(2)}, u32[]{:S(2)}) async-start(bf16[32,64,512]{2,1,0:T(8,128)(2,1)} %bitcast.43), calls=%async_computation | async-start | bytes 4194304 | tf_op jit(solution)/shard_map/all_to_all | solution.py:644
  91.5 30.3 %all-to-all-start.1 = ((bf16[32,64,256]{2,1,0:T(8,128)(2,1)}), bf16[32,64,256]{2,1,0:T(8,128)(2,1)S(1)}, u32[]{:S(2)}, u32[]{:S(2)}) async-start(bf16[32,64,256]{2,1,0:T(8,128)(2,1)} %bitcast.44), calls=%async_computation.1 | async-start | bytes 2097152 | tf_op jit(solution)/shard_map/all_to_all | solution.py:644
  121.7 32.0 %all-to-all-start.2 = ((bf16[32,64,256]{2,1,0:T(8,128)(2,1)}), bf16[32,64,256]{2,1,0:T(8,128)(2,1)S(1)}, u32[]{:S(2)}, u32[]{:S(2)}) async-start(bf16[32,64,256]{2,1,0:T(8,128)(2,1)} %bitcast.42), calls=%async_computation.2 | async-start | bytes 2097152 | tf_op jit(solution)/shard_map/all_to_all | solution.py:644
  125.4 2.4 %collective-permute-start.8 = (bf16[1152,256]{1,0:T(8,128)(2,1)S(1)}, bf16[1152,256]{1,0:T(8,128)(2,1)S(1)}, u32[]{:S(2)}, u32[]{:S(2)}) collective-permute-start(bf16[1152,256]{1,0:T(8,128)(2,1)S(1)} %copy-done.14), channel_id=1, source_target_pairs={{0,1},{1,0},{2,3},{3,2},{4,5},{5,4},{6,7},{7,6},{8,9},{9,8},{10,11... | collective-permute-start | bytes 1769480 | tf_op jit(solution)/shard_map/ppermute | solution.py:585
  129.2 10.9 %collective-permute-start.9 = (bf16[288,256]{1,0:T(8,128)(2,1)S(1)}, bf16[288,256]{1,0:T(8,128)(2,1)S(1)}, u32[]{:S(2)}, u32[]{:S(2)}) collective-permute-start(bf16[288,256]{1,0:T(8,128)(2,1)S(1)} %get-tuple-element.66), channel_id=1, source_target_pairs={{0,2},{1,3},{2,0},{3,1},{4,6},{5,7},{6,4},{7,5},{8,10},{9,11},{10,... | collective-permute-start | bytes 442376 | tf_op jit(solution)/shard_map/ppermute | solution.py:585
  131.0 9.6 %collective-permute-start.10 = (bf16[288,256]{1,0:T(8,128)(2,1)S(1)}, bf16[288,256]{1,0:T(8,128)(2,1)S(1)}, u32[]{:S(2)}, u32[]{:S(2)}) collective-permute-start(bf16[288,256]{1,0:T(8,128)(2,1)S(1)} %get-tuple-element.68), channel_id=1, source_target_pairs={{0,4},{1,5},{2,6},{3,7},{4,0},{5,1},{6,2},{7,3},{8,12},{9,13},{10,... | collective-permute-start | bytes 442376 | tf_op jit(solution)/shard_map/ppermute | solution.py:585
  140.6 4.5 %collective-permute-start.11 = (bf16[144,256]{1,0:T(8,128)(2,1)S(1)}, bf16[144,256]{1,0:T(8,128)(2,1)S(1)}, u32[]{:S(2)}, u32[]{:S(2)}) collective-permute-start(bf16[144,256]{1,0:T(8,128)(2,1)S(1)} %get-tuple-element.70), channel_id=1, source_target_pairs={{0,4},{1,5},{2,6},{3,7},{4,0},{5,1},{6,2},{7,3},{8,12},{9,13},{10,... | collective-permute-start | bytes 221192 | tf_op jit(solution)/shard_map/ppermute | solution.py:585
  141.4 4.4 %collective-permute-start.12 = (bf16[144,256]{1,0:T(8,128)(2,1)S(1)}, bf16[144,256]{1,0:T(8,128)(2,1)S(1)}, u32[]{:S(2)}, u32[]{:S(2)}) collective-permute-start(bf16[144,256]{1,0:T(8,128)(2,1)S(1)} %get-tuple-element.72), channel_id=1, source_target_pairs={{0,2},{1,3},{2,0},{3,1},{4,6},{5,7},{6,4},{7,5},{8,10},{9,11},{10,... | collective-permute-start | bytes 221192 | tf_op jit(solution)/shard_map/ppermute | solution.py:585
  145.8 7.1 %collective-permute-start.13 = (bf16[288,256]{1,0:T(8,128)(2,1)S(1)}, bf16[288,256]{1,0:T(8,128)(2,1)S(1)}, u32[]{:S(2)}, u32[]{:S(2)}) collective-permute-start(bf16[288,256]{1,0:T(8,128)(2,1)S(1)} %shard_map.200.refs_0_), channel_id=1, source_target_pairs={{0,8},{8,0},{16,24},{24,16},{1,9},{9,1},{17,25},{25,17},{2,10},{10... | collective-permute-start | bytes 442376 | tf_op jit(solution)/shard_map/ppermute | solution.py:585
  152.9 7.9 %collective-permute-start.14 = (bf16[288,256]{1,0:T(8,128)(2,1)S(1)}, bf16[288,256]{1,0:T(8,128)(2,1)S(1)}, u32[]{:S(2)}, u32[]{:S(2)}) collective-permute-start(bf16[288,256]{1,0:T(8,128)(2,1)S(1)} %shard_map.201.refs_0_), channel_id=1, source_target_pairs={{0,16},{8,24},{16,0},{24,8},{1,17},{9,25},{17,1},{25,9},{2,18},{10... | collective-permute-start | bytes 442376 | tf_op jit(solution)/shard_map/ppermute | solution.py:585
  160.9 10.1 %collective-permute-start.15 = (bf16[288,256]{1,0:T(8,128)(2,1)S(1)}, bf16[288,256]{1,0:T(8,128)(2,1)S(1)}, u32[]{:S(2)}, u32[]{:S(2)}) collective-permute-start(bf16[288,256]{1,0:T(8,128)(2,1)S(1)} %shard_map.202.refs_1_), channel_id=1, source_target_pairs={{0,4},{1,5},{2,6},{3,7},{4,0},{5,1},{6,2},{7,3},{8,12},{9,13},{10,... | collective-permute-start | bytes 442376 | tf_op jit(solution)/shard_map/ppermute | solution.py:585
  162.7 4.1 %collective-permute-start.4 = (bf16[64,256]{1,0:T(8,128)(2,1)S(1)}, bf16[64,256]{1,0:T(8,128)(2,1)S(1)}, u32[]{:S(2)}, u32[]{:S(2)}) collective-permute-start(bf16[64,256]{1,0:T(8,128)(2,1)S(1)} %get-tuple-element.57), channel_id=1, source_target_pairs={{0,8},{8,16},{16,24},{1,9},{9,17},{17,25},{2,10},{10,18},{18,26},{... | collective-permute-start | bytes 98312 | tf_op jit(solution)/shard_map/ppermute | solution.py:581
  165.2 5.8 %collective-permute-start.5 = (bf16[64,256]{1,0:T(8,128)(2,1)S(1)}, bf16[64,256]{1,0:T(8,128)(2,1)S(1)}, u32[]{:S(2)}, u32[]{:S(2)}) collective-permute-start(bf16[64,256]{1,0:T(8,128)(2,1)S(1)} %get-tuple-element.58), channel_id=1, source_target_pairs={{8,0},{16,8},{24,16},{9,1},{17,9},{25,17},{10,2},{18,10},{26,18},{... | collective-permute-start | bytes 98312 | tf_op jit(solution)/shard_map/ppermute | solution.py:581
  171.0 10.6 %collective-permute-start.16 = (bf16[576,256]{1,0:T(8,128)(2,1)S(1)}, bf16[576,256]{1,0:T(8,128)(2,1)S(1)}, u32[]{:S(2)}, u32[]{:S(2)}) collective-permute-start(bf16[576,256]{1,0:T(8,128)(2,1)S(1)} %shard_map.203.refs_1_), channel_id=1, source_target_pairs={{0,2},{1,3},{2,0},{3,1},{4,6},{5,7},{6,4},{7,5},{8,10},{9,11},{10,... | collective-permute-start | bytes 884744 | tf_op jit(solution)/shard_map/ppermute | solution.py:585
  171.7 12.6 %all-to-all-start.3 = ((bf16[32,8,256]{2,1,0:T(8,128)(2,1)}), bf16[32,8,256]{2,1,0:T(8,128)(2,1)S(1)}, u32[]{:S(2)}, u32[]{:S(2)}) async-start(bf16[32,8,256]{2,1,0:T(8,128)(2,1)} %bitcast.16), calls=%async_computation.3 | async-start | bytes 262144 | tf_op jit(solution)/shard_map/all_to_all | solution.py:644
  175.2 3.5 %collective-permute-start.6 = (bf16[64,256]{1,0:T(8,128)(2,1)S(1)}, bf16[64,256]{1,0:T(8,128)(2,1)S(1)}, u32[]{:S(2)}, u32[]{:S(2)}) collective-permute-start(bf16[64,256]{1,0:T(8,128)(2,1)S(1)} %get-tuple-element.59), channel_id=1, source_target_pairs={{0,1},{1,2},{2,3},{3,4},{4,5},{5,6},{6,7},{8,9},{9,10},{10,11},{11... | collective-permute-start | bytes 98312 | tf_op jit(solution)/shard_map/ppermute | solution.py:581
  177.4 4.2 %collective-permute-start.7 = (bf16[64,256]{1,0:T(8,128)(2,1)S(1)}, bf16[64,256]{1,0:T(8,128)(2,1)S(1)}, u32[]{:S(2)}, u32[]{:S(2)}) collective-permute-start(bf16[64,256]{1,0:T(8,128)(2,1)S(1)} %get-tuple-element.60), channel_id=1, source_target_pairs={{1,0},{2,1},{3,2},{4,3},{5,4},{6,5},{7,6},{9,8},{10,9},{11,10},{12... | collective-permute-start | bytes 98312 | tf_op jit(solution)/shard_map/ppermute | solution.py:581
  181.6 18.0 %collective-permute-start.17 = (bf16[1152,256]{1,0:T(8,128)(2,1)S(1)}, bf16[1152,256]{1,0:T(8,128)(2,1)S(1)}, u32[]{:S(2)}, u32[]{:S(2)}) collective-permute-start(bf16[1152,256]{1,0:T(8,128)(2,1)S(1)} %shard_map.204.refs_1_), channel_id=1, source_target_pairs={{0,1},{1,0},{2,3},{3,2},{4,5},{5,4},{6,7},{7,6},{8,9},{9,8},{10,11... | collective-permute-start | bytes 1769480 | tf_op jit(solution)/shard_map/ppermute | solution.py:585
  185.2 13.7 %all-to-all-start.4 = ((bf16[32,8,256]{2,1,0:T(8,128)(2,1)}), bf16[32,8,256]{2,1,0:T(8,128)(2,1)S(1)}, u32[]{:S(2)}, u32[]{:S(2)}) async-start(bf16[32,8,256]{2,1,0:T(8,128)(2,1)} %bitcast.18), calls=%async_computation.4 | async-start | bytes 262144 | tf_op jit(solution)/shard_map/all_to_all | solution.py:644
  (14 other events, 365.8 us)

commit v5 on v4

--- a/solution.py
+++ b/solution.py
@@ -62,16 +62,45 @@
     return jnp.transpose(jnp.broadcast_to(row, (LANES, count)))
 
 
+def parts_of(value):
+    high = lax.shift_right_arithmetic(value, 8)
+    return high.astype(f32), (value - high * 256).astype(f32)
+
+
 def pick_rows(column, depth):
     count = column.shape[0]
-    lane = iota((count, LANES), 1)
+    zero = jnp.zeros((count, LANES), bf16)
+    one = jnp.ones((count, LANES), bf16)
+    high, low = (part.astype(bf16) for part in parts_of(column))
+    lane = iota((count, LANES), 1).astype(f32)
+    halves = [jnp.where(low == (lane + float(at)).astype(bf16), one, zero) for at in (0, LANES)]
+    pieces = []
+    for block in range(depth // 256):
+        here = high == jnp.full((count, LANES), block, bf16)
+        pieces += [jnp.where(here, half, zero) for half in halves]
+    return jnp.concatenate(pieces, axis=1)
+
+
+def mark_low(row):
+    count = row.shape[1]
+    high, low = parts_of(row)
+    high = jnp.broadcast_to(high, (16, count)).astype(bf16)
+    low = jnp.broadcast_to(low, (16, count)).astype(bf16)
+    zero = jnp.zeros((16, count), bf16)
+    one = jnp.ones((16, count), bf16)
+    index = iota((16, count), 0).astype(f32)
+    return high, jnp.concatenate(
+        [jnp.where(low == (index + float(at)).astype(bf16), one, zero) for at in range(0, 256, 16)], axis=0
+    )
+
+
+def mark_block(high, low_ref, block):
+    count = low_ref.shape[1]
+    zero = jnp.zeros((16, count), bf16)
+    here = high == jnp.full((16, count), block, bf16)
     return jnp.concatenate(
-        [marks(column == lane + base) for base in range(0, depth, LANES)], axis=1
-    )
-
-
-def mark_slots(row, start, count):
-    return marks(iota((count, row.shape[1]), 0) + start == row)
+        [jnp.where(here, low_ref[pl.ds(at, 16), :], zero) for at in range(0, 256, 16)], axis=0
+    )
 
 
 def route_kernel(
@@ -105,12 +134,13 @@
     return marks(iota((rows, listed.shape[1]), 0) == listed)
 
 
-def pack_rows(slots_ref, rows_ref, packed_out, stage_ref, sems):
-    slots = slots_ref[...]
+def pack_rows(slots_ref, rows_ref, packed_out, stage_ref, low_ref, sems):
+    high, low_ref[...] = mark_low(slots_ref[...])
     copies = []
     for at, start in enumerate(range(0, packed_out.shape[0], WIDE)):
+        marked = [mark_block(high, low_ref, block) for block in range(start // 256, (start + WIDE) // 256)]
         place = pl.ds(start, WIDE)
-        stage_ref[place, :] = dot(mark_slots(slots, start, WIDE), rows_ref[...]).astype(bf16)
+        stage_ref[place, :] = dot(jnp.concatenate(marked, axis=0), rows_ref[...]).astype(bf16)
         copies.append(pltpu.make_async_copy(stage_ref.at[place], packed_out.at[place], sems.at[at]))
         copies[-1].start()
     for copy in copies:
@@ -167,7 +197,7 @@
 def lift_kernel(
     slots_ref, points_ref, grad_ref, halo0, halo1, halo2, halo3, table_ref, w_ref,
     average_out, pre_out, packed_out,
-    average_ref, pre_ref, both_ref, stage_ref, sems, pack_sems, *, neighbours
+    average_ref, pre_ref, both_ref, stage_ref, low_ref, sems, pack_sems, *, neighbours
 ):
     width = points_ref.shape[1]
     ext = jnp.concatenate([points_ref[...], halo0[...], halo1[...], halo2[...], halo3[...]], axis=0)
@@ -184,7 +214,7 @@
             points_ref[here, :].astype(f32) + gelu_tanh(pre_ref[here, :])
         ).astype(bf16)
     both_ref[:, width:] = grad_ref[...]
-    pack_rows(slots_ref, both_ref, packed_out, stage_ref, pack_sems)
+    pack_rows(slots_ref, both_ref, packed_out, stage_ref, low_ref, pack_sems)
     keep_average.wait()
     keep_pre.wait()
 
@@ -245,12 +275,6 @@
     out_ref[...] = (row_ref[...] + total).astype(bf16)
 
 
-def near_sum_kernel(parts_ref, share_ref, *, share):
-    rows = parts_ref.shape[0]
-    same = lax.rem(iota((rows, rows), 0), share) == lax.rem(iota((rows, rows), 1), share)
-    share_ref[...] = dot(marks(same), parts_ref[...]).astype(bf16)
-
-
 def full_taps(conv_ref, groups, inner):
     width = groups * inner
     rows = conv_ref.shape[0]
@@ -271,7 +295,7 @@
     zorder_ref, conv_ref, gain_one_ref, gain_two_ref, up_ref, down_ref, came_in,
     serial_out, state_out, back_out,
     lifted_ref, serial_ref, state_ref, taps_ref, normed_ref, before_ref, here_ref, after_ref, second_ref, hidden_ref,
-    result_ref, stage_ref, sems, pack_sems, *, groups, inner
+    result_ref, stage_ref, low_ref, sems, pack_sems, *, groups, inner
 ):
     slots, width = lifted_ref.shape
     fetch = pltpu.make_async_copy(came_in.at[:, pl.ds(0, width)], lifted_ref, sems.at[2, 0])
@@ -329,7 +353,7 @@
 
     fetch.wait()
     lax.fori_loop(0, slots // PATCH, patch, 0)
-    pack_rows(zorder_ref, result_ref, back_out, stage_ref, pack_sems)
+    pack_rows(zorder_ref, result_ref, back_out, stage_ref, low_ref, pack_sems)
     for at in range(slots // PATCH):
         for copy in keep(at):
             copy.wait()
@@ -340,7 +364,7 @@
     back_out, keep_out, send_out,
     grad_ref, serial_ref, state_ref, out_grad_ref, serial_grad_ref, stage_ref, weights_ref, taps_ref,
     second_ref, hidden_ref, pre_grad_ref, state_grad_ref, mixed_ref, mixed_half_ref, before_ref, here_ref,
-    after_ref, normed_ref, conv_sum_ref, gains_ref, sems, pack_sems, *, groups, inner
+    after_ref, normed_ref, conv_sum_ref, gains_ref, low_ref, sems, pack_sems, *, groups, inner
 ):
     slots, width = serial_ref.shape
     hidden_width = up_ref.shape[1]
@@ -456,7 +480,7 @@
     ]
     for copy in hand_out:
         copy.start()
-    pack_rows(zorder_ref, serial_grad_ref, back_out, stage_ref, pack_sems)
+    pack_rows(zorder_ref, serial_grad_ref, back_out, stage_ref, low_ref, pack_sems)
     for copy in hand_out:
         copy.wait()
 
@@ -492,10 +516,18 @@
     split_rows(bit1_ref[0], added(mine1, came1), scratch1, keep1, send1)
 
 
-def add_join_kernel(mine0, came0, mine1, came1, share_ref):
+def add_join_kernel(mine0, came0, mine1, came1, near_ref, share_ref):
     half = mine0.shape[0]
     share_ref[0:half, :] = added(mine0, came0).astype(bf16)
-    share_ref[half:, :] = added(mine1, came1).astype(bf16)
+    share_ref[half : 2 * half, :] = added(mine1, came1).astype(bf16)
+    lines, rows, width = near_ref.shape
+    total = near_ref[0].astype(f32)
+    for line in range(1, lines):
+        total = total + near_ref[line].astype(f32)
+    spare = share_ref.shape[0] - 2 * half - rows
+    if spare:
+        total = jnp.concatenate([total, jnp.zeros((spare, width), f32)], axis=0)
+    share_ref[2 * half :, :] = total.astype(bf16)
 
 
 def add_kernel(mine_ref, came_ref, total_ref):
@@ -510,12 +542,14 @@
 
 
 def spread_kernel(
-    bit_ref, mine_ref, came_ref, up_ref, down_ref, conv_ref, gain_one_ref, gain_two_ref,
+    bit_ref, mine_ref, came_ref, up_ref, down_ref, conv_ref, gain_one_ref, gain_two_ref, near_ref,
     joined_ref, sums_ref, *, bits, scale
 ):
     join_kernel(bit_ref, mine_ref, came_ref, joined_ref)
     rows = sums_ref.shape[0]
     piece = (rows >> bits) // 2
+    share = joined_ref.shape[0] >> bits
+    near_rows = near_ref.shape[0] >> bits
     for at in range(1 << bits):
         digits = [(at >> (bits - 1 - bit)) & 1 for bit in range(bits)]
         for part, order in enumerate((digits[1:], digits[:0:-1])):
@@ -523,8 +557,12 @@
             for digit in order:
                 place = 2 * place + digit
             start = digits[0] * (rows // 2) + part * (rows // 4) + place * piece
-            source = (2 * at + part) * piece
+            source = at * share + part * piece
             sums_ref[start : start + piece, :] = joined_ref[source : source + piece, :]
+        line = sum(digit << bit for bit, digit in enumerate(digits))
+        source = at * share + 2 * piece
+        part = joined_ref[source : source + share - 2 * piece, :].astype(f32) * scale
+        near_ref[line * near_rows : (line + 1) * near_rows, :] = part[:near_rows]
     width, hidden_width = up_ref.shape
     taps, groups, inner = conv_ref.shape[:3]
     down_ref[...] = sums_ref[0:hidden_width, :].astype(f32) * scale
@@ -548,7 +586,8 @@
     specs = [pl.BlockSpec(memory_space=pltpu.SMEM)] * smem
     specs += [pl.BlockSpec(memory_space=pltpu.VMEM)] * (len(args) - smem - held)
     specs += [pl.BlockSpec(memory_space=pltpu.HBM)] * held
-    specs += [pl.BlockSpec(memory_space=pl.ANY)] * len(after)
+    specs += [pl.BlockSpec(memory_space=pltpu.HBM if a.shape[0] >= PATCH else pl.ANY) for a in after]
+    after = [pltpu.with_memory_space_constraint(a, pltpu.HBM) if a.shape[0] >= PATCH else a for a in after]
     out_specs = [pl.BlockSpec(memory_space=pltpu.HBM)] * stored
     shapes = [pltpu.HBM(a.shape, a.dtype) for a in outs[:stored]] + list(outs[stored:])
     first_held = len(args) - held
@@ -593,7 +632,7 @@
     return [1 << at for at in range(int(math.log2(lax.axis_size(axis))))]
 
 
-def sum_over_mesh(keep, send, early, late, returned):
+def scatter_sums(keep, send, early):
     width = keep.shape[1]
     steps = steps_of("ty")
     orders = steps[1:], steps[:0:-1]
@@ -619,21 +658,33 @@
             pairs += [parts[2 * which], partner(parts[2 * which + 1], "ty", order[at])]
         if at + 1 < len(orders[0]):
             parts = halves(next_split_kernel, rows, at + 1, pairs)
-    (share,) = call(add_join_kernel, [shaped(2 * rows, width)], pairs, flops=1e6)
-    for step in steps_of("tx"):
+    return pairs
+
+
+def gather_sums(pairs, near_parts, late):
+    rows, width = pairs[0].shape
+    steps = steps_of("ty")
+    near_rows = -(-near_parts.shape[1] // 16) * 16
+    (share,) = call(
+        add_join_kernel,
+        [shaped(2 * rows + near_rows, width)],
+        [*pairs, near_parts],
+        after=late[0],
+        flops=1e6,
+    )
+    for at, step in enumerate(steps_of("tx")):
         (share,) = call(
             add_kernel,
             [shaped(*share.shape)],
             [share, partner(share, "tx", step)],
-            after=late if step == steps_of("tx")[-1] else (),
+            after=late[1 + at],
             flops=1e6,
         )
-    for at, step in enumerate(steps[:0:-1]):
+    for step in steps[:0:-1]:
         (share,) = call(
             join_kernel,
             [shaped(2 * share.shape[0], width)],
             [bit_of("ty", step), share, partner(share, "ty", step)],
-            after=returned[2 * at : 2 * at + 2],
             smem=1,
             flops=1e6,
         )
@@ -719,6 +770,7 @@
             pltpu.VMEM((tile_rows, width), f32),
             pltpu.VMEM((tile_rows, 2 * width), bf16),
             pltpu.VMEM((slots_count, 2 * width), bf16),
+            pltpu.VMEM((256, tile_rows), bf16),
             pltpu.SemaphoreType.DMA((2,)),
             pltpu.SemaphoreType.DMA((slots_count // WIDE,)),
         ],
@@ -752,6 +804,7 @@
             pltpu.VMEM((PATCH, hidden), bf16),
             pltpu.VMEM((slots_count, width), bf16),
             pltpu.VMEM((slots_count, width), bf16),
+            pltpu.VMEM((256, slots_count), bf16),
             pltpu.SemaphoreType.DMA((3, slots_count // PATCH)),
             pltpu.SemaphoreType.DMA((slots_count // WIDE,)),
         ],
@@ -804,6 +857,7 @@
             pltpu.VMEM((PATCH, width), bf16),
             pltpu.VMEM((taps, width, width), f32),
             pltpu.VMEM((16, width), f32),
+            pltpu.VMEM((256, slots_count), bf16),
             pltpu.SemaphoreType.DMA((5,)),
             pltpu.SemaphoreType.DMA((slots_count // WIDE,)),
         ],
@@ -818,7 +872,7 @@
         hold_kernel,
         [shaped(slots_count, width)],
         [back_grad],
-        after=[came_result],
+        after=[came_result.reshape(tiles, capacity, width)],
         held=1,
         stored=1,
         same={0: 0},
@@ -827,12 +881,13 @@
     (out_rows,) = call(
         unpack_kernel, [shaped(tile_rows, width)], [slots, came_result], flops=4e9
     )
+    pairs = scatter_sums(keep, send, [out_rows])
     row_grad, near_grad, *halo_grad = call(
         tile_back_kernel,
         [shaped(tile_rows, width, dtype=f32), shaped(width, width)]
         + [shaped(border_rows, width)] * 4,
         [slots, came_back, w_near, kept_table, average, pre_act],
-        after=[out_rows],
+        after=pairs[1::2],
         scratch=[
             pltpu.VMEM((tile_rows, width), f32),
             pltpu.VMEM((ext, tile_rows), bf16),
@@ -854,16 +909,6 @@
         shifted(halo_grad[2], "ty", 1),
         shifted(halo_grad[3], "ty", -1),
     ]
-    totals = sum_over_mesh(keep, send, [out_rows], [near_grad], returned)
-    (near_share,) = call(
-        near_sum_kernel,
-        [shaped(width, width)],
-        [exchange(near_grad, tiles)],
-        after=returned,
-        flops=1e6,
-        share=width // tiles,
-    )
-    near_sum = exchange(near_share, tiles)
     (grad_points,) = call(
         finish_kernel,
         [shaped(tile_rows, width)],
@@ -872,8 +917,12 @@
         held=1,
         flops=1e9,
     )
+    near_parts = lax.all_to_all(
+        near_grad.reshape(lines, width // lines, width), "ty", split_axis=0, concat_axis=0, tiled=True
+    )
+    totals = gather_sums(pairs, near_parts, [returned[:2], returned[2:], [grad_points]])
     scale = 1.0 / math.sqrt(tiles * tile_rows)
-    up_sum, down_sum, conv_sum, gain_one_sum, gain_two_sum = call(
+    up_sum, down_sum, conv_sum, gain_one_sum, gain_two_sum, near_sum = call(
         spread_kernel,
         [
             shaped(width, hidden, dtype=f32),
@@ -881,9 +930,13 @@
             shaped(*conv_w.shape, dtype=f32),
             shaped(1, width, dtype=f32),
             shaped(1, width, dtype=f32),
+            shaped(width, width, dtype=f32),
         ],
         [bit_of("ty", 1), *totals],
-        scratch=[pltpu.VMEM((sums_rows, width), bf16)] * 2,
+        scratch=[
+            pltpu.VMEM((2 * totals[0].shape[0], width), bf16),
+            pltpu.VMEM((sums_rows, width), bf16),
+        ],
         smem=1,
         flops=1e6,
         bits=len(steps_of("ty")),
@@ -892,7 +945,7 @@
     return (
         out_rows[None],
         grad_points[None],
-        near_sum.astype(f32) * scale,
+        near_sum,
         gain_one_sum[0],
         conv_sum,
         gain_two_sum[0],

time: 202 us -> 209 us (1.035)
  waiting for transfers between devices: 82.6 us -> 98.3 us
  starting transfers between devices: 53.2 us -> 47.3 us
    ppermute x10, waiting for transfers between devices: 18.7 us -> 33 us  [partner(): lax.ppermute(value, axis, [(at, at ^ step) for at in range(lax.axis_size(...]
    all_to_all x5 -> x3, starting transfers between devices: 22.3 us -> 13.5 us  [exchange(): lax.all_to_all(rows, ('tx', 'ty'), split_axis=0, concat_axis=0, tiled=True)]
    all_to_all x0 -> x1, starting transfers between devices: none -> 3.69 us  [body(): lax.all_to_all(near_grad.reshape(lines, width // lines, width), 'ty', spl...]
    pallas_call x18 -> x17, Pallas kernels: 62.1 us -> 61.4 us  [call(): pl.pallas_call(run, out_shape=tuple(shapes), in_specs=specs, out_specs=tu...]
    all_to_all x5 -> x3, waiting for transfers between devices: 56.5 us -> 56.8 us  [exchange(): lax.all_to_all(rows, ('tx', 'ty'), split_axis=0, concat_axis=0, tiled=True)]
  transfers between devices with their start and end apart: 23 -> 22, of which waited for: 12 -> 13; matrix products, arithmetic and copies ran while one was open for 0% -> 0% of each run, Pallas kernels for 21% -> 17%
where the time goes in v5:
time: 209 us
  waiting for transfers between devices  98.3 us (47%)
  Pallas kernels  61.4 us (29%)
  starting transfers between devices  47.3 us (23%)
    pallas_call x17, Pallas kernels, call(): pl.pallas_call(run, out_shape=tuple(shapes), in_specs=specs, out_specs=tu...  61.4 us
    all_to_all x3, waiting for transfers between devices, exchange(): lax.all_to_all(rows, ('tx', 'ty'), split_axis=0, concat_axis=0, tiled=True)  56.8 us
    ppermute x10, waiting for transfers between devices, partner(): lax.ppermute(value, axis, [(at, at ^ step) for at in range(lax.axis_size(...  33 us
    ppermute x8, starting transfers between devices, shifted(): lax.ppermute(value, axis, [(source, source + steps) for source in range(i...  17.4 us
    all_to_all x3, starting transfers between devices, exchange(): lax.all_to_all(rows, ('tx', 'ty'), split_axis=0, concat_axis=0, tiled=True)  13.5 us
    ppermute x10, starting transfers between devices, partner(): lax.ppermute(value, axis, [(at, at ^ step) for at in range(lax.axis_size(...  12.7 us
    ppermute x8, waiting for transfers between devices, shifted(): lax.ppermute(value, axis, [(source, source + steps) for source in range(i...  8.46 us
  transfers between devices with their start and end apart: 22, of which 13 were waited for; matrix products, arithmetic and copies ran while one was open for 0% of the time, Pallas kernels for 17%

profile of v5, /device:TPU:0, one launch (start us, length us, event | category | flops | bytes accessed | tf_op | source)
XLA Modules:
  0.0 208.7 jit_solution(6937936371669476877)
XLA Ops:
  4.5 5.6 %collective-permute-start.1 = (bf16[64,256]{1,0:T(8,128)(2,1)S(1)}, bf16[64,256]{1,0:T(8,128)(2,1)S(1)}, u32[]{:S(2)}, u32[]{:S(2)}) collective-permute-start(bf16[64,256]{1,0:T(8,128)(2,1)S(1)} %get-tuple-element.46), channel_id=1, source_target_pairs={{0,8},{8,16},{16,24},{1,9},{9,17},{17,25},{2,10},{10,18},{18,26},{... | collective-permute-start | bytes 98312 | tf_op jit(solution)/shard_map/ppermute | solution.py:620
  11.4 3.0 %collective-permute-start.3 = (bf16[64,256]{1,0:T(8,128)(2,1)S(1)}, bf16[64,256]{1,0:T(8,128)(2,1)S(1)}, u32[]{:S(2)}, u32[]{:S(2)}) collective-permute-start(bf16[64,256]{1,0:T(8,128)(2,1)S(1)} %get-tuple-element.48), channel_id=1, source_target_pairs={{0,1},{1,2},{2,3},{3,4},{4,5},{5,6},{6,7},{8,9},{9,10},{10,11},{11... | collective-permute-start | bytes 98312 | tf_op jit(solution)/shard_map/ppermute | solution.py:620
  14.4 5.9 %shard_map.189 = (bf16[1280,1024]{1,0:T(8,128)(2,1)}, bf16[1280,1024]{1,0:T(8,128)(2,1)S(1)}) custom-call(s32[16,1024]{1,0:T(8,128)S(1)} %bitcast.28), custom_call_target="tpu_custom_call" | custom-call | flops 8000000000 | bytes 5308416 | tf_op jit(solution)/shard_map/pallas_call | solution.py:601
  20.4 4.2 %shard_map.190 = (bf16[256,1024]{1,0:T(8,128)(2,1)}, f32[1024,256]{1,0:T(8,128)}, bf16[2048,512]{1,0:T(8,128)(2,1)}) custom-call(s32[1,1024]{1,0:T(1,128)S(1)} %get-tuple-element.44.refs_0_, bf16[1024,256]{1,0:T(8,128)(2,1)S(1)} %bitcast.24, bf16[1024,256]{1,0:T(8,128)(2,1)S(1)} %bitcast.25, bf16[64,256]{1,0:T(8,128)(2,1)S(1)} %collective-permute-done.refs_3_, ...), custom_call_target="tpu_custom_call" | custom-call | flops 4000000000 | bytes 7606272 | tf_op jit(solution)/shard_map/pallas_call | solution.py:601
  24.7 5.5 %all-to-all-start = ((bf16[32,64,512]{2,1,0:T(8,128)(2,1)}), bf16[32,64,512]{2,1,0:T(8,128)(2,1)}, u32[]{:S(2)}, u32[]{:S(2)}) async-start(bf16[32,64,512]{2,1,0:T(8,128)(2,1)} %bitcast.36), calls=%async_computation | async-start | bytes 4194304 | tf_op jit(solution)/shard_map/all_to_all | solution.py:695
  30.2 48.9 %all-to-all-done = bf16[32,64,512]{2,1,0:T(8,128)(2,1)} async-done(((bf16[32,64,512]{2,1,0:T(8,128)(2,1)}), bf16[32,64,512]{2,1,0:T(8,128)(2,1)}, u32[]{:S(2)}, u32[]{:S(2)}) %all-to-all-start) | async-done | bytes 2097184 | tf_op jit(solution)/shard_map/all_to_all | solution.py:695
  79.1 12.4 %shard_map.191 = (bf16[2048,256]{1,0:T(8,128)(2,1)}, f32[2048,256]{1,0:T(8,128)}, bf16[2048,256]{1,0:T(8,128)(2,1)}) custom-call(s32[1,2048]{1,0:T(1,128)S(1)} %copy-done.8, bf16[768,32]{1,0:T(8,128)(2,1)S(1)} %bitcast.26, f32[1,256]{1,0:T(1,128)S(1)} %bitcast.31, f32[1,256]{1,0:T(1,128)S(1)} %bitcast.33, bf16[256,1024]{1,0:T(8,128)(2,1)S(1)} %copy-done.3, ...), custom_call_target="tpu_custom_call" | custom-call | flops 10000000000 | bytes 7399424 | tf_op jit(solution)/shard_map/pallas_call | solution.py:601
  91.5 4.2 %all-to-all-start.1 = ((bf16[32,64,256]{2,1,0:T(8,128)(2,1)}), bf16[32,64,256]{2,1,0:T(8,128)(2,1)S(1)}, u32[]{:S(2)}, u32[]{:S(2)}) async-start(bf16[32,64,256]{2,1,0:T(8,128)(2,1)} %bitcast.37), calls=%async_computation.1 | async-start | bytes 2097152 | tf_op jit(solution)/shard_map/all_to_all | solution.py:695
  95.7 24.0 %shard_map.193 = (bf16[2048,256]{1,0:T(8,128)(2,1)}, bf16[1152,256]{1,0:T(8,128)(2,1)}, bf16[1152,256]{1,0:T(8,128)(2,1)}) custom-call(s32[1]{0:T(128)} %bitcast.12.refs_0_, s32[1,2048]{1,0:T(1,128)S(1)} %copy-done.8, bf16[768,32]{1,0:T(8,128)(2,1)S(1)} %bitcast.27, f32[1,256]{1,0:T(1,128)S(1)} %bitcast.32, f32[1,256]{1,0:T(1,128)S(1)} %bitcast.34, ...), custom_call_target="tpu_custom_call" | custom-call | flops 40000000000 | bytes 8579076 | tf_op jit(solution)/shard_map/pallas_call | solution.py:601
  121.7 3.9 %all-to-all-start.2 = ((bf16[32,64,256]{2,1,0:T(8,128)(2,1)}), bf16[32,64,256]{2,1,0:T(8,128)(2,1)S(1)}, u32[]{:S(2)}, u32[]{:S(2)}) async-start(bf16[32,64,256]{2,1,0:T(8,128)(2,1)} %bitcast.35), calls=%async_computation.2 | async-start | bytes 2097152 | tf_op jit(solution)/shard_map/all_to_all | solution.py:695
  125.7 2.1 %shard_map.192.refs_4_ = bf16[1024,256]{1,0:T(8,128)(2,1)} custom-call(s32[1,1024]{1,0:T(1,128)S(1)} %get-tuple-element.44.refs_0_, bf16[2048,256]{1,0:T(8,128)(2,1)S(1)} %bitcast.21), custom_call_target="tpu_custom_call" | custom-call | flops 4000000000 | bytes 1576960 | tf_op jit(solution)/shard_map/pallas_call | solution.py:601
  131.4 8.4 %collective-permute-done.5.refs_3_ = bf16[288,256]{1,0:T(8,128)(2,1)S(1)} collective-permute-done((bf16[288,256]{1,0:T(8,128)(2,1)S(1)}, bf16[288,256]{1,0:T(8,128)(2,1)S(1)}, u32[]{:S(2)}, u32[]{:S(2)}) %collective-permute-start.5) | collective-permute-done | bytes 147488 | tf_op jit(solution)/shard_map/ppermute | solution.py:624
  142.1 2.7 %collective-permute-done.7.refs_6_.refs_1_ = bf16[144,256]{1,0:T(8,128)(2,1)S(1)} collective-permute-done((bf16[144,256]{1,0:T(8,128)(2,1)S(1)}, bf16[144,256]{1,0:T(8,128)(2,1)S(1)}, u32[]{:S(2)}, u32[]{:S(2)}) %collective-permute-start.7) | collective-permute-done | bytes 73760 | tf_op jit(solution)/shard_map/ppermute | solution.py:624
  145.7 5.9 %all-to-all-done.2 = bf16[32,64,256]{2,1,0:T(8,128)(2,1)S(1)} async-done(((bf16[32,64,256]{2,1,0:T(8,128)(2,1)}), bf16[32,64,256]{2,1,0:T(8,128)(2,1)S(1)}, u32[]{:S(2)}, u32[]{:S(2)}) %all-to-all-start.2) | async-done | bytes 1048608 | tf_op jit(solution)/shard_map/all_to_all | solution.py:695
  151.6 5.7 %shard_map.197 = (f32[1024,256]{1,0:T(8,128)}, bf16[256,256]{1,0:T(8,128)(2,1)}, bf16[64,256]{1,0:T(8,128)(2,1)S(1)}, bf16[64,256]{1,0:T(8,128)(2,1)S(1)}, bf16[...) custom-call(s32[1,1024]{1,0:T(1,128)S(1)} %get-tuple-element.44.refs_0_, bf16[2048,256]{1,0:T(8,128)(2,1)S(1)} %bitcast.22, ...), custom_call_target="tpu_custom_call" | custom-call | flops 6000000000 | bytes 6688768 | tf_op jit(solution)/shard_map/pallas_call | solution.py:601
  157.4 3.7 %all-to-all-start.3 = ((bf16[8,32,256]{2,1,0:T(8,128)(2,1)}), bf16[8,32,256]{2,1,0:T(8,128)(2,1)S(1)}, u32[]{:S(2)}, u32[]{:S(2)}) async-start(bf16[8,32,256]{2,1,0:T(8,128)(2,1)} %bitcast.18), calls=%async_computation.3 | async-start | bytes 262144 | tf_op jit(solution)/shard_map/all_to_all | solution.py:920
  161.1 2.4 %collective-permute-start.9 = (bf16[64,256]{1,0:T(8,128)(2,1)S(1)}, bf16[64,256]{1,0:T(8,128)(2,1)S(1)}, u32[]{:S(2)}, u32[]{:S(2)}) collective-permute-start(bf16[64,256]{1,0:T(8,128)(2,1)S(1)} %get-tuple-element.66), channel_id=1, source_target_pairs={{0,8},{8,16},{16,24},{1,9},{9,17},{17,25},{2,10},{10,18},{18,26},{... | collective-permute-start | bytes 98312 | tf_op jit(solution)/shard_map/ppermute | solution.py:620
  165.1 4.2 %collective-permute-done.10.refs_2_.refs_6_ = bf16[64,256]{1,0:T(8,128)(2,1)S(1)} collective-permute-done((bf16[64,256]{1,0:T(8,128)(2,1)S(1)}, bf16[64,256]{1,0:T(8,128)(2,1)S(1)}, u32[]{:S(2)}, u32[]{:S(2)}) %collective-permute-start.10) | collective-permute-done | bytes 32800 | tf_op jit(solution)/shard_map/ppermute | solution.py:620
  172.6 3.9 %collective-permute-done.12.refs_4_.refs_3_ = bf16[64,256]{1,0:T(8,128)(2,1)S(1)} collective-permute-done((bf16[64,256]{1,0:T(8,128)(2,1)S(1)}, bf16[64,256]{1,0:T(8,128)(2,1)S(1)}, u32[]{:S(2)}, u32[]{:S(2)}) %collective-permute-start.12) | collective-permute-done | bytes 32800 | tf_op jit(solution)/shard_map/ppermute | solution.py:620
  177.7 2.6 %shard_map.198.refs_2_ = bf16[1024,256]{1,0:T(8,128)(2,1)} custom-call(s32[4,64]{1,0:T(4,128)S(1)} %bitcast.30, bf16[64,256]{1,0:T(8,128)(2,1)S(1)} %collective-permute-done.9.refs_1_.refs_5_, bf16[64,256]{1,0:T(8,128)(2,1)S(1)} %collective-permute-done.10.refs_2_.refs_6_, bf16[64,256]{1,0:T(8,128)(2,1)S(1)} %collective-permute-done.11.refs_3_.refs_2_, ...), custom_call_target="tpu_custom_call" | custom-call | flops 1000000000 | bytes 1704960 | tf_op jit(solution)/shard_map/pallas_call | solution.py:601
  180.3 6.7 %collective-permute-done.14.refs_1_ = bf16[320,256]{1,0:T(8,128)(2,1)S(1)} collective-permute-done((bf16[320,256]{1,0:T(8,128)(2,1)S(1)}, bf16[320,256]{1,0:T(8,128)(2,1)S(1)}, u32[]{:S(2)}, u32[]{:S(2)}) %collective-permute-start.14) | collective-permute-done | bytes 163872 | tf_op jit(solution)/shard_map/ppermute | solution.py:624
  187.1 4.3 %collective-permute-start.15 = (bf16[320,256]{1,0:T(8,128)(2,1)S(1)}, bf16[320,256]{1,0:T(8,128)(2,1)S(1)}, u32[]{:S(2)}, u32[]{:S(2)}) collective-permute-start(bf16[320,256]{1,0:T(8,128)(2,1)S(1)} %shard_map.201.refs_1_), channel_id=1, source_target_pairs={{0,4},{1,5},{2,6},{3,7},{4,0},{5,1},{6,2},{7,3},{8,12},{9,13},{10,... | collective-permute-start | bytes 491528 | tf_op jit(solution)/shard_map/ppermute | solution.py:624
  191.4 4.2 %collective-permute-done.15.refs_2_ = bf16[320,256]{1,0:T(8,128)(2,1)S(1)} collective-permute-done((bf16[320,256]{1,0:T(8,128)(2,1)S(1)}, bf16[320,256]{1,0:T(8,128)(2,1)S(1)}, u32[]{:S(2)}, u32[]{:S(2)}) %collective-permute-start.15) | collective-permute-done | bytes 163872 | tf_op jit(solution)/shard_map/ppermute | solution.py:624
  196.7 7.9 %collective-permute-done.16.refs_2_ = bf16[640,256]{1,0:T(8,128)(2,1)S(1)} collective-permute-done((bf16[640,256]{1,0:T(8,128)(2,1)S(1)}, bf16[640,256]{1,0:T(8,128)(2,1)S(1)}, u32[]{:S(2)}, u32[]{:S(2)}) %collective-permute-start.16) | collective-permute-done | bytes 327712 | tf_op jit(solution)/shard_map/ppermute | solution.py:624
  (63 shorter events, 24.7 us)
Async XLA Ops:
  3.2 17.1 %collective-permute-start = (bf16[64,256]{1,0:T(8,128)(2,1)S(1)}, bf16[64,256]{1,0:T(8,128)(2,1)S(1)}, u32[]{:S(2)}, u32[]{:S(2)}) collective-permute-start(bf16[64,256]{1,0:T(8,128)(2,1)S(1)} %get-tuple-element.45), channel_id=1, source_target_pairs={{8,0},{16,8},{24,16},{9,1},{17,9},{25,17},{10,2},{18,10},{26,18},{... | collective-permute-start | bytes 98312 | tf_op jit(solution)/shard_map/ppermute | solution.py:620
  4.5 15.8 %collective-permute-start.1 = (bf16[64,256]{1,0:T(8,128)(2,1)S(1)}, bf16[64,256]{1,0:T(8,128)(2,1)S(1)}, u32[]{:S(2)}, u32[]{:S(2)}) collective-permute-start(bf16[64,256]{1,0:T(8,128)(2,1)S(1)} %get-tuple-element.46), channel_id=1, source_target_pairs={{0,8},{8,16},{16,24},{1,9},{9,17},{17,25},{2,10},{10,18},{18,26},{... | collective-permute-start | bytes 98312 | tf_op jit(solution)/shard_map/ppermute | solution.py:620
  10.1 10.3 %collective-permute-start.2 = (bf16[64,256]{1,0:T(8,128)(2,1)S(1)}, bf16[64,256]{1,0:T(8,128)(2,1)S(1)}, u32[]{:S(2)}, u32[]{:S(2)}) collective-permute-start(bf16[64,256]{1,0:T(8,128)(2,1)S(1)} %get-tuple-element.47), channel_id=1, source_target_pairs={{1,0},{2,1},{3,2},{4,3},{5,4},{6,5},{7,6},{9,8},{10,9},{11,10},{12... | collective-permute-start | bytes 98312 | tf_op jit(solution)/shard_map/ppermute | solution.py:620
  11.4 9.0 %collective-permute-start.3 = (bf16[64,256]{1,0:T(8,128)(2,1)S(1)}, bf16[64,256]{1,0:T(8,128)(2,1)S(1)}, u32[]{:S(2)}, u32[]{:S(2)}) collective-permute-start(bf16[64,256]{1,0:T(8,128)(2,1)S(1)} %get-tuple-element.48), channel_id=1, source_target_pairs={{0,1},{1,2},{2,3},{3,4},{4,5},{5,6},{6,7},{8,9},{9,10},{10,11},{11... | collective-permute-start | bytes 98312 | tf_op jit(solution)/shard_map/ppermute | solution.py:620
  24.6 54.4 %copy-start.3 = (bf16[256,1024]{1,0:T(8,128)(2,1)S(1)}, bf16[256,1024]{1,0:T(8,128)(2,1)}, u32[]{:S(2)}) copy-start(bf16[256,1024]{1,0:T(8,128)(2,1)} %refs_5_.3) | copy-start | bytes 1572868
  24.6 54.4 %copy-start.4 = (bf16[1024,256]{1,0:T(8,128)(2,1)S(1)}, bf16[1024,256]{1,0:T(8,128)(2,1)}, u32[]{:S(2)}) copy-start(bf16[1024,256]{1,0:T(8,128)(2,1)} %refs_6_.1) | copy-start | bytes 1572868
  24.7 54.3 %all-to-all-start = ((bf16[32,64,512]{2,1,0:T(8,128)(2,1)}), bf16[32,64,512]{2,1,0:T(8,128)(2,1)}, u32[]{:S(2)}, u32[]{:S(2)}) async-start(bf16[32,64,512]{2,1,0:T(8,128)(2,1)} %bitcast.36), calls=%async_computation | async-start | bytes 4194304 | tf_op jit(solution)/shard_map/all_to_all | solution.py:695
  91.5 30.3 %all-to-all-start.1 = ((bf16[32,64,256]{2,1,0:T(8,128)(2,1)}), bf16[32,64,256]{2,1,0:T(8,128)(2,1)S(1)}, u32[]{:S(2)}, u32[]{:S(2)}) async-start(bf16[32,64,256]{2,1,0:T(8,128)(2,1)} %bitcast.37), calls=%async_computation.1 | async-start | bytes 2097152 | tf_op jit(solution)/shard_map/all_to_all | solution.py:695
  121.7 29.9 %all-to-all-start.2 = ((bf16[32,64,256]{2,1,0:T(8,128)(2,1)}), bf16[32,64,256]{2,1,0:T(8,128)(2,1)S(1)}, u32[]{:S(2)}, u32[]{:S(2)}) async-start(bf16[32,64,256]{2,1,0:T(8,128)(2,1)} %bitcast.35), calls=%async_computation.2 | async-start | bytes 2097152 | tf_op jit(solution)/shard_map/all_to_all | solution.py:695
  125.6 2.2 %collective-permute-start.4 = (bf16[1152,256]{1,0:T(8,128)(2,1)S(1)}, bf16[1152,256]{1,0:T(8,128)(2,1)S(1)}, u32[]{:S(2)}, u32[]{:S(2)}) collective-permute-start(bf16[1152,256]{1,0:T(8,128)(2,1)S(1)} %copy-done.12), channel_id=1, source_target_pairs={{0,1},{1,0},{2,3},{3,2},{4,5},{5,4},{6,7},{7,6},{8,9},{9,8},{10,11... | collective-permute-start | bytes 1769480 | tf_op jit(solution)/shard_map/ppermute | solution.py:624
  128.2 11.6 %collective-permute-start.5 = (bf16[288,256]{1,0:T(8,128)(2,1)S(1)}, bf16[288,256]{1,0:T(8,128)(2,1)S(1)}, u32[]{:S(2)}, u32[]{:S(2)}) collective-permute-start(bf16[288,256]{1,0:T(8,128)(2,1)S(1)} %get-tuple-element.61), channel_id=1, source_target_pairs={{0,2},{1,3},{2,0},{3,1},{4,6},{5,7},{6,4},{7,5},{8,10},{9,11},{10,... | collective-permute-start | bytes 442376 | tf_op jit(solution)/shard_map/ppermute | solution.py:624
  129.9 9.9 %collective-permute-start.6 = (bf16[288,256]{1,0:T(8,128)(2,1)S(1)}, bf16[288,256]{1,0:T(8,128)(2,1)S(1)}, u32[]{:S(2)}, u32[]{:S(2)}) collective-permute-start(bf16[288,256]{1,0:T(8,128)(2,1)S(1)} %get-tuple-element.63), channel_id=1, source_target_pairs={{0,4},{1,5},{2,6},{3,7},{4,0},{5,1},{6,2},{7,3},{8,12},{9,13},{10,... | collective-permute-start | bytes 442376 | tf_op jit(solution)/shard_map/ppermute | solution.py:624
  140.0 4.8 %collective-permute-start.7 = (bf16[144,256]{1,0:T(8,128)(2,1)S(1)}, bf16[144,256]{1,0:T(8,128)(2,1)S(1)}, u32[]{:S(2)}, u32[]{:S(2)}) collective-permute-start(bf16[144,256]{1,0:T(8,128)(2,1)S(1)} %get-tuple-element.64), channel_id=1, source_target_pairs={{0,4},{1,5},{2,6},{3,7},{4,0},{5,1},{6,2},{7,3},{8,12},{9,13},{10,... | collective-permute-start | bytes 221192 | tf_op jit(solution)/shard_map/ppermute | solution.py:624
  141.4 4.4 %collective-permute-start.8 = (bf16[144,256]{1,0:T(8,128)(2,1)S(1)}, bf16[144,256]{1,0:T(8,128)(2,1)S(1)}, u32[]{:S(2)}, u32[]{:S(2)}) collective-permute-start(bf16[144,256]{1,0:T(8,128)(2,1)S(1)} %get-tuple-element.65), channel_id=1, source_target_pairs={{0,2},{1,3},{2,0},{3,1},{4,6},{5,7},{6,4},{7,5},{8,10},{9,11},{10,... | collective-permute-start | bytes 221192 | tf_op jit(solution)/shard_map/ppermute | solution.py:624
  157.4 11.9 %all-to-all-start.3 = ((bf16[8,32,256]{2,1,0:T(8,128)(2,1)}), bf16[8,32,256]{2,1,0:T(8,128)(2,1)S(1)}, u32[]{:S(2)}, u32[]{:S(2)}) async-start(bf16[8,32,256]{2,1,0:T(8,128)(2,1)} %bitcast.18), calls=%async_computation.3 | async-start | bytes 262144 | tf_op jit(solution)/shard_map/all_to_all | solution.py:920
  161.1 4.0 %collective-permute-start.9 = (bf16[64,256]{1,0:T(8,128)(2,1)S(1)}, bf16[64,256]{1,0:T(8,128)(2,1)S(1)}, u32[]{:S(2)}, u32[]{:S(2)}) collective-permute-start(bf16[64,256]{1,0:T(8,128)(2,1)S(1)} %get-tuple-element.66), channel_id=1, source_target_pairs={{0,8},{8,16},{16,24},{1,9},{9,17},{17,25},{2,10},{10,18},{18,26},{... | collective-permute-start | bytes 98312 | tf_op jit(solution)/shard_map/ppermute | solution.py:620
  163.5 5.8 %collective-permute-start.10 = (bf16[64,256]{1,0:T(8,128)(2,1)S(1)}, bf16[64,256]{1,0:T(8,128)(2,1)S(1)}, u32[]{:S(2)}, u32[]{:S(2)}) collective-permute-start(bf16[64,256]{1,0:T(8,128)(2,1)S(1)} %get-tuple-element.67), channel_id=1, source_target_pairs={{8,0},{16,8},{24,16},{9,1},{17,9},{25,17},{10,2},{18,10},{26,18},{... | collective-permute-start | bytes 98312 | tf_op jit(solution)/shard_map/ppermute | solution.py:620
  169.4 7.1 %collective-permute-start.13 = (bf16[320,256]{1,0:T(8,128)(2,1)S(1)}, bf16[320,256]{1,0:T(8,128)(2,1)S(1)}, u32[]{:S(2)}, u32[]{:S(2)}) collective-permute-start(bf16[320,256]{1,0:T(8,128)(2,1)S(1)} %shard_map.199.refs_0_), channel_id=1, source_target_pairs={{0,8},{8,0},{16,24},{24,16},{1,9},{9,1},{17,25},{25,17},{2,10},{10... | collective-permute-start | bytes 491528 | tf_op jit(solution)/shard_map/ppermute | solution.py:624
  170.0 2.6 %collective-permute-start.11 = (bf16[64,256]{1,0:T(8,128)(2,1)S(1)}, bf16[64,256]{1,0:T(8,128)(2,1)S(1)}, u32[]{:S(2)}, u32[]{:S(2)}) collective-permute-start(bf16[64,256]{1,0:T(8,128)(2,1)S(1)} %get-tuple-element.68), channel_id=1, source_target_pairs={{0,1},{1,2},{2,3},{3,4},{4,5},{5,6},{6,7},{8,9},{9,10},{10,11},{11... | collective-permute-start | bytes 98312 | tf_op jit(solution)/shard_map/ppermute | solution.py:620
  171.3 5.3 %collective-permute-start.12 = (bf16[64,256]{1,0:T(8,128)(2,1)S(1)}, bf16[64,256]{1,0:T(8,128)(2,1)S(1)}, u32[]{:S(2)}, u32[]{:S(2)}) collective-permute-start(bf16[64,256]{1,0:T(8,128)(2,1)S(1)} %get-tuple-element.69), channel_id=1, source_target_pairs={{1,0},{2,1},{3,2},{4,3},{5,4},{6,5},{7,6},{9,8},{10,9},{11,10},{12... | collective-permute-start | bytes 98312 | tf_op jit(solution)/shard_map/ppermute | solution.py:620
  176.6 10.5 %collective-permute-start.14 = (bf16[320,256]{1,0:T(8,128)(2,1)S(1)}, bf16[320,256]{1,0:T(8,128)(2,1)S(1)}, u32[]{:S(2)}, u32[]{:S(2)}) collective-permute-start(bf16[320,256]{1,0:T(8,128)(2,1)S(1)} %shard_map.200.refs_0_), channel_id=1, source_target_pairs={{0,16},{8,24},{16,0},{24,8},{1,17},{9,25},{17,1},{25,9},{2,18},{10... | collective-permute-start | bytes 491528 | tf_op jit(solution)/shard_map/ppermute | solution.py:624
  187.1 8.5 %collective-permute-start.15 = (bf16[320,256]{1,0:T(8,128)(2,1)S(1)}, bf16[320,256]{1,0:T(8,128)(2,1)S(1)}, u32[]{:S(2)}, u32[]{:S(2)}) collective-permute-start(bf16[320,256]{1,0:T(8,128)(2,1)S(1)} %shard_map.201.refs_1_), channel_id=1, source_target_pairs={{0,4},{1,5},{2,6},{3,7},{4,0},{5,1},{6,2},{7,3},{8,12},{9,13},{10,... | collective-permute-start | bytes 491528 | tf_op jit(solution)/shard_map/ppermute | solution.py:624
  195.6 9.1 %collective-permute-start.16 = (bf16[640,256]{1,0:T(8,128)(2,1)S(1)}, bf16[640,256]{1,0:T(8,128)(2,1)S(1)}, u32[]{:S(2)}, u32[]{:S(2)}) collective-permute-start(bf16[640,256]{1,0:T(8,128)(2,1)S(1)} %shard_map.202.refs_1_), channel_id=1, source_target_pairs={{0,2},{1,3},{2,0},{3,1},{4,6},{5,7},{6,4},{7,5},{8,10},{9,11},{10,... | collective-permute-start | bytes 983048 | tf_op jit(solution)/shard_map/ppermute | solution.py:624
  204.7 2.2 %collective-permute-start.17 = (bf16[1280,256]{1,0:T(8,128)(2,1)S(1)}, bf16[1280,256]{1,0:T(8,128)(2,1)S(1)}, u32[]{:S(2)}, u32[]{:S(2)}) collective-permute-start(bf16[1280,256]{1,0:T(8,128)(2,1)S(1)} %shard_map.203.refs_1_), channel_id=1, source_target_pairs={{0,1},{1,0},{2,3},{3,2},{4,5},{5,4},{6,7},{7,6},{8,9},{9,8},{10,11... | collective-permute-start | bytes 1966088 | tf_op jit(solution)/shard_map/ppermute | solution.py:624
  (11 other events, 280.6 us)

commit v6 on v4

--- a/solution.py
+++ b/solution.py
@@ -236,11 +236,8 @@
 def finish_kernel(lists_ref, back0, back1, back2, back3, row_in, out_ref, row_ref, sems):
     fetch = pltpu.make_async_copy(row_in, row_ref, sems.at[0])
     fetch.start()
-    rows = row_ref.shape[0]
-    total = sum(
-        dot(chosen_rows(lists_ref, direction, rows), came[...])
-        for direction, came in enumerate((back0, back1, back2, back3))
-    )
+    came = jnp.concatenate([back0[...], back1[...], back2[...], back3[...]], axis=0)
+    total = dot(chosen_rows(lists_ref, 0, row_ref.shape[0]), came)
     fetch.wait()
     out_ref[...] = (row_ref[...] + total).astype(bf16)
 
@@ -510,7 +507,7 @@
 
 
 def spread_kernel(
-    bit_ref, mine_ref, came_ref, up_ref, down_ref, conv_ref, gain_one_ref, gain_two_ref,
+    bit_ref, mine_ref, came_ref, total_ref, up_ref, down_ref, conv_ref, gain_one_ref, gain_two_ref, near_ref,
     joined_ref, sums_ref, *, bits, scale
 ):
     join_kernel(bit_ref, mine_ref, came_ref, joined_ref)
@@ -541,6 +538,7 @@
     gains = sums_ref[at : at + 16, :].astype(f32) * scale
     gain_one_ref[...] = gains[0:1, :]
     gain_two_ref[...] = gains[1:2, :]
+    near_ref[...] = total_ref[...].astype(f32) * scale
 
 
 def call(kernel, outs, args, scratch=(), smem=0, flops=0, limit=16, held=0, stored=0, after=(), same=None, **static):
@@ -548,7 +546,8 @@
     specs = [pl.BlockSpec(memory_space=pltpu.SMEM)] * smem
     specs += [pl.BlockSpec(memory_space=pltpu.VMEM)] * (len(args) - smem - held)
     specs += [pl.BlockSpec(memory_space=pltpu.HBM)] * held
-    specs += [pl.BlockSpec(memory_space=pl.ANY)] * len(after)
+    specs += [pl.BlockSpec(memory_space=pltpu.HBM if a.shape[0] >= PATCH else pl.ANY) for a in after]
+    after = [pltpu.with_memory_space_constraint(a, pltpu.HBM) if a.shape[0] >= PATCH else a for a in after]
     out_specs = [pl.BlockSpec(memory_space=pltpu.HBM)] * stored
     shapes = [pltpu.HBM(a.shape, a.dtype) for a in outs[:stored]] + list(outs[stored:])
     first_held = len(args) - held
@@ -593,7 +592,7 @@
     return [1 << at for at in range(int(math.log2(lax.axis_size(axis))))]
 
 
-def sum_over_mesh(keep, send, early, late, returned):
+def sum_over_mesh(keep, send, early, late):
     width = keep.shape[1]
     steps = steps_of("ty")
     orders = steps[1:], steps[:0:-1]
@@ -625,15 +624,15 @@
             add_kernel,
             [shaped(*share.shape)],
             [share, partner(share, "tx", step)],
-            after=late if step == steps_of("tx")[-1] else (),
+            after=late.pop(0) if late else (),
             flops=1e6,
         )
-    for at, step in enumerate(steps[:0:-1]):
+    for step in steps[:0:-1]:
         (share,) = call(
             join_kernel,
             [shaped(2 * share.shape[0], width)],
             [bit_of("ty", step), share, partner(share, "ty", step)],
-            after=returned[2 * at : 2 * at + 2],
+            after=late.pop(0) if late else (),
             smem=1,
             flops=1e6,
         )
@@ -818,7 +817,7 @@
         hold_kernel,
         [shaped(slots_count, width)],
         [back_grad],
-        after=[came_result],
+        after=[came_result.reshape(tiles, capacity, width)],
         held=1,
         stored=1,
         same={0: 0},
@@ -854,26 +853,28 @@
         shifted(halo_grad[2], "ty", 1),
         shifted(halo_grad[3], "ty", -1),
     ]
-    totals = sum_over_mesh(keep, send, [out_rows], [near_grad], returned)
     (near_share,) = call(
         near_sum_kernel,
         [shaped(width, width)],
         [exchange(near_grad, tiles)],
-        after=returned,
+        after=returned[:2],
         flops=1e6,
         share=width // tiles,
     )
-    near_sum = exchange(near_share, tiles)
+    near_total = exchange(near_share, tiles)
+    totals = sum_over_mesh(
+        keep, send, [out_rows], [[near_grad], returned[:2], [near_share], [near_total, *returned[2:]]]
+    )
     (grad_points,) = call(
         finish_kernel,
         [shaped(tile_rows, width)],
-        [lists, *returned, row_grad],
+        [border.reshape(1, edge), *returned, row_grad],
         scratch=[pltpu.VMEM((tile_rows, width), f32), pltpu.SemaphoreType.DMA((1,))],
         held=1,
         flops=1e9,
     )
     scale = 1.0 / math.sqrt(tiles * tile_rows)
-    up_sum, down_sum, conv_sum, gain_one_sum, gain_two_sum = call(
+    up_sum, down_sum, conv_sum, gain_one_sum, gain_two_sum, near_sum = call(
         spread_kernel,
         [
             shaped(width, hidden, dtype=f32),
@@ -881,8 +882,9 @@
             shaped(*conv_w.shape, dtype=f32),
             shaped(1, width, dtype=f32),
             shaped(1, width, dtype=f32),
+            shaped(width, width, dtype=f32),
         ],
-        [bit_of("ty", 1), *totals],
+        [bit_of("ty", 1), *totals, near_total],
         scratch=[pltpu.VMEM((sums_rows, width), bf16)] * 2,
         smem=1,
         flops=1e6,
@@ -892,7 +894,7 @@
     return (
         out_rows[None],
         grad_points[None],
-        near_sum.astype(f32) * scale,
+        near_sum,
         gain_one_sum[0],
         conv_sum,
         gain_two_sum[0],

time: 202 us -> 197 us (0.975)
    ppermute x10, waiting for transfers between devices: 18.7 us -> 15.3 us  [partner(): lax.ppermute(value, axis, [(at, at ^ step) for at in range(lax.axis_size(...]
where the time goes in v6:
time: 197 us; the launch traced here: 196 us
  waiting for transfers between devices  80.6 us (41%)
  Pallas kernels  61.8 us (31%)
  starting transfers between devices  51.9 us (26%)
    pallas_call x18, Pallas kernels, call(): pl.pallas_call(run, out_shape=tuple(shapes), in_specs=specs, out_specs=tu...  61.8 us
    all_to_all x5, waiting for transfers between devices, exchange(): lax.all_to_all(rows, ('tx', 'ty'), split_axis=0, concat_axis=0, tiled=True)  57.9 us
    all_to_all x5, starting transfers between devices, exchange(): lax.all_to_all(rows, ('tx', 'ty'), split_axis=0, concat_axis=0, tiled=True)  21.5 us
    ppermute x8, starting transfers between devices, shifted(): lax.ppermute(value, axis, [(source, source + steps) for source in range(i...  19.6 us
    ppermute x10, waiting for transfers between devices, partner(): lax.ppermute(value, axis, [(at, at ^ step) for at in range(lax.axis_size(...  15.3 us
    ppermute x10, starting transfers between devices, partner(): lax.ppermute(value, axis, [(at, at ^ step) for at in range(lax.axis_size(...  10.8 us
    ppermute x8, waiting for transfers between devices, shifted(): lax.ppermute(value, axis, [(source, source + steps) for source in range(i...  7.45 us
  transfers between devices with their start and end apart: 23, of which 12 were waited for; matrix products, arithmetic and copies ran while one was open for 0% of the time, Pallas kernels for 21%

profile of v6, /device:TPU:0, one launch (start us, length us, event | category | flops | bytes accessed | tf_op | source)
XLA Modules:
  0.0 196.1 jit_solution(14536780061423789622)
XLA Ops:
  4.5 5.6 %collective-permute-start.1 = (bf16[64,256]{1,0:T(8,128)(2,1)S(1)}, bf16[64,256]{1,0:T(8,128)(2,1)S(1)}, u32[]{:S(2)}, u32[]{:S(2)}) collective-permute-start(bf16[64,256]{1,0:T(8,128)(2,1)S(1)} %get-tuple-element.46), channel_id=1, source_target_pairs={{0,8},{8,16},{16,24},{1,9},{9,17},{17,25},{2,10},{10,18},{18,26},{... | collective-permute-start | bytes 98312 | tf_op jit(solution)/shard_map/ppermute | solution.py:580
  11.4 3.0 %collective-permute-start.3 = (bf16[64,256]{1,0:T(8,128)(2,1)S(1)}, bf16[64,256]{1,0:T(8,128)(2,1)S(1)}, u32[]{:S(2)}, u32[]{:S(2)}) collective-permute-start(bf16[64,256]{1,0:T(8,128)(2,1)S(1)} %get-tuple-element.48), channel_id=1, source_target_pairs={{0,1},{1,2},{2,3},{3,4},{4,5},{5,6},{6,7},{8,9},{9,10},{10,11},{11... | collective-permute-start | bytes 98312 | tf_op jit(solution)/shard_map/ppermute | solution.py:580
  14.4 5.8 %shard_map.189 = (bf16[1280,1024]{1,0:T(8,128)(2,1)}, bf16[1280,1024]{1,0:T(8,128)(2,1)S(1)}) custom-call(s32[16,1024]{1,0:T(8,128)S(1)} %bitcast.34), custom_call_target="tpu_custom_call" | custom-call | flops 8000000000 | bytes 5308416 | tf_op jit(solution)/shard_map/pallas_call | solution.py:561
  20.4 4.3 %shard_map.190 = (bf16[256,1024]{1,0:T(8,128)(2,1)}, f32[1024,256]{1,0:T(8,128)}, bf16[2048,512]{1,0:T(8,128)(2,1)}) custom-call(s32[1,1024]{1,0:T(1,128)S(1)} %get-tuple-element.44.refs_0_, bf16[1024,256]{1,0:T(8,128)(2,1)S(1)} %bitcast.30, bf16[1024,256]{1,0:T(8,128)(2,1)S(1)} %bitcast.31, bf16[64,256]{1,0:T(8,128)(2,1)S(1)} %collective-permute-done.refs_3_, ...), custom_call_target="tpu_custom_call" | custom-call | flops 4000000000 | bytes 7606272 | tf_op jit(solution)/shard_map/pallas_call | solution.py:561
  24.8 5.5 %all-to-all-start = ((bf16[32,64,512]{2,1,0:T(8,128)(2,1)}), bf16[32,64,512]{2,1,0:T(8,128)(2,1)}, u32[]{:S(2)}, u32[]{:S(2)}) async-start(bf16[32,64,512]{2,1,0:T(8,128)(2,1)} %bitcast.40), calls=%async_computation | async-start | bytes 4194304 | tf_op jit(solution)/shard_map/all_to_all | solution.py:643
  30.3 48.9 %all-to-all-done = bf16[32,64,512]{2,1,0:T(8,128)(2,1)} async-done(((bf16[32,64,512]{2,1,0:T(8,128)(2,1)}), bf16[32,64,512]{2,1,0:T(8,128)(2,1)}, u32[]{:S(2)}, u32[]{:S(2)}) %all-to-all-start) | async-done | bytes 2097184 | tf_op jit(solution)/shard_map/all_to_all | solution.py:643
  79.2 12.3 %shard_map.191 = (bf16[2048,256]{1,0:T(8,128)(2,1)}, f32[2048,256]{1,0:T(8,128)}, bf16[2048,256]{1,0:T(8,128)(2,1)}) custom-call(s32[1,2048]{1,0:T(1,128)S(1)} %copy-done.8, bf16[768,32]{1,0:T(8,128)(2,1)S(1)} %bitcast.32, f32[1,256]{1,0:T(1,128)S(1)} %bitcast.35, f32[1,256]{1,0:T(1,128)S(1)} %bitcast.37, bf16[256,1024]{1,0:T(8,128)(2,1)S(1)} %copy-done.3, ...), custom_call_target="tpu_custom_call" | custom-call | flops 10000000000 | bytes 7399424 | tf_op jit(solution)/shard_map/pallas_call | solution.py:561
  91.5 4.2 %all-to-all-start.1 = ((bf16[32,64,256]{2,1,0:T(8,128)(2,1)}), bf16[32,64,256]{2,1,0:T(8,128)(2,1)S(1)}, u32[]{:S(2)}, u32[]{:S(2)}) async-start(bf16[32,64,256]{2,1,0:T(8,128)(2,1)} %bitcast.41), calls=%async_computation.1 | async-start | bytes 2097152 | tf_op jit(solution)/shard_map/all_to_all | solution.py:643
  95.7 24.0 %shard_map.193 = (bf16[2048,256]{1,0:T(8,128)(2,1)}, bf16[1152,256]{1,0:T(8,128)(2,1)}, bf16[1152,256]{1,0:T(8,128)(2,1)}) custom-call(s32[1]{0:T(128)} %bitcast.12.refs_0_, s32[1,2048]{1,0:T(1,128)S(1)} %copy-done.8, bf16[768,32]{1,0:T(8,128)(2,1)S(1)} %bitcast.33, f32[1,256]{1,0:T(1,128)S(1)} %bitcast.36, f32[1,256]{1,0:T(1,128)S(1)} %bitcast.38, ...), custom_call_target="tpu_custom_call" | custom-call | flops 40000000000 | bytes 8579076 | tf_op jit(solution)/shard_map/pallas_call | solution.py:561
  119.7 2.0 %all-to-all-done.1.refs_1_ = bf16[32,64,256]{2,1,0:T(8,128)(2,1)S(1)} async-done(((bf16[32,64,256]{2,1,0:T(8,128)(2,1)}), bf16[32,64,256]{2,1,0:T(8,128)(2,1)S(1)}, u32[]{:S(2)}, u32[]{:S(2)}) %all-to-all-start.1) | async-done | bytes 1048608 | tf_op jit(solution)/shard_map/all_to_all | solution.py:643
  121.8 3.7 %all-to-all-start.2 = ((bf16[32,64,256]{2,1,0:T(8,128)(2,1)}), bf16[32,64,256]{2,1,0:T(8,128)(2,1)S(1)}, u32[]{:S(2)}, u32[]{:S(2)}) async-start(bf16[32,64,256]{2,1,0:T(8,128)(2,1)} %bitcast.39), calls=%async_computation.2 | async-start | bytes 2097152 | tf_op jit(solution)/shard_map/all_to_all | solution.py:643
  125.8 2.1 %shard_map.192.refs_6_.refs_4_ = bf16[1024,256]{1,0:T(8,128)(2,1)} custom-call(s32[1,1024]{1,0:T(1,128)S(1)} %get-tuple-element.44.refs_0_, bf16[2048,256]{1,0:T(8,128)(2,1)S(1)} %bitcast.24), custom_call_target="tpu_custom_call" | custom-call | flops 4000000000 | bytes 1576960 | tf_op jit(solution)/shard_map/pallas_call | solution.py:561
  131.4 7.0 %collective-permute-done.10.refs_5_ = bf16[288,256]{1,0:T(8,128)(2,1)S(1)} collective-permute-done((bf16[288,256]{1,0:T(8,128)(2,1)S(1)}, bf16[288,256]{1,0:T(8,128)(2,1)S(1)}, u32[]{:S(2)}, u32[]{:S(2)}) %collective-permute-start.10) | collective-permute-done | bytes 147488 | tf_op jit(solution)/shard_map/ppermute | solution.py:584
  142.1 3.0 %collective-permute-done.11.refs_1_ = bf16[144,256]{1,0:T(8,128)(2,1)S(1)} collective-permute-done((bf16[144,256]{1,0:T(8,128)(2,1)S(1)}, bf16[144,256]{1,0:T(8,128)(2,1)S(1)}, u32[]{:S(2)}, u32[]{:S(2)}) %collective-permute-start.11) | collective-permute-done | bytes 73760 | tf_op jit(solution)/shard_map/ppermute | solution.py:584
  146.6 5.2 %all-to-all-done.2 = bf16[32,64,256]{2,1,0:T(8,128)(2,1)S(1)} async-done(((bf16[32,64,256]{2,1,0:T(8,128)(2,1)}), bf16[32,64,256]{2,1,0:T(8,128)(2,1)S(1)}, u32[]{:S(2)}, u32[]{:S(2)}) %all-to-all-start.2) | async-done | bytes 1048608 | tf_op jit(solution)/shard_map/all_to_all | solution.py:643
  151.8 5.7 %shard_map.195 = (f32[1024,256]{1,0:T(8,128)}, bf16[256,256]{1,0:T(8,128)(2,1)}, bf16[64,256]{1,0:T(8,128)(2,1)S(1)}, bf16[64,256]{1,0:T(8,128)(2,1)S(1)}, bf16[...) custom-call(s32[1,1024]{1,0:T(1,128)S(1)} %get-tuple-element.44.refs_0_, bf16[2048,256]{1,0:T(8,128)(2,1)S(1)} %bitcast.27, ...), custom_call_target="tpu_custom_call" | custom-call | flops 6000000000 | bytes 6688768 | tf_op jit(solution)/shard_map/pallas_call | solution.py:561
  158.3 4.4 %all-to-all-start.3 = ((bf16[32,8,256]{2,1,0:T(8,128)(2,1)}), bf16[32,8,256]{2,1,0:T(8,128)(2,1)S(1)}, u32[]{:S(2)}, u32[]{:S(2)}) async-start(bf16[32,8,256]{2,1,0:T(8,128)(2,1)} %bitcast.18), calls=%async_computation.3 | async-start | bytes 262144 | tf_op jit(solution)/shard_map/all_to_all | solution.py:643
  162.7 3.7 %collective-permute-start.4 = (bf16[64,256]{1,0:T(8,128)(2,1)S(1)}, bf16[64,256]{1,0:T(8,128)(2,1)S(1)}, u32[]{:S(2)}, u32[]{:S(2)}) collective-permute-start(bf16[64,256]{1,0:T(8,128)(2,1)S(1)} %get-tuple-element.58), channel_id=1, source_target_pairs={{0,8},{8,16},{16,24},{1,9},{9,17},{17,25},{2,10},{10,18},{18,26},{... | collective-permute-start | bytes 98312 | tf_op jit(solution)/shard_map/ppermute | solution.py:580
  168.0 4.2 %collective-permute-done.5.refs_2_.refs_3_ = bf16[64,256]{1,0:T(8,128)(2,1)S(1)} collective-permute-done((bf16[64,256]{1,0:T(8,128)(2,1)S(1)}, bf16[64,256]{1,0:T(8,128)(2,1)S(1)}, u32[]{:S(2)}, u32[]{:S(2)}) %collective-permute-start.5) | collective-permute-done | bytes 32800 | tf_op jit(solution)/shard_map/ppermute | solution.py:580
  174.6 2.8 %collective-permute-done.15.refs_2_ = bf16[288,256]{1,0:T(8,128)(2,1)S(1)} collective-permute-done((bf16[288,256]{1,0:T(8,128)(2,1)S(1)}, bf16[288,256]{1,0:T(8,128)(2,1)S(1)}, u32[]{:S(2)}, u32[]{:S(2)}) %collective-permute-start.15) | collective-permute-done | bytes 147488 | tf_op jit(solution)/shard_map/ppermute | solution.py:584
  179.0 3.7 %all-to-all-start.4 = ((bf16[32,8,256]{2,1,0:T(8,128)(2,1)}), bf16[32,8,256]{2,1,0:T(8,128)(2,1)S(1)}, u32[]{:S(2)}, u32[]{:S(2)}) async-start(bf16[32,8,256]{2,1,0:T(8,128)(2,1)} %bitcast.20), calls=%async_computation.4 | async-start | bytes 262144 | tf_op jit(solution)/shard_map/all_to_all | solution.py:643
  182.8 2.2 %collective-permute-start.6 = (bf16[64,256]{1,0:T(8,128)(2,1)S(1)}, bf16[64,256]{1,0:T(8,128)(2,1)S(1)}, u32[]{:S(2)}, u32[]{:S(2)}) collective-permute-start(bf16[64,256]{1,0:T(8,128)(2,1)S(1)} %get-tuple-element.60), channel_id=1, source_target_pairs={{0,1},{1,2},{2,3},{3,4},{4,5},{5,6},{6,7},{8,9},{9,10},{10,11},{11... | collective-permute-start | bytes 98312 | tf_op jit(solution)/shard_map/ppermute | solution.py:580
  186.2 2.9 %collective-permute-done.7.refs_4_.refs_5_ = bf16[64,256]{1,0:T(8,128)(2,1)S(1)} collective-permute-done((bf16[64,256]{1,0:T(8,128)(2,1)S(1)}, bf16[64,256]{1,0:T(8,128)(2,1)S(1)}, u32[]{:S(2)}, u32[]{:S(2)}) %collective-permute-start.7) | collective-permute-done | bytes 32800 | tf_op jit(solution)/shard_map/ppermute | solution.py:580
  192.0 2.2 %shard_map.196 = bf16[1024,256]{1,0:T(8,128)(2,1)} custom-call(s32[1,256]{1,0:T(1,128)S(1)} %reshape.57.refs_0_, bf16[64,256]{1,0:T(8,128)(2,1)S(1)} %collective-permute-done.4.refs_1_.refs_2_, bf16[64,256]{1,0:T(8,128)(2,1)S(1)} %collective-permute-done.5.refs_2_.refs_3_, bf16[64,256]{1,0:T(8,128)(2,1)S(1)} %collective-permute-done.6.refs_3_.refs_4_, ...), custom_call_target="tpu_custom_call" | custom-call | flops 1000000000 | bytes 1704960 | tf_op jit(solution)/shard_map/pallas_call | solution.py:561
  (67 shorter events, 25.9 us)
Async XLA Ops:
  3.2 17.1 %collective-permute-start = (bf16[64,256]{1,0:T(8,128)(2,1)S(1)}, bf16[64,256]{1,0:T(8,128)(2,1)S(1)}, u32[]{:S(2)}, u32[]{:S(2)}) collective-permute-start(bf16[64,256]{1,0:T(8,128)(2,1)S(1)} %get-tuple-element.45), channel_id=1, source_target_pairs={{8,0},{16,8},{24,16},{9,1},{17,9},{25,17},{10,2},{18,10},{26,18},{... | collective-permute-start | bytes 98312 | tf_op jit(solution)/shard_map/ppermute | solution.py:580
  4.5 15.8 %collective-permute-start.1 = (bf16[64,256]{1,0:T(8,128)(2,1)S(1)}, bf16[64,256]{1,0:T(8,128)(2,1)S(1)}, u32[]{:S(2)}, u32[]{:S(2)}) collective-permute-start(bf16[64,256]{1,0:T(8,128)(2,1)S(1)} %get-tuple-element.46), channel_id=1, source_target_pairs={{0,8},{8,16},{16,24},{1,9},{9,17},{17,25},{2,10},{10,18},{18,26},{... | collective-permute-start | bytes 98312 | tf_op jit(solution)/shard_map/ppermute | solution.py:580
  10.1 10.3 %collective-permute-start.2 = (bf16[64,256]{1,0:T(8,128)(2,1)S(1)}, bf16[64,256]{1,0:T(8,128)(2,1)S(1)}, u32[]{:S(2)}, u32[]{:S(2)}) collective-permute-start(bf16[64,256]{1,0:T(8,128)(2,1)S(1)} %get-tuple-element.47), channel_id=1, source_target_pairs={{1,0},{2,1},{3,2},{4,3},{5,4},{6,5},{7,6},{9,8},{10,9},{11,10},{12... | collective-permute-start | bytes 98312 | tf_op jit(solution)/shard_map/ppermute | solution.py:580
  11.4 9.0 %collective-permute-start.3 = (bf16[64,256]{1,0:T(8,128)(2,1)S(1)}, bf16[64,256]{1,0:T(8,128)(2,1)S(1)}, u32[]{:S(2)}, u32[]{:S(2)}) collective-permute-start(bf16[64,256]{1,0:T(8,128)(2,1)S(1)} %get-tuple-element.48), channel_id=1, source_target_pairs={{0,1},{1,2},{2,3},{3,4},{4,5},{5,6},{6,7},{8,9},{9,10},{10,11},{11... | collective-permute-start | bytes 98312 | tf_op jit(solution)/shard_map/ppermute | solution.py:580
  24.7 54.4 %copy-start.3 = (bf16[256,1024]{1,0:T(8,128)(2,1)S(1)}, bf16[256,1024]{1,0:T(8,128)(2,1)}, u32[]{:S(2)}) copy-start(bf16[256,1024]{1,0:T(8,128)(2,1)} %refs_5_.3) | copy-start | bytes 1572868
  24.8 54.4 %all-to-all-start = ((bf16[32,64,512]{2,1,0:T(8,128)(2,1)}), bf16[32,64,512]{2,1,0:T(8,128)(2,1)}, u32[]{:S(2)}, u32[]{:S(2)}) async-start(bf16[32,64,512]{2,1,0:T(8,128)(2,1)} %bitcast.40), calls=%async_computation | async-start | bytes 4194304 | tf_op jit(solution)/shard_map/all_to_all | solution.py:643
  91.5 30.3 %all-to-all-start.1 = ((bf16[32,64,256]{2,1,0:T(8,128)(2,1)}), bf16[32,64,256]{2,1,0:T(8,128)(2,1)S(1)}, u32[]{:S(2)}, u32[]{:S(2)}) async-start(bf16[32,64,256]{2,1,0:T(8,128)(2,1)} %bitcast.41), calls=%async_computation.1 | async-start | bytes 2097152 | tf_op jit(solution)/shard_map/all_to_all | solution.py:643
  121.8 30.0 %all-to-all-start.2 = ((bf16[32,64,256]{2,1,0:T(8,128)(2,1)}), bf16[32,64,256]{2,1,0:T(8,128)(2,1)S(1)}, u32[]{:S(2)}, u32[]{:S(2)}) async-start(bf16[32,64,256]{2,1,0:T(8,128)(2,1)} %bitcast.39), calls=%async_computation.2 | async-start | bytes 2097152 | tf_op jit(solution)/shard_map/all_to_all | solution.py:643
  125.5 2.4 %collective-permute-start.8 = (bf16[1152,256]{1,0:T(8,128)(2,1)S(1)}, bf16[1152,256]{1,0:T(8,128)(2,1)S(1)}, u32[]{:S(2)}, u32[]{:S(2)}) collective-permute-start(bf16[1152,256]{1,0:T(8,128)(2,1)S(1)} %copy-done.12), channel_id=1, source_target_pairs={{0,1},{1,0},{2,3},{3,2},{4,5},{5,4},{6,7},{7,6},{8,9},{9,8},{10,11... | collective-permute-start | bytes 1769480 | tf_op jit(solution)/shard_map/ppermute | solution.py:584
  128.2 10.2 %collective-permute-start.10 = (bf16[288,256]{1,0:T(8,128)(2,1)S(1)}, bf16[288,256]{1,0:T(8,128)(2,1)S(1)}, u32[]{:S(2)}, u32[]{:S(2)}) collective-permute-start(bf16[288,256]{1,0:T(8,128)(2,1)S(1)} %get-tuple-element.68), channel_id=1, source_target_pairs={{0,4},{1,5},{2,6},{3,7},{4,0},{5,1},{6,2},{7,3},{8,12},{9,13},{10,... | collective-permute-start | bytes 442376 | tf_op jit(solution)/shard_map/ppermute | solution.py:584
  130.0 10.3 %collective-permute-start.9 = (bf16[288,256]{1,0:T(8,128)(2,1)S(1)}, bf16[288,256]{1,0:T(8,128)(2,1)S(1)}, u32[]{:S(2)}, u32[]{:S(2)}) collective-permute-start(bf16[288,256]{1,0:T(8,128)(2,1)S(1)} %get-tuple-element.66), channel_id=1, source_target_pairs={{0,2},{1,3},{2,0},{3,1},{4,6},{5,7},{6,4},{7,5},{8,10},{9,11},{10,... | collective-permute-start | bytes 442376 | tf_op jit(solution)/shard_map/ppermute | solution.py:584
  140.3 4.8 %collective-permute-start.11 = (bf16[144,256]{1,0:T(8,128)(2,1)S(1)}, bf16[144,256]{1,0:T(8,128)(2,1)S(1)}, u32[]{:S(2)}, u32[]{:S(2)}) collective-permute-start(bf16[144,256]{1,0:T(8,128)(2,1)S(1)} %get-tuple-element.70), channel_id=1, source_target_pairs={{0,4},{1,5},{2,6},{3,7},{4,0},{5,1},{6,2},{7,3},{8,12},{9,13},{10,... | collective-permute-start | bytes 221192 | tf_op jit(solution)/shard_map/ppermute | solution.py:584
  141.4 4.4 %collective-permute-start.12 = (bf16[144,256]{1,0:T(8,128)(2,1)S(1)}, bf16[144,256]{1,0:T(8,128)(2,1)S(1)}, u32[]{:S(2)}, u32[]{:S(2)}) collective-permute-start(bf16[144,256]{1,0:T(8,128)(2,1)S(1)} %get-tuple-element.72), channel_id=1, source_target_pairs={{0,2},{1,3},{2,0},{3,1},{4,6},{5,7},{6,4},{7,5},{8,10},{9,11},{10,... | collective-permute-start | bytes 221192 | tf_op jit(solution)/shard_map/ppermute | solution.py:584
  145.8 11.7 %collective-permute-start.13 = (bf16[288,256]{1,0:T(8,128)(2,1)S(1)}, bf16[288,256]{1,0:T(8,128)(2,1)S(1)}, u32[]{:S(2)}, u32[]{:S(2)}) collective-permute-start(bf16[288,256]{1,0:T(8,128)(2,1)S(1)} %shard_map.199.refs_0_), channel_id=1, source_target_pairs={{0,8},{8,0},{16,24},{24,16},{1,9},{9,1},{17,25},{25,17},{2,10},{10... | collective-permute-start | bytes 442376 | tf_op jit(solution)/shard_map/ppermute | solution.py:584
  157.6 14.6 %collective-permute-start.14 = (bf16[288,256]{1,0:T(8,128)(2,1)S(1)}, bf16[288,256]{1,0:T(8,128)(2,1)S(1)}, u32[]{:S(2)}, u32[]{:S(2)}) collective-permute-start(bf16[288,256]{1,0:T(8,128)(2,1)S(1)} %shard_map.200.refs_0_), channel_id=1, source_target_pairs={{0,16},{8,24},{16,0},{24,8},{1,17},{9,25},{17,1},{25,9},{2,18},{10... | collective-permute-start | bytes 442376 | tf_op jit(solution)/shard_map/ppermute | solution.py:584
  158.3 15.5 %all-to-all-start.3 = ((bf16[32,8,256]{2,1,0:T(8,128)(2,1)}), bf16[32,8,256]{2,1,0:T(8,128)(2,1)S(1)}, u32[]{:S(2)}, u32[]{:S(2)}) async-start(bf16[32,8,256]{2,1,0:T(8,128)(2,1)} %bitcast.18), calls=%async_computation.3 | async-start | bytes 262144 | tf_op jit(solution)/shard_map/all_to_all | solution.py:643
  162.7 5.3 %collective-permute-start.4 = (bf16[64,256]{1,0:T(8,128)(2,1)S(1)}, bf16[64,256]{1,0:T(8,128)(2,1)S(1)}, u32[]{:S(2)}, u32[]{:S(2)}) collective-permute-start(bf16[64,256]{1,0:T(8,128)(2,1)S(1)} %get-tuple-element.58), channel_id=1, source_target_pairs={{0,8},{8,16},{16,24},{1,9},{9,17},{17,25},{2,10},{10,18},{18,26},{... | collective-permute-start | bytes 98312 | tf_op jit(solution)/shard_map/ppermute | solution.py:580
  166.4 5.8 %collective-permute-start.5 = (bf16[64,256]{1,0:T(8,128)(2,1)S(1)}, bf16[64,256]{1,0:T(8,128)(2,1)S(1)}, u32[]{:S(2)}, u32[]{:S(2)}) collective-permute-start(bf16[64,256]{1,0:T(8,128)(2,1)S(1)} %get-tuple-element.59), channel_id=1, source_target_pairs={{8,0},{16,8},{24,16},{9,1},{17,9},{25,17},{10,2},{18,10},{26,18},{... | collective-permute-start | bytes 98312 | tf_op jit(solution)/shard_map/ppermute | solution.py:580
  172.3 5.2 %collective-permute-start.15 = (bf16[288,256]{1,0:T(8,128)(2,1)S(1)}, bf16[288,256]{1,0:T(8,128)(2,1)S(1)}, u32[]{:S(2)}, u32[]{:S(2)}) collective-permute-start(bf16[288,256]{1,0:T(8,128)(2,1)S(1)} %shard_map.201.refs_1_), channel_id=1, source_target_pairs={{0,4},{1,5},{2,6},{3,7},{4,0},{5,1},{6,2},{7,3},{8,12},{9,13},{10,... | collective-permute-start | bytes 442376 | tf_op jit(solution)/shard_map/ppermute | solution.py:584
  177.5 13.5 %collective-permute-start.16 = (bf16[576,256]{1,0:T(8,128)(2,1)S(1)}, bf16[576,256]{1,0:T(8,128)(2,1)S(1)}, u32[]{:S(2)}, u32[]{:S(2)}) collective-permute-start(bf16[576,256]{1,0:T(8,128)(2,1)S(1)} %shard_map.203.refs_1_), channel_id=1, source_target_pairs={{0,2},{1,3},{2,0},{3,1},{4,6},{5,7},{6,4},{7,5},{8,10},{9,11},{10,... | collective-permute-start | bytes 884744 | tf_op jit(solution)/shard_map/ppermute | solution.py:584
  179.0 12.0 %all-to-all-start.4 = ((bf16[32,8,256]{2,1,0:T(8,128)(2,1)}), bf16[32,8,256]{2,1,0:T(8,128)(2,1)S(1)}, u32[]{:S(2)}, u32[]{:S(2)}) async-start(bf16[32,8,256]{2,1,0:T(8,128)(2,1)} %bitcast.20), calls=%async_computation.4 | async-start | bytes 262144 | tf_op jit(solution)/shard_map/all_to_all | solution.py:643
  182.8 3.5 %collective-permute-start.6 = (bf16[64,256]{1,0:T(8,128)(2,1)S(1)}, bf16[64,256]{1,0:T(8,128)(2,1)S(1)}, u32[]{:S(2)}, u32[]{:S(2)}) collective-permute-start(bf16[64,256]{1,0:T(8,128)(2,1)S(1)} %get-tuple-element.60), channel_id=1, source_target_pairs={{0,1},{1,2},{2,3},{3,4},{4,5},{5,6},{6,7},{8,9},{9,10},{10,11},{11... | collective-permute-start | bytes 98312 | tf_op jit(solution)/shard_map/ppermute | solution.py:580
  184.9 4.2 %collective-permute-start.7 = (bf16[64,256]{1,0:T(8,128)(2,1)S(1)}, bf16[64,256]{1,0:T(8,128)(2,1)S(1)}, u32[]{:S(2)}, u32[]{:S(2)}) collective-permute-start(bf16[64,256]{1,0:T(8,128)(2,1)S(1)} %get-tuple-element.61), channel_id=1, source_target_pairs={{1,0},{2,1},{3,2},{4,3},{5,4},{6,5},{7,6},{9,8},{10,9},{11,10},{12... | collective-permute-start | bytes 98312 | tf_op jit(solution)/shard_map/ppermute | solution.py:580
  191.0 3.2 %collective-permute-start.17 = (bf16[1152,256]{1,0:T(8,128)(2,1)S(1)}, bf16[1152,256]{1,0:T(8,128)(2,1)S(1)}, u32[]{:S(2)}, u32[]{:S(2)}) collective-permute-start(bf16[1152,256]{1,0:T(8,128)(2,1)S(1)} %shard_map.204.refs_1_), channel_id=1, source_target_pairs={{0,1},{1,0},{2,3},{3,2},{4,5},{5,4},{6,7},{7,6},{8,9},{9,8},{10,11... | collective-permute-start | bytes 1769480 | tf_op jit(solution)/shard_map/ppermute | solution.py:584
  (12 other events, 343.2 us)

commit v7 on v6

--- a/solution.py
+++ b/solution.py
@@ -191,55 +191,68 @@
 
 def tile_back_kernel(
     slots_ref, back_ref, w_ref, table_in, average_in, pre_in,
-    row_out, near_ref, halo0, halo1, halo2, halo3,
-    row_ref, table_ref, average_ref, pre_ref, act_ref, spread_ref, sems, *, neighbours
+    lifted_out, spread_out, near_ref, halo0, halo1, halo2, halo3,
+    table_ref, average_ref, pre_ref, lifted_ref, act_ref, spread_ref, sems, *, neighbours
 ):
-    rows = row_ref.shape[0]
+    rows = lifted_ref.shape[0]
+    halo_rows = table_ref.shape[0]
     fetch_pre = pltpu.make_async_copy(pre_in, pre_ref, sems.at[0])
     fetch_average = pltpu.make_async_copy(average_in, average_ref, sems.at[1])
-    fetch_table = pltpu.make_async_copy(table_in, table_ref, sems.at[2])
-
-    def keep_row(start):
-        place = pl.ds(start, WIDE)
-        return pltpu.make_async_copy(row_ref.at[place], row_out.at[place], sems.at[3 + start // WIDE])
-
+    fetch_table = pltpu.make_async_copy(table_in.at[pl.ds(rows, halo_rows)], table_ref, sems.at[2])
     fetch_pre.start()
     fetch_average.start()
     fetch_table.start()
-    fetch_pre.wait()
+    keep_lifted = pltpu.make_async_copy(lifted_ref, lifted_out, sems.at[3])
+    keep_spread = pltpu.make_async_copy(spread_ref, spread_out, sems.at[4])
     for start in range(0, rows, CHUNK):
         column = column_of(slots_ref[:, start : start + CHUNK], CHUNK)
         wide = dot(pick_rows(column, back_ref.shape[0]), back_ref[...])
+        if start == 0:
+            fetch_pre.wait()
         for row in range(0, CHUNK, BLOCK):
             here = pl.ds(start + row, BLOCK)
             lifted_grad = wide[row : row + BLOCK]
-            row_ref[here, :] = lifted_grad
+            lifted_ref[here, :] = lifted_grad.astype(bf16)
             value = pre_ref[here, :]
             square, tangent = gelu_parts(value)
             act_ref[here, :] = (lifted_grad * slope_of(value, square, tangent)).astype(bf16)
+    keep_lifted.start()
+    spread_ref[...] = (dot(act_ref[...], w_ref[...], NT) * (1.0 / neighbours)).astype(bf16)
+    keep_spread.start()
     fetch_average.wait()
     near_ref[...] = dot(average_ref[...], act_ref[...]).astype(near_ref.dtype)
-    spread_ref[...] = (dot(act_ref[...], w_ref[...], NT) * (1.0 / neighbours)).astype(bf16)
     fetch_table.wait()
-    halo = dot(table_ref[rows:, :], spread_ref[...]).astype(bf16)
+    halo = dot(table_ref[...], spread_ref[...]).astype(bf16)
     size = halo0.shape[0]
     for direction, halo_ref in enumerate((halo0, halo1, halo2, halo3)):
         halo_ref[...] = halo[direction * size : (direction + 1) * size]
+    keep_lifted.wait()
+    keep_spread.wait()
+
+
+def finish_kernel(
+    lists_ref, back0, back1, back2, back3, table_in, spread_in, lifted_in,
+    out_ref, table_ref, spread_ref, lifted_ref, sems
+):
+    rows = out_ref.shape[0]
+    fetch_spread = pltpu.make_async_copy(spread_in, spread_ref, sems.at[0])
+    fetch_table = pltpu.make_async_copy(table_in.at[pl.ds(0, rows)], table_ref, sems.at[1])
+    fetch_lifted = pltpu.make_async_copy(lifted_in, lifted_ref, sems.at[2])
+    fetch_spread.start()
+    fetch_table.start()
+    fetch_lifted.start()
+    came = jnp.concatenate([back0[...], back1[...], back2[...], back3[...]], axis=0)
+    returned = dot(chosen_rows(lists_ref, 0, rows), came)
+    fetch_spread.wait()
+    fetch_table.wait()
+    fetch_lifted.wait()
     for start in range(0, rows, WIDE):
         here = pl.ds(start, WIDE)
-        row_ref[here, :] = row_ref[here, :] + dot(table_ref[here, :], spread_ref[...])
-        keep_row(start).start()
-    for start in range(0, rows, WIDE):
-        keep_row(start).wait()
-
-
-def finish_kernel(lists_ref, back0, back1, back2, back3, row_in, out_ref, row_ref, sems):
-    fetch = pltpu.make_async_copy(row_in, row_ref, sems.at[0])
-    fetch.start()
-    came = jnp.concatenate([back0[...], back1[...], back2[...], back3[...]], axis=0)
-    total = dot(chosen_rows(lists_ref, 0, row_ref.shape[0]), came)
-    fetch.wait()
-    out_ref[...] = (row_ref[...] + total).astype(bf16)
+        out_ref[here, :] = (
+            lifted_ref[here, :].astype(f32)
+            + dot(table_ref[here, :], spread_ref[...])
+            + returned[start : start + WIDE]
+        ).astype(bf16)
 
 
 def near_sum_kernel(parts_ref, share_ref, *, share):
@@ -275,57 +288,70 @@
     fetch.start()
     hidden_width = up_ref.shape[1]
     taps_ref[...] = full_taps(conv_ref, groups, inner)
-    padded_zeros(before_ref)
-    padded_zeros(after_ref)
 
     def keep(at):
-        place = pl.ds(pl.multiple_of(at * PATCH, PATCH), PATCH)
+        place = pl.ds(at * PATCH, PATCH)
         return (
             pltpu.make_async_copy(serial_ref.at[place], serial_out.at[place], sems.at[0, at]),
             pltpu.make_async_copy(state_ref.at[place], state_out.at[place], sems.at[1, at]),
         )
 
-    def patch(at, _):
-        origin = pl.multiple_of(at * PATCH, PATCH)
+    def patch(at):
+        origin = at * PATCH
+        normed_at, second_at, hidden_at = normed_ref.at[at], second_ref.at[at], hidden_ref.at[at]
+        before_at, here_at, after_at = before_ref.at[at], here_ref.at[at], after_ref.at[at]
+        padded_zeros(before_at)
+        padded_zeros(after_at)
         for start in range(0, PATCH, WIDE):
-            column = column_of(zorder_ref[:, pl.ds(origin + start, WIDE)], WIDE)
+            column = column_of(zorder_ref[:, origin + start : origin + start + WIDE], WIDE)
             wide = dot(pick_rows(column, slots), lifted_ref[...])
             for row in range(0, WIDE, BLOCK):
                 serial = wide[row : row + BLOCK]
                 serial_ref[pl.ds(origin + start + row, BLOCK), :] = serial.astype(bf16)
                 normed = serial * inverse_rms(serial) * gain_one_ref[...]
-                normed_ref[pl.ds(start + row, BLOCK), :] = normed.astype(bf16)
-        before_ref[pl.ds(PAD, PATCH), :] = dot(normed_ref[...], taps_ref[0:width, :])
-        here_ref[...] = dot(normed_ref[...], taps_ref[width : 2 * width, :])
-        after_ref[pl.ds(PAD, PATCH), :] = dot(normed_ref[...], taps_ref[2 * width :, :])
+                normed_at[pl.ds(start + row, BLOCK), :] = normed.astype(bf16)
+            yield
+        before_at[pl.ds(PAD, PATCH), :] = dot(normed_at[...], taps_ref[0:width, :])
+        here_at[...] = dot(normed_at[...], taps_ref[width : 2 * width, :])
+        after_at[pl.ds(PAD, PATCH), :] = dot(normed_at[...], taps_ref[2 * width :, :])
+        yield
         for row in range(0, PATCH, BLOCK):
             place = pl.ds(origin + row, BLOCK)
             state = serial_ref[place, :].astype(f32) + (
-                before_ref[pl.ds(PAD + row - 1, BLOCK), :]
-                + here_ref[pl.ds(row, BLOCK), :]
-                + after_ref[pl.ds(PAD + row + 1, BLOCK), :]
+                before_at[pl.ds(PAD + row - 1, BLOCK), :]
+                + here_at[pl.ds(row, BLOCK), :]
+                + after_at[pl.ds(PAD + row + 1, BLOCK), :]
             )
             state_ref[place, :] = state
             second = state * inverse_rms(state) * gain_two_ref[...]
-            second_ref[pl.ds(row, BLOCK), :] = second.astype(bf16)
+            second_at[pl.ds(row, BLOCK), :] = second.astype(bf16)
         for copy in keep(at):
             copy.start()
+        yield
         for start in range(0, PATCH, CHUNK):
-            value = dot(second_ref[pl.ds(start, CHUNK), :], up_ref[...])
+            value = dot(second_at[pl.ds(start, CHUNK), :], up_ref[...])
             for row in range(0, CHUNK, 16):
                 for col in range(0, hidden_width, 2 * LANES):
-                    hidden_ref[pl.ds(start + row, 16), pl.ds(col, 2 * LANES)] = gelu_tanh(
+                    hidden_at[pl.ds(start + row, 16), pl.ds(col, 2 * LANES)] = gelu_tanh(
                         value[row : row + 16, col : col + 2 * LANES]
                     ).astype(bf16)
+            if start + CHUNK == PATCH // 2:
+                yield
+        yield
         for start in range(0, PATCH, WIDE):
             place = pl.ds(origin + start, WIDE)
             result_ref[place, :] = (
-                state_ref[place, :] + dot(hidden_ref[pl.ds(start, WIDE), :], down_ref[...])
+                state_ref[place, :] + dot(hidden_at[pl.ds(start, WIDE), :], down_ref[...])
             ).astype(bf16)
-        return 0
+        yield
 
     fetch.wait()
-    lax.fori_loop(0, slots // PATCH, patch, 0)
+    waiting = [patch(at) for at in range(slots // PATCH)]
+    running = []
+    while waiting or running:
+        if waiting:
+            running.append(waiting.pop(0))
+        running = [work for work in running if next(work, work) is not work]
     pack_rows(zorder_ref, result_ref, back_out, stage_ref, pack_sems)
     for at in range(slots // PATCH):
         for copy in keep(at):
@@ -726,6 +752,7 @@
         neighbours=neighbours,
     )
     came = exchange(packed, tiles)
+    patches = slots_count // PATCH
     patch_scratch = [
         pltpu.VMEM((PATCH + 2 * PAD, width), f32),
         pltpu.VMEM((PATCH, width), f32),
@@ -745,17 +772,19 @@
             pltpu.VMEM((slots_count, width), bf16),
             pltpu.VMEM((slots_count, width), f32),
             pltpu.VMEM((taps * width, width), bf16),
-            pltpu.VMEM((PATCH, width), bf16),
-            *patch_scratch,
-            pltpu.VMEM((PATCH, width), bf16),
-            pltpu.VMEM((PATCH, hidden), bf16),
+            pltpu.VMEM((patches, PATCH, width), bf16),
+            pltpu.VMEM((patches, PATCH + 2 * PAD, width), f32),
+            pltpu.VMEM((patches, PATCH, width), f32),
+            pltpu.VMEM((patches, PATCH + 2 * PAD, width), f32),
+            pltpu.VMEM((patches, PATCH, width), bf16),
+            pltpu.VMEM((patches, PATCH, hidden), bf16),
             pltpu.VMEM((slots_count, width), bf16),
             pltpu.VMEM((slots_count, width), bf16),
             pltpu.SemaphoreType.DMA((3, slots_count // PATCH)),
             pltpu.SemaphoreType.DMA((slots_count // WIDE,)),
         ],
         flops=10e9,
-        limit=32,
+        limit=44,
         stored=3,
         groups=groups,
         inner=inner,
@@ -826,25 +855,25 @@
     (out_rows,) = call(
         unpack_kernel, [shaped(tile_rows, width)], [slots, came_result], flops=4e9
     )
-    row_grad, near_grad, *halo_grad = call(
+    lifted_grad, spread, near_grad, *halo_grad = call(
         tile_back_kernel,
-        [shaped(tile_rows, width, dtype=f32), shaped(width, width)]
+        [shaped(tile_rows, width), shaped(tile_rows, width), shaped(width, width)]
         + [shaped(border_rows, width)] * 4,
         [slots, came_back, w_near, kept_table, average, pre_act],
         after=[out_rows],
         scratch=[
-            pltpu.VMEM((tile_rows, width), f32),
-            pltpu.VMEM((ext, tile_rows), bf16),
+            pltpu.VMEM((edge, tile_rows), bf16),
             pltpu.VMEM((width, tile_rows), bf16),
             pltpu.VMEM((tile_rows, width), f32),
             pltpu.VMEM((tile_rows, width), bf16),
             pltpu.VMEM((tile_rows, width), bf16),
-            pltpu.SemaphoreType.DMA((3 + tile_rows // WIDE,)),
+            pltpu.VMEM((tile_rows, width), bf16),
+            pltpu.SemaphoreType.DMA((5,)),
         ],
         flops=6e9,
         limit=24,
         held=3,
-        stored=1,
+        stored=2,
         neighbours=neighbours,
     )
     returned = [
@@ -868,9 +897,14 @@
     (grad_points,) = call(
         finish_kernel,
         [shaped(tile_rows, width)],
-        [border.reshape(1, edge), *returned, row_grad],
-        scratch=[pltpu.VMEM((tile_rows, width), f32), pltpu.SemaphoreType.DMA((1,))],
-        held=1,
+        [border.reshape(1, edge), *returned, kept_table, spread, lifted_grad],
+        scratch=[
+            pltpu.VMEM((tile_rows, tile_rows), bf16),
+            pltpu.VMEM((tile_rows, width), bf16),
+            pltpu.VMEM((tile_rows, width), bf16),
+            pltpu.SemaphoreType.DMA((3,)),
+        ],
+        held=3,
         flops=1e9,
     )
     scale = 1.0 / math.sqrt(tiles * tile_rows)

time: 197 us -> 197 us (level)
  no operation moved by 1% of the time
where the time goes in v7:
time: 197 us; the launch traced here: 196 us
  waiting for transfers between devices  80.4 us (41%)
  Pallas kernels  61.7 us (31%)
  starting transfers between devices  52 us (26%)
    pallas_call x18, Pallas kernels, call(): pl.pallas_call(run, out_shape=tuple(shapes), in_specs=specs, out_specs=tu...  61.7 us
    all_to_all x5, waiting for transfers between devices, exchange(): lax.all_to_all(rows, ('tx', 'ty'), split_axis=0, concat_axis=0, tiled=True)  57.7 us
    all_to_all x5, starting transfers between devices, exchange(): lax.all_to_all(rows, ('tx', 'ty'), split_axis=0, concat_axis=0, tiled=True)  21.7 us
    ppermute x8, starting transfers between devices, shifted(): lax.ppermute(value, axis, [(source, source + steps) for source in range(i...  19.6 us
    ppermute x10, waiting for transfers between devices, partner(): lax.ppermute(value, axis, [(at, at ^ step) for at in range(lax.axis_size(...  15.3 us
    ppermute x10, starting transfers between devices, partner(): lax.ppermute(value, axis, [(at, at ^ step) for at in range(lax.axis_size(...  10.8 us
    ppermute x8, waiting for transfers between devices, shifted(): lax.ppermute(value, axis, [(source, source + steps) for source in range(i...  7.45 us
  transfers between devices with their start and end apart: 23, of which 12 were waited for; matrix products, arithmetic and copies ran while one was open for 0% of the time, Pallas kernels for 21%

profile of v7, /device:TPU:0, one launch (start us, length us, event | category | flops | bytes accessed | tf_op | source)
XLA Modules:
  0.0 196.0 jit_solution(5912664008984659195)
XLA Ops:
  4.5 5.6 %collective-permute-start.1 = (bf16[64,256]{1,0:T(8,128)(2,1)S(1)}, bf16[64,256]{1,0:T(8,128)(2,1)S(1)}, u32[]{:S(2)}, u32[]{:S(2)}) collective-permute-start(bf16[64,256]{1,0:T(8,128)(2,1)S(1)} %get-tuple-element.47), channel_id=1, source_target_pairs={{0,8},{8,16},{16,24},{1,9},{9,17},{17,25},{2,10},{10,18},{18,26},{... | collective-permute-start | bytes 98312 | tf_op jit(solution)/shard_map/ppermute | solution.py:606
  11.4 3.0 %collective-permute-start.3 = (bf16[64,256]{1,0:T(8,128)(2,1)S(1)}, bf16[64,256]{1,0:T(8,128)(2,1)S(1)}, u32[]{:S(2)}, u32[]{:S(2)}) collective-permute-start(bf16[64,256]{1,0:T(8,128)(2,1)S(1)} %get-tuple-element.49), channel_id=1, source_target_pairs={{0,1},{1,2},{2,3},{3,4},{4,5},{5,6},{6,7},{8,9},{9,10},{10,11},{11... | collective-permute-start | bytes 98312 | tf_op jit(solution)/shard_map/ppermute | solution.py:606
  14.4 5.8 %shard_map.189 = (bf16[1280,1024]{1,0:T(8,128)(2,1)}, bf16[1280,1024]{1,0:T(8,128)(2,1)S(1)}) custom-call(s32[16,1024]{1,0:T(8,128)S(1)} %bitcast.34), custom_call_target="tpu_custom_call" | custom-call | flops 8000000000 | bytes 5308416 | tf_op jit(solution)/shard_map/pallas_call | solution.py:587
  20.4 4.3 %shard_map.190 = (bf16[256,1024]{1,0:T(8,128)(2,1)}, f32[1024,256]{1,0:T(8,128)}, bf16[2048,512]{1,0:T(8,128)(2,1)}) custom-call(s32[1,1024]{1,0:T(1,128)S(1)} %get-tuple-element.45.refs_0_, bf16[1024,256]{1,0:T(8,128)(2,1)S(1)} %bitcast.30, bf16[1024,256]{1,0:T(8,128)(2,1)S(1)} %bitcast.31, bf16[64,256]{1,0:T(8,128)(2,1)S(1)} %collective-permute-done.refs_3_, ...), custom_call_target="tpu_custom_call" | custom-call | flops 4000000000 | bytes 7606272 | tf_op jit(solution)/shard_map/pallas_call | solution.py:587
  24.8 5.7 %all-to-all-start = ((bf16[32,64,512]{2,1,0:T(8,128)(2,1)}), bf16[32,64,512]{2,1,0:T(8,128)(2,1)}, u32[]{:S(2)}, u32[]{:S(2)}) async-start(bf16[32,64,512]{2,1,0:T(8,128)(2,1)} %bitcast.40), calls=%async_computation | async-start | bytes 4194304 | tf_op jit(solution)/shard_map/all_to_all | solution.py:669
  30.4 48.7 %all-to-all-done = bf16[32,64,512]{2,1,0:T(8,128)(2,1)} async-done(((bf16[32,64,512]{2,1,0:T(8,128)(2,1)}), bf16[32,64,512]{2,1,0:T(8,128)(2,1)}, u32[]{:S(2)}, u32[]{:S(2)}) %all-to-all-start) | async-done | bytes 2097184 | tf_op jit(solution)/shard_map/all_to_all | solution.py:669
  79.2 11.9 %shard_map.191 = (bf16[2048,256]{1,0:T(8,128)(2,1)}, f32[2048,256]{1,0:T(8,128)}, bf16[2048,256]{1,0:T(8,128)(2,1)}) custom-call(s32[1,2048]{1,0:T(1,128)S(1)} %copy-done.8, bf16[768,32]{1,0:T(8,128)(2,1)S(1)} %bitcast.32, f32[1,256]{1,0:T(1,128)S(1)} %bitcast.35, f32[1,256]{1,0:T(1,128)S(1)} %bitcast.37, bf16[256,1024]{1,0:T(8,128)(2,1)S(1)} %copy-done.3, ...), custom_call_target="tpu_custom_call" | custom-call | flops 10000000000 | bytes 7399424 | tf_op jit(solution)/shard_map/pallas_call | solution.py:587
  91.2 4.2 %all-to-all-start.1 = ((bf16[32,64,256]{2,1,0:T(8,128)(2,1)}), bf16[32,64,256]{2,1,0:T(8,128)(2,1)S(1)}, u32[]{:S(2)}, u32[]{:S(2)}) async-start(bf16[32,64,256]{2,1,0:T(8,128)(2,1)} %bitcast.41), calls=%async_computation.1 | async-start | bytes 2097152 | tf_op jit(solution)/shard_map/all_to_all | solution.py:669
  95.4 24.0 %shard_map.193 = (bf16[2048,256]{1,0:T(8,128)(2,1)}, bf16[1152,256]{1,0:T(8,128)(2,1)}, bf16[1152,256]{1,0:T(8,128)(2,1)}) custom-call(s32[1]{0:T(128)} %bitcast.12.refs_0_, s32[1,2048]{1,0:T(1,128)S(1)} %copy-done.8, bf16[768,32]{1,0:T(8,128)(2,1)S(1)} %bitcast.33, f32[1,256]{1,0:T(1,128)S(1)} %bitcast.36, f32[1,256]{1,0:T(1,128)S(1)} %bitcast.38, ...), custom_call_target="tpu_custom_call" | custom-call | flops 40000000000 | bytes 8579076 | tf_op jit(solution)/shard_map/pallas_call | solution.py:587
  119.4 2.0 %all-to-all-done.1.refs_1_ = bf16[32,64,256]{2,1,0:T(8,128)(2,1)S(1)} async-done(((bf16[32,64,256]{2,1,0:T(8,128)(2,1)}), bf16[32,64,256]{2,1,0:T(8,128)(2,1)S(1)}, u32[]{:S(2)}, u32[]{:S(2)}) %all-to-all-start.1) | async-done | bytes 1048608 | tf_op jit(solution)/shard_map/all_to_all | solution.py:669
  121.4 3.7 %all-to-all-start.2 = ((bf16[32,64,256]{2,1,0:T(8,128)(2,1)}), bf16[32,64,256]{2,1,0:T(8,128)(2,1)S(1)}, u32[]{:S(2)}, u32[]{:S(2)}) async-start(bf16[32,64,256]{2,1,0:T(8,128)(2,1)} %bitcast.39), calls=%async_computation.2 | async-start | bytes 2097152 | tf_op jit(solution)/shard_map/all_to_all | solution.py:669
  125.4 2.1 %shard_map.192.refs_6_.refs_4_ = bf16[1024,256]{1,0:T(8,128)(2,1)} custom-call(s32[1,1024]{1,0:T(1,128)S(1)} %get-tuple-element.45.refs_0_, bf16[2048,256]{1,0:T(8,128)(2,1)S(1)} %bitcast.24), custom_call_target="tpu_custom_call" | custom-call | flops 4000000000 | bytes 1576960 | tf_op jit(solution)/shard_map/pallas_call | solution.py:587
  131.0 7.0 %collective-permute-done.10.refs_5_ = bf16[288,256]{1,0:T(8,128)(2,1)S(1)} collective-permute-done((bf16[288,256]{1,0:T(8,128)(2,1)S(1)}, bf16[288,256]{1,0:T(8,128)(2,1)S(1)}, u32[]{:S(2)}, u32[]{:S(2)}) %collective-permute-start.10) | collective-permute-done | bytes 147488 | tf_op jit(solution)/shard_map/ppermute | solution.py:610
  141.7 3.0 %collective-permute-done.11.refs_1_ = bf16[144,256]{1,0:T(8,128)(2,1)S(1)} collective-permute-done((bf16[144,256]{1,0:T(8,128)(2,1)S(1)}, bf16[144,256]{1,0:T(8,128)(2,1)S(1)}, u32[]{:S(2)}, u32[]{:S(2)}) %collective-permute-start.11) | collective-permute-done | bytes 73760 | tf_op jit(solution)/shard_map/ppermute | solution.py:610
  146.2 5.2 %all-to-all-done.2 = bf16[32,64,256]{2,1,0:T(8,128)(2,1)S(1)} async-done(((bf16[32,64,256]{2,1,0:T(8,128)(2,1)}), bf16[32,64,256]{2,1,0:T(8,128)(2,1)S(1)}, u32[]{:S(2)}, u32[]{:S(2)}) %all-to-all-start.2) | async-done | bytes 1048608 | tf_op jit(solution)/shard_map/all_to_all | solution.py:669
  151.4 4.6 %shard_map.195 = (bf16[1024,256]{1,0:T(8,128)(2,1)}, bf16[1024,256]{1,0:T(8,128)(2,1)}, bf16[256,256]{1,0:T(8,128)(2,1)}, bf16[64,256]{1,0:T(8,128)(2,1)S(1)}, b...) custom-call(s32[1,1024]{1,0:T(1,128)S(1)} %get-tuple-element.45.refs_0_, ...), custom_call_target="tpu_custom_call" | custom-call | flops 6000000000 | bytes 6688768 | tf_op jit(solution)/shard_map/pallas_call | solution.py:587
  156.8 4.4 %all-to-all-start.3 = ((bf16[32,8,256]{2,1,0:T(8,128)(2,1)}), bf16[32,8,256]{2,1,0:T(8,128)(2,1)S(1)}, u32[]{:S(2)}, u32[]{:S(2)}) async-start(bf16[32,8,256]{2,1,0:T(8,128)(2,1)} %bitcast.18), calls=%async_computation.3 | async-start | bytes 262144 | tf_op jit(solution)/shard_map/all_to_all | solution.py:669
  161.2 3.7 %collective-permute-start.4 = (bf16[64,256]{1,0:T(8,128)(2,1)S(1)}, bf16[64,256]{1,0:T(8,128)(2,1)S(1)}, u32[]{:S(2)}, u32[]{:S(2)}) collective-permute-start(bf16[64,256]{1,0:T(8,128)(2,1)S(1)} %get-tuple-element.59), channel_id=1, source_target_pairs={{0,8},{8,16},{16,24},{1,9},{9,17},{17,25},{2,10},{10,18},{18,26},{... | collective-permute-start | bytes 98312 | tf_op jit(solution)/shard_map/ppermute | solution.py:606
  166.5 4.2 %collective-permute-done.5.refs_2_.refs_3_ = bf16[64,256]{1,0:T(8,128)(2,1)S(1)} collective-permute-done((bf16[64,256]{1,0:T(8,128)(2,1)S(1)}, bf16[64,256]{1,0:T(8,128)(2,1)S(1)}, u32[]{:S(2)}, u32[]{:S(2)}) %collective-permute-start.5) | collective-permute-done | bytes 32800 | tf_op jit(solution)/shard_map/ppermute | solution.py:606
  173.2 2.8 %collective-permute-done.15.refs_2_ = bf16[288,256]{1,0:T(8,128)(2,1)S(1)} collective-permute-done((bf16[288,256]{1,0:T(8,128)(2,1)S(1)}, bf16[288,256]{1,0:T(8,128)(2,1)S(1)}, u32[]{:S(2)}, u32[]{:S(2)}) %collective-permute-start.15) | collective-permute-done | bytes 147488 | tf_op jit(solution)/shard_map/ppermute | solution.py:610
  177.5 3.7 %all-to-all-start.4 = ((bf16[32,8,256]{2,1,0:T(8,128)(2,1)}), bf16[32,8,256]{2,1,0:T(8,128)(2,1)S(1)}, u32[]{:S(2)}, u32[]{:S(2)}) async-start(bf16[32,8,256]{2,1,0:T(8,128)(2,1)} %bitcast.20), calls=%async_computation.4 | async-start | bytes 262144 | tf_op jit(solution)/shard_map/all_to_all | solution.py:669
  181.3 2.2 %collective-permute-start.6 = (bf16[64,256]{1,0:T(8,128)(2,1)S(1)}, bf16[64,256]{1,0:T(8,128)(2,1)S(1)}, u32[]{:S(2)}, u32[]{:S(2)}) collective-permute-start(bf16[64,256]{1,0:T(8,128)(2,1)S(1)} %get-tuple-element.61), channel_id=1, source_target_pairs={{0,1},{1,2},{2,3},{3,4},{4,5},{5,6},{6,7},{8,9},{9,10},{10,11},{11... | collective-permute-start | bytes 98312 | tf_op jit(solution)/shard_map/ppermute | solution.py:606
  184.8 2.9 %collective-permute-done.7.refs_4_.refs_5_ = bf16[64,256]{1,0:T(8,128)(2,1)S(1)} collective-permute-done((bf16[64,256]{1,0:T(8,128)(2,1)S(1)}, bf16[64,256]{1,0:T(8,128)(2,1)S(1)}, u32[]{:S(2)}, u32[]{:S(2)}) %collective-permute-start.7) | collective-permute-done | bytes 32800 | tf_op jit(solution)/shard_map/ppermute | solution.py:606
  190.5 3.6 %shard_map.196 = bf16[1024,256]{1,0:T(8,128)(2,1)} custom-call(s32[1,256]{1,0:T(1,128)S(1)} %reshape.57.refs_0_, bf16[64,256]{1,0:T(8,128)(2,1)S(1)} %collective-permute-done.4.refs_1_.refs_2_, bf16[64,256]{1,0:T(8,128)(2,1)S(1)} %collective-permute-done.5.refs_2_.refs_3_, bf16[64,256]{1,0:T(8,128)(2,1)S(1)} %collective-permute-done.6.refs_3_.refs_4_, ...), custom_call_target="tpu_custom_call" | custom-call | flops 1000000000 | bytes 4326400 | tf_op jit(solution)/shard_map/pallas_call | solution.py:587
  (67 shorter events, 25.9 us)
Async XLA Ops:
  3.2 17.1 %collective-permute-start = (bf16[64,256]{1,0:T(8,128)(2,1)S(1)}, bf16[64,256]{1,0:T(8,128)(2,1)S(1)}, u32[]{:S(2)}, u32[]{:S(2)}) collective-permute-start(bf16[64,256]{1,0:T(8,128)(2,1)S(1)} %get-tuple-element.46), channel_id=1, source_target_pairs={{8,0},{16,8},{24,16},{9,1},{17,9},{25,17},{10,2},{18,10},{26,18},{... | collective-permute-start | bytes 98312 | tf_op jit(solution)/shard_map/ppermute | solution.py:606
  4.5 15.8 %collective-permute-start.1 = (bf16[64,256]{1,0:T(8,128)(2,1)S(1)}, bf16[64,256]{1,0:T(8,128)(2,1)S(1)}, u32[]{:S(2)}, u32[]{:S(2)}) collective-permute-start(bf16[64,256]{1,0:T(8,128)(2,1)S(1)} %get-tuple-element.47), channel_id=1, source_target_pairs={{0,8},{8,16},{16,24},{1,9},{9,17},{17,25},{2,10},{10,18},{18,26},{... | collective-permute-start | bytes 98312 | tf_op jit(solution)/shard_map/ppermute | solution.py:606
  10.1 10.3 %collective-permute-start.2 = (bf16[64,256]{1,0:T(8,128)(2,1)S(1)}, bf16[64,256]{1,0:T(8,128)(2,1)S(1)}, u32[]{:S(2)}, u32[]{:S(2)}) collective-permute-start(bf16[64,256]{1,0:T(8,128)(2,1)S(1)} %get-tuple-element.48), channel_id=1, source_target_pairs={{1,0},{2,1},{3,2},{4,3},{5,4},{6,5},{7,6},{9,8},{10,9},{11,10},{12... | collective-permute-start | bytes 98312 | tf_op jit(solution)/shard_map/ppermute | solution.py:606
  11.4 9.0 %collective-permute-start.3 = (bf16[64,256]{1,0:T(8,128)(2,1)S(1)}, bf16[64,256]{1,0:T(8,128)(2,1)S(1)}, u32[]{:S(2)}, u32[]{:S(2)}) collective-permute-start(bf16[64,256]{1,0:T(8,128)(2,1)S(1)} %get-tuple-element.49), channel_id=1, source_target_pairs={{0,1},{1,2},{2,3},{3,4},{4,5},{5,6},{6,7},{8,9},{9,10},{10,11},{11... | collective-permute-start | bytes 98312 | tf_op jit(solution)/shard_map/ppermute | solution.py:606
  24.7 54.5 %copy-start.3 = (bf16[256,1024]{1,0:T(8,128)(2,1)S(1)}, bf16[256,1024]{1,0:T(8,128)(2,1)}, u32[]{:S(2)}) copy-start(bf16[256,1024]{1,0:T(8,128)(2,1)} %refs_5_.3) | copy-start | bytes 1572868
  24.8 54.4 %all-to-all-start = ((bf16[32,64,512]{2,1,0:T(8,128)(2,1)}), bf16[32,64,512]{2,1,0:T(8,128)(2,1)}, u32[]{:S(2)}, u32[]{:S(2)}) async-start(bf16[32,64,512]{2,1,0:T(8,128)(2,1)} %bitcast.40), calls=%async_computation | async-start | bytes 4194304 | tf_op jit(solution)/shard_map/all_to_all | solution.py:669
  91.2 30.2 %all-to-all-start.1 = ((bf16[32,64,256]{2,1,0:T(8,128)(2,1)}), bf16[32,64,256]{2,1,0:T(8,128)(2,1)S(1)}, u32[]{:S(2)}, u32[]{:S(2)}) async-start(bf16[32,64,256]{2,1,0:T(8,128)(2,1)} %bitcast.41), calls=%async_computation.1 | async-start | bytes 2097152 | tf_op jit(solution)/shard_map/all_to_all | solution.py:669
  121.4 30.0 %all-to-all-start.2 = ((bf16[32,64,256]{2,1,0:T(8,128)(2,1)}), bf16[32,64,256]{2,1,0:T(8,128)(2,1)S(1)}, u32[]{:S(2)}, u32[]{:S(2)}) async-start(bf16[32,64,256]{2,1,0:T(8,128)(2,1)} %bitcast.39), calls=%async_computation.2 | async-start | bytes 2097152 | tf_op jit(solution)/shard_map/all_to_all | solution.py:669
  125.1 2.4 %collective-permute-start.8 = (bf16[1152,256]{1,0:T(8,128)(2,1)S(1)}, bf16[1152,256]{1,0:T(8,128)(2,1)S(1)}, u32[]{:S(2)}, u32[]{:S(2)}) collective-permute-start(bf16[1152,256]{1,0:T(8,128)(2,1)S(1)} %copy-done.12), channel_id=1, source_target_pairs={{0,1},{1,0},{2,3},{3,2},{4,5},{5,4},{6,7},{7,6},{8,9},{9,8},{10,11... | collective-permute-start | bytes 1769480 | tf_op jit(solution)/shard_map/ppermute | solution.py:610
  127.8 10.2 %collective-permute-start.10 = (bf16[288,256]{1,0:T(8,128)(2,1)S(1)}, bf16[288,256]{1,0:T(8,128)(2,1)S(1)}, u32[]{:S(2)}, u32[]{:S(2)}) collective-permute-start(bf16[288,256]{1,0:T(8,128)(2,1)S(1)} %get-tuple-element.70), channel_id=1, source_target_pairs={{0,4},{1,5},{2,6},{3,7},{4,0},{5,1},{6,2},{7,3},{8,12},{9,13},{10,... | collective-permute-start | bytes 442376 | tf_op jit(solution)/shard_map/ppermute | solution.py:610
  129.6 10.3 %collective-permute-start.9 = (bf16[288,256]{1,0:T(8,128)(2,1)S(1)}, bf16[288,256]{1,0:T(8,128)(2,1)S(1)}, u32[]{:S(2)}, u32[]{:S(2)}) collective-permute-start(bf16[288,256]{1,0:T(8,128)(2,1)S(1)} %get-tuple-element.68), channel_id=1, source_target_pairs={{0,2},{1,3},{2,0},{3,1},{4,6},{5,7},{6,4},{7,5},{8,10},{9,11},{10,... | collective-permute-start | bytes 442376 | tf_op jit(solution)/shard_map/ppermute | solution.py:610
  140.0 4.8 %collective-permute-start.11 = (bf16[144,256]{1,0:T(8,128)(2,1)S(1)}, bf16[144,256]{1,0:T(8,128)(2,1)S(1)}, u32[]{:S(2)}, u32[]{:S(2)}) collective-permute-start(bf16[144,256]{1,0:T(8,128)(2,1)S(1)} %get-tuple-element.72), channel_id=1, source_target_pairs={{0,4},{1,5},{2,6},{3,7},{4,0},{5,1},{6,2},{7,3},{8,12},{9,13},{10,... | collective-permute-start | bytes 221192 | tf_op jit(solution)/shard_map/ppermute | solution.py:610
  141.1 4.4 %collective-permute-start.12 = (bf16[144,256]{1,0:T(8,128)(2,1)S(1)}, bf16[144,256]{1,0:T(8,128)(2,1)S(1)}, u32[]{:S(2)}, u32[]{:S(2)}) collective-permute-start(bf16[144,256]{1,0:T(8,128)(2,1)S(1)} %get-tuple-element.74), channel_id=1, source_target_pairs={{0,2},{1,3},{2,0},{3,1},{4,6},{5,7},{6,4},{7,5},{8,10},{9,11},{10,... | collective-permute-start | bytes 221192 | tf_op jit(solution)/shard_map/ppermute | solution.py:610
  145.4 10.6 %collective-permute-start.13 = (bf16[288,256]{1,0:T(8,128)(2,1)S(1)}, bf16[288,256]{1,0:T(8,128)(2,1)S(1)}, u32[]{:S(2)}, u32[]{:S(2)}) collective-permute-start(bf16[288,256]{1,0:T(8,128)(2,1)S(1)} %shard_map.199.refs_0_), channel_id=1, source_target_pairs={{0,8},{8,0},{16,24},{24,16},{1,9},{9,1},{17,25},{25,17},{2,10},{10... | collective-permute-start | bytes 442376 | tf_op jit(solution)/shard_map/ppermute | solution.py:610
  156.1 14.6 %collective-permute-start.14 = (bf16[288,256]{1,0:T(8,128)(2,1)S(1)}, bf16[288,256]{1,0:T(8,128)(2,1)S(1)}, u32[]{:S(2)}, u32[]{:S(2)}) collective-permute-start(bf16[288,256]{1,0:T(8,128)(2,1)S(1)} %shard_map.200.refs_0_), channel_id=1, source_target_pairs={{0,16},{8,24},{16,0},{24,8},{1,17},{9,25},{17,1},{25,9},{2,18},{10... | collective-permute-start | bytes 442376 | tf_op jit(solution)/shard_map/ppermute | solution.py:610
  156.8 15.5 %all-to-all-start.3 = ((bf16[32,8,256]{2,1,0:T(8,128)(2,1)}), bf16[32,8,256]{2,1,0:T(8,128)(2,1)S(1)}, u32[]{:S(2)}, u32[]{:S(2)}) async-start(bf16[32,8,256]{2,1,0:T(8,128)(2,1)} %bitcast.18), calls=%async_computation.3 | async-start | bytes 262144 | tf_op jit(solution)/shard_map/all_to_all | solution.py:669
  161.2 5.3 %collective-permute-start.4 = (bf16[64,256]{1,0:T(8,128)(2,1)S(1)}, bf16[64,256]{1,0:T(8,128)(2,1)S(1)}, u32[]{:S(2)}, u32[]{:S(2)}) collective-permute-start(bf16[64,256]{1,0:T(8,128)(2,1)S(1)} %get-tuple-element.59), channel_id=1, source_target_pairs={{0,8},{8,16},{16,24},{1,9},{9,17},{17,25},{2,10},{10,18},{18,26},{... | collective-permute-start | bytes 98312 | tf_op jit(solution)/shard_map/ppermute | solution.py:606
  164.9 5.8 %collective-permute-start.5 = (bf16[64,256]{1,0:T(8,128)(2,1)S(1)}, bf16[64,256]{1,0:T(8,128)(2,1)S(1)}, u32[]{:S(2)}, u32[]{:S(2)}) collective-permute-start(bf16[64,256]{1,0:T(8,128)(2,1)S(1)} %get-tuple-element.60), channel_id=1, source_target_pairs={{8,0},{16,8},{24,16},{9,1},{17,9},{25,17},{10,2},{18,10},{26,18},{... | collective-permute-start | bytes 98312 | tf_op jit(solution)/shard_map/ppermute | solution.py:606
  170.8 5.2 %collective-permute-start.15 = (bf16[288,256]{1,0:T(8,128)(2,1)S(1)}, bf16[288,256]{1,0:T(8,128)(2,1)S(1)}, u32[]{:S(2)}, u32[]{:S(2)}) collective-permute-start(bf16[288,256]{1,0:T(8,128)(2,1)S(1)} %shard_map.201.refs_1_), channel_id=1, source_target_pairs={{0,4},{1,5},{2,6},{3,7},{4,0},{5,1},{6,2},{7,3},{8,12},{9,13},{10,... | collective-permute-start | bytes 442376 | tf_op jit(solution)/shard_map/ppermute | solution.py:610
  176.0 13.5 %collective-permute-start.16 = (bf16[576,256]{1,0:T(8,128)(2,1)S(1)}, bf16[576,256]{1,0:T(8,128)(2,1)S(1)}, u32[]{:S(2)}, u32[]{:S(2)}) collective-permute-start(bf16[576,256]{1,0:T(8,128)(2,1)S(1)} %shard_map.203.refs_1_), channel_id=1, source_target_pairs={{0,2},{1,3},{2,0},{3,1},{4,6},{5,7},{6,4},{7,5},{8,10},{9,11},{10,... | collective-permute-start | bytes 884744 | tf_op jit(solution)/shard_map/ppermute | solution.py:610
  177.5 12.0 %all-to-all-start.4 = ((bf16[32,8,256]{2,1,0:T(8,128)(2,1)}), bf16[32,8,256]{2,1,0:T(8,128)(2,1)S(1)}, u32[]{:S(2)}, u32[]{:S(2)}) async-start(bf16[32,8,256]{2,1,0:T(8,128)(2,1)} %bitcast.20), calls=%async_computation.4 | async-start | bytes 262144 | tf_op jit(solution)/shard_map/all_to_all | solution.py:669
  181.3 3.5 %collective-permute-start.6 = (bf16[64,256]{1,0:T(8,128)(2,1)S(1)}, bf16[64,256]{1,0:T(8,128)(2,1)S(1)}, u32[]{:S(2)}, u32[]{:S(2)}) collective-permute-start(bf16[64,256]{1,0:T(8,128)(2,1)S(1)} %get-tuple-element.61), channel_id=1, source_target_pairs={{0,1},{1,2},{2,3},{3,4},{4,5},{5,6},{6,7},{8,9},{9,10},{10,11},{11... | collective-permute-start | bytes 98312 | tf_op jit(solution)/shard_map/ppermute | solution.py:606
  183.4 4.2 %collective-permute-start.7 = (bf16[64,256]{1,0:T(8,128)(2,1)S(1)}, bf16[64,256]{1,0:T(8,128)(2,1)S(1)}, u32[]{:S(2)}, u32[]{:S(2)}) collective-permute-start(bf16[64,256]{1,0:T(8,128)(2,1)S(1)} %get-tuple-element.62), channel_id=1, source_target_pairs={{1,0},{2,1},{3,2},{4,3},{5,4},{6,5},{7,6},{9,8},{10,9},{11,10},{12... | collective-permute-start | bytes 98312 | tf_op jit(solution)/shard_map/ppermute | solution.py:606
  189.6 4.6 %collective-permute-start.17 = (bf16[1152,256]{1,0:T(8,128)(2,1)S(1)}, bf16[1152,256]{1,0:T(8,128)(2,1)S(1)}, u32[]{:S(2)}, u32[]{:S(2)}) collective-permute-start(bf16[1152,256]{1,0:T(8,128)(2,1)S(1)} %shard_map.204.refs_1_), channel_id=1, source_target_pairs={{0,1},{1,0},{2,3},{3,2},{4,5},{5,4},{6,7},{7,6},{8,9},{9,8},{10,11... | collective-permute-start | bytes 1769480 | tf_op jit(solution)/shard_map/ppermute | solution.py:610
  (12 other events, 343.4 us)

commit v8 on v7

--- a/solution.py
+++ b/solution.py
@@ -75,7 +75,7 @@
 
 
 def route_kernel(
-    counts_ref, owner_in, lists_in, points_in, slots_ref, sent0, sent1, sent2, sent3,
+    bits_ref, counts_ref, owner_in, lists_in, points_in, slots_ref, sent0, sent1, sent2, sent3,
     owner_ref, lists_ref, points_ref, sems, *, tiles, capacity
 ):
     fetches = [
@@ -86,8 +86,7 @@
     ]
     for fetch in fetches:
         fetch.start()
-    for fetch in fetches:
-        fetch.wait()
+    fetches[0].wait()
     rows = owner_ref.shape[1]
     live = iota((1, rows), 1) < counts_ref[0]
     owned = jnp.where(live, owner_ref[...], tiles)
@@ -96,12 +95,28 @@
     before = dot(marks(members), earlier)
     rank = jnp.sum(jnp.where(members, before, 0.0), axis=0, keepdims=True)
     slots_ref[...] = jnp.where(live, owned * capacity + rank.astype(jnp.int32), -1)
-    for direction, sent_ref in enumerate((sent0, sent1, sent2, sent3)):
+    fetches[1].wait()
+    fetches[2].wait()
+    for direction, sent_ref in zip(turns(bits_ref), (sent0, sent1, sent2, sent3)):
         sent_ref[...] = dot(chosen_rows(lists_ref, direction, rows), points_ref[...], TN).astype(bf16)
 
 
+def turns(bits_ref):
+    column, line = bits_ref[0], bits_ref[1]
+    return 1 - column, column, 3 - line, 2 + line
+
+
+def blocks(bits_ref):
+    column, line = bits_ref[0], bits_ref[1]
+    return column, 1 - column, 2 + line, 3 - line
+
+
+def block_of(index, size, start=0):
+    return pl.ds(pl.multiple_of(start + index * size, 16), size)
+
+
 def chosen_rows(lists_ref, direction, rows):
-    listed = lists_ref[direction : direction + 1, :]
+    listed = lists_ref[pl.ds(direction, 1), :]
     return marks(iota((rows, listed.shape[1]), 0) == listed)
 
 
@@ -125,16 +140,12 @@
         ).astype(bf16)
 
 
-def count_kernel(near_ref, kept_ref, table_ref, sems):
+def count_kernel(near_ref, table_ref):
     neighbours, rows = near_ref.shape
     step = 16
     zero = jnp.zeros((step, LANES), bf16)
     one = jnp.ones((step, LANES), bf16)
     row_blocks = table_ref.shape[0] // CHUNK
-
-    def copy_out(row_block):
-        place = pl.ds(pl.multiple_of(row_block * CHUNK, CHUNK), CHUNK)
-        return pltpu.make_async_copy(table_ref.at[place], kept_ref.at[place], sems.at[row_block])
 
     def rows_of(row_block, _):
         row_at = pl.multiple_of(row_block * CHUNK, CHUNK)
@@ -156,22 +167,24 @@
             return 0
 
         lax.fori_loop(0, rows // LANES, block, 0)
-        copy_out(row_block).start()
         return 0
 
     lax.fori_loop(0, row_blocks, rows_of, 0)
-    for row_block in range(row_blocks):
-        copy_out(row_block).wait()
 
 
 def lift_kernel(
-    slots_ref, points_ref, grad_ref, halo0, halo1, halo2, halo3, table_ref, w_ref,
-    average_out, pre_out, packed_out,
-    average_ref, pre_ref, both_ref, stage_ref, sems, pack_sems, *, neighbours
+    bits_ref, slots_ref, points_ref, grad_ref, halo0, halo1, halo2, halo3, table_ref, w_ref,
+    table_out, average_out, pre_out, packed_out,
+    ext_ref, average_ref, pre_ref, both_ref, stage_ref, sems, pack_sems, *, neighbours
 ):
     width = points_ref.shape[1]
-    ext = jnp.concatenate([points_ref[...], halo0[...], halo1[...], halo2[...], halo3[...]], axis=0)
-    average = (dot(ext, table_ref[...], TN) * (1.0 / neighbours)).astype(bf16)
+    keep_table = pltpu.make_async_copy(table_ref, table_out, sems.at[2])
+    keep_table.start()
+    rows = points_ref.shape[0]
+    ext_ref[0:rows, :] = points_ref[...]
+    for block, halo in zip(blocks(bits_ref), (halo0, halo1, halo2, halo3)):
+        ext_ref[block_of(block, halo.shape[0], rows), :] = halo[...]
+    average = (dot(ext_ref[...], table_ref[...], TN) * (1.0 / neighbours)).astype(bf16)
     average_ref[...] = average
     keep_average = pltpu.make_async_copy(average_ref, average_out, sems.at[0])
     keep_average.start()
@@ -187,12 +200,13 @@
     pack_rows(slots_ref, both_ref, packed_out, stage_ref, pack_sems)
     keep_average.wait()
     keep_pre.wait()
+    keep_table.wait()
 
 
 def tile_back_kernel(
-    slots_ref, back_ref, w_ref, table_in, average_in, pre_in,
+    bits_ref, slots_ref, back_ref, w_ref, table_in, average_in, pre_in,
     lifted_out, spread_out, near_ref, halo0, halo1, halo2, halo3,
-    table_ref, average_ref, pre_ref, lifted_ref, act_ref, spread_ref, sems, *, neighbours
+    table_ref, average_ref, pre_ref, lifted_ref, act_ref, spread_ref, halo_ref, sems, *, neighbours
 ):
     rows = lifted_ref.shape[0]
     halo_rows = table_ref.shape[0]
@@ -222,17 +236,16 @@
     fetch_average.wait()
     near_ref[...] = dot(average_ref[...], act_ref[...]).astype(near_ref.dtype)
     fetch_table.wait()
-    halo = dot(table_ref[...], spread_ref[...]).astype(bf16)
-    size = halo0.shape[0]
-    for direction, halo_ref in enumerate((halo0, halo1, halo2, halo3)):
-        halo_ref[...] = halo[direction * size : (direction + 1) * size]
+    halo_ref[...] = dot(table_ref[...], spread_ref[...]).astype(bf16)
+    for block, back in zip(blocks(bits_ref), (halo0, halo1, halo2, halo3)):
+        back[...] = halo_ref[block_of(block, back.shape[0]), :]
     keep_lifted.wait()
     keep_spread.wait()
 
 
 def finish_kernel(
-    lists_ref, back0, back1, back2, back3, table_in, spread_in, lifted_in,
-    out_ref, table_ref, spread_ref, lifted_ref, sems
+    bits_ref, lists_ref, back0, back1, back2, back3, table_in, spread_in, lifted_in,
+    out_ref, came_ref, table_ref, spread_ref, lifted_ref, sems
 ):
     rows = out_ref.shape[0]
     fetch_spread = pltpu.make_async_copy(spread_in, spread_ref, sems.at[0])
@@ -241,8 +254,9 @@
     fetch_spread.start()
     fetch_table.start()
     fetch_lifted.start()
-    came = jnp.concatenate([back0[...], back1[...], back2[...], back3[...]], axis=0)
-    returned = dot(chosen_rows(lists_ref, 0, rows), came)
+    for direction, back in zip(turns(bits_ref), (back0, back1, back2, back3)):
+        came_ref[block_of(direction, back.shape[0]), :] = back[...]
+    returned = dot(chosen_rows(lists_ref, 0, rows), came_ref[...])
     fetch_spread.wait()
     fetch_table.wait()
     fetch_lifted.wait()
@@ -600,10 +614,12 @@
     return jax.ShapeDtypeStruct(shape, dtype)
 
 
-def shifted(value, axis, steps):
+def pairwise(first, second, axis):
     count = lax.axis_size(axis)
-    initial, last = (max(0, -steps), min(count, count - steps))
-    return lax.ppermute(value, axis, [(source, source + steps) for source in range(initial, last)])
+    pairs = [
+        [pair for at in range(start, count - 1, 2) for pair in ((at, at + 1), (at + 1, at))] for start in (0, 1)
+    ]
+    return [lax.ppermute(rows, axis, pair) for rows, pair in zip((first, second), pairs)]
 
 
 def partner(value, axis, step):
@@ -701,54 +717,46 @@
     gain_two_row = gain_two.reshape(1, width)
     hidden = w_up.shape[1]
 
+    bits = jnp.concatenate([bit_of("tx", 1), bit_of("ty", 1)])
     slots, *sent = call(
         route_kernel,
         [shaped(1, tile_rows, dtype=jnp.int32)] + [shaped(border_rows, width)] * 4,
-        [counts, owner, lists, points_tile],
+        [bits, counts, owner, lists, points_tile],
         scratch=[
             pltpu.VMEM((1, tile_rows), jnp.int32),
             pltpu.VMEM((4, border_rows), jnp.int32),
             pltpu.VMEM((tile_rows, width), bf16),
             pltpu.SemaphoreType.DMA((3,)),
         ],
-        smem=1,
+        smem=2,
         held=3,
         flops=4e9,
         tiles=tiles,
         capacity=capacity,
     )
-    halos = [
-        shifted(sent[0], "tx", -1),
-        shifted(sent[1], "tx", 1),
-        shifted(sent[2], "ty", -1),
-        shifted(sent[3], "ty", 1),
-    ]
-    kept_table, table = call(
-        count_kernel,
-        [shaped(ext, tile_rows), shaped(ext, tile_rows)],
-        [near_tile],
-        scratch=[pltpu.SemaphoreType.DMA((ext // CHUNK,))],
-        flops=8e9,
-        stored=1,
-    )
-    average, pre_act, packed = call(
+    halos = pairwise(sent[0], sent[1], "tx") + pairwise(sent[2], sent[3], "ty")
+    (table,) = call(count_kernel, [shaped(ext, tile_rows)], [near_tile], flops=8e9)
+    kept_table, average, pre_act, packed = call(
         lift_kernel,
         [
+            shaped(ext, tile_rows),
             shaped(width, tile_rows),
             shaped(tile_rows, width, dtype=f32),
             shaped(slots_count, 2 * width),
         ],
-        [slots, points_tile, grad_out[0], *halos, table, w_near],
+        [bits, slots, points_tile, grad_out[0], *halos, table, w_near],
+        smem=1,
         scratch=[
+            pltpu.VMEM((ext, width), bf16),
             pltpu.VMEM((width, tile_rows), bf16),
             pltpu.VMEM((tile_rows, width), f32),
             pltpu.VMEM((tile_rows, 2 * width), bf16),
             pltpu.VMEM((slots_count, 2 * width), bf16),
-            pltpu.SemaphoreType.DMA((2,)),
+            pltpu.SemaphoreType.DMA((3,)),
             pltpu.SemaphoreType.DMA((slots_count // WIDE,)),
         ],
         flops=4e9,
-        stored=3,
+        stored=4,
         neighbours=neighbours,
     )
     came = exchange(packed, tiles)
@@ -859,7 +867,8 @@
         tile_back_kernel,
         [shaped(tile_rows, width), shaped(tile_rows, width), shaped(width, width)]
         + [shaped(border_rows, width)] * 4,
-        [slots, came_back, w_near, kept_table, average, pre_act],
+        [bits, slots, came_back, w_near, kept_table, average, pre_act],
+        smem=1,
         after=[out_rows],
         scratch=[
             pltpu.VMEM((edge, tile_rows), bf16),
@@ -868,6 +877,7 @@
             pltpu.VMEM((tile_rows, width), bf16),
             pltpu.VMEM((tile_rows, width), bf16),
             pltpu.VMEM((tile_rows, width), bf16),
+            pltpu.VMEM((edge, width), bf16),
             pltpu.SemaphoreType.DMA((5,)),
         ],
         flops=6e9,
@@ -876,12 +886,7 @@
         stored=2,
         neighbours=neighbours,
     )
-    returned = [
-        shifted(halo_grad[0], "tx", 1),
-        shifted(halo_grad[1], "tx", -1),
-        shifted(halo_grad[2], "ty", 1),
-        shifted(halo_grad[3], "ty", -1),
-    ]
+    returned = pairwise(halo_grad[0], halo_grad[1], "tx") + pairwise(halo_grad[2], halo_grad[3], "ty")
     (near_share,) = call(
         near_sum_kernel,
         [shaped(width, width)],
@@ -897,8 +902,10 @@
     (grad_points,) = call(
         finish_kernel,
         [shaped(tile_rows, width)],
-        [border.reshape(1, edge), *returned, kept_table, spread, lifted_grad],
+        [bits, border.reshape(1, edge), *returned, kept_table, spread, lifted_grad],
+        smem=1,
         scratch=[
+            pltpu.VMEM((edge, width), bf16),
             pltpu.VMEM((tile_rows, tile_rows), bf16),
             pltpu.VMEM((tile_rows, width), bf16),
             pltpu.VMEM((tile_rows, width), bf16),

time: 197 us -> 192 us (0.975)
  blocking collectives: 0 us -> 57.3 us
  waiting for transfers between devices: 80.4 us -> 35.2 us
  starting transfers between devices: 52 us -> 33.4 us
    all_to_all x0 -> x1, blocking collectives: none -> 57.3 us  [exchange(): lax.all_to_all(rows, ('tx', 'ty'), split_axis=0, concat_axis=0, tiled=True)]
    all_to_all x5 -> x4, waiting for transfers between devices: 57.7 us -> 14.5 us  [exchange(): lax.all_to_all(rows, ('tx', 'ty'), split_axis=0, concat_axis=0, tiled=True)]
    ppermute x8, starting transfers between devices: 19.6 us -> 7.93 us  [pairwise(): lax.ppermute(rows, axis, pair)]
    all_to_all x5 -> x4, starting transfers between devices: 21.7 us -> 15.5 us  [exchange(): lax.all_to_all(rows, ('tx', 'ty'), split_axis=0, concat_axis=0, tiled=True)]
    ppermute x8, waiting for transfers between devices: 7.45 us -> 4.64 us  [pairwise(): lax.ppermute(rows, axis, pair)]
  transfers between devices with their start and end apart: 23 -> 22, of which waited for: 12 -> 11; matrix products, arithmetic and copies ran while one was open for 0% -> 0% of each run, Pallas kernels for 21% -> 22%
where the time goes in v8:
time: 192 us; the launch traced here: 191 us
  Pallas kernels  63.6 us (33%)
  blocking collectives  57.3 us (30%)
  waiting for transfers between devices  35.2 us (18%)
  starting transfers between devices  33.4 us (17%)
    pallas_call x18, Pallas kernels, call(): pl.pallas_call(run, out_shape=tuple(shapes), in_specs=specs, out_specs=tu...  63.6 us
    all_to_all x1, blocking collectives, exchange(): lax.all_to_all(rows, ('tx', 'ty'), split_axis=0, concat_axis=0, tiled=True)  57.3 us
    ppermute x10, waiting for transfers between devices, partner(): lax.ppermute(value, axis, [(at, at ^ step) for at in range(lax.axis_size(...  16.1 us
    all_to_all x4, starting transfers between devices, exchange(): lax.all_to_all(rows, ('tx', 'ty'), split_axis=0, concat_axis=0, tiled=True)  15.5 us
    all_to_all x4, waiting for transfers between devices, exchange(): lax.all_to_all(rows, ('tx', 'ty'), split_axis=0, concat_axis=0, tiled=True)  14.5 us
    ppermute x10, starting transfers between devices, partner(): lax.ppermute(value, axis, [(at, at ^ step) for at in range(lax.axis_size(...  9.94 us
    ppermute x8, starting transfers between devices, pairwise(): lax.ppermute(rows, axis, pair)  7.93 us
    ppermute x8, waiting for transfers between devices, pairwise(): lax.ppermute(rows, axis, pair)  4.64 us
  transfers between devices with their start and end apart: 22, of which 11 were waited for; matrix products, arithmetic and copies ran while one was open for 0% of the time, Pallas kernels for 22%

profile of v8, /device:TPU:0, one launch (start us, length us, event | category | flops | bytes accessed | tf_op | source)
XLA Modules:
  0.0 191.5 jit_solution(6059326397040777065)
XLA Ops:
  1.4 2.2 %shard_map.188 = (s32[1,1024]{1,0:T(1,128)S(1)}, bf16[64,256]{1,0:T(8,128)(2,1)S(1)}, bf16[64,256]{1,0:T(8,128)(2,1)S(1)}, bf16[64,256]{1,0:T(8,128)(2,1)S(1)}, bf16[64,256]{1,0:T(8,128)(2,1)S(1)}) custom-call(s32[2]{0:T(128)S(1)} %pad_add_fusion.refs_0_, s32[1]{0:T(128)S(6)} %copy.23.refs_1_, s32[1,1024]{1,0:T(1,128)} %refs_2_.1, s32[4,64]{1,0:T(4,128)} %bitcast.47, ...), custom_call_target="tpu_custom_call" | custom-call | flops 4000000000 | bytes 664588 | tf_op jit(solution)/shard_map/pallas_call | solution.py:601
  3.5 3.1 %collective-permute-start = (bf16[64,256]{1,0:T(8,128)(2,1)S(1)}, bf16[64,256]{1,0:T(8,128)(2,1)S(1)}, u32[]{:S(2)}, u32[]{:S(2)}) collective-permute-start(bf16[64,256]{1,0:T(8,128)(2,1)S(1)} %get-tuple-element.45), channel_id=1, source_target_pairs={{0,8},{8,0},{16,24},{24,16},{1,9},{9,1},{17,25},{25,17},{2,10},{10... | collective-permute-start | bytes 98312 | tf_op jit(solution)/shard_map/ppermute | solution.py:622
  8.1 5.0 %shard_map.189.refs_8_ = bf16[1280,1024]{1,0:T(8,128)(2,1)S(1)} custom-call(s32[16,1024]{1,0:T(8,128)S(1)} %bitcast.35), custom_call_target="tpu_custom_call" | custom-call | flops 8000000000 | bytes 2686976 | tf_op jit(solution)/shard_map/pallas_call | solution.py:601
  13.2 5.6 %shard_map.190 = (bf16[1280,1024]{1,0:T(8,128)(2,1)}, bf16[256,1024]{1,0:T(8,128)(2,1)}, f32[1024,256]{1,0:T(8,128)}, bf16[2048,512]{1,0:T(8,128)(2,1)}) custom-call(s32[2]{0:T(128)S(1)} %pad_add_fusion.refs_0_, s32[1,1024]{1,0:T(1,128)S(1)} %get-tuple-element.44.refs_1_.refs_0_, bf16[1024,256]{1,0:T(8,128)(2,1)S(1)} %bitcast.31, ...), custom_call_target="tpu_custom_call" | custom-call | flops 4000000000 | bytes 10227720 | tf_op jit(solution)/shard_map/pallas_call | solution.py:601
  18.8 57.3 %all_to_all.55 = bf16[32,64,512]{2,1,0:T(8,128)(2,1)} all-to-all(bf16[32,64,512]{2,1,0:T(8,128)(2,1)} %bitcast.43), channel_id=1, replica_groups=mesh['tx'=4,'ty'=8] {'tx','ty'}, dimensions={0} | all-to-all | bytes 4194304 | tf_op jit(solution)/shard_map/all_to_all | solution.py:685
  76.2 12.0 %shard_map.191 = (bf16[2048,256]{1,0:T(8,128)(2,1)}, f32[2048,256]{1,0:T(8,128)}, bf16[2048,256]{1,0:T(8,128)(2,1)}) custom-call(s32[1,2048]{1,0:T(1,128)S(1)} %copy-done.8, bf16[768,32]{1,0:T(8,128)(2,1)S(1)} %bitcast.33, f32[1,256]{1,0:T(1,128)S(1)} %bitcast.36, f32[1,256]{1,0:T(1,128)S(1)} %bitcast.38, bf16[256,1024]{1,0:T(8,128)(2,1)S(1)} %copy-done.3, ...), custom_call_target="tpu_custom_call" | custom-call | flops 10000000000 | bytes 7399424 | tf_op jit(solution)/shard_map/pallas_call | solution.py:601
  88.2 3.9 %all-to-all-start.1 = ((bf16[32,64,256]{2,1,0:T(8,128)(2,1)}), bf16[32,64,256]{2,1,0:T(8,128)(2,1)S(1)}, u32[]{:S(2)}, u32[]{:S(2)}) async-start(bf16[32,64,256]{2,1,0:T(8,128)(2,1)} %bitcast.44), calls=%async_computation.1 | async-start | bytes 2097152 | tf_op jit(solution)/shard_map/all_to_all | solution.py:685
  92.1 24.1 %shard_map.193 = (bf16[2048,256]{1,0:T(8,128)(2,1)}, bf16[1152,256]{1,0:T(8,128)(2,1)}, bf16[1152,256]{1,0:T(8,128)(2,1)}) custom-call(s32[1]{0:T(128)} %bitcast.1.refs_0_, s32[1,2048]{1,0:T(1,128)S(1)} %copy-done.8, bf16[768,32]{1,0:T(8,128)(2,1)S(1)} %bitcast.34, f32[1,256]{1,0:T(1,128)S(1)} %bitcast.37, f32[1,256]{1,0:T(1,128)S(1)} %bitcast.39, ...), custom_call_target="tpu_custom_call" | custom-call | flops 40000000000 | bytes 8579076 | tf_op jit(solution)/shard_map/pallas_call | solution.py:601
  116.2 1.9 all-to-all-done.1.refs_1_
  118.1 3.8 %all-to-all-start.2 = ((bf16[32,64,256]{2,1,0:T(8,128)(2,1)}), bf16[32,64,256]{2,1,0:T(8,128)(2,1)S(1)}, u32[]{:S(2)}, u32[]{:S(2)}) async-start(bf16[32,64,256]{2,1,0:T(8,128)(2,1)} %bitcast.40), calls=%async_computation.2 | async-start | bytes 2097152 | tf_op jit(solution)/shard_map/all_to_all | solution.py:685
  122.2 2.1 %shard_map.192.refs_7_.refs_4_ = bf16[1024,256]{1,0:T(8,128)(2,1)} custom-call(s32[1,1024]{1,0:T(1,128)S(1)} %get-tuple-element.44.refs_1_.refs_0_, bf16[2048,256]{1,0:T(8,128)(2,1)S(1)} %bitcast.25), custom_call_target="tpu_custom_call" | custom-call | flops 4000000000 | bytes 1576960 | tf_op jit(solution)/shard_map/pallas_call | solution.py:601
  127.9 7.0 %collective-permute-done.10.refs_5_ = bf16[288,256]{1,0:T(8,128)(2,1)S(1)} collective-permute-done((bf16[288,256]{1,0:T(8,128)(2,1)S(1)}, bf16[288,256]{1,0:T(8,128)(2,1)S(1)}, u32[]{:S(2)}, u32[]{:S(2)}) %collective-permute-start.10) | collective-permute-done | bytes 147488 | tf_op jit(solution)/shard_map/ppermute | solution.py:626
  138.6 3.0 %collective-permute-done.11.refs_1_ = bf16[144,256]{1,0:T(8,128)(2,1)S(1)} collective-permute-done((bf16[144,256]{1,0:T(8,128)(2,1)S(1)}, bf16[144,256]{1,0:T(8,128)(2,1)S(1)}, u32[]{:S(2)}, u32[]{:S(2)}) %collective-permute-start.11) | collective-permute-done | bytes 73760 | tf_op jit(solution)/shard_map/ppermute | solution.py:626
  143.1 5.2 %all-to-all-done.2 = bf16[32,64,256]{2,1,0:T(8,128)(2,1)S(1)} async-done(((bf16[32,64,256]{2,1,0:T(8,128)(2,1)}), bf16[32,64,256]{2,1,0:T(8,128)(2,1)S(1)}, u32[]{:S(2)}, u32[]{:S(2)}) %all-to-all-start.2) | async-done | bytes 1048608 | tf_op jit(solution)/shard_map/all_to_all | solution.py:685
  148.2 5.2 %shard_map.195 = (bf16[1024,256]{1,0:T(8,128)(2,1)}, bf16[1024,256]{1,0:T(8,128)(2,1)}, bf16[256,256]{1,0:T(8,128)(2,1)}, bf16[64,256]{1,0:T(8,128)(2,1)S(1)}, b...) custom-call(s32[2]{0:T(128)S(1)} %pad_add_fusion.refs_0_, ...), custom_call_target="tpu_custom_call" | custom-call | flops 6000000000 | bytes 6688776 | tf_op jit(solution)/shard_map/pallas_call | solution.py:601
  154.2 4.4 %all-to-all-start.3 = ((bf16[32,8,256]{2,1,0:T(8,128)(2,1)}), bf16[32,8,256]{2,1,0:T(8,128)(2,1)S(1)}, u32[]{:S(2)}, u32[]{:S(2)}) async-start(bf16[32,8,256]{2,1,0:T(8,128)(2,1)} %bitcast.19), calls=%async_computation.3 | async-start | bytes 262144 | tf_op jit(solution)/shard_map/all_to_all | solution.py:685
  158.6 1.8 collective-permute-start.4
  161.1 4.3 %collective-permute-done.4.refs_2_.refs_1_ = bf16[64,256]{1,0:T(8,128)(2,1)S(1)} collective-permute-done((bf16[64,256]{1,0:T(8,128)(2,1)S(1)}, bf16[64,256]{1,0:T(8,128)(2,1)S(1)}, u32[]{:S(2)}, u32[]{:S(2)}) %collective-permute-start.4) | collective-permute-done | bytes 32800 | tf_op jit(solution)/shard_map/ppermute | solution.py:622
  167.7 3.6 %collective-permute-done.15.refs_2_ = bf16[288,256]{1,0:T(8,128)(2,1)S(1)} collective-permute-done((bf16[288,256]{1,0:T(8,128)(2,1)S(1)}, bf16[288,256]{1,0:T(8,128)(2,1)S(1)}, u32[]{:S(2)}, u32[]{:S(2)}) %collective-permute-start.15) | collective-permute-done | bytes 147488 | tf_op jit(solution)/shard_map/ppermute | solution.py:626
  171.4 2.0 %collective-permute-start.16 = (bf16[576,256]{1,0:T(8,128)(2,1)S(1)}, bf16[576,256]{1,0:T(8,128)(2,1)S(1)}, u32[]{:S(2)}, u32[]{:S(2)}) collective-permute-start(bf16[576,256]{1,0:T(8,128)(2,1)S(1)} %shard_map.203.refs_1_), channel_id=1, source_target_pairs={{0,2},{1,3},{2,0},{3,1},{4,6},{5,7},{6,4},{7,5},{8,10},{9,11},{10,... | collective-permute-start | bytes 884744 | tf_op jit(solution)/shard_map/ppermute | solution.py:626
  173.3 3.4 %all-to-all-start.4 = ((bf16[32,8,256]{2,1,0:T(8,128)(2,1)}), bf16[32,8,256]{2,1,0:T(8,128)(2,1)S(1)}, u32[]{:S(2)}, u32[]{:S(2)}) async-start(bf16[32,8,256]{2,1,0:T(8,128)(2,1)} %bitcast.21), calls=%async_computation.4 | async-start | bytes 262144 | tf_op jit(solution)/shard_map/all_to_all | solution.py:685
  178.0 7.0 %all-to-all-done.4 = bf16[32,8,256]{2,1,0:T(8,128)(2,1)S(1)} async-done(((bf16[32,8,256]{2,1,0:T(8,128)(2,1)}), bf16[32,8,256]{2,1,0:T(8,128)(2,1)S(1)}, u32[]{:S(2)}, u32[]{:S(2)}) %all-to-all-start.4) | async-done | bytes 131104 | tf_op jit(solution)/shard_map/all_to_all | solution.py:685
  185.4 4.2 %shard_map.196 = bf16[1024,256]{1,0:T(8,128)(2,1)} custom-call(s32[2]{0:T(128)S(1)} %pad_add_fusion.refs_0_, s32[1,256]{1,0:T(1,128)S(1)} %reshape.63.refs_1_, bf16[64,256]{1,0:T(8,128)(2,1)S(1)} %collective-permute-done.4.refs_2_.refs_1_, bf16[64,256]{1,0:T(8,128)(2,1)S(1)} %collective-permute-done.5.refs_3_.refs_2_, ...), custom_call_target="tpu_custom_call" | custom-call | flops 1000000000 | bytes 4326408 | tf_op jit(solution)/shard_map/pallas_call | solution.py:601
  189.6 1.9 shard_map.205
  (67 shorter events, 16.0 us)
Async XLA Ops:
  3.5 9.5 %collective-permute-start = (bf16[64,256]{1,0:T(8,128)(2,1)S(1)}, bf16[64,256]{1,0:T(8,128)(2,1)S(1)}, u32[]{:S(2)}, u32[]{:S(2)}) collective-permute-start(bf16[64,256]{1,0:T(8,128)(2,1)S(1)} %get-tuple-element.45), channel_id=1, source_target_pairs={{0,8},{8,0},{16,24},{24,16},{1,9},{9,1},{17,25},{25,17},{2,10},{10... | collective-permute-start | bytes 98312 | tf_op jit(solution)/shard_map/ppermute | solution.py:622
  6.6 6.5 %collective-permute-start.1 = (bf16[64,256]{1,0:T(8,128)(2,1)S(1)}, bf16[64,256]{1,0:T(8,128)(2,1)S(1)}, u32[]{:S(2)}, u32[]{:S(2)}) collective-permute-start(bf16[64,256]{1,0:T(8,128)(2,1)S(1)} %get-tuple-element.46), channel_id=1, source_target_pairs={{8,16},{16,8},{9,17},{17,9},{10,18},{18,10},{11,19},{19,11},{12,20... | collective-permute-start | bytes 98312 | tf_op jit(solution)/shard_map/ppermute | solution.py:622
  7.3 5.8 %collective-permute-start.2 = (bf16[64,256]{1,0:T(8,128)(2,1)S(1)}, bf16[64,256]{1,0:T(8,128)(2,1)S(1)}, u32[]{:S(2)}, u32[]{:S(2)}) collective-permute-start(bf16[64,256]{1,0:T(8,128)(2,1)S(1)} %get-tuple-element.47), channel_id=1, source_target_pairs={{0,1},{1,0},{2,3},{3,2},{4,5},{5,4},{6,7},{7,6},{8,9},{9,8},{10,11... | collective-permute-start | bytes 98312 | tf_op jit(solution)/shard_map/ppermute | solution.py:622
  7.4 5.8 %collective-permute-start.3 = (bf16[64,256]{1,0:T(8,128)(2,1)S(1)}, bf16[64,256]{1,0:T(8,128)(2,1)S(1)}, u32[]{:S(2)}, u32[]{:S(2)}) collective-permute-start(bf16[64,256]{1,0:T(8,128)(2,1)S(1)} %get-tuple-element.48), channel_id=1, source_target_pairs={{1,2},{2,1},{3,4},{4,3},{5,6},{6,5},{9,10},{10,9},{11,12},{12,11},... | collective-permute-start | bytes 98312 | tf_op jit(solution)/shard_map/ppermute | solution.py:622
  18.7 57.4 %copy-start.3 = (bf16[256,1024]{1,0:T(8,128)(2,1)S(1)}, bf16[256,1024]{1,0:T(8,128)(2,1)}, u32[]{:S(2)}) copy-start(bf16[256,1024]{1,0:T(8,128)(2,1)} %refs_5_.3) | copy-start | bytes 1572868
  18.7 57.4 %copy-start.4 = (bf16[1024,256]{1,0:T(8,128)(2,1)S(1)}, bf16[1024,256]{1,0:T(8,128)(2,1)}, u32[]{:S(2)}) copy-start(bf16[1024,256]{1,0:T(8,128)(2,1)} %refs_6_.1) | copy-start | bytes 1572868
  88.2 29.9 %all-to-all-start.1 = ((bf16[32,64,256]{2,1,0:T(8,128)(2,1)}), bf16[32,64,256]{2,1,0:T(8,128)(2,1)S(1)}, u32[]{:S(2)}, u32[]{:S(2)}) async-start(bf16[32,64,256]{2,1,0:T(8,128)(2,1)} %bitcast.44), calls=%async_computation.1 | async-start | bytes 2097152 | tf_op jit(solution)/shard_map/all_to_all | solution.py:685
  118.1 30.1 %all-to-all-start.2 = ((bf16[32,64,256]{2,1,0:T(8,128)(2,1)}), bf16[32,64,256]{2,1,0:T(8,128)(2,1)S(1)}, u32[]{:S(2)}, u32[]{:S(2)}) async-start(bf16[32,64,256]{2,1,0:T(8,128)(2,1)} %bitcast.40), calls=%async_computation.2 | async-start | bytes 2097152 | tf_op jit(solution)/shard_map/all_to_all | solution.py:685
  121.9 2.4 %collective-permute-start.8 = (bf16[1152,256]{1,0:T(8,128)(2,1)S(1)}, bf16[1152,256]{1,0:T(8,128)(2,1)S(1)}, u32[]{:S(2)}, u32[]{:S(2)}) collective-permute-start(bf16[1152,256]{1,0:T(8,128)(2,1)S(1)} %copy-done.12), channel_id=1, source_target_pairs={{0,1},{1,0},{2,3},{3,2},{4,5},{5,4},{6,7},{7,6},{8,9},{9,8},{10,11... | collective-permute-start | bytes 1769480 | tf_op jit(solution)/shard_map/ppermute | solution.py:626
  124.7 10.2 %collective-permute-start.10 = (bf16[288,256]{1,0:T(8,128)(2,1)S(1)}, bf16[288,256]{1,0:T(8,128)(2,1)S(1)}, u32[]{:S(2)}, u32[]{:S(2)}) collective-permute-start(bf16[288,256]{1,0:T(8,128)(2,1)S(1)} %get-tuple-element.68), channel_id=1, source_target_pairs={{0,4},{1,5},{2,6},{3,7},{4,0},{5,1},{6,2},{7,3},{8,12},{9,13},{10,... | collective-permute-start | bytes 442376 | tf_op jit(solution)/shard_map/ppermute | solution.py:626
  126.4 10.2 %collective-permute-start.9 = (bf16[288,256]{1,0:T(8,128)(2,1)S(1)}, bf16[288,256]{1,0:T(8,128)(2,1)S(1)}, u32[]{:S(2)}, u32[]{:S(2)}) collective-permute-start(bf16[288,256]{1,0:T(8,128)(2,1)S(1)} %get-tuple-element.66), channel_id=1, source_target_pairs={{0,2},{1,3},{2,0},{3,1},{4,6},{5,7},{6,4},{7,5},{8,10},{9,11},{10,... | collective-permute-start | bytes 442376 | tf_op jit(solution)/shard_map/ppermute | solution.py:626
  136.8 4.8 %collective-permute-start.11 = (bf16[144,256]{1,0:T(8,128)(2,1)S(1)}, bf16[144,256]{1,0:T(8,128)(2,1)S(1)}, u32[]{:S(2)}, u32[]{:S(2)}) collective-permute-start(bf16[144,256]{1,0:T(8,128)(2,1)S(1)} %get-tuple-element.70), channel_id=1, source_target_pairs={{0,4},{1,5},{2,6},{3,7},{4,0},{5,1},{6,2},{7,3},{8,12},{9,13},{10,... | collective-permute-start | bytes 221192 | tf_op jit(solution)/shard_map/ppermute | solution.py:626
  137.9 4.4 %collective-permute-start.12 = (bf16[144,256]{1,0:T(8,128)(2,1)S(1)}, bf16[144,256]{1,0:T(8,128)(2,1)S(1)}, u32[]{:S(2)}, u32[]{:S(2)}) collective-permute-start(bf16[144,256]{1,0:T(8,128)(2,1)S(1)} %get-tuple-element.72), channel_id=1, source_target_pairs={{0,2},{1,3},{2,0},{3,1},{4,6},{5,7},{6,4},{7,5},{8,10},{9,11},{10,... | collective-permute-start | bytes 221192 | tf_op jit(solution)/shard_map/ppermute | solution.py:626
  142.3 11.2 %collective-permute-start.13 = (bf16[288,256]{1,0:T(8,128)(2,1)S(1)}, bf16[288,256]{1,0:T(8,128)(2,1)S(1)}, u32[]{:S(2)}, u32[]{:S(2)}) collective-permute-start(bf16[288,256]{1,0:T(8,128)(2,1)S(1)} %shard_map.199.refs_0_), channel_id=1, source_target_pairs={{0,8},{8,0},{16,24},{24,16},{1,9},{9,1},{17,25},{25,17},{2,10},{10... | collective-permute-start | bytes 442376 | tf_op jit(solution)/shard_map/ppermute | solution.py:626
  153.5 11.9 %collective-permute-start.14 = (bf16[288,256]{1,0:T(8,128)(2,1)S(1)}, bf16[288,256]{1,0:T(8,128)(2,1)S(1)}, u32[]{:S(2)}, u32[]{:S(2)}) collective-permute-start(bf16[288,256]{1,0:T(8,128)(2,1)S(1)} %shard_map.200.refs_0_), channel_id=1, source_target_pairs={{0,16},{8,24},{16,0},{24,8},{1,17},{9,25},{17,1},{25,9},{2,18},{10... | collective-permute-start | bytes 442376 | tf_op jit(solution)/shard_map/ppermute | solution.py:626
  154.2 12.7 %all-to-all-start.3 = ((bf16[32,8,256]{2,1,0:T(8,128)(2,1)}), bf16[32,8,256]{2,1,0:T(8,128)(2,1)S(1)}, u32[]{:S(2)}, u32[]{:S(2)}) async-start(bf16[32,8,256]{2,1,0:T(8,128)(2,1)} %bitcast.19), calls=%async_computation.3 | async-start | bytes 262144 | tf_op jit(solution)/shard_map/all_to_all | solution.py:685
  158.6 6.8 %collective-permute-start.4 = (bf16[64,256]{1,0:T(8,128)(2,1)S(1)}, bf16[64,256]{1,0:T(8,128)(2,1)S(1)}, u32[]{:S(2)}, u32[]{:S(2)}) collective-permute-start(bf16[64,256]{1,0:T(8,128)(2,1)S(1)} %get-tuple-element.57), channel_id=1, source_target_pairs={{0,8},{8,0},{16,24},{24,16},{1,9},{9,1},{17,25},{25,17},{2,10},{10... | collective-permute-start | bytes 98312 | tf_op jit(solution)/shard_map/ppermute | solution.py:622
  160.4 5.0 %collective-permute-start.5 = (bf16[64,256]{1,0:T(8,128)(2,1)S(1)}, bf16[64,256]{1,0:T(8,128)(2,1)S(1)}, u32[]{:S(2)}, u32[]{:S(2)}) collective-permute-start(bf16[64,256]{1,0:T(8,128)(2,1)S(1)} %get-tuple-element.58), channel_id=1, source_target_pairs={{8,16},{16,8},{9,17},{17,9},{10,18},{18,10},{11,19},{19,11},{12,20... | collective-permute-start | bytes 98312 | tf_op jit(solution)/shard_map/ppermute | solution.py:622
  165.5 5.9 %collective-permute-start.15 = (bf16[288,256]{1,0:T(8,128)(2,1)S(1)}, bf16[288,256]{1,0:T(8,128)(2,1)S(1)}, u32[]{:S(2)}, u32[]{:S(2)}) collective-permute-start(bf16[288,256]{1,0:T(8,128)(2,1)S(1)} %shard_map.201.refs_1_), channel_id=1, source_target_pairs={{0,4},{1,5},{2,6},{3,7},{4,0},{5,1},{6,2},{7,3},{8,12},{9,13},{10,... | collective-permute-start | bytes 442376 | tf_op jit(solution)/shard_map/ppermute | solution.py:626
  171.4 13.6 %collective-permute-start.16 = (bf16[576,256]{1,0:T(8,128)(2,1)S(1)}, bf16[576,256]{1,0:T(8,128)(2,1)S(1)}, u32[]{:S(2)}, u32[]{:S(2)}) collective-permute-start(bf16[576,256]{1,0:T(8,128)(2,1)S(1)} %shard_map.203.refs_1_), channel_id=1, source_target_pairs={{0,2},{1,3},{2,0},{3,1},{4,6},{5,7},{6,4},{7,5},{8,10},{9,11},{10,... | collective-permute-start | bytes 884744 | tf_op jit(solution)/shard_map/ppermute | solution.py:626
  173.3 11.7 %all-to-all-start.4 = ((bf16[32,8,256]{2,1,0:T(8,128)(2,1)}), bf16[32,8,256]{2,1,0:T(8,128)(2,1)S(1)}, u32[]{:S(2)}, u32[]{:S(2)}) async-start(bf16[32,8,256]{2,1,0:T(8,128)(2,1)} %bitcast.21), calls=%async_computation.4 | async-start | bytes 262144 | tf_op jit(solution)/shard_map/all_to_all | solution.py:685
  176.8 1.3 collective-permute-start.6
  177.1 1.0 collective-permute-start.7
  185.0 4.5 %collective-permute-start.17 = (bf16[1152,256]{1,0:T(8,128)(2,1)S(1)}, bf16[1152,256]{1,0:T(8,128)(2,1)S(1)}, u32[]{:S(2)}, u32[]{:S(2)}) collective-permute-start(bf16[1152,256]{1,0:T(8,128)(2,1)S(1)} %shard_map.204.refs_1_), channel_id=1, source_target_pairs={{0,1},{1,0},{2,3},{3,2},{4,5},{5,4},{6,7},{7,6},{8,9},{9,8},{10,11... | collective-permute-start | bytes 1769480 | tf_op jit(solution)/shard_map/ppermute | solution.py:626
  (11 other events, 289.3 us)

commit v9 on v8

--- a/solution.py
+++ b/solution.py
@@ -106,13 +106,15 @@
     return 1 - column, column, 3 - line, 2 + line
 
 
-def blocks(bits_ref):
-    column, line = bits_ref[0], bits_ref[1]
-    return column, 1 - column, 2 + line, 3 - line
-
-
-def block_of(index, size, start=0):
-    return pl.ds(pl.multiple_of(start + index * size, 16), size)
+def swapped(bits_ref, rows):
+    column, line = bits_ref[0] == 0, bits_ref[1] == 0
+    first, second, third, fourth = rows
+    return [
+        jnp.where(column, first, second),
+        jnp.where(column, second, first),
+        jnp.where(line, third, fourth),
+        jnp.where(line, fourth, third),
+    ]
 
 
 def chosen_rows(lists_ref, direction, rows):
@@ -140,12 +142,16 @@
         ).astype(bf16)
 
 
-def count_kernel(near_ref, table_ref):
+def count_kernel(near_ref, kept_ref, table_ref, sems):
     neighbours, rows = near_ref.shape
     step = 16
     zero = jnp.zeros((step, LANES), bf16)
     one = jnp.ones((step, LANES), bf16)
     row_blocks = table_ref.shape[0] // CHUNK
+
+    def copy_out(row_block):
+        place = pl.ds(pl.multiple_of(row_block * CHUNK, CHUNK), CHUNK)
+        return pltpu.make_async_copy(table_ref.at[place], kept_ref.at[place], sems.at[row_block])
 
     def rows_of(row_block, _):
         row_at = pl.multiple_of(row_block * CHUNK, CHUNK)
@@ -167,24 +173,23 @@
             return 0
 
         lax.fori_loop(0, rows // LANES, block, 0)
+        copy_out(row_block).start()
         return 0
 
     lax.fori_loop(0, row_blocks, rows_of, 0)
+    for row_block in range(row_blocks):
+        copy_out(row_block).wait()
 
 
 def lift_kernel(
     bits_ref, slots_ref, points_ref, grad_ref, halo0, halo1, halo2, halo3, table_ref, w_ref,
-    table_out, average_out, pre_out, packed_out,
-    ext_ref, average_ref, pre_ref, both_ref, stage_ref, sems, pack_sems, *, neighbours
+    average_out, pre_out, packed_out,
+    average_ref, pre_ref, both_ref, stage_ref, sems, pack_sems, *, neighbours
 ):
     width = points_ref.shape[1]
-    keep_table = pltpu.make_async_copy(table_ref, table_out, sems.at[2])
-    keep_table.start()
-    rows = points_ref.shape[0]
-    ext_ref[0:rows, :] = points_ref[...]
-    for block, halo in zip(blocks(bits_ref), (halo0, halo1, halo2, halo3)):
-        ext_ref[block_of(block, halo.shape[0], rows), :] = halo[...]
-    average = (dot(ext_ref[...], table_ref[...], TN) * (1.0 / neighbours)).astype(bf16)
+    halo = swapped(bits_ref, [halo0[...], halo1[...], halo2[...], halo3[...]])
+    ext = jnp.concatenate([points_ref[...], *halo], axis=0)
+    average = (dot(ext, table_ref[...], TN) * (1.0 / neighbours)).astype(bf16)
     average_ref[...] = average
     keep_average = pltpu.make_async_copy(average_ref, average_out, sems.at[0])
     keep_average.start()
@@ -200,13 +205,12 @@
     pack_rows(slots_ref, both_ref, packed_out, stage_ref, pack_sems)
     keep_average.wait()
     keep_pre.wait()
-    keep_table.wait()
 
 
 def tile_back_kernel(
     bits_ref, slots_ref, back_ref, w_ref, table_in, average_in, pre_in,
     lifted_out, spread_out, near_ref, halo0, halo1, halo2, halo3,
-    table_ref, average_ref, pre_ref, lifted_ref, act_ref, spread_ref, halo_ref, sems, *, neighbours
+    table_ref, average_ref, pre_ref, lifted_ref, act_ref, spread_ref, sems, *, neighbours
 ):
     rows = lifted_ref.shape[0]
     halo_rows = table_ref.shape[0]
@@ -236,16 +240,18 @@
     fetch_average.wait()
     near_ref[...] = dot(average_ref[...], act_ref[...]).astype(near_ref.dtype)
     fetch_table.wait()
-    halo_ref[...] = dot(table_ref[...], spread_ref[...]).astype(bf16)
-    for block, back in zip(blocks(bits_ref), (halo0, halo1, halo2, halo3)):
-        back[...] = halo_ref[block_of(block, back.shape[0]), :]
+    halo = dot(table_ref[...], spread_ref[...])
+    size = halo0.shape[0]
+    parts = swapped(bits_ref, [halo[at * size : (at + 1) * size] for at in range(4)])
+    for part, back in zip(parts, (halo0, halo1, halo2, halo3)):
+        back[...] = part.astype(bf16)
     keep_lifted.wait()
     keep_spread.wait()
 
 
 def finish_kernel(
     bits_ref, lists_ref, back0, back1, back2, back3, table_in, spread_in, lifted_in,
-    out_ref, came_ref, table_ref, spread_ref, lifted_ref, sems
+    out_ref, table_ref, spread_ref, lifted_ref, sems
 ):
     rows = out_ref.shape[0]
     fetch_spread = pltpu.make_async_copy(spread_in, spread_ref, sems.at[0])
@@ -254,9 +260,8 @@
     fetch_spread.start()
     fetch_table.start()
     fetch_lifted.start()
-    for direction, back in zip(turns(bits_ref), (back0, back1, back2, back3)):
-        came_ref[block_of(direction, back.shape[0]), :] = back[...]
-    returned = dot(chosen_rows(lists_ref, 0, rows), came_ref[...])
+    came = swapped(bits_ref, [back1[...], back0[...], back3[...], back2[...]])
+    returned = dot(chosen_rows(lists_ref, 0, rows), jnp.concatenate(came, axis=0))
     fetch_spread.wait()
     fetch_table.wait()
     fetch_lifted.wait()
@@ -735,11 +740,17 @@
         capacity=capacity,
     )
     halos = pairwise(sent[0], sent[1], "tx") + pairwise(sent[2], sent[3], "ty")
-    (table,) = call(count_kernel, [shaped(ext, tile_rows)], [near_tile], flops=8e9)
-    kept_table, average, pre_act, packed = call(
+    kept_table, table = call(
+        count_kernel,
+        [shaped(ext, tile_rows), shaped(ext, tile_rows)],
+        [near_tile],
+        scratch=[pltpu.SemaphoreType.DMA((ext // CHUNK,))],
+        flops=8e9,
+        stored=1,
+    )
+    average, pre_act, packed = call(
         lift_kernel,
         [
-            shaped(ext, tile_rows),
             shaped(width, tile_rows),
             shaped(tile_rows, width, dtype=f32),
             shaped(slots_count, 2 * width),
@@ -747,16 +758,15 @@
         [bits, slots, points_tile, grad_out[0], *halos, table, w_near],
         smem=1,
         scratch=[
-            pltpu.VMEM((ext, width), bf16),
             pltpu.VMEM((width, tile_rows), bf16),
             pltpu.VMEM((tile_rows, width), f32),
             pltpu.VMEM((tile_rows, 2 * width), bf16),
             pltpu.VMEM((slots_count, 2 * width), bf16),
-            pltpu.SemaphoreType.DMA((3,)),
+            pltpu.SemaphoreType.DMA((2,)),
             pltpu.SemaphoreType.DMA((slots_count // WIDE,)),
         ],
         flops=4e9,
-        stored=4,
+        stored=3,
         neighbours=neighbours,
     )
     came = exchange(packed, tiles)
@@ -877,7 +887,6 @@
             pltpu.VMEM((tile_rows, width), bf16),
             pltpu.VMEM((tile_rows, width), bf16),
             pltpu.VMEM((tile_rows, width), bf16),
-            pltpu.VMEM((edge, width), bf16),
             pltpu.SemaphoreType.DMA((5,)),
         ],
         flops=6e9,
@@ -896,16 +905,13 @@
         share=width // tiles,
     )
     near_total = exchange(near_share, tiles)
-    totals = sum_over_mesh(
-        keep, send, [out_rows], [[near_grad], returned[:2], [near_share], [near_total, *returned[2:]]]
-    )
     (grad_points,) = call(
         finish_kernel,
         [shaped(tile_rows, width)],
         [bits, border.reshape(1, edge), *returned, kept_table, spread, lifted_grad],
+        after=[near_total],
         smem=1,
         scratch=[
-            pltpu.VMEM((edge, width), bf16),
             pltpu.VMEM((tile_rows, tile_rows), bf16),
             pltpu.VMEM((tile_rows, width), bf16),
             pltpu.VMEM((tile_rows, width), bf16),
@@ -913,6 +919,9 @@
         ],
         held=3,
         flops=1e9,
+    )
+    totals = sum_over_mesh(
+        keep, send, [out_rows], [[near_grad], returned[:2], [near_share, *returned[2:]], [grad_points]]
     )
     scale = 1.0 / math.sqrt(tiles * tile_rows)
     up_sum, down_sum, conv_sum, gain_one_sum, gain_two_sum, near_sum = call(

time: 192 us -> 195 us (1.016)
  starting transfers between devices: 33.4 us -> 38.6 us
  waiting for transfers between devices: 35.2 us -> 32.6 us
    ppermute x10, starting transfers between devices: 9.94 us -> 17.1 us  [partner(): lax.ppermute(value, axis, [(at, at ^ step) for at in range(lax.axis_size(...]
    all_to_all x4, waiting for transfers between devices: 14.5 us -> 7.82 us  [exchange(): lax.all_to_all(rows, ('tx', 'ty'), split_axis=0, concat_axis=0, tiled=True)]
    ppermute x10, waiting for transfers between devices: 16.1 us -> 22.5 us  [partner(): lax.ppermute(value, axis, [(at, at ^ step) for at in range(lax.axis_size(...]
    ppermute x8, waiting for transfers between devices: 4.64 us -> 2.28 us  [pairwise(): lax.ppermute(rows, axis, pair)]
  transfers between devices with their start and end apart: 22 -> 22, of which waited for: 11 -> 12; matrix products, arithmetic and copies ran while one was open for 0% -> 0% of each run, Pallas kernels for 22% -> 22%
where the time goes in v9:
time: 195 us; the launch traced here: 194 us
  Pallas kernels  63.8 us (33%)
  blocking collectives  57.3 us (29%)
  starting transfers between devices  38.6 us (20%)
  waiting for transfers between devices  32.6 us (17%)
    pallas_call x18, Pallas kernels, call(): pl.pallas_call(run, out_shape=tuple(shapes), in_specs=specs, out_specs=tu...  63.8 us
    all_to_all x1, blocking collectives, exchange(): lax.all_to_all(rows, ('tx', 'ty'), split_axis=0, concat_axis=0, tiled=True)  57.3 us
    ppermute x10, waiting for transfers between devices, partner(): lax.ppermute(value, axis, [(at, at ^ step) for at in range(lax.axis_size(...  22.5 us
    ppermute x10, starting transfers between devices, partner(): lax.ppermute(value, axis, [(at, at ^ step) for at in range(lax.axis_size(...  17.1 us
    all_to_all x4, starting transfers between devices, exchange(): lax.all_to_all(rows, ('tx', 'ty'), split_axis=0, concat_axis=0, tiled=True)  13.9 us
    all_to_all x4, waiting for transfers between devices, exchange(): lax.all_to_all(rows, ('tx', 'ty'), split_axis=0, concat_axis=0, tiled=True)  7.82 us
    ppermute x8, starting transfers between devices, pairwise(): lax.ppermute(rows, axis, pair)  7.59 us
  transfers between devices with their start and end apart: 22, of which 12 were waited for; matrix products, arithmetic and copies ran while one was open for 0% of the time, Pallas kernels for 22%

profile of v9, /device:TPU:0, one launch (start us, length us, event | category | flops | bytes accessed | tf_op | source)
XLA Modules:
  0.0 194.1 jit_solution(2996345428498326385)
XLA Ops:
  1.4 2.2 %shard_map.188 = (s32[1,1024]{1,0:T(1,128)S(1)}, bf16[64,256]{1,0:T(8,128)(2,1)S(1)}, bf16[64,256]{1,0:T(8,128)(2,1)S(1)}, bf16[64,256]{1,0:T(8,128)(2,1)S(1)}, bf16[64,256]{1,0:T(8,128)(2,1)S(1)}) custom-call(s32[2]{0:T(128)S(1)} %pad_add_fusion.refs_0_, s32[1]{0:T(128)S(6)} %copy.23.refs_1_, s32[1,1024]{1,0:T(1,128)} %refs_2_.1, s32[4,64]{1,0:T(4,128)} %bitcast.47, ...), custom_call_target="tpu_custom_call" | custom-call | flops 4000000000 | bytes 664588 | tf_op jit(solution)/shard_map/pallas_call | solution.py:606
  3.5 3.1 %collective-permute-start = (bf16[64,256]{1,0:T(8,128)(2,1)S(1)}, bf16[64,256]{1,0:T(8,128)(2,1)S(1)}, u32[]{:S(2)}, u32[]{:S(2)}) collective-permute-start(bf16[64,256]{1,0:T(8,128)(2,1)S(1)} %get-tuple-element.46), channel_id=1, source_target_pairs={{0,8},{8,0},{16,24},{24,16},{1,9},{9,1},{17,25},{25,17},{2,10},{10... | collective-permute-start | bytes 98312 | tf_op jit(solution)/shard_map/ppermute | solution.py:627
  8.1 5.9 %shard_map.189 = (bf16[1280,1024]{1,0:T(8,128)(2,1)}, bf16[1280,1024]{1,0:T(8,128)(2,1)S(1)}) custom-call(s32[16,1024]{1,0:T(8,128)S(1)} %bitcast.35), custom_call_target="tpu_custom_call" | custom-call | flops 8000000000 | bytes 5308416 | tf_op jit(solution)/shard_map/pallas_call | solution.py:606
  14.0 4.9 %shard_map.190 = (bf16[256,1024]{1,0:T(8,128)(2,1)}, f32[1024,256]{1,0:T(8,128)}, bf16[2048,512]{1,0:T(8,128)(2,1)}) custom-call(s32[2]{0:T(128)S(1)} %pad_add_fusion.refs_0_, s32[1,1024]{1,0:T(1,128)S(1)} %get-tuple-element.45.refs_1_.refs_0_, bf16[1024,256]{1,0:T(8,128)(2,1)S(1)} %bitcast.31, bf16[1024,256]{1,0:T(8,128)(2,1)S(1)} %bitcast.32, ...), custom_call_target="tpu_custom_call" | custom-call | flops 4000000000 | bytes 7606280 | tf_op jit(solution)/shard_map/pallas_call | solution.py:606
  19.0 57.3 %all_to_all.55 = bf16[32,64,512]{2,1,0:T(8,128)(2,1)} all-to-all(bf16[32,64,512]{2,1,0:T(8,128)(2,1)} %bitcast.43), channel_id=1, replica_groups=mesh['tx'=4,'ty'=8] {'tx','ty'}, dimensions={0} | all-to-all | bytes 4194304 | tf_op jit(solution)/shard_map/all_to_all | solution.py:690
  76.4 12.0 %shard_map.191 = (bf16[2048,256]{1,0:T(8,128)(2,1)}, f32[2048,256]{1,0:T(8,128)}, bf16[2048,256]{1,0:T(8,128)(2,1)}) custom-call(s32[1,2048]{1,0:T(1,128)S(1)} %copy-done.8, bf16[768,32]{1,0:T(8,128)(2,1)S(1)} %bitcast.33, f32[1,256]{1,0:T(1,128)S(1)} %bitcast.36, f32[1,256]{1,0:T(1,128)S(1)} %bitcast.38, bf16[256,1024]{1,0:T(8,128)(2,1)S(1)} %copy-done.3, ...), custom_call_target="tpu_custom_call" | custom-call | flops 10000000000 | bytes 7399424 | tf_op jit(solution)/shard_map/pallas_call | solution.py:606
  88.4 3.9 %all-to-all-start.1 = ((bf16[32,64,256]{2,1,0:T(8,128)(2,1)}), bf16[32,64,256]{2,1,0:T(8,128)(2,1)S(1)}, u32[]{:S(2)}, u32[]{:S(2)}) async-start(bf16[32,64,256]{2,1,0:T(8,128)(2,1)} %bitcast.45), calls=%async_computation.1 | async-start | bytes 2097152 | tf_op jit(solution)/shard_map/all_to_all | solution.py:690
  92.3 24.1 %shard_map.193 = (bf16[2048,256]{1,0:T(8,128)(2,1)}, bf16[1152,256]{1,0:T(8,128)(2,1)}, bf16[1152,256]{1,0:T(8,128)(2,1)}) custom-call(s32[1]{0:T(128)} %bitcast.1.refs_0_, s32[1,2048]{1,0:T(1,128)S(1)} %copy-done.8, bf16[768,32]{1,0:T(8,128)(2,1)S(1)} %bitcast.34, f32[1,256]{1,0:T(1,128)S(1)} %bitcast.37, f32[1,256]{1,0:T(1,128)S(1)} %bitcast.39, ...), custom_call_target="tpu_custom_call" | custom-call | flops 40000000000 | bytes 8579076 | tf_op jit(solution)/shard_map/pallas_call | solution.py:606
  116.4 1.9 all-to-all-done.1.refs_1_
  118.3 3.8 %all-to-all-start.2 = ((bf16[32,64,256]{2,1,0:T(8,128)(2,1)}), bf16[32,64,256]{2,1,0:T(8,128)(2,1)S(1)}, u32[]{:S(2)}, u32[]{:S(2)}) async-start(bf16[32,64,256]{2,1,0:T(8,128)(2,1)} %bitcast.40), calls=%async_computation.2 | async-start | bytes 2097152 | tf_op jit(solution)/shard_map/all_to_all | solution.py:690
  122.4 2.1 %shard_map.192.refs_7_.refs_4_ = bf16[1024,256]{1,0:T(8,128)(2,1)} custom-call(s32[1,1024]{1,0:T(1,128)S(1)} %get-tuple-element.45.refs_1_.refs_0_, bf16[2048,256]{1,0:T(8,128)(2,1)S(1)} %bitcast.25), custom_call_target="tpu_custom_call" | custom-call | flops 4000000000 | bytes 1576960 | tf_op jit(solution)/shard_map/pallas_call | solution.py:606
  128.0 7.0 %collective-permute-done.10.refs_5_ = bf16[288,256]{1,0:T(8,128)(2,1)S(1)} collective-permute-done((bf16[288,256]{1,0:T(8,128)(2,1)S(1)}, bf16[288,256]{1,0:T(8,128)(2,1)S(1)}, u32[]{:S(2)}, u32[]{:S(2)}) %collective-permute-start.10) | collective-permute-done | bytes 147488 | tf_op jit(solution)/shard_map/ppermute | solution.py:631
  138.7 3.0 %collective-permute-done.11.refs_1_ = bf16[144,256]{1,0:T(8,128)(2,1)S(1)} collective-permute-done((bf16[144,256]{1,0:T(8,128)(2,1)S(1)}, bf16[144,256]{1,0:T(8,128)(2,1)S(1)}, u32[]{:S(2)}, u32[]{:S(2)}) %collective-permute-start.11) | collective-permute-done | bytes 73760 | tf_op jit(solution)/shard_map/ppermute | solution.py:631
  143.2 5.2 %all-to-all-done.2 = bf16[32,64,256]{2,1,0:T(8,128)(2,1)S(1)} async-done(((bf16[32,64,256]{2,1,0:T(8,128)(2,1)}), bf16[32,64,256]{2,1,0:T(8,128)(2,1)S(1)}, u32[]{:S(2)}, u32[]{:S(2)}) %all-to-all-start.2) | async-done | bytes 1048608 | tf_op jit(solution)/shard_map/all_to_all | solution.py:690
  148.4 5.2 %shard_map.195 = (bf16[1024,256]{1,0:T(8,128)(2,1)}, bf16[1024,256]{1,0:T(8,128)(2,1)}, bf16[256,256]{1,0:T(8,128)(2,1)}, bf16[64,256]{1,0:T(8,128)(2,1)S(1)}, b...) custom-call(s32[2]{0:T(128)S(1)} %pad_add_fusion.refs_0_, ...), custom_call_target="tpu_custom_call" | custom-call | flops 6000000000 | bytes 6688776 | tf_op jit(solution)/shard_map/pallas_call | solution.py:606
  153.6 3.6 %all-to-all-start.3 = ((bf16[32,8,256]{2,1,0:T(8,128)(2,1)}), bf16[32,8,256]{2,1,0:T(8,128)(2,1)S(1)}, u32[]{:S(2)}, u32[]{:S(2)}) async-start(bf16[32,8,256]{2,1,0:T(8,128)(2,1)} %bitcast.16), calls=%async_computation.3 | async-start | bytes 262144 | tf_op jit(solution)/shard_map/all_to_all | solution.py:690
  157.3 2.7 %collective-permute-start.14 = (bf16[288,256]{1,0:T(8,128)(2,1)S(1)}, bf16[288,256]{1,0:T(8,128)(2,1)S(1)}, u32[]{:S(2)}, u32[]{:S(2)}) collective-permute-start(bf16[288,256]{1,0:T(8,128)(2,1)S(1)} %shard_map.201.refs_0_), channel_id=1, source_target_pairs={{0,16},{8,24},{16,0},{24,8},{1,17},{9,25},{17,1},{25,9},{2,18},{10... | collective-permute-start | bytes 442376 | tf_op jit(solution)/shard_map/ppermute | solution.py:631
  162.2 2.0 %collective-permute-done.4.refs_1_.refs_2_ = bf16[64,256]{1,0:T(8,128)(2,1)S(1)} collective-permute-done((bf16[64,256]{1,0:T(8,128)(2,1)S(1)}, bf16[64,256]{1,0:T(8,128)(2,1)S(1)}, u32[]{:S(2)}, u32[]{:S(2)}) %collective-permute-start.4) | collective-permute-done | bytes 32800 | tf_op jit(solution)/shard_map/ppermute | solution.py:627
  164.2 6.3 %collective-permute-done.14.refs_1_ = bf16[288,256]{1,0:T(8,128)(2,1)S(1)} collective-permute-done((bf16[288,256]{1,0:T(8,128)(2,1)S(1)}, bf16[288,256]{1,0:T(8,128)(2,1)S(1)}, u32[]{:S(2)}, u32[]{:S(2)}) %collective-permute-start.14) | collective-permute-done | bytes 147488 | tf_op jit(solution)/shard_map/ppermute | solution.py:631
  172.9 2.6 %all-to-all-start.4 = ((bf16[32,8,256]{2,1,0:T(8,128)(2,1)}), bf16[32,8,256]{2,1,0:T(8,128)(2,1)S(1)}, u32[]{:S(2)}, u32[]{:S(2)}) async-start(bf16[32,8,256]{2,1,0:T(8,128)(2,1)} %bitcast.18), calls=%async_computation.4 | async-start | bytes 262144 | tf_op jit(solution)/shard_map/all_to_all | solution.py:690
  176.8 6.1 %collective-permute-start.16 = (bf16[576,256]{1,0:T(8,128)(2,1)S(1)}, bf16[576,256]{1,0:T(8,128)(2,1)S(1)}, u32[]{:S(2)}, u32[]{:S(2)}) collective-permute-start(bf16[576,256]{1,0:T(8,128)(2,1)S(1)} %shard_map.203.refs_1_), channel_id=1, source_target_pairs={{0,2},{1,3},{2,0},{3,1},{4,6},{5,7},{6,4},{7,5},{8,10},{9,11},{10,... | collective-permute-start | bytes 884744 | tf_op jit(solution)/shard_map/ppermute | solution.py:631
  183.7 4.2 %shard_map.197.refs_3_ = bf16[1024,256]{1,0:T(8,128)(2,1)} custom-call(s32[2]{0:T(128)S(1)} %pad_add_fusion.refs_0_, s32[1,256]{1,0:T(1,128)S(1)} %reshape.63.refs_1_, bf16[64,256]{1,0:T(8,128)(2,1)S(1)} %collective-permute-done.4.refs_1_.refs_2_, bf16[64,256]{1,0:T(8,128)(2,1)S(1)} %collective-permute-done.5.refs_2_.refs_3_, ...), custom_call_target="tpu_custom_call" | custom-call | flops 1000000000 | bytes 4326408 | tf_op jit(solution)/shard_map/pallas_call | solution.py:606
  187.9 2.1 %collective-permute-done.16.refs_2_ = bf16[576,256]{1,0:T(8,128)(2,1)S(1)} collective-permute-done((bf16[576,256]{1,0:T(8,128)(2,1)S(1)}, bf16[576,256]{1,0:T(8,128)(2,1)S(1)}, u32[]{:S(2)}, u32[]{:S(2)}) %collective-permute-start.16) | collective-permute-done | bytes 294944 | tf_op jit(solution)/shard_map/ppermute | solution.py:631
  192.3 1.8 shard_map.205
  (67 shorter events, 19.7 us)
Async XLA Ops:
  3.5 10.4 %collective-permute-start = (bf16[64,256]{1,0:T(8,128)(2,1)S(1)}, bf16[64,256]{1,0:T(8,128)(2,1)S(1)}, u32[]{:S(2)}, u32[]{:S(2)}) collective-permute-start(bf16[64,256]{1,0:T(8,128)(2,1)S(1)} %get-tuple-element.46), channel_id=1, source_target_pairs={{0,8},{8,0},{16,24},{24,16},{1,9},{9,1},{17,25},{25,17},{2,10},{10... | collective-permute-start | bytes 98312 | tf_op jit(solution)/shard_map/ppermute | solution.py:627
  6.6 7.3 %collective-permute-start.1 = (bf16[64,256]{1,0:T(8,128)(2,1)S(1)}, bf16[64,256]{1,0:T(8,128)(2,1)S(1)}, u32[]{:S(2)}, u32[]{:S(2)}) collective-permute-start(bf16[64,256]{1,0:T(8,128)(2,1)S(1)} %get-tuple-element.47), channel_id=1, source_target_pairs={{8,16},{16,8},{9,17},{17,9},{10,18},{18,10},{11,19},{19,11},{12,20... | collective-permute-start | bytes 98312 | tf_op jit(solution)/shard_map/ppermute | solution.py:627
  7.3 6.7 %collective-permute-start.2 = (bf16[64,256]{1,0:T(8,128)(2,1)S(1)}, bf16[64,256]{1,0:T(8,128)(2,1)S(1)}, u32[]{:S(2)}, u32[]{:S(2)}) collective-permute-start(bf16[64,256]{1,0:T(8,128)(2,1)S(1)} %get-tuple-element.48), channel_id=1, source_target_pairs={{0,1},{1,0},{2,3},{3,2},{4,5},{5,4},{6,7},{7,6},{8,9},{9,8},{10,11... | collective-permute-start | bytes 98312 | tf_op jit(solution)/shard_map/ppermute | solution.py:627
  7.4 6.6 %collective-permute-start.3 = (bf16[64,256]{1,0:T(8,128)(2,1)S(1)}, bf16[64,256]{1,0:T(8,128)(2,1)S(1)}, u32[]{:S(2)}, u32[]{:S(2)}) collective-permute-start(bf16[64,256]{1,0:T(8,128)(2,1)S(1)} %get-tuple-element.49), channel_id=1, source_target_pairs={{1,2},{2,1},{3,4},{4,3},{5,6},{6,5},{9,10},{10,9},{11,12},{12,11},... | collective-permute-start | bytes 98312 | tf_op jit(solution)/shard_map/ppermute | solution.py:627
  18.9 57.4 %copy-start.3 = (bf16[256,1024]{1,0:T(8,128)(2,1)S(1)}, bf16[256,1024]{1,0:T(8,128)(2,1)}, u32[]{:S(2)}) copy-start(bf16[256,1024]{1,0:T(8,128)(2,1)} %refs_5_.3) | copy-start | bytes 1572868
  18.9 57.4 %copy-start.4 = (bf16[1024,256]{1,0:T(8,128)(2,1)S(1)}, bf16[1024,256]{1,0:T(8,128)(2,1)}, u32[]{:S(2)}) copy-start(bf16[1024,256]{1,0:T(8,128)(2,1)} %refs_6_.1) | copy-start | bytes 1572868
  88.4 29.9 %all-to-all-start.1 = ((bf16[32,64,256]{2,1,0:T(8,128)(2,1)}), bf16[32,64,256]{2,1,0:T(8,128)(2,1)S(1)}, u32[]{:S(2)}, u32[]{:S(2)}) async-start(bf16[32,64,256]{2,1,0:T(8,128)(2,1)} %bitcast.45), calls=%async_computation.1 | async-start | bytes 2097152 | tf_op jit(solution)/shard_map/all_to_all | solution.py:690
  118.3 30.1 %all-to-all-start.2 = ((bf16[32,64,256]{2,1,0:T(8,128)(2,1)}), bf16[32,64,256]{2,1,0:T(8,128)(2,1)S(1)}, u32[]{:S(2)}, u32[]{:S(2)}) async-start(bf16[32,64,256]{2,1,0:T(8,128)(2,1)} %bitcast.40), calls=%async_computation.2 | async-start | bytes 2097152 | tf_op jit(solution)/shard_map/all_to_all | solution.py:690
  122.1 2.4 %collective-permute-start.8 = (bf16[1152,256]{1,0:T(8,128)(2,1)S(1)}, bf16[1152,256]{1,0:T(8,128)(2,1)S(1)}, u32[]{:S(2)}, u32[]{:S(2)}) collective-permute-start(bf16[1152,256]{1,0:T(8,128)(2,1)S(1)} %copy-done.12), channel_id=1, source_target_pairs={{0,1},{1,0},{2,3},{3,2},{4,5},{5,4},{6,7},{7,6},{8,9},{9,8},{10,11... | collective-permute-start | bytes 1769480 | tf_op jit(solution)/shard_map/ppermute | solution.py:631
  124.8 10.2 %collective-permute-start.10 = (bf16[288,256]{1,0:T(8,128)(2,1)S(1)}, bf16[288,256]{1,0:T(8,128)(2,1)S(1)}, u32[]{:S(2)}, u32[]{:S(2)}) collective-permute-start(bf16[288,256]{1,0:T(8,128)(2,1)S(1)} %get-tuple-element.71), channel_id=1, source_target_pairs={{0,4},{1,5},{2,6},{3,7},{4,0},{5,1},{6,2},{7,3},{8,12},{9,13},{10,... | collective-permute-start | bytes 442376 | tf_op jit(solution)/shard_map/ppermute | solution.py:631
  126.6 10.2 %collective-permute-start.9 = (bf16[288,256]{1,0:T(8,128)(2,1)S(1)}, bf16[288,256]{1,0:T(8,128)(2,1)S(1)}, u32[]{:S(2)}, u32[]{:S(2)}) collective-permute-start(bf16[288,256]{1,0:T(8,128)(2,1)S(1)} %get-tuple-element.69), channel_id=1, source_target_pairs={{0,2},{1,3},{2,0},{3,1},{4,6},{5,7},{6,4},{7,5},{8,10},{9,11},{10,... | collective-permute-start | bytes 442376 | tf_op jit(solution)/shard_map/ppermute | solution.py:631
  137.0 4.8 %collective-permute-start.11 = (bf16[144,256]{1,0:T(8,128)(2,1)S(1)}, bf16[144,256]{1,0:T(8,128)(2,1)S(1)}, u32[]{:S(2)}, u32[]{:S(2)}) collective-permute-start(bf16[144,256]{1,0:T(8,128)(2,1)S(1)} %get-tuple-element.73), channel_id=1, source_target_pairs={{0,4},{1,5},{2,6},{3,7},{4,0},{5,1},{6,2},{7,3},{8,12},{9,13},{10,... | collective-permute-start | bytes 221192 | tf_op jit(solution)/shard_map/ppermute | solution.py:631
  138.0 4.4 %collective-permute-start.12 = (bf16[144,256]{1,0:T(8,128)(2,1)S(1)}, bf16[144,256]{1,0:T(8,128)(2,1)S(1)}, u32[]{:S(2)}, u32[]{:S(2)}) collective-permute-start(bf16[144,256]{1,0:T(8,128)(2,1)S(1)} %get-tuple-element.75), channel_id=1, source_target_pairs={{0,2},{1,3},{2,0},{3,1},{4,6},{5,7},{6,4},{7,5},{8,10},{9,11},{10,... | collective-permute-start | bytes 221192 | tf_op jit(solution)/shard_map/ppermute | solution.py:631
  142.4 14.8 %collective-permute-start.13 = (bf16[288,256]{1,0:T(8,128)(2,1)S(1)}, bf16[288,256]{1,0:T(8,128)(2,1)S(1)}, u32[]{:S(2)}, u32[]{:S(2)}) collective-permute-start(bf16[288,256]{1,0:T(8,128)(2,1)S(1)} %shard_map.200.refs_0_), channel_id=1, source_target_pairs={{0,8},{8,0},{16,24},{24,16},{1,9},{9,1},{17,25},{25,17},{2,10},{10... | collective-permute-start | bytes 442376 | tf_op jit(solution)/shard_map/ppermute | solution.py:631
  153.6 18.5 %all-to-all-start.3 = ((bf16[32,8,256]{2,1,0:T(8,128)(2,1)}), bf16[32,8,256]{2,1,0:T(8,128)(2,1)S(1)}, u32[]{:S(2)}, u32[]{:S(2)}) async-start(bf16[32,8,256]{2,1,0:T(8,128)(2,1)} %bitcast.16), calls=%async_computation.3 | async-start | bytes 262144 | tf_op jit(solution)/shard_map/all_to_all | solution.py:690
  157.3 13.2 %collective-permute-start.14 = (bf16[288,256]{1,0:T(8,128)(2,1)S(1)}, bf16[288,256]{1,0:T(8,128)(2,1)S(1)}, u32[]{:S(2)}, u32[]{:S(2)}) collective-permute-start(bf16[288,256]{1,0:T(8,128)(2,1)S(1)} %shard_map.201.refs_0_), channel_id=1, source_target_pairs={{0,16},{8,24},{16,0},{24,8},{1,17},{9,25},{17,1},{25,9},{2,18},{10... | collective-permute-start | bytes 442376 | tf_op jit(solution)/shard_map/ppermute | solution.py:631
  160.0 4.1 %collective-permute-start.4 = (bf16[64,256]{1,0:T(8,128)(2,1)S(1)}, bf16[64,256]{1,0:T(8,128)(2,1)S(1)}, u32[]{:S(2)}, u32[]{:S(2)}) collective-permute-start(bf16[64,256]{1,0:T(8,128)(2,1)S(1)} %get-tuple-element.59), channel_id=1, source_target_pairs={{0,8},{8,0},{16,24},{24,16},{1,9},{9,1},{17,25},{25,17},{2,10},{10... | collective-permute-start | bytes 98312 | tf_op jit(solution)/shard_map/ppermute | solution.py:627
  161.5 2.6 %collective-permute-start.5 = (bf16[64,256]{1,0:T(8,128)(2,1)S(1)}, bf16[64,256]{1,0:T(8,128)(2,1)S(1)}, u32[]{:S(2)}, u32[]{:S(2)}) collective-permute-start(bf16[64,256]{1,0:T(8,128)(2,1)S(1)} %get-tuple-element.60), channel_id=1, source_target_pairs={{8,16},{16,8},{9,17},{17,9},{10,18},{18,10},{11,19},{19,11},{12,20... | collective-permute-start | bytes 98312 | tf_op jit(solution)/shard_map/ppermute | solution.py:627
  170.5 6.3 %collective-permute-start.15 = (bf16[288,256]{1,0:T(8,128)(2,1)S(1)}, bf16[288,256]{1,0:T(8,128)(2,1)S(1)}, u32[]{:S(2)}, u32[]{:S(2)}) collective-permute-start(bf16[288,256]{1,0:T(8,128)(2,1)S(1)} %shard_map.202.refs_1_), channel_id=1, source_target_pairs={{0,4},{1,5},{2,6},{3,7},{4,0},{5,1},{6,2},{7,3},{8,12},{9,13},{10,... | collective-permute-start | bytes 442376 | tf_op jit(solution)/shard_map/ppermute | solution.py:631
  172.9 10.8 %all-to-all-start.4 = ((bf16[32,8,256]{2,1,0:T(8,128)(2,1)}), bf16[32,8,256]{2,1,0:T(8,128)(2,1)S(1)}, u32[]{:S(2)}, u32[]{:S(2)}) async-start(bf16[32,8,256]{2,1,0:T(8,128)(2,1)} %bitcast.18), calls=%async_computation.4 | async-start | bytes 262144 | tf_op jit(solution)/shard_map/all_to_all | solution.py:690
  175.5 1.3 collective-permute-start.6
  175.8 1.0 collective-permute-start.7
  176.8 13.2 %collective-permute-start.16 = (bf16[576,256]{1,0:T(8,128)(2,1)S(1)}, bf16[576,256]{1,0:T(8,128)(2,1)S(1)}, u32[]{:S(2)}, u32[]{:S(2)}) collective-permute-start(bf16[576,256]{1,0:T(8,128)(2,1)S(1)} %shard_map.203.refs_1_), channel_id=1, source_target_pairs={{0,2},{1,3},{2,0},{3,1},{4,6},{5,7},{6,4},{7,5},{8,10},{9,11},{10,... | collective-permute-start | bytes 884744 | tf_op jit(solution)/shard_map/ppermute | solution.py:631
  190.0 2.3 %collective-permute-start.17 = (bf16[1152,256]{1,0:T(8,128)(2,1)S(1)}, bf16[1152,256]{1,0:T(8,128)(2,1)S(1)}, u32[]{:S(2)}, u32[]{:S(2)}) collective-permute-start(bf16[1152,256]{1,0:T(8,128)(2,1)S(1)} %shard_map.204.refs_1_), channel_id=1, source_target_pairs={{0,1},{1,0},{2,3},{3,2},{4,5},{5,4},{6,7},{7,6},{8,9},{9,8},{10,11... | collective-permute-start | bytes 1769480 | tf_op jit(solution)/shard_map/ppermute | solution.py:631
  (11 other events, 289.3 us)

commit v10 on v8

--- a/solution.py
+++ b/solution.py
@@ -218,12 +218,12 @@
     fetch_table.start()
     keep_lifted = pltpu.make_async_copy(lifted_ref, lifted_out, sems.at[3])
     keep_spread = pltpu.make_async_copy(spread_ref, spread_out, sems.at[4])
-    for start in range(0, rows, CHUNK):
-        column = column_of(slots_ref[:, start : start + CHUNK], CHUNK)
+    for start in range(0, rows, WIDE):
+        column = column_of(slots_ref[:, start : start + WIDE], WIDE)
         wide = dot(pick_rows(column, back_ref.shape[0]), back_ref[...])
         if start == 0:
             fetch_pre.wait()
-        for row in range(0, CHUNK, BLOCK):
+        for row in range(0, WIDE, BLOCK):
             here = pl.ds(start + row, BLOCK)
             lifted_grad = wide[row : row + BLOCK]
             lifted_ref[here, :] = lifted_grad.astype(bf16)
@@ -342,14 +342,14 @@
         for copy in keep(at):
             copy.start()
         yield
-        for start in range(0, PATCH, CHUNK):
-            value = dot(second_at[pl.ds(start, CHUNK), :], up_ref[...])
-            for row in range(0, CHUNK, 16):
+        for start in range(0, PATCH, WIDE):
+            value = dot(second_at[pl.ds(start, WIDE), :], up_ref[...])
+            for row in range(0, WIDE, 16):
                 for col in range(0, hidden_width, 2 * LANES):
                     hidden_at[pl.ds(start + row, 16), pl.ds(col, 2 * LANES)] = gelu_tanh(
                         value[row : row + 16, col : col + 2 * LANES]
                     ).astype(bf16)
-            if start + CHUNK == PATCH // 2:
+            if start + WIDE == PATCH // 2:
                 yield
         yield
         for start in range(0, PATCH, WIDE):

time: 192 us -> 192 us (level)
  no operation moved by 1% of the time
where the time goes in v10:
time: 192 us; the launch traced here: 191 us
  Pallas kernels  63.4 us (33%)
  blocking collectives  57.3 us (30%)
  waiting for transfers between devices  35.2 us (18%)
  starting transfers between devices  33.4 us (17%)
    pallas_call x18, Pallas kernels, call(): pl.pallas_call(run, out_shape=tuple(shapes), in_specs=specs, out_specs=tu...  63.4 us
    all_to_all x1, blocking collectives, exchange(): lax.all_to_all(rows, ('tx', 'ty'), split_axis=0, concat_axis=0, tiled=True)  57.3 us
    ppermute x10, waiting for transfers between devices, partner(): lax.ppermute(value, axis, [(at, at ^ step) for at in range(lax.axis_size(...  16.1 us
    all_to_all x4, starting transfers between devices, exchange(): lax.all_to_all(rows, ('tx', 'ty'), split_axis=0, concat_axis=0, tiled=True)  15.5 us
    all_to_all x4, waiting for transfers between devices, exchange(): lax.all_to_all(rows, ('tx', 'ty'), split_axis=0, concat_axis=0, tiled=True)  14.5 us
    ppermute x10, starting transfers between devices, partner(): lax.ppermute(value, axis, [(at, at ^ step) for at in range(lax.axis_size(...  9.94 us
    ppermute x8, starting transfers between devices, pairwise(): lax.ppermute(rows, axis, pair)  7.93 us
    ppermute x8, waiting for transfers between devices, pairwise(): lax.ppermute(rows, axis, pair)  4.63 us
  transfers between devices with their start and end apart: 22, of which 11 were waited for; matrix products, arithmetic and copies ran while one was open for 0% of the time, Pallas kernels for 22%

profile of v10, /device:TPU:0, one launch (start us, length us, event | category | flops | bytes accessed | tf_op | source)
XLA Modules:
  0.0 191.3 jit_solution(1917829400315505913)
XLA Ops:
  1.4 2.2 %shard_map.188 = (s32[1,1024]{1,0:T(1,128)S(1)}, bf16[64,256]{1,0:T(8,128)(2,1)S(1)}, bf16[64,256]{1,0:T(8,128)(2,1)S(1)}, bf16[64,256]{1,0:T(8,128)(2,1)S(1)}, bf16[64,256]{1,0:T(8,128)(2,1)S(1)}) custom-call(s32[2]{0:T(128)S(1)} %pad_add_fusion.refs_0_, s32[1]{0:T(128)S(6)} %copy.23.refs_1_, s32[1,1024]{1,0:T(1,128)} %refs_2_.1, s32[4,64]{1,0:T(4,128)} %bitcast.47, ...), custom_call_target="tpu_custom_call" | custom-call | flops 4000000000 | bytes 664588 | tf_op jit(solution)/shard_map/pallas_call | solution.py:601
  3.5 3.1 %collective-permute-start = (bf16[64,256]{1,0:T(8,128)(2,1)S(1)}, bf16[64,256]{1,0:T(8,128)(2,1)S(1)}, u32[]{:S(2)}, u32[]{:S(2)}) collective-permute-start(bf16[64,256]{1,0:T(8,128)(2,1)S(1)} %get-tuple-element.45), channel_id=1, source_target_pairs={{0,8},{8,0},{16,24},{24,16},{1,9},{9,1},{17,25},{25,17},{2,10},{10... | collective-permute-start | bytes 98312 | tf_op jit(solution)/shard_map/ppermute | solution.py:622
  8.1 5.0 %shard_map.189.refs_8_ = bf16[1280,1024]{1,0:T(8,128)(2,1)S(1)} custom-call(s32[16,1024]{1,0:T(8,128)S(1)} %bitcast.35), custom_call_target="tpu_custom_call" | custom-call | flops 8000000000 | bytes 2686976 | tf_op jit(solution)/shard_map/pallas_call | solution.py:601
  13.2 5.6 %shard_map.190 = (bf16[1280,1024]{1,0:T(8,128)(2,1)}, bf16[256,1024]{1,0:T(8,128)(2,1)}, f32[1024,256]{1,0:T(8,128)}, bf16[2048,512]{1,0:T(8,128)(2,1)}) custom-call(s32[2]{0:T(128)S(1)} %pad_add_fusion.refs_0_, s32[1,1024]{1,0:T(1,128)S(1)} %get-tuple-element.44.refs_1_.refs_0_, bf16[1024,256]{1,0:T(8,128)(2,1)S(1)} %bitcast.31, ...), custom_call_target="tpu_custom_call" | custom-call | flops 4000000000 | bytes 10227720 | tf_op jit(solution)/shard_map/pallas_call | solution.py:601
  18.8 57.3 %all_to_all.55 = bf16[32,64,512]{2,1,0:T(8,128)(2,1)} all-to-all(bf16[32,64,512]{2,1,0:T(8,128)(2,1)} %bitcast.43), channel_id=1, replica_groups=mesh['tx'=4,'ty'=8] {'tx','ty'}, dimensions={0} | all-to-all | bytes 4194304 | tf_op jit(solution)/shard_map/all_to_all | solution.py:685
  76.2 11.9 %shard_map.191 = (bf16[2048,256]{1,0:T(8,128)(2,1)}, f32[2048,256]{1,0:T(8,128)}, bf16[2048,256]{1,0:T(8,128)(2,1)}) custom-call(s32[1,2048]{1,0:T(1,128)S(1)} %copy-done.8, bf16[768,32]{1,0:T(8,128)(2,1)S(1)} %bitcast.33, f32[1,256]{1,0:T(1,128)S(1)} %bitcast.36, f32[1,256]{1,0:T(1,128)S(1)} %bitcast.38, bf16[256,1024]{1,0:T(8,128)(2,1)S(1)} %copy-done.3, ...), custom_call_target="tpu_custom_call" | custom-call | flops 10000000000 | bytes 7399424 | tf_op jit(solution)/shard_map/pallas_call | solution.py:601
  88.1 3.9 %all-to-all-start.1 = ((bf16[32,64,256]{2,1,0:T(8,128)(2,1)}), bf16[32,64,256]{2,1,0:T(8,128)(2,1)S(1)}, u32[]{:S(2)}, u32[]{:S(2)}) async-start(bf16[32,64,256]{2,1,0:T(8,128)(2,1)} %bitcast.44), calls=%async_computation.1 | async-start | bytes 2097152 | tf_op jit(solution)/shard_map/all_to_all | solution.py:685
  92.0 24.1 %shard_map.193 = (bf16[2048,256]{1,0:T(8,128)(2,1)}, bf16[1152,256]{1,0:T(8,128)(2,1)}, bf16[1152,256]{1,0:T(8,128)(2,1)}) custom-call(s32[1]{0:T(128)} %bitcast.1.refs_0_, s32[1,2048]{1,0:T(1,128)S(1)} %copy-done.8, bf16[768,32]{1,0:T(8,128)(2,1)S(1)} %bitcast.34, f32[1,256]{1,0:T(1,128)S(1)} %bitcast.37, f32[1,256]{1,0:T(1,128)S(1)} %bitcast.39, ...), custom_call_target="tpu_custom_call" | custom-call | flops 40000000000 | bytes 8579076 | tf_op jit(solution)/shard_map/pallas_call | solution.py:601
  116.2 1.9 all-to-all-done.1.refs_1_
  118.0 3.8 %all-to-all-start.2 = ((bf16[32,64,256]{2,1,0:T(8,128)(2,1)}), bf16[32,64,256]{2,1,0:T(8,128)(2,1)S(1)}, u32[]{:S(2)}, u32[]{:S(2)}) async-start(bf16[32,64,256]{2,1,0:T(8,128)(2,1)} %bitcast.40), calls=%async_computation.2 | async-start | bytes 2097152 | tf_op jit(solution)/shard_map/all_to_all | solution.py:685
  122.2 2.1 %shard_map.192.refs_7_.refs_4_ = bf16[1024,256]{1,0:T(8,128)(2,1)} custom-call(s32[1,1024]{1,0:T(1,128)S(1)} %get-tuple-element.44.refs_1_.refs_0_, bf16[2048,256]{1,0:T(8,128)(2,1)S(1)} %bitcast.25), custom_call_target="tpu_custom_call" | custom-call | flops 4000000000 | bytes 1576960 | tf_op jit(solution)/shard_map/pallas_call | solution.py:601
  127.8 7.0 %collective-permute-done.10.refs_5_ = bf16[288,256]{1,0:T(8,128)(2,1)S(1)} collective-permute-done((bf16[288,256]{1,0:T(8,128)(2,1)S(1)}, bf16[288,256]{1,0:T(8,128)(2,1)S(1)}, u32[]{:S(2)}, u32[]{:S(2)}) %collective-permute-start.10) | collective-permute-done | bytes 147488 | tf_op jit(solution)/shard_map/ppermute | solution.py:626
  138.5 3.0 %collective-permute-done.11.refs_1_ = bf16[144,256]{1,0:T(8,128)(2,1)S(1)} collective-permute-done((bf16[144,256]{1,0:T(8,128)(2,1)S(1)}, bf16[144,256]{1,0:T(8,128)(2,1)S(1)}, u32[]{:S(2)}, u32[]{:S(2)}) %collective-permute-start.11) | collective-permute-done | bytes 73760 | tf_op jit(solution)/shard_map/ppermute | solution.py:626
  143.0 5.2 %all-to-all-done.2 = bf16[32,64,256]{2,1,0:T(8,128)(2,1)S(1)} async-done(((bf16[32,64,256]{2,1,0:T(8,128)(2,1)}), bf16[32,64,256]{2,1,0:T(8,128)(2,1)S(1)}, u32[]{:S(2)}, u32[]{:S(2)}) %all-to-all-start.2) | async-done | bytes 1048608 | tf_op jit(solution)/shard_map/all_to_all | solution.py:685
  148.2 5.1 %shard_map.195 = (bf16[1024,256]{1,0:T(8,128)(2,1)}, bf16[1024,256]{1,0:T(8,128)(2,1)}, bf16[256,256]{1,0:T(8,128)(2,1)}, bf16[64,256]{1,0:T(8,128)(2,1)S(1)}, b...) custom-call(s32[2]{0:T(128)S(1)} %pad_add_fusion.refs_0_, ...), custom_call_target="tpu_custom_call" | custom-call | flops 6000000000 | bytes 6688776 | tf_op jit(solution)/shard_map/pallas_call | solution.py:601
  154.0 4.4 %all-to-all-start.3 = ((bf16[32,8,256]{2,1,0:T(8,128)(2,1)}), bf16[32,8,256]{2,1,0:T(8,128)(2,1)S(1)}, u32[]{:S(2)}, u32[]{:S(2)}) async-start(bf16[32,8,256]{2,1,0:T(8,128)(2,1)} %bitcast.19), calls=%async_computation.3 | async-start | bytes 262144 | tf_op jit(solution)/shard_map/all_to_all | solution.py:685
  158.5 1.8 collective-permute-start.4
  161.0 4.3 %collective-permute-done.4.refs_2_.refs_1_ = bf16[64,256]{1,0:T(8,128)(2,1)S(1)} collective-permute-done((bf16[64,256]{1,0:T(8,128)(2,1)S(1)}, bf16[64,256]{1,0:T(8,128)(2,1)S(1)}, u32[]{:S(2)}, u32[]{:S(2)}) %collective-permute-start.4) | collective-permute-done | bytes 32800 | tf_op jit(solution)/shard_map/ppermute | solution.py:622
  167.6 3.6 %collective-permute-done.15.refs_2_ = bf16[288,256]{1,0:T(8,128)(2,1)S(1)} collective-permute-done((bf16[288,256]{1,0:T(8,128)(2,1)S(1)}, bf16[288,256]{1,0:T(8,128)(2,1)S(1)}, u32[]{:S(2)}, u32[]{:S(2)}) %collective-permute-start.15) | collective-permute-done | bytes 147488 | tf_op jit(solution)/shard_map/ppermute | solution.py:626
  171.2 2.0 %collective-permute-start.16 = (bf16[576,256]{1,0:T(8,128)(2,1)S(1)}, bf16[576,256]{1,0:T(8,128)(2,1)S(1)}, u32[]{:S(2)}, u32[]{:S(2)}) collective-permute-start(bf16[576,256]{1,0:T(8,128)(2,1)S(1)} %shard_map.203.refs_1_), channel_id=1, source_target_pairs={{0,2},{1,3},{2,0},{3,1},{4,6},{5,7},{6,4},{7,5},{8,10},{9,11},{10,... | collective-permute-start | bytes 884744 | tf_op jit(solution)/shard_map/ppermute | solution.py:626
  173.2 3.4 %all-to-all-start.4 = ((bf16[32,8,256]{2,1,0:T(8,128)(2,1)}), bf16[32,8,256]{2,1,0:T(8,128)(2,1)S(1)}, u32[]{:S(2)}, u32[]{:S(2)}) async-start(bf16[32,8,256]{2,1,0:T(8,128)(2,1)} %bitcast.21), calls=%async_computation.4 | async-start | bytes 262144 | tf_op jit(solution)/shard_map/all_to_all | solution.py:685
  177.9 7.0 %all-to-all-done.4 = bf16[32,8,256]{2,1,0:T(8,128)(2,1)S(1)} async-done(((bf16[32,8,256]{2,1,0:T(8,128)(2,1)}), bf16[32,8,256]{2,1,0:T(8,128)(2,1)S(1)}, u32[]{:S(2)}, u32[]{:S(2)}) %all-to-all-start.4) | async-done | bytes 131104 | tf_op jit(solution)/shard_map/all_to_all | solution.py:685
  185.3 4.2 %shard_map.196 = bf16[1024,256]{1,0:T(8,128)(2,1)} custom-call(s32[2]{0:T(128)S(1)} %pad_add_fusion.refs_0_, s32[1,256]{1,0:T(1,128)S(1)} %reshape.63.refs_1_, bf16[64,256]{1,0:T(8,128)(2,1)S(1)} %collective-permute-done.4.refs_2_.refs_1_, bf16[64,256]{1,0:T(8,128)(2,1)S(1)} %collective-permute-done.5.refs_3_.refs_2_, ...), custom_call_target="tpu_custom_call" | custom-call | flops 1000000000 | bytes 4326408 | tf_op jit(solution)/shard_map/pallas_call | solution.py:601
  189.5 1.9 shard_map.205
  (67 shorter events, 16.0 us)
Async XLA Ops:
  3.5 9.5 %collective-permute-start = (bf16[64,256]{1,0:T(8,128)(2,1)S(1)}, bf16[64,256]{1,0:T(8,128)(2,1)S(1)}, u32[]{:S(2)}, u32[]{:S(2)}) collective-permute-start(bf16[64,256]{1,0:T(8,128)(2,1)S(1)} %get-tuple-element.45), channel_id=1, source_target_pairs={{0,8},{8,0},{16,24},{24,16},{1,9},{9,1},{17,25},{25,17},{2,10},{10... | collective-permute-start | bytes 98312 | tf_op jit(solution)/shard_map/ppermute | solution.py:622
  6.6 6.5 %collective-permute-start.1 = (bf16[64,256]{1,0:T(8,128)(2,1)S(1)}, bf16[64,256]{1,0:T(8,128)(2,1)S(1)}, u32[]{:S(2)}, u32[]{:S(2)}) collective-permute-start(bf16[64,256]{1,0:T(8,128)(2,1)S(1)} %get-tuple-element.46), channel_id=1, source_target_pairs={{8,16},{16,8},{9,17},{17,9},{10,18},{18,10},{11,19},{19,11},{12,20... | collective-permute-start | bytes 98312 | tf_op jit(solution)/shard_map/ppermute | solution.py:622
  7.3 5.8 %collective-permute-start.2 = (bf16[64,256]{1,0:T(8,128)(2,1)S(1)}, bf16[64,256]{1,0:T(8,128)(2,1)S(1)}, u32[]{:S(2)}, u32[]{:S(2)}) collective-permute-start(bf16[64,256]{1,0:T(8,128)(2,1)S(1)} %get-tuple-element.47), channel_id=1, source_target_pairs={{0,1},{1,0},{2,3},{3,2},{4,5},{5,4},{6,7},{7,6},{8,9},{9,8},{10,11... | collective-permute-start | bytes 98312 | tf_op jit(solution)/shard_map/ppermute | solution.py:622
  7.4 5.8 %collective-permute-start.3 = (bf16[64,256]{1,0:T(8,128)(2,1)S(1)}, bf16[64,256]{1,0:T(8,128)(2,1)S(1)}, u32[]{:S(2)}, u32[]{:S(2)}) collective-permute-start(bf16[64,256]{1,0:T(8,128)(2,1)S(1)} %get-tuple-element.48), channel_id=1, source_target_pairs={{1,2},{2,1},{3,4},{4,3},{5,6},{6,5},{9,10},{10,9},{11,12},{12,11},... | collective-permute-start | bytes 98312 | tf_op jit(solution)/shard_map/ppermute | solution.py:622
  18.7 57.4 %copy-start.3 = (bf16[256,1024]{1,0:T(8,128)(2,1)S(1)}, bf16[256,1024]{1,0:T(8,128)(2,1)}, u32[]{:S(2)}) copy-start(bf16[256,1024]{1,0:T(8,128)(2,1)} %refs_5_.3) | copy-start | bytes 1572868
  18.7 57.4 %copy-start.4 = (bf16[1024,256]{1,0:T(8,128)(2,1)S(1)}, bf16[1024,256]{1,0:T(8,128)(2,1)}, u32[]{:S(2)}) copy-start(bf16[1024,256]{1,0:T(8,128)(2,1)} %refs_6_.1) | copy-start | bytes 1572868
  88.1 29.9 %all-to-all-start.1 = ((bf16[32,64,256]{2,1,0:T(8,128)(2,1)}), bf16[32,64,256]{2,1,0:T(8,128)(2,1)S(1)}, u32[]{:S(2)}, u32[]{:S(2)}) async-start(bf16[32,64,256]{2,1,0:T(8,128)(2,1)} %bitcast.44), calls=%async_computation.1 | async-start | bytes 2097152 | tf_op jit(solution)/shard_map/all_to_all | solution.py:685
  118.0 30.1 %all-to-all-start.2 = ((bf16[32,64,256]{2,1,0:T(8,128)(2,1)}), bf16[32,64,256]{2,1,0:T(8,128)(2,1)S(1)}, u32[]{:S(2)}, u32[]{:S(2)}) async-start(bf16[32,64,256]{2,1,0:T(8,128)(2,1)} %bitcast.40), calls=%async_computation.2 | async-start | bytes 2097152 | tf_op jit(solution)/shard_map/all_to_all | solution.py:685
  121.8 2.4 %collective-permute-start.8 = (bf16[1152,256]{1,0:T(8,128)(2,1)S(1)}, bf16[1152,256]{1,0:T(8,128)(2,1)S(1)}, u32[]{:S(2)}, u32[]{:S(2)}) collective-permute-start(bf16[1152,256]{1,0:T(8,128)(2,1)S(1)} %copy-done.12), channel_id=1, source_target_pairs={{0,1},{1,0},{2,3},{3,2},{4,5},{5,4},{6,7},{7,6},{8,9},{9,8},{10,11... | collective-permute-start | bytes 1769480 | tf_op jit(solution)/shard_map/ppermute | solution.py:626
  124.6 10.2 %collective-permute-start.10 = (bf16[288,256]{1,0:T(8,128)(2,1)S(1)}, bf16[288,256]{1,0:T(8,128)(2,1)S(1)}, u32[]{:S(2)}, u32[]{:S(2)}) collective-permute-start(bf16[288,256]{1,0:T(8,128)(2,1)S(1)} %get-tuple-element.68), channel_id=1, source_target_pairs={{0,4},{1,5},{2,6},{3,7},{4,0},{5,1},{6,2},{7,3},{8,12},{9,13},{10,... | collective-permute-start | bytes 442376 | tf_op jit(solution)/shard_map/ppermute | solution.py:626
  126.3 10.2 %collective-permute-start.9 = (bf16[288,256]{1,0:T(8,128)(2,1)S(1)}, bf16[288,256]{1,0:T(8,128)(2,1)S(1)}, u32[]{:S(2)}, u32[]{:S(2)}) collective-permute-start(bf16[288,256]{1,0:T(8,128)(2,1)S(1)} %get-tuple-element.66), channel_id=1, source_target_pairs={{0,2},{1,3},{2,0},{3,1},{4,6},{5,7},{6,4},{7,5},{8,10},{9,11},{10,... | collective-permute-start | bytes 442376 | tf_op jit(solution)/shard_map/ppermute | solution.py:626
  136.7 4.8 %collective-permute-start.11 = (bf16[144,256]{1,0:T(8,128)(2,1)S(1)}, bf16[144,256]{1,0:T(8,128)(2,1)S(1)}, u32[]{:S(2)}, u32[]{:S(2)}) collective-permute-start(bf16[144,256]{1,0:T(8,128)(2,1)S(1)} %get-tuple-element.70), channel_id=1, source_target_pairs={{0,4},{1,5},{2,6},{3,7},{4,0},{5,1},{6,2},{7,3},{8,12},{9,13},{10,... | collective-permute-start | bytes 221192 | tf_op jit(solution)/shard_map/ppermute | solution.py:626
  137.8 4.4 %collective-permute-start.12 = (bf16[144,256]{1,0:T(8,128)(2,1)S(1)}, bf16[144,256]{1,0:T(8,128)(2,1)S(1)}, u32[]{:S(2)}, u32[]{:S(2)}) collective-permute-start(bf16[144,256]{1,0:T(8,128)(2,1)S(1)} %get-tuple-element.72), channel_id=1, source_target_pairs={{0,2},{1,3},{2,0},{3,1},{4,6},{5,7},{6,4},{7,5},{8,10},{9,11},{10,... | collective-permute-start | bytes 221192 | tf_op jit(solution)/shard_map/ppermute | solution.py:626
  142.2 11.1 %collective-permute-start.13 = (bf16[288,256]{1,0:T(8,128)(2,1)S(1)}, bf16[288,256]{1,0:T(8,128)(2,1)S(1)}, u32[]{:S(2)}, u32[]{:S(2)}) collective-permute-start(bf16[288,256]{1,0:T(8,128)(2,1)S(1)} %shard_map.199.refs_0_), channel_id=1, source_target_pairs={{0,8},{8,0},{16,24},{24,16},{1,9},{9,1},{17,25},{25,17},{2,10},{10... | collective-permute-start | bytes 442376 | tf_op jit(solution)/shard_map/ppermute | solution.py:626
  153.3 11.9 %collective-permute-start.14 = (bf16[288,256]{1,0:T(8,128)(2,1)S(1)}, bf16[288,256]{1,0:T(8,128)(2,1)S(1)}, u32[]{:S(2)}, u32[]{:S(2)}) collective-permute-start(bf16[288,256]{1,0:T(8,128)(2,1)S(1)} %shard_map.200.refs_0_), channel_id=1, source_target_pairs={{0,16},{8,24},{16,0},{24,8},{1,17},{9,25},{17,1},{25,9},{2,18},{10... | collective-permute-start | bytes 442376 | tf_op jit(solution)/shard_map/ppermute | solution.py:626
  154.0 12.7 %all-to-all-start.3 = ((bf16[32,8,256]{2,1,0:T(8,128)(2,1)}), bf16[32,8,256]{2,1,0:T(8,128)(2,1)S(1)}, u32[]{:S(2)}, u32[]{:S(2)}) async-start(bf16[32,8,256]{2,1,0:T(8,128)(2,1)} %bitcast.19), calls=%async_computation.3 | async-start | bytes 262144 | tf_op jit(solution)/shard_map/all_to_all | solution.py:685
  158.5 6.8 %collective-permute-start.4 = (bf16[64,256]{1,0:T(8,128)(2,1)S(1)}, bf16[64,256]{1,0:T(8,128)(2,1)S(1)}, u32[]{:S(2)}, u32[]{:S(2)}) collective-permute-start(bf16[64,256]{1,0:T(8,128)(2,1)S(1)} %get-tuple-element.57), channel_id=1, source_target_pairs={{0,8},{8,0},{16,24},{24,16},{1,9},{9,1},{17,25},{25,17},{2,10},{10... | collective-permute-start | bytes 98312 | tf_op jit(solution)/shard_map/ppermute | solution.py:622
  160.3 5.0 %collective-permute-start.5 = (bf16[64,256]{1,0:T(8,128)(2,1)S(1)}, bf16[64,256]{1,0:T(8,128)(2,1)S(1)}, u32[]{:S(2)}, u32[]{:S(2)}) collective-permute-start(bf16[64,256]{1,0:T(8,128)(2,1)S(1)} %get-tuple-element.58), channel_id=1, source_target_pairs={{8,16},{16,8},{9,17},{17,9},{10,18},{18,10},{11,19},{19,11},{12,20... | collective-permute-start | bytes 98312 | tf_op jit(solution)/shard_map/ppermute | solution.py:622
  165.3 5.9 %collective-permute-start.15 = (bf16[288,256]{1,0:T(8,128)(2,1)S(1)}, bf16[288,256]{1,0:T(8,128)(2,1)S(1)}, u32[]{:S(2)}, u32[]{:S(2)}) collective-permute-start(bf16[288,256]{1,0:T(8,128)(2,1)S(1)} %shard_map.201.refs_1_), channel_id=1, source_target_pairs={{0,4},{1,5},{2,6},{3,7},{4,0},{5,1},{6,2},{7,3},{8,12},{9,13},{10,... | collective-permute-start | bytes 442376 | tf_op jit(solution)/shard_map/ppermute | solution.py:626
  171.2 13.6 %collective-permute-start.16 = (bf16[576,256]{1,0:T(8,128)(2,1)S(1)}, bf16[576,256]{1,0:T(8,128)(2,1)S(1)}, u32[]{:S(2)}, u32[]{:S(2)}) collective-permute-start(bf16[576,256]{1,0:T(8,128)(2,1)S(1)} %shard_map.203.refs_1_), channel_id=1, source_target_pairs={{0,2},{1,3},{2,0},{3,1},{4,6},{5,7},{6,4},{7,5},{8,10},{9,11},{10,... | collective-permute-start | bytes 884744 | tf_op jit(solution)/shard_map/ppermute | solution.py:626
  173.2 11.7 %all-to-all-start.4 = ((bf16[32,8,256]{2,1,0:T(8,128)(2,1)}), bf16[32,8,256]{2,1,0:T(8,128)(2,1)S(1)}, u32[]{:S(2)}, u32[]{:S(2)}) async-start(bf16[32,8,256]{2,1,0:T(8,128)(2,1)} %bitcast.21), calls=%async_computation.4 | async-start | bytes 262144 | tf_op jit(solution)/shard_map/all_to_all | solution.py:685
  176.6 1.3 collective-permute-start.6
  177.0 1.0 collective-permute-start.7
  184.9 4.5 %collective-permute-start.17 = (bf16[1152,256]{1,0:T(8,128)(2,1)S(1)}, bf16[1152,256]{1,0:T(8,128)(2,1)S(1)}, u32[]{:S(2)}, u32[]{:S(2)}) collective-permute-start(bf16[1152,256]{1,0:T(8,128)(2,1)S(1)} %shard_map.204.refs_1_), channel_id=1, source_target_pairs={{0,1},{1,0},{2,3},{3,2},{4,5},{5,4},{6,7},{7,6},{8,9},{9,8},{10,11... | collective-permute-start | bytes 1769480 | tf_op jit(solution)/shard_map/ppermute | solution.py:626
  (11 other events, 289.3 us)
